TPU v7x, 32 devices: a whole 2x2x4 slice. The times are simulated.
32 devices in a mesh: ctx: 8 (over y, x, core), tp: 4 (over z).
Axes of the slice: x: 2, y: 2, z: 4, core: 2. Of those that a mesh axis runs over, the one named last changes fastest.
Arguments:
- queries: float32 [2048, 2048], P('ctx', 'tp'), may hold values from -6 to 6
- key_vectors: float32 [2048, 2048], P('ctx', 'tp'), may hold values from -6 to 6
- values: float32 [2048, 4096], P('ctx', 'tp'), may hold values from -6 to 6
- decays: float32 [32, 2048], P('tp', 'ctx'), may hold values from 0.5 to 0.99995
- strengths: float32 [32, 2048], P('tp', 'ctx'), may hold values from 0.0001 to 0.95
- out_gate: float32 [2048, 4096], P('ctx', 'tp'), may hold values from -6 to 6
- norm_gain: float32 [128], replicated, may hold values from 0.5 to 1.5
- out_weight: float32 [4096, 2048], P('tp'), may hold values from -0.09375 to 0.09375
Outputs:
- layer_out: float32 [2048, 2048], P(('ctx', 'tp'))
All inputs are finite; a program needn't handle non-finite values.
Results may differ from a plain program's by a relative error of at most 0.0003.
Values sent between devices are 32-bit elements; how exact they have to be, the bound alone decides.
No kernel may reach another device: no remote copies, remote signals or barrier semaphores. Data moves between devices by JAX's collectives and lax.ppermute only.
A program may use at most 128 MiB of HBM per device.

v0:
```python
import jax
import jax.numpy as jnp
from jax import lax
from jax.sharding import PartitionSpec as P

DK = 128
DV = 128
GROUP = 64


TOP_PRECISION = lax.Precision.HIGHEST


def shifted(value, axis, steps):
    count = lax.axis_size(axis)
    leading, last = (max(0, -steps), min(count, count - steps))
    return lax.ppermute(value, axis, [(source, source + steps) for source in range(leading, last)])


def unit_heads(matrix, nheads, hwidth):
    shaped = matrix.reshape(matrix.shape[0], nheads, hwidth)
    return shaped * lax.rsqrt(jnp.sum(shaped * shaped, axis=-1, keepdims=True) + 1e-06)


def group_pieces(q_unit, k_unit, value_rows, decay_rows, strength_rows, block_len):
    tokens_here, key_heads, key_width = k_unit.shape
    value_heads = value_rows.shape[1]
    value_width = value_rows.shape[2]
    repeat = value_heads // key_heads
    blocks = tokens_here // block_len

    def by_head(tensor, width_now):
        return tensor.transpose(1, 0, 2).reshape(tensor.shape[1], blocks, block_len, width_now)

    queries_h = jnp.repeat(by_head(q_unit, key_width), repeat, axis=0) * key_width ** (-0.5)
    keys_h = jnp.repeat(by_head(k_unit, key_width), repeat, axis=0)
    values_h = by_head(value_rows, value_width)
    cumlog = jnp.cumsum(jnp.log(decay_rows).reshape(value_heads, blocks, block_len), axis=-1)
    weights_b = strength_rows.reshape(value_heads, blocks, block_len)
    row_index = lax.broadcasted_iota(jnp.int32, (block_len, block_len), 0)
    col_index = lax.broadcasted_iota(jnp.int32, (block_len, block_len), 1)
    strict = row_index > col_index
    inclusive = row_index >= col_index
    spread = cumlog[..., :, None] - cumlog[..., None, :]
    damp_strict = jnp.where(strict, jnp.exp(jnp.where(strict, spread, 0.0)), 0.0)
    damp_incl = jnp.where(inclusive, jnp.exp(jnp.where(inclusive, spread, 0.0)), 0.0)
    gram = jnp.einsum("hnid,hnjd->hnij", keys_h, keys_h, precision=TOP_PRECISION)
    lower = weights_b[..., :, None] * gram * damp_strict
    identity = jnp.eye(block_len, dtype=jnp.float32)
    inverse = identity - lower
    power = lower
    for level in range(block_len.bit_length() - 2):
        power = jnp.einsum("hnij,hnjk->hnik", power, power, precision=TOP_PRECISION)
        inverse = jnp.einsum("hnij,hnjk->hnik", inverse, identity + power, precision=TOP_PRECISION)
    scaled_keys = (weights_b * jnp.exp(cumlog))[..., None] * keys_h
    w_fac = jnp.einsum("hnij,hnjd->hnid", inverse, scaled_keys, precision=TOP_PRECISION)
    update_factor = jnp.einsum(
        "hnij,hnjd->hnid", inverse, weights_b[..., None] * values_h, precision=TOP_PRECISION
    )
    scores = jnp.einsum("hnid,hnjd->hnij", queries_h, keys_h, precision=TOP_PRECISION) * damp_incl
    q_decayed = jnp.exp(cumlog)[..., None] * queries_h
    k_ending = jnp.exp(cumlog[..., -1:] - cumlog)[..., None] * keys_h
    end_decay = jnp.exp(cumlog[..., -1])
    return (w_fac, update_factor, scores, q_decayed, k_ending, end_decay)


def block_outputs(states, w_fac, update_factor, scores, q_decayed):
    fresh = update_factor - jnp.einsum("hnid,hnde->hnie", w_fac, states, precision=TOP_PRECISION)
    core = jnp.einsum("hnid,hnde->hnie", q_decayed, states, precision=TOP_PRECISION)
    core = core + jnp.einsum("hnij,hnje->hnie", scores, fresh, precision=TOP_PRECISION)
    return (core, fresh)


def gated_norm(core, out_gate, norm_gain):
    scaled = core * lax.rsqrt(jnp.mean(core * core, axis=-1, keepdims=True) + 1e-06) * norm_gain
    return scaled.reshape(core.shape[0], -1) * jax.nn.silu(out_gate)


def matmul_heads(left_mat, right_mat):
    return jnp.einsum("hde,hef->hdf", left_mat, right_mat, precision=TOP_PRECISION)


def per_device(queries, key_vectors, values, decays, strengths, out_gate, norm_gain, out_weight):
    tok_local = queries.shape[0]
    key_heads = queries.shape[1] // DK
    value_heads = values.shape[1] // DV
    q_unit = unit_heads(queries, key_heads, DK)
    k_unit = unit_heads(key_vectors, key_heads, DK)
    value_rows = values.reshape(tok_local, value_heads, DV)
    w_fac, update_factor, scores, q_dec, key_final, end_decay = group_pieces(
        q_unit, k_unit, value_rows, decays, strengths, GROUP
    )
    eye_key = jnp.eye(DK, dtype=jnp.float32)
    state_transitions = end_decay[..., None, None] * eye_key
    state_transitions = state_transitions - jnp.einsum(
        "gwpc,gwpv->gwcv", key_final, w_fac, precision=TOP_PRECISION
    )
    added_terms = jnp.einsum("gwpc,gwpv->gwcv", key_final, update_factor, precision=TOP_PRECISION)

    def compose(running, step_pair):
        prefix_map, prefix_state = running
        step_map, step_add = step_pair
        updated = (
            matmul_heads(step_map, prefix_map),
            matmul_heads(step_map, prefix_state) + step_add,
        )
        return (updated, (prefix_map, prefix_state))

    start_map = jnp.broadcast_to(eye_key, (value_heads, DK, DK))
    start_state = jnp.zeros((value_heads, DK, DV), jnp.float32)
    device_pair, entries = lax.scan(
        compose,
        (start_map, start_state),
        (state_transitions.transpose(1, 0, 2, 3), added_terms.transpose(1, 0, 2, 3)),
    )
    device_map, device_add = device_pair
    entry_maps, entry_adds = entries

    def relay(step_index, entering):
        leaving = matmul_heads(device_map, entering) + device_add
        return shifted(leaving, "ctx", 1)

    incoming = lax.fori_loop(0, lax.axis_size("ctx") - 1, relay, start_state)
    states = jnp.einsum(
        "nhde,hef->hndf", entry_maps, incoming, precision=TOP_PRECISION
    ) + entry_adds.transpose(1, 0, 2, 3)
    core, fresh = block_outputs(states, w_fac, update_factor, scores, q_dec)
    core = core.reshape(value_heads, tok_local, DV).transpose(1, 0, 2)
    normed = gated_norm(core, out_gate, norm_gain)
    return lax.psum_scatter(
        jnp.dot(normed, out_weight, precision=TOP_PRECISION, preferred_element_type=jnp.float32),
        "tp",
        scatter_dimension=0,
        tiled=True,
    )


def solution(mesh):
    return jax.shard_map(
        per_device,
        mesh=mesh,
        in_specs=(
            P("ctx", "tp"),
            P("ctx", "tp"),
            P("ctx", "tp"),
            P("tp", "ctx"),
            P("tp", "ctx"),
            P("ctx", "tp"),
            P(),
            P("tp", None),
        ),
        out_specs=P(("ctx", "tp"), None),
        check_vma=False,
    )
```

profile of v0, /device:TPU:0, one launch (start us, length us, event | category | flops | bytes accessed | tf_op | source)
XLA Modules:
  0.0 229.2 jit_solution(16754428719557719238)
XLA Ops:
  8.5 1.2 reshape.97
  11.8 1.9 fusion.11
  13.7 1.2 fusion.46
  14.9 1.2 fusion.47
  16.1 1.2 fusion.33
  17.3 1.2 fusion.48
  18.5 1.2 fusion.31
  19.7 1.2 fusion.49
  20.9 1.2 fusion.29
  22.1 1.5 convolution_add_fusion.3
  23.6 1.2 fusion.27
  25.2 1.2 fusion.50
  26.5 1.2 fusion.25
  28.3 2.2 fusion.51
  30.6 4.8 %convolution_bitcast_fusion = f32[4,8,128,128]{3,2,0,1:T(8,128)} fusion(f32[8,4,64,128]{3,2,1,0:T(8,128)S(1)} %get-tuple-element.137, f32[8,4,64,128]{3,2,1,0:T(8,128)S(1)} %fusion.25), kind=kOutput, calls=%fused_computation.17 | convolution fusion | flops 402653184 | bytes 4194304 | tf_op jit(solution)/shard_map/gwpc,gwpv->gwcv/dot_general | solution.py:98
  35.5 15.6 %bitcast_subtract_fusion = f32[4,8,128,128]{3,2,0,1:T(8,128)S(1)} fusion(f32[8,4,64,128]{3,2,1,0:T(8,128)} %copy-done.8, f32[8,4,64,128]{3,2,1,0:T(8,128)S(1)} %copy-done.4, f32[128,128]{1,0:T(8,128)S(1)} %fusion.43, f32[4,8]{0,1:T(8,128)S(1)} %copy.29), kind=kOutput, calls=%fused_computation.16 | convolution fusion | flops 403701760 | bytes 4259968 | tf_op jit(solution)/shard_map/gwpc,gwpv->gwcv/dot_general | solution.py:95
  51.1 14.2 %while.28 = (s32[]{:T(128)}, f32[8,128,128]{2,1,0:T(8,128)S(1)}, f32[8,128,128]{2,1,0:T(8,128)S(1)}, f32[4,8,128,128]{3,2,0,1:T(8,128)}, f32[4,8,128,128]{3,2,0,...) while((s32[]{:T(128)}, f32[8,128,128]{2,1,0:T(8,128)S(1)}, ...), condition=%wide.region_4.5_spmd.clone, body=%wide.region_3.4_spmd.clone.sunk | while | flops 403046400 | bytes 7865964 | solution.py:111
  51.2 1.1 bitcast_dynamic-update-slice_fusion.3
  52.3 1.7 convolution_add_fusion.7
  54.8 1.1 bitcast_dynamic-update-slice_fusion.3
  55.9 1.7 convolution_add_fusion.7
  58.3 1.1 bitcast_dynamic-update-slice_fusion.3
  59.4 1.7 convolution_add_fusion.7
  61.9 1.1 bitcast_dynamic-update-slice_fusion.3
  63.0 1.7 convolution_add_fusion.7
  65.4 71.6 %while.27 = (s32[]{:T(128)}, f32[8,128,128]{2,1,0:T(8,128)S(1)}, f32[8,128,128]{2,1,0:T(8,128)S(1)}, f32[8,128,128]{2,1,0:T(8,128)S(1)}, s32[]{:T(128)}) while((s32[]{:T(128)}, f32[8,128,128]{2,1,0:T(8,128)S(1)}, f32[8,128,128]{2,1,0:T(8,128)S(1)}, f32[8,128,128]{2,1,0:T(8,128)S(1)}, s32[]{:T(128)}) %tuple.47), condition=%wide.region_6.7_spmd, body=%wide.region_5.6_spmd.sunk | while | flops 201457664 | bytes 4194405 | solution.py:123
  66.0 2.4 %collective-permute-start = (f32[8,128,128]{2,1,0:T(8,128)S(1)}, f32[8,128,128]{2,1,0:T(8,128)S(1)}, u32[]{:S(2)}, u32[]{:S(2)}) collective-permute-start(f32[8,128,128]{2,1,0:T(8,128)S(1)} %convolution_add_fusion.6), channel_id=1, source_target_pairs={{0,4},{4,8},{8,12},{12,16},{16,20},{20,24},{24,28},{1,5},{5,9},{9,... | collective-permute-start | bytes 1572872 | tf_op jit(solution)/shard_map/while/body/eval_jaxpr/ppermute | solution.py:17
  68.4 1.5 collective-permute-done
  70.6 9.1 %collective-permute-start = (f32[8,128,128]{2,1,0:T(8,128)S(1)}, f32[8,128,128]{2,1,0:T(8,128)S(1)}, u32[]{:S(2)}, u32[]{:S(2)}) collective-permute-start(f32[8,128,128]{2,1,0:T(8,128)S(1)} %convolution_add_fusion.6), channel_id=1, source_target_pairs={{0,4},{4,8},{8,12},{12,16},{16,20},{20,24},{24,28},{1,5},{5,9},{9,... | collective-permute-start | bytes 1572872 | tf_op jit(solution)/shard_map/while/body/eval_jaxpr/ppermute | solution.py:17
  79.7 1.5 collective-permute-done
  81.8 9.0 %collective-permute-start = (f32[8,128,128]{2,1,0:T(8,128)S(1)}, f32[8,128,128]{2,1,0:T(8,128)S(1)}, u32[]{:S(2)}, u32[]{:S(2)}) collective-permute-start(f32[8,128,128]{2,1,0:T(8,128)S(1)} %convolution_add_fusion.6), channel_id=1, source_target_pairs={{0,4},{4,8},{8,12},{12,16},{16,20},{20,24},{24,28},{1,5},{5,9},{9,... | collective-permute-start | bytes 1572872 | tf_op jit(solution)/shard_map/while/body/eval_jaxpr/ppermute | solution.py:17
  90.9 1.5 collective-permute-done
  93.0 9.0 %collective-permute-start = (f32[8,128,128]{2,1,0:T(8,128)S(1)}, f32[8,128,128]{2,1,0:T(8,128)S(1)}, u32[]{:S(2)}, u32[]{:S(2)}) collective-permute-start(f32[8,128,128]{2,1,0:T(8,128)S(1)} %convolution_add_fusion.6), channel_id=1, source_target_pairs={{0,4},{4,8},{8,12},{12,16},{16,20},{20,24},{24,28},{1,5},{5,9},{9,... | collective-permute-start | bytes 1572872 | tf_op jit(solution)/shard_map/while/body/eval_jaxpr/ppermute | solution.py:17
  102.0 1.5 collective-permute-done
  104.2 9.0 %collective-permute-start = (f32[8,128,128]{2,1,0:T(8,128)S(1)}, f32[8,128,128]{2,1,0:T(8,128)S(1)}, u32[]{:S(2)}, u32[]{:S(2)}) collective-permute-start(f32[8,128,128]{2,1,0:T(8,128)S(1)} %convolution_add_fusion.6), channel_id=1, source_target_pairs={{0,4},{4,8},{8,12},{12,16},{16,20},{20,24},{24,28},{1,5},{5,9},{9,... | collective-permute-start | bytes 1572872 | tf_op jit(solution)/shard_map/while/body/eval_jaxpr/ppermute | solution.py:17
  113.2 1.5 collective-permute-done
  115.3 9.0 %collective-permute-start = (f32[8,128,128]{2,1,0:T(8,128)S(1)}, f32[8,128,128]{2,1,0:T(8,128)S(1)}, u32[]{:S(2)}, u32[]{:S(2)}) collective-permute-start(f32[8,128,128]{2,1,0:T(8,128)S(1)} %convolution_add_fusion.6), channel_id=1, source_target_pairs={{0,4},{4,8},{8,12},{12,16},{16,20},{20,24},{24,28},{1,5},{5,9},{9,... | collective-permute-start | bytes 1572872 | tf_op jit(solution)/shard_map/while/body/eval_jaxpr/ppermute | solution.py:17
  124.3 1.5 collective-permute-done
  126.5 9.0 %collective-permute-start = (f32[8,128,128]{2,1,0:T(8,128)S(1)}, f32[8,128,128]{2,1,0:T(8,128)S(1)}, u32[]{:S(2)}, u32[]{:S(2)}) collective-permute-start(f32[8,128,128]{2,1,0:T(8,128)S(1)} %convolution_add_fusion.6), channel_id=1, source_target_pairs={{0,4},{4,8},{8,12},{12,16},{16,20},{20,24},{24,28},{1,5},{5,9},{9,... | collective-permute-start | bytes 1572872 | tf_op jit(solution)/shard_map/while/body/eval_jaxpr/ppermute | solution.py:17
  135.5 1.5 collective-permute-done
  137.0 4.4 %bitcast_add_fusion = f32[8,4,128,128]{3,2,1,0:T(8,128)S(1)} fusion(f32[4,8,128,128]{3,2,0,1:T(8,128)} %get-tuple-element.71, f32[4,8,128,128]{3,2,0,1:T(8,128)} %get-tuple-element.67, f32[8,128,128]{2,1,0:T(8,128)S(1)} %get-tuple-element.70), kind=kOutput, calls=%fused_computation.15 | convolution fusion | flops 805830656 | bytes 6815744 | tf_op jit(solution)/shard_map/nhde,hef->hndf/dot_general | solution.py:124
  141.4 2.1 convolution_subtract_fusion
  144.9 1.2 copy-done.1
  146.0 2.1 fusion.52
  148.2 1.8 convolution_multiply_fusion
  150.0 1.2 convolution_add_fusion.2
  152.5 11.1 %fusion.16 = f32[256,2048]{1,0:T(8,128)} fusion(f32[1024,2048]{1,0:T(8,128)} %param.19, f32[256,1024]{1,0:T(8,128)S(1)} %copy-done.9, f32[256,8,128]{2,0,1:T(8,128)S(1)} %fusion.19), kind=kOutput, calls=%fused_computation.33 | convolution fusion | flops 6443761664 | bytes 12582912 | tf_op jit(solution)/shard_map/dot_general | solution.py:131
  163.6 58.6 %reduce-scatter.2.cloned.1.call-done = f32[64,2048]{1,0:T(8,128)} async-done(((f32[256,2048]{1,0:T(8,128)}), f32[64,2048]{1,0:T(8,128)}) %reduce-scatter.2.cloned.1.call-update) | async-done | bytes 524304 | tf_op jit(solution)/shard_map/reduce_scatter | solution.py:130
  (87 shorter events, 15.0 us)
Async XLA Ops:
  6.5 215.6 %reduce-scatter.2.cloned.1.call-start = ((), (), s32[]{:S(2)}) async-start(), calls=%async_computation.1 | async-start | bytes 2621440 | tf_op jit(solution)/shard_map/reduce_scatter | solution.py:130
  8.5 2.0 copy-start.12
  10.8 1.0 copy-start.2
  23.6 1.2 copy-start.10
  27.7 3.0 %copy-start.6 = (f32[8,4,64,128]{3,2,1,0:T(8,128)}, f32[8,4,64,128]{3,2,1,0:T(8,128)S(1)}, u32[]{:S(2)}) copy-start(f32[8,4,64,128]{3,2,1,0:T(8,128)S(1)} %fusion.25) | copy-start | bytes 3145732
  28.3 2.3 %copy-start.8 = (f32[8,4,64,128]{3,2,1,0:T(8,128)}, f32[8,4,64,128]{3,2,1,0:T(8,128)S(1)}, u32[]{:S(2)}) copy-start(f32[8,4,64,128]{3,2,1,0:T(8,128)S(1)} %get-tuple-element.137) | copy-start | bytes 3145732
  30.6 4.8 %copy-start.4 = (f32[8,4,64,128]{3,2,1,0:T(8,128)S(1)}, f32[8,4,64,128]{3,2,1,0:T(8,128)}, u32[]{:S(2)}) copy-start(f32[8,4,64,128]{3,2,1,0:T(8,128)} %fusion.51) | copy-start | bytes 3145732
  66.0 3.9 %collective-permute-start = (f32[8,128,128]{2,1,0:T(8,128)S(1)}, f32[8,128,128]{2,1,0:T(8,128)S(1)}, u32[]{:S(2)}, u32[]{:S(2)}) collective-permute-start(f32[8,128,128]{2,1,0:T(8,128)S(1)} %convolution_add_fusion.6), channel_id=1, source_target_pairs={{0,4},{4,8},{8,12},{12,16},{16,20},{20,24},{24,28},{1,5},{5,9},{9,... | collective-permute-start | bytes 1572872 | tf_op jit(solution)/shard_map/while/body/eval_jaxpr/ppermute | solution.py:17
  70.6 10.6 %collective-permute-start = (f32[8,128,128]{2,1,0:T(8,128)S(1)}, f32[8,128,128]{2,1,0:T(8,128)S(1)}, u32[]{:S(2)}, u32[]{:S(2)}) collective-permute-start(f32[8,128,128]{2,1,0:T(8,128)S(1)} %convolution_add_fusion.6), channel_id=1, source_target_pairs={{0,4},{4,8},{8,12},{12,16},{16,20},{20,24},{24,28},{1,5},{5,9},{9,... | collective-permute-start | bytes 1572872 | tf_op jit(solution)/shard_map/while/body/eval_jaxpr/ppermute | solution.py:17
  81.8 10.5 %collective-permute-start = (f32[8,128,128]{2,1,0:T(8,128)S(1)}, f32[8,128,128]{2,1,0:T(8,128)S(1)}, u32[]{:S(2)}, u32[]{:S(2)}) collective-permute-start(f32[8,128,128]{2,1,0:T(8,128)S(1)} %convolution_add_fusion.6), channel_id=1, source_target_pairs={{0,4},{4,8},{8,12},{12,16},{16,20},{20,24},{24,28},{1,5},{5,9},{9,... | collective-permute-start | bytes 1572872 | tf_op jit(solution)/shard_map/while/body/eval_jaxpr/ppermute | solution.py:17
  93.0 10.5 %collective-permute-start = (f32[8,128,128]{2,1,0:T(8,128)S(1)}, f32[8,128,128]{2,1,0:T(8,128)S(1)}, u32[]{:S(2)}, u32[]{:S(2)}) collective-permute-start(f32[8,128,128]{2,1,0:T(8,128)S(1)} %convolution_add_fusion.6), channel_id=1, source_target_pairs={{0,4},{4,8},{8,12},{12,16},{16,20},{20,24},{24,28},{1,5},{5,9},{9,... | collective-permute-start | bytes 1572872 | tf_op jit(solution)/shard_map/while/body/eval_jaxpr/ppermute | solution.py:17
  104.2 10.5 %collective-permute-start = (f32[8,128,128]{2,1,0:T(8,128)S(1)}, f32[8,128,128]{2,1,0:T(8,128)S(1)}, u32[]{:S(2)}, u32[]{:S(2)}) collective-permute-start(f32[8,128,128]{2,1,0:T(8,128)S(1)} %convolution_add_fusion.6), channel_id=1, source_target_pairs={{0,4},{4,8},{8,12},{12,16},{16,20},{20,24},{24,28},{1,5},{5,9},{9,... | collective-permute-start | bytes 1572872 | tf_op jit(solution)/shard_map/while/body/eval_jaxpr/ppermute | solution.py:17
  115.3 10.5 %collective-permute-start = (f32[8,128,128]{2,1,0:T(8,128)S(1)}, f32[8,128,128]{2,1,0:T(8,128)S(1)}, u32[]{:S(2)}, u32[]{:S(2)}) collective-permute-start(f32[8,128,128]{2,1,0:T(8,128)S(1)} %convolution_add_fusion.6), channel_id=1, source_target_pairs={{0,4},{4,8},{8,12},{12,16},{16,20},{20,24},{24,28},{1,5},{5,9},{9,... | collective-permute-start | bytes 1572872 | tf_op jit(solution)/shard_map/while/body/eval_jaxpr/ppermute | solution.py:17
  126.5 10.5 %collective-permute-start = (f32[8,128,128]{2,1,0:T(8,128)S(1)}, f32[8,128,128]{2,1,0:T(8,128)S(1)}, u32[]{:S(2)}, u32[]{:S(2)}) collective-permute-start(f32[8,128,128]{2,1,0:T(8,128)S(1)} %convolution_add_fusion.6), channel_id=1, source_target_pairs={{0,4},{4,8},{8,12},{12,16},{16,20},{20,24},{24,28},{1,5},{5,9},{9,... | collective-permute-start | bytes 1572872 | tf_op jit(solution)/shard_map/while/body/eval_jaxpr/ppermute | solution.py:17
  137.0 4.4 %copy-start.5 = (f32[8,4,64,128]{3,2,1,0:T(8,128)S(1)}, f32[8,4,64,128]{3,2,1,0:T(8,128)}, u32[]{:S(2)}) copy-start(f32[8,4,64,128]{3,2,1,0:T(8,128)} %fusion.51) | copy-start | bytes 3145732
  137.0 4.4 %copy-start.7 = (f32[8,4,64,128]{3,2,1,0:T(8,128)S(1)}, f32[8,4,64,128]{3,2,1,0:T(8,128)}, u32[]{:S(2)}) copy-start(f32[8,4,64,128]{3,2,1,0:T(8,128)} %copy-done.6) | copy-start | bytes 3145732
  141.4 2.1 copy-start
  141.4 2.2 copy-start.11
  144.4 1.6 copy-start.1
  146.0 2.1 copy-start.3
  150.0 1.6 copy-start.13
  151.2 1.2 copy-start.9
Sparse Core Ops, SparseCore 0:
  163.7 58.4 reduce-scatter.1
where the time goes:
time: 233 us; the launch traced here: 229 us
  matrix products  74.5 us (32%)
  waiting for transfers between devices  69 us (30%)
  starting transfers between devices  56.5 us (24%)
  between operations  14.1 us (6%)
  other arithmetic  8.44 us (4%)
  local copies, waits for them, and re-layouts  6.25 us (3%)
    reduce_scatter x1, waiting for transfers between devices, per_device(): lax.psum_scatter(jnp.dot(normed, out_weight, precision=TOP_PRECISION, pre...  58.6 us
    ppermute x7, starting transfers between devices, shifted(): lax.ppermute(value, axis, [(source, source + steps) for source in range(l...  56.5 us
    dot_general x1, matrix products, per_device(): jnp.einsum('gwpc,gwpv->gwcv', key_final, w_fac, precision=TOP_PRECISION)  15.6 us
    dot_general x15, matrix products, matmul_heads(): jnp.einsum('hde,hef->hdf', left_mat, right_mat, precision=TOP_PRECISION)  13.8 us
    dot_general x1, matrix products, per_device(): jnp.dot(normed, out_weight, precision=TOP_PRECISION, preferred_element_ty...  11.1 us
    ppermute x7, waiting for transfers between devices, shifted(): lax.ppermute(value, axis, [(source, source + steps) for source in range(l...  10.4 us
    dot_general x5, matrix products, group_pieces(): power = jnp.einsum('hnij,hnjk->hnik', power, power, precision=TOP_PRECISION)  6.27 us
    dot_general x5, matrix products, group_pieces(): jnp.einsum('hnij,hnjk->hnik', inverse, identity + power, precision=TOP_PR...  5.98 us
  transfers between devices with their start and end apart: 8, of which 8 were waited for; matrix products, arithmetic and copies ran while one was open for 0% of the time, Pallas kernels for 0%

commit v1 on v0

v1 whole, which is shorter than its diff:
```python
import functools
import typing

import jax
import jax.numpy as jnp
from jax import lax
from jax.experimental import pallas as pl
from jax.experimental.pallas import tpu as pltpu
from jax.sharding import PartitionSpec as P

DK = 128
DV = 128
BLOCK = 128
SMALL = 32
BAND = 256
WEIGHT_ROWS = 128
MOST_VMEM = 56
SCAN_VMEM = 51
WEIGHT_VMEM = 40
FIRST_VMEM = 24
LATER_VMEM = 24
HEADS_AT_ONCE = 4
EPS = 1e-06


HBM = pl.BlockSpec(memory_space=pltpu.HBM)
VMEM = pl.BlockSpec(memory_space=pltpu.VMEM)


def dot(left, right):
    return jnp.dot(left, right, precision=lax.Precision.HIGH, preferred_element_type=jnp.float32)


def dot_transposed(left, right):
    return lax.dot_general(
        left,
        right,
        (((1,), (1,)), ((), ())),
        precision=lax.Precision.HIGH,
        preferred_element_type=jnp.float32,
    )


def iota(shape, dim):
    return lax.broadcasted_iota(jnp.int32, shape, dim)


def unit(rows):
    return rows * lax.rsqrt(jnp.sum(rows * rows, axis=-1, keepdims=True) + EPS)


def cumulative_logs(decays):
    tokens = decays.shape[1]
    upto = jnp.where(iota((tokens, tokens), 0) <= iota((tokens, tokens), 1), 1.0, 0.0)
    rows = jnp.dot(
        jnp.log(decays), upto, precision=lax.Precision.HIGHEST, preferred_element_type=jnp.float32
    )
    return rows, rows.T


def spread_diagonal(packed):
    size = packed.shape[0]
    place = iota(packed.shape, 1) // size
    return jnp.concatenate(
        [jnp.where(place == block, packed, 0.0) for block in range(BLOCK // size)], axis=0
    )


def lower_inverses(lowers):
    row = iota((SMALL, BLOCK), 0)
    lane = iota((SMALL, BLOCK), 1)
    column = lane % SMALL
    place = lane // SMALL
    eye = jnp.where(row == column, 1.0, 0.0)
    in_8 = row // 8 == column // 8
    in_16 = row // 16 == column // 16
    packed = []
    for lower in lowers:
        blocks = jnp.zeros((SMALL, BLOCK), jnp.float32)
        for block in range(BLOCK // SMALL):
            blocks = jnp.where(place == block, lower[block * SMALL : (block + 1) * SMALL], blocks)
        packed.append(blocks)
    nil = [jnp.where(in_8, blocks, 0.0) for blocks in packed]
    nil_2 = [dot(n, spread_diagonal(n)) for n in nil]
    wide_2 = [spread_diagonal(n) for n in nil_2]
    start = [eye - n for n in nil]
    nil_4 = [dot(n, w) for n, w in zip(nil_2, wide_2)]
    start = [s + dot(s, w) for s, w in zip(start, wide_2)]
    inv = [s + dot(s, spread_diagonal(n)) for s, n in zip(start, nil_4)]
    step_16 = [spread_diagonal(jnp.where(in_16 & ~in_8, blocks, 0.0)) for blocks in packed]
    half = [jnp.concatenate([d[8:16], d[24:32]], axis=0) for d in inv]
    half = [dot(h, w) for h, w in zip(half, step_16)]
    half = [dot(h, spread_diagonal(d)) for h, d in zip(half, inv)]
    inv = [
        jnp.concatenate([d[:8], d[8:16] - h[:8], d[16:24], d[24:] - h[8:]], axis=0)
        for d, h in zip(inv, half)
    ]
    step_32 = [spread_diagonal(jnp.where(in_16, 0.0, blocks)) for blocks in packed]
    half = [dot(d[16:], w) for d, w in zip(inv, step_32)]
    half = [dot(h, spread_diagonal(d)) for h, d in zip(half, inv)]
    inv = [jnp.concatenate([d[:16], d[16:] - h], axis=0) for d, h in zip(inv, half)]
    odd = place % 2 == 1
    zeros = jnp.zeros((SMALL, BLOCK), jnp.float32)
    low = [jnp.where(odd, d, 0.0) for d in inv]
    wide = [
        spread_diagonal(jnp.concatenate([jnp.where(odd, 0.0, d), l], axis=0)) for d, l in zip(inv, low)
    ]
    step_64 = [
        spread_diagonal(
            jnp.concatenate(
                [
                    zeros,
                    jnp.where(
                        place == 0, lower[32:64], jnp.where(place == 2, lower[96:128], 0.0)
                    ),
                ],
                axis=0,
            )
        )
        for lower in lowers
    ]
    half = [dot(l, w) for l, w in zip(low, step_64)]
    half = [dot(h, w) for h, w in zip(half, wide)]
    inv = [
        jnp.concatenate([jnp.where(odd, 0.0, d), l - h], axis=0) for d, l, h in zip(inv, low, half)
    ]
    left = iota((64, BLOCK), 1) < 64
    low = [jnp.where(left, 0.0, d) for d in inv]
    wide = [jnp.concatenate([jnp.where(left, d, 0.0), l], axis=0) for d, l in zip(inv, low)]
    step_128 = [
        jnp.concatenate(
            [jnp.zeros((64, BLOCK), jnp.float32), jnp.where(left, lower[64:], 0.0)], axis=0
        )
        for lower in lowers
    ]
    half = [dot(l, w) for l, w in zip(low, step_128)]
    half = [dot(h, w) for h, w in zip(half, wide)]
    return [jnp.concatenate([w[:64], w[64:] - h], axis=0) for w, h in zip(wide, half)]


def block(index):
    return slice(index * BLOCK, (index + 1) * BLOCK)


def fetch(pairs, sems):
    copies = [pltpu.make_async_copy(src, dst, sems.at[i]) for i, (src, dst) in enumerate(pairs)]
    for copy in copies:
        copy.start()
    return copies


def partner(place, swap):
    return lax.axis_index("ctx") ^ place if swap else place


def summary_kernel(decay_hbm, strength_hbm, k_hbm, v_hbm, factor_hbm, *rest, swap):
    *summaries, decay_ref, strength_ref, k_ref, v_ref, sems, factor_ref, summary_ref, out_sems = rest
    copies = fetch(
        [(decay_hbm, decay_ref), (strength_hbm, strength_ref), (k_hbm, k_ref), (v_hbm, v_ref)], sems
    )
    for copy in copies[:3]:
        copy.wait()
    tokens = k_ref.shape[0]
    key_heads = k_ref.shape[1] // DK
    value_heads = v_ref.shape[1] // DV
    repeat = value_heads // key_heads
    blocks = tokens // BLOCK
    rows, columns = cumulative_logs(decay_ref[...])
    strengths = strength_ref[...].T
    strict = iota((BLOCK, BLOCK), 0) > iota((BLOCK, BLOCK), 1)
    eye = jnp.where(iota((BLOCK, DK + DV), 0) == iota((BLOCK, DK + DV), 1), 1.0, 0.0)
    leaving = []
    for first in range(0, value_heads, HEADS_AT_ONCE):
        heads = range(first, min(first + HEADS_AT_ONCE, value_heads))
        keys = {}
        gram = {}
        for key_head in sorted({head // repeat for head in heads}):
            unit_rows = unit(k_ref[:, key_head * DK : (key_head + 1) * DK])
            keys[key_head] = [unit_rows[block(p)] for p in range(blocks)]
            gram[key_head] = {
                (p, r): dot_transposed(keys[key_head][p], keys[key_head][r])
                for p in range(blocks)
                for r in range(p + 1)
            }
        lower = {}
        for head in heads:
            for p in range(blocks):
                at = columns[block(p), head : head + 1]
                weight = strengths[block(p), head : head + 1]
                for r in range(p + 1):
                    spread = at - rows[head : head + 1, block(r)]
                    if p == r:
                        damp = jnp.where(strict, jnp.exp(jnp.where(strict, spread, 0.0)), 0.0)
                    else:
                        damp = jnp.exp(spread)
                    lower[head, p, r] = weight * gram[head // repeat][p, r] * damp
        inverse = lower_inverses([lower[head, p, p] for head in heads for p in range(blocks)])
        inverse = {
            (head, p): inverse[i * blocks + p] for i, head in enumerate(heads) for p in range(blocks)
        }
        if first == 0:
            copies[3].wait()
        factors = {}
        for p in range(blocks):
            for head in heads:
                at = columns[block(p), head : head + 1]
                weight = strengths[block(p), head : head + 1]
                right = jnp.concatenate(
                    [
                        keys[head // repeat][p] * (-weight * jnp.exp(at)),
                        v_ref[block(p), head * DV : (head + 1) * DV] * weight,
                    ],
                    axis=1,
                )
                for r in range(p):
                    right = right - dot(lower[head, p, r], factors[head, r])
                factors[head, p] = dot(inverse[head, p], right)
                factor_ref[head, block(p), :] = factors[head, p]
        flipped = {key_head: [k.T for k in keys[key_head]] for key_head in keys}
        for head in heads:
            last = rows[head : head + 1, tokens - 1 : tokens]
            total = jnp.exp(last) * eye
            for p in range(blocks):
                ending = jnp.exp(last - columns[block(p), head : head + 1])
                total = total + dot(flipped[head // repeat][p], factors[head, p] * ending)
            summary_ref[head] = total
        group = pl.ds(first, len(heads))
        leaving.append(
            pltpu.make_async_copy(
                factor_ref.at[group], factor_hbm.at[group], out_sems.at[len(leaving)]
            )
        )
        leaving[-1].start()
    for place, out_ref in enumerate(summaries):
        out_ref[...] = summary_ref[partner(place, swap)]
    for copy in leaving:
        copy.wait()


def output_kernel(
    decay_hbm,
    q_hbm,
    k_hbm,
    factor_hbm,
    map_hbm,
    decay_ref,
    q_ref,
    k_ref,
    factor_ref,
    sems,
    map_ref,
    out_sems,
):
    copies = fetch(
        [(decay_hbm, decay_ref), (q_hbm, q_ref), (k_hbm, k_ref), (factor_hbm, factor_ref)], sems
    )
    leaving = []
    for copy in copies[:3]:
        copy.wait()
    tokens = q_ref.shape[0]
    key_heads = q_ref.shape[1] // DK
    value_heads = factor_ref.shape[0]
    repeat = value_heads // key_heads
    blocks = tokens // BLOCK
    rows, columns = cumulative_logs(decay_ref[...])
    inclusive = iota((BLOCK, BLOCK), 0) >= iota((BLOCK, BLOCK), 1)
    for key_head in range(key_heads):
        lanes = slice(key_head * DK, (key_head + 1) * DK)
        queries = unit(q_ref[:, lanes]) * DK**-0.5
        keys = unit(k_ref[:, lanes])
        for p in range(blocks):
            scores = [dot_transposed(queries[block(p)], keys[block(r)]) for r in range(p + 1)]
            if key_head == 0 and p == 0:
                copies[3].wait()
            for head in range(key_head * repeat, (key_head + 1) * repeat):
                at = columns[block(p), head : head + 1]
                total = jnp.concatenate(
                    [queries[block(p)] * jnp.exp(at), jnp.zeros((BLOCK, DV), jnp.float32)], axis=1
                )
                for r in range(p + 1):
                    spread = at - rows[head : head + 1, block(r)]
                    if p == r:
                        damp = jnp.where(inclusive, jnp.exp(jnp.where(inclusive, spread, 0.0)), 0.0)
                    else:
                        damp = jnp.exp(spread)
                    total = total + dot(scores[r] * damp, factor_ref[head, block(r), :])
                map_ref[head, block(p), :] = total
        group = pl.ds(key_head * repeat, repeat)
        leaving.append(
            pltpu.make_async_copy(map_ref.at[group], map_hbm.at[group], out_sems.at[key_head])
        )
        leaving[-1].start()
    for copy in leaving:
        copy.wait()


def scan_kernel(held_ref, entry_ref):
    count, held, key_width, width = entry_ref.shape
    for head in range(held):
        state = jnp.zeros((key_width, width), jnp.float32)
        entry_ref[0, head] = state
        for source in range(count - 1):
            added = held_ref[source, head, :, key_width:]
            if source:
                added = added + dot(held_ref[source, head, :, :key_width], state)
            state = added
            entry_ref[source + 1, head] = state


def ordered_scan_kernel(own_hbm, *rest):
    *arrays, held_ref, entry_ref, sems = rest
    count = entry_ref.shape[0]
    held, own_entry_hbm, entries = arrays[: count - 1], arrays[count - 1], arrays[count:]
    here = partner(0, True)
    own = pltpu.make_async_copy(own_hbm, held_ref.at[here], sems.at[0])
    own.start()
    for i, summary in enumerate(held):
        held_ref[partner(i + 1, True)] = summary[...]
    own.wait()
    state = jnp.zeros(entry_ref.shape[1:], jnp.float32)
    entry_ref[0] = state
    for source in range(count - 1):
        added = held_ref[source, :, DK:]
        if source:
            added = added + dot(held_ref[source, :, :DK], state)
        state = added
        entry_ref[source + 1] = state
    own = pltpu.make_async_copy(entry_ref.at[here], own_entry_hbm, sems.at[1])
    own.start()
    for i, entry in enumerate(entries):
        entry[...] = entry_ref[partner(i + 1, True)]
    own.wait()


def split(value):
    high = value.astype(jnp.bfloat16)
    return high, (value - high.astype(jnp.float32)).astype(jnp.bfloat16)


def weight_kernel(weight_ref, parts_ref):
    parts_ref[0], parts_ref[1] = split(weight_ref[...])


def projection_kernel(map_hbm, gate_hbm, gain_ref, parts_ref, own_hbm, *rest, pieces, swap):
    *arrays, map_ref, gate_ref, state_ref, high_ref, low_ref, gate_sems, map_sems, state_sems = rest
    outs = arrays[-len(pieces) :]
    states = arrays[: -len(pieces)]
    heads = state_ref.shape[0]
    rows = outs[0].shape[0]
    blocks = sorted({index for index, _ in pieces})
    own = fetch([(own_hbm, state_ref.at[partner(0, swap.heads)])], state_sems)
    places = []
    for i, index in enumerate(blocks):
        start = (lax.axis_index("tp") ^ index) * rows if swap.rows else index * rows
        places.append((pl.ds(pl.multiple_of(start, rows), rows), pl.ds(i * rows, rows)))
    gates = fetch([(gate_hbm.at[s, :], gate_ref.at[t, :]) for s, t in places], gate_sems)
    maps = fetch(
        [
            (map_hbm.at[head, s, :], map_ref.at[head, t, :])
            for head in range(heads)
            for s, t in places
        ],
        map_sems,
    )
    for i, state in enumerate(states):
        state_ref[partner(i + 1, swap.heads)] = state[...]
    for copy in own + gates:
        copy.wait()
    gain = gain_ref[...]
    for head in range(heads):
        lanes = slice(head * DV, (head + 1) * DV)
        gate = gate_ref[:, lanes]
        factor = gate / (1.0 + jnp.exp(-gate)) * gain
        for copy in maps[head * len(blocks) : (head + 1) * len(blocks)]:
            copy.wait()
        core = map_ref[head, :, DK:] + dot(map_ref[head, :, :DK], state_ref[head])
        scale = lax.rsqrt(jnp.mean(core * core, axis=-1, keepdims=True) + EPS)
        high_ref[:, lanes], low_ref[:, lanes] = split(core * scale * factor)
    total = len(blocks) * rows
    for band in range(0, parts_ref.shape[2], BAND):
        lanes = slice(band, band + BAND)
        both = jnp.concatenate([high_ref[...], low_ref[...]], axis=0)
        sums = jnp.dot(both, parts_ref[0, :, lanes], preferred_element_type=jnp.float32)
        last = jnp.dot(high_ref[...], parts_ref[1, :, lanes], preferred_element_type=jnp.float32)
        result = sums[:total] + (sums[total:] + last)
        for (index, start), out_ref in zip(pieces, outs):
            if start <= band < start + out_ref.shape[1]:
                at = blocks.index(index) * rows
                out_ref[:, band - start : band - start + BAND] = result[at : at + rows]


def shape(*dims):
    return jax.ShapeDtypeStruct(dims, jnp.float32)


def params(mebibytes):
    return pltpu.CompilerParams(vmem_limit_bytes=mebibytes * 1024 * 1024)


def cost(flops, *arrays):
    return pl.CostEstimate(
        flops=flops, bytes_accessed=4 * sum(a.size for a in arrays), transcendentals=0
    )


def partners_swap(arrays, axis):
    count = len(arrays)
    away = [
        lax.ppermute(arrays[i], axis, [(d, d ^ i) for d in range(count)])
        for i in range(count - 1, 0, -1)
    ]
    return [arrays[0]] + away[::-1]


class Swap(typing.NamedTuple):
    heads: bool
    rows: bool


def swap_is_possible(heads, count):
    return heads == count and count & (count - 1) == 0 and count <= 8


def entering_states(summaries, swap, beside, after):
    heads = len(summaries)
    count = lax.axis_size("ctx")
    if swap:
        held = partners_swap(summaries, "ctx")
        held, beside = lax.optimization_barrier((held, beside))
        entry = shape(DK, DV)
        entries = pl.pallas_call(
            ordered_scan_kernel,
            in_specs=[HBM] + [VMEM] * (count - 1),
            out_specs=[HBM] + [VMEM] * (count - 1),
            out_shape=[entry] * count,
            scratch_shapes=[
                pltpu.VMEM((count, DK, DK + DV), jnp.float32),
                pltpu.VMEM((count, DK, DV), jnp.float32),
                pltpu.SemaphoreType.DMA((2,)),
            ],
            compiler_params=params(SCAN_VMEM),
            name="state_scan",
        )(*held)
        entries, after = lax.optimization_barrier((entries, after))
        return partners_swap(entries, "ctx"), beside, after
    parts = max(1, count // heads)
    per_owner = max(1, heads // count)
    width = DV // parts
    groups = heads // per_owner
    summary = jnp.stack(summaries)
    maps = summary[:, :, :DK].reshape(groups, 1, per_owner, DK, DK)
    maps = jnp.broadcast_to(maps, (groups, parts, per_owner, DK, DK))
    adds = summary[:, :, DK:].reshape(groups, per_owner, DK, parts, width)
    payload = jnp.concatenate([maps, adds.transpose(0, 3, 1, 2, 4)], axis=-1)
    payload = payload.reshape(count, per_owner, DK, DK + width)
    held = lax.all_to_all(payload, "ctx", split_axis=0, concat_axis=0, tiled=True)
    entries = pl.pallas_call(
        scan_kernel,
        out_shape=shape(count, per_owner, DK, width),
        compiler_params=params(32),
        name="state_scan",
    )(held)
    back = lax.all_to_all(entries, "ctx", split_axis=0, concat_axis=0, tiled=True)
    back = back.reshape(groups, parts, per_owner, DK, width).transpose(0, 2, 3, 1, 4)
    back = back.reshape(heads, DK, DV)
    return [back[head] for head in range(heads)], beside, after


def project_and_sum(project, columns, axis):
    count = lax.axis_size(axis)
    if count != 4:
        whole = jnp.concatenate(project([(i, 0, columns) for i in range(count)], LATER_VMEM), axis=0)
        return lax.psum_scatter(whole, axis, scatter_dimension=0, tiled=True)
    half = columns // 2
    halves = [(0, half), (half, half)]
    *first, opposite = project([(3, *h) for h in halves] + [(3, 0, columns)], FIRST_VMEM)
    from_end = [lax.ppermute(piece, axis, [(0, 1), (3, 2)]) for piece in first]
    from_inner = lax.ppermute(opposite, axis, [(1, 2), (2, 1)])
    *across, near, own = project(
        [(2, *h) for h in halves] + [(1, 0, columns), (0, 0, columns)], LATER_VMEM
    )
    from_end[1], near = lax.optimization_barrier((from_end[1], near))
    from_across = [
        lax.ppermute(piece + came, axis, [(i, i ^ 2) for i in range(4)])
        for piece, came in zip(across, from_end)
    ]
    from_near = lax.ppermute(near, axis, [(i, i ^ 1) for i in range(4)])
    return (own + from_inner) + (from_near + jnp.concatenate(from_across, axis=1))


def per_device(queries, key_vectors, values, decays, strengths, out_gate, norm_gain, out_weight):
    tokens = queries.shape[0]
    heads = values.shape[1] // DV
    depth, columns = out_weight.shape
    rows = tokens // lax.axis_size("tp")
    gain = norm_gain.reshape(1, DV)
    swap = Swap(
        heads=swap_is_possible(heads, lax.axis_size("ctx")), rows=lax.axis_size("tp") == 4
    )

    def buffers(*arrays):
        return [pltpu.VMEM(a.shape, a.dtype) for a in arrays] + [
            pltpu.SemaphoreType.DMA((len(arrays),))
        ]

    factor_shape = shape(heads, tokens, DK + DV)
    groups = pl.cdiv(heads, HEADS_AT_ONCE)
    factors, *summaries = pl.pallas_call(
        functools.partial(summary_kernel, swap=swap.heads),
        in_specs=[HBM] * 4,
        out_specs=[HBM] + [VMEM] * heads,
        out_shape=[factor_shape] + [shape(DK, DK + DV)] * heads,
        scratch_shapes=buffers(decays, strengths, key_vectors, values)
        + [pltpu.VMEM(factor_shape.shape, jnp.float32), pltpu.VMEM((heads, DK, DK + DV), jnp.float32)]
        + [pltpu.SemaphoreType.DMA((groups,))],
        compiler_params=params(MOST_VMEM),
        name="state_summary",
    )(decays, strengths, key_vectors, values)
    maps = pl.pallas_call(
        output_kernel,
        in_specs=[HBM] * 4,
        out_specs=HBM,
        out_shape=factor_shape,
        scratch_shapes=buffers(decays, queries, key_vectors, factors)
        + [pltpu.VMEM(factor_shape.shape, jnp.float32)]
        + [pltpu.SemaphoreType.DMA((queries.shape[1] // DK,))],
        compiler_params=params(MOST_VMEM),
        cost_estimate=cost(3 * 2 * heads * tokens * tokens * 384, factors, factors, queries),
        name="output_maps",
    )(decays, queries, key_vectors, factors)
    states, maps, weights = entering_states(summaries, swap.heads, maps, out_weight)
    parts = pl.pallas_call(
        weight_kernel,
        grid=(depth // WEIGHT_ROWS,),
        in_specs=[pl.BlockSpec((WEIGHT_ROWS, columns), lambda i: (i, 0))],
        out_specs=pl.BlockSpec((2, WEIGHT_ROWS, columns), lambda i: (0, i, 0)),
        out_shape=jax.ShapeDtypeStruct((2, depth, columns), jnp.bfloat16),
        compiler_params=params(WEIGHT_VMEM),
        cost_estimate=cost(6 * weights.size, weights, weights),
        name="weight_parts",
    )(weights)

    def project(pieces, vmem):
        total = len({piece[0] for piece in pieces}) * rows
        normed = pltpu.VMEM((total, depth), jnp.bfloat16)
        counts = (total // rows, heads * total // rows, 1)
        return pl.pallas_call(
            functools.partial(
                projection_kernel, pieces=[(index, start) for index, start, _ in pieces], swap=swap
            ),
            in_specs=[HBM] * 2 + [VMEM] * 2 + [HBM] + [VMEM] * (heads - 1),
            out_shape=[shape(rows, width) for _, _, width in pieces],
            scratch_shapes=[
                pltpu.VMEM((heads, total, DK + DV), jnp.float32),
                pltpu.VMEM((total, heads * DV), jnp.float32),
                pltpu.VMEM((heads, DK, DV), jnp.float32),
                normed,
                normed,
            ]
            + [pltpu.SemaphoreType.DMA((n,)) for n in counts],
            compiler_params=params(vmem),
            cost_estimate=cost(3 * 2 * total * depth * columns, out_weight),
            name="projection",
        )(maps, out_gate, gain, parts, *states)

    return project_and_sum(project, columns, "tp")


def solution(mesh):
    return jax.shard_map(
        per_device,
        mesh=mesh,
        in_specs=(
            P("ctx", "tp"),
            P("ctx", "tp"),
            P("ctx", "tp"),
            P("tp", "ctx"),
            P("tp", "ctx"),
            P("ctx", "tp"),
            P(),
            P("tp", None),
        ),
        out_specs=P(("ctx", "tp"), None),
        check_vma=False,
    )
```

time: 233 us -> 92 us (0.39); the launches traced: 229 us -> 91.7 us
  matrix products: 74.5 us -> 0 us
  waiting for transfers between devices: 69 us -> 25.1 us
  Pallas kernels: 0 us -> 37.1 us
  starting transfers between devices: 56.5 us -> 27.4 us
  between operations: 14.1 us -> 0.2 us
  other arithmetic: 8.44 us -> 1.03 us
  local copies, waits for them, and re-layouts: 6.25 us -> 0.92 us
    dot_general x36 -> x0, matrix products: 74.5 us -> none  [the longest x1 15.6 us: per_device(): jnp.einsum('gwpc,gwpv->gwcv', key_final, w_fac, precision=TOP_PRECISION)]
    reduce_scatter x1 -> x0, waiting for transfers between devices: 58.6 us -> none  [per_device(): lax.psum_scatter(jnp.dot(normed, out_weight, precision=TOP_PRECISION, pre...]
    pallas_call x0 -> x6, Pallas kernels: none -> 37.1 us  [the longest x2 11.8 us: project(): pl.pallas_call(functools.partial(projection_kernel, pieces=[(index, start...]
    ppermute x7 -> x20, starting transfers between devices: 56.5 us -> 27.4 us  [the longest x14 16 us: partners_swap(): lax.ppermute(arrays[i], axis, [(d, d ^ i) for d in range(count)])]
    ppermute x7 -> x20, waiting for transfers between devices: 10.4 us -> 25.1 us  [the longest x2 23.4 us: project_and_sum(): lax.ppermute(piece + came, axis, [(i, i ^ 2) for i in range(4)])]
    dynamic_update_slice x4 -> x0, other arithmetic: 4.38 us -> none  [per_device(): lax.scan(compose, (start_map, start_state), (state_transitions.transpose(...]
  transfers between devices with their start and end apart: 8 -> 20, of which waited for: 8 -> 4; matrix products, arithmetic and copies ran while one was open for 0% -> 0% of each run, Pallas kernels for 0% -> 21%
where the time goes in v1:
time: 92 us; the launch traced here: 91.7 us
  Pallas kernels  37.1 us (40%)
  starting transfers between devices  27.4 us (30%)
  waiting for transfers between devices  25.1 us (27%)
  other arithmetic  1.03 us (1%)
  local copies, waits for them, and re-layouts  0.92 us (1%)
    ppermute x2, waiting for transfers between devices, project_and_sum(): lax.ppermute(piece + came, axis, [(i, i ^ 2) for i in range(4)])  23.4 us
    ppermute x14, starting transfers between devices, partners_swap(): lax.ppermute(arrays[i], axis, [(d, d ^ i) for d in range(count)])  16 us
    pallas_call x2, Pallas kernels, project(): pl.pallas_call(functools.partial(projection_kernel, pieces=[(index, start...  11.8 us
    pallas_call x1, Pallas kernels, per_device(): pl.pallas_call(functools.partial(summary_kernel, swap=swap.heads), in_spe...  11.6 us
    pallas_call x1, Pallas kernels, per_device(): pl.pallas_call(weight_kernel, grid=(depth // WEIGHT_ROWS,), in_specs=[pl....  6.31 us
    pallas_call x1, Pallas kernels, per_device(): pl.pallas_call(output_kernel, in_specs=[HBM] * 4, out_specs=HBM, out_shap...  6 us
    ppermute x2, starting transfers between devices, project_and_sum(): from_end = [lax.ppermute(piece, axis, [(0, 1), (3, 2)]) for piece in first]  4.8 us
    ppermute x2, starting transfers between devices, project_and_sum(): lax.ppermute(piece + came, axis, [(i, i ^ 2) for i in range(4)])  3.68 us
  transfers between devices with their start and end apart: 20, of which 4 were waited for; matrix products, arithmetic and copies ran while one was open for 0% of the time, Pallas kernels for 21%

profile of v1, /device:TPU:0, one launch (start us, length us, event | category | flops | bytes accessed | tf_op | source)
XLA Modules:
  0.0 91.7 jit_solution(7672330148127674812)
XLA Ops:
  0.0 11.6 %state_summary.1 = (f32[8,256,256]{2,1,0:T(8,128)}, f32[128,256]{1,0:T(8,128)}, f32[128,256]{1,0:T(8,128)}, f32[128,256]{1,0:T(8,128)}, f32[128,256]{1,0:T(8,128...) custom-call(f32[8,256]{1,0:T(8,128)} %decay_hbm.3, ...), custom_call_target="tpu_custom_call" | custom-call | tf_op jit(solution)/shard_map/state_summary/pallas_call | solution.py:508
  11.6 0.5 collective-permute-start
  12.1 2.6 %collective-permute-start.1 = (f32[128,256]{1,0:T(8,128)}, f32[128,256]{1,0:T(8,128)S(1)}, u32[]{:S(2)}, u32[]{:S(2)}) collective-permute-start(f32[128,256]{1,0:T(8,128)} %get-tuple-element.51), channel_id=1, source_target_pairs={{0,8},{4,12},{8,0},{12,4},{16,24},{20,28},{24,16},{28,20},{1,9},{5... | collective-permute-start | bytes 393224 | tf_op jit(solution)/shard_map/ppermute | solution.py:409
  14.6 0.1 collective-permute-start.2
  14.7 1.8 %collective-permute-start.3 = (f32[128,256]{1,0:T(8,128)}, f32[128,256]{1,0:T(8,128)S(1)}, u32[]{:S(2)}, u32[]{:S(2)}) collective-permute-start(f32[128,256]{1,0:T(8,128)} %get-tuple-element.53), channel_id=1, source_target_pairs={{0,16},{4,20},{8,24},{12,28},{16,0},{20,4},{24,8},{28,12},{1,17},{... | collective-permute-start | bytes 393224 | tf_op jit(solution)/shard_map/ppermute | solution.py:409
  16.5 0.0 collective-permute-start.4
  16.5 0.0 collective-permute-done.rest_0_
  16.5 2.6 %collective-permute-start.5 = (f32[128,256]{1,0:T(8,128)}, f32[128,256]{1,0:T(8,128)S(1)}, u32[]{:S(2)}, u32[]{:S(2)}) collective-permute-start(f32[128,256]{1,0:T(8,128)} %get-tuple-element.55), channel_id=1, source_target_pairs={{0,24},{4,28},{8,16},{12,20},{16,8},{20,12},{24,0},{28,4},{1,25},{... | collective-permute-start | bytes 393224 | tf_op jit(solution)/shard_map/ppermute | solution.py:409
  19.1 0.1 collective-permute-done.1.rest_1_
  19.2 1.7 %collective-permute-start.6 = (f32[128,256]{1,0:T(8,128)}, f32[128,256]{1,0:T(8,128)S(1)}, u32[]{:S(2)}, u32[]{:S(2)}) collective-permute-start(f32[128,256]{1,0:T(8,128)} %get-tuple-element.56), channel_id=1, source_target_pairs={{0,28},{4,24},{8,20},{12,16},{16,12},{20,8},{24,4},{28,0},{1,29},{... | collective-permute-start | bytes 393224 | tf_op jit(solution)/shard_map/ppermute | solution.py:409
  20.9 6.0 %output_maps.1.map_hbm = f32[8,256,256]{2,1,0:T(8,128)} custom-call(f32[8,256]{1,0:T(8,128)} %decay_hbm.3, f32[256,512]{1,0:T(8,128)} %q_hbm.1, f32[256,512]{1,0:T(8,128)} %k_hbm.3, f32[8,256,256]{2,1,0:T(8,128)} %get-tuple-element.57.factor_hbm), custom_call_target="tpu_custom_call" | custom-call | flops 1207959552 | bytes 4718592 | tf_op jit(solution)/shard_map/output_maps/pallas_call | solution.py:519
  26.9 0.0 collective-permute-done.2.rest_2_
  26.9 0.0 collective-permute-done.3.rest_3_
  27.0 1.5 %collective-permute-done.4.rest_4_ = f32[128,256]{1,0:T(8,128)S(1)} collective-permute-done((f32[128,256]{1,0:T(8,128)}, f32[128,256]{1,0:T(8,128)S(1)}, u32[]{:S(2)}, u32[]{:S(2)}) %collective-permute-start.4) | collective-permute-done | bytes 131104 | tf_op jit(solution)/shard_map/ppermute | solution.py:409
  28.5 0.0 collective-permute-done.5.rest_5_
  28.5 0.0 collective-permute-done.6.rest_6_
  28.5 0.9 copy-done.2
  29.4 1.4 %state_scan.1 = (f32[128,128]{1,0:T(8,128)S(1)}, f32[128,128]{1,0:T(8,128)S(1)}, f32[128,128]{1,0:T(8,128)S(1)}, f32[128,128]{1,0:T(8,128)S(1)}, f32[128,128]{1,...) custom-call(f32[128,256]{1,0:T(8,128)S(1)} %copy-done.2, ...), custom_call_target="tpu_custom_call" | custom-call | tf_op jit(solution)/shard_map/state_scan/pallas_call | solution.py:431
  30.8 0.0 copy-start.1
  30.8 0.0 copy-start.3
  30.8 0.5 collective-permute-start.7
  31.3 1.7 %collective-permute-start.8 = (f32[128,128]{1,0:T(8,128)S(1)}, f32[128,128]{1,0:T(8,128)S(1)}, u32[]{:S(2)}, u32[]{:S(2)}) collective-permute-start(f32[128,128]{1,0:T(8,128)S(1)} %get-tuple-element.78), channel_id=1, source_target_pairs={{0,8},{4,12},{8,0},{12,4},{16,24},{20,28},{24,16},{28,20},{1,9},{5... | collective-permute-start | bytes 196616 | tf_op jit(solution)/shard_map/ppermute | solution.py:409
  33.0 0.0 collective-permute-start.9
  33.0 1.5 %collective-permute-start.10 = (f32[128,128]{1,0:T(8,128)S(1)}, f32[128,128]{1,0:T(8,128)S(1)}, u32[]{:S(2)}, u32[]{:S(2)}) collective-permute-start(f32[128,128]{1,0:T(8,128)S(1)} %get-tuple-element.80), channel_id=1, source_target_pairs={{0,16},{4,20},{8,24},{12,28},{16,0},{20,4},{24,8},{28,12},{1,17},{... | collective-permute-start | bytes 196616 | tf_op jit(solution)/shard_map/ppermute | solution.py:409
  34.6 0.3 collective-permute-start.11
  34.8 0.0 collective-permute-done.7.rest_0_
  34.8 2.7 %collective-permute-start.12 = (f32[128,128]{1,0:T(8,128)S(1)}, f32[128,128]{1,0:T(8,128)S(1)}, u32[]{:S(2)}, u32[]{:S(2)}) collective-permute-start(f32[128,128]{1,0:T(8,128)S(1)} %get-tuple-element.82), channel_id=1, source_target_pairs={{0,24},{4,28},{8,16},{12,20},{16,8},{20,12},{24,0},{28,4},{1,25},{... | collective-permute-start | bytes 196616 | tf_op jit(solution)/shard_map/ppermute | solution.py:409
  37.5 0.0 collective-permute-done.8.rest_1_
  37.5 0.0 collective-permute-start.13
  37.5 6.3 %weight_parts.1.parts_ref = bf16[2,1024,2048]{2,1,0:T(8,128)(2,1)S(1)} custom-call(f32[1024,2048]{1,0:T(8,128)} %weight_ref), custom_call_target="tpu_custom_call" | custom-call | flops 12582912 | bytes 16777216 | tf_op jit(solution)/shard_map/weight_parts/pallas_call | solution.py:532
  43.8 0.0 collective-permute-done.9.rest_2_
  43.8 0.0 collective-permute-done.10.rest_3_
  43.9 0.0 collective-permute-done.11.rest_4_
  43.9 0.0 collective-permute-done.12.rest_5_
  43.9 0.0 collective-permute-done.13.rest_6_
  43.9 4.4 %projection.3 = (f32[64,1024]{1,0:T(8,128)S(1)}, f32[64,1024]{1,0:T(8,128)S(1)}, f32[64,2048]{1,0:T(8,128)S(1)}) custom-call(f32[8,256,256]{2,1,0:T(8,128)S(1)} %copy-done, f32[256,1024]{1,0:T(8,128)S(1)} %copy-done.1, f32[1,128]{1,0:T(1,128)S(1)} %bitcast.1, bf16[2,1024,2048]{2,1,0:T(8,128)(2,1)S(1)} %weight_parts.1.parts_ref, ...), custom_call_target="tpu_custom_call" | custom-call | flops 805306368 | bytes 8388608 | tf_op jit(solution)/shard_map/projection/pallas_call | solution.py:547
  48.4 3.5 %collective-permute-start.15 = (f32[64,1024]{1,0:T(8,128)S(1)}, f32[64,1024]{1,0:T(8,128)S(1)}, u32[]{:S(2)}, u32[]{:S(2)}) collective-permute-start(f32[64,1024]{1,0:T(8,128)S(1)} %get-tuple-element.86), channel_id=1, source_target_pairs={{0,1},{3,2},{4,5},{7,6},{8,9},{11,10},{12,13},{15,14},{16,17},{19,... | collective-permute-start | bytes 786440 | tf_op jit(solution)/shard_map/ppermute | solution.py:477
  51.9 1.3 %collective-permute-start.17 = (f32[64,1024]{1,0:T(8,128)S(1)}, f32[64,1024]{1,0:T(8,128)S(1)}, u32[]{:S(2)}, u32[]{:S(2)}) collective-permute-start(f32[64,1024]{1,0:T(8,128)S(1)} %get-tuple-element.90), channel_id=1, source_target_pairs={{0,1},{3,2},{4,5},{7,6},{8,9},{11,10},{12,13},{15,14},{16,17},{19,... | collective-permute-start | bytes 786440 | tf_op jit(solution)/shard_map/ppermute | solution.py:477
  53.2 0.7 collective-permute-start.14
  53.9 7.4 %projection.2 = (f32[64,1024]{1,0:T(8,128)S(1)}, f32[64,1024]{1,0:T(8,128)S(1)}, f32[64,2048]{1,0:T(8,128)S(1)}, f32[64,2048]{1,0:T(8,128)S(1)}) custom-call(f32[8,256,256]{2,1,0:T(8,128)S(1)} %copy-done, f32[256,1024]{1,0:T(8,128)S(1)} %copy-done.1, f32[1,128]{1,0:T(1,128)S(1)} %bitcast.2, bf16[2,1024,2048]{2,1,0:T(8,128)(2,1)S(1)} %weight_parts.1.parts_ref, ...), custom_call_target="tpu_custom_call" | custom-call | flops 2415919104 | bytes 8388608 | tf_op jit(solution)/shard_map/projection/pallas_call | solution.py:547
  61.3 0.0 collective-permute-done.15
  61.3 2.2 %collective-permute-start.16 = (f32[64,2048]{1,0:T(8,128)S(1)}, f32[64,2048]{1,0:T(8,128)S(1)}, u32[]{:S(2)}, u32[]{:S(2)}) collective-permute-start(f32[64,2048]{1,0:T(8,128)S(1)} %get-tuple-element.88), channel_id=1, source_target_pairs={{0,1},{1,0},{2,3},{3,2},{4,5},{5,4},{6,7},{7,6},{8,9},{9,8},{10,11... | collective-permute-start | bytes 1572872 | tf_op jit(solution)/shard_map/ppermute | solution.py:487
  63.6 1.0 %collective-permute-start.19 = (f32[64,1024]{1,0:T(8,128)S(1)}, f32[64,1024]{1,0:T(8,128)S(1)}, u32[]{:S(2)}, u32[]{:S(2)}) collective-permute-start(f32[64,1024]{1,0:T(8,128)S(1)} %add.17), channel_id=1, source_target_pairs={{0,2},{1,3},{2,0},{3,1},{4,6},{5,7},{6,4},{7,5},{8,10},{9,11},{10,... | collective-permute-start | bytes 786440 | tf_op jit(solution)/shard_map/ppermute | solution.py:484
  64.5 0.0 collective-permute-done.17
  64.6 2.7 %collective-permute-start.18 = (f32[64,1024]{1,0:T(8,128)S(1)}, f32[64,1024]{1,0:T(8,128)S(1)}, u32[]{:S(2)}, u32[]{:S(2)}) collective-permute-start(f32[64,1024]{1,0:T(8,128)S(1)} %add.16), channel_id=1, source_target_pairs={{0,2},{1,3},{2,0},{3,1},{4,6},{5,7},{6,4},{7,5},{8,10},{9,11},{10,... | collective-permute-start | bytes 786440 | tf_op jit(solution)/shard_map/ppermute | solution.py:484
  67.3 14.0 %collective-permute-done.19 = f32[64,1024]{1,0:T(8,128)S(1)} collective-permute-done((f32[64,1024]{1,0:T(8,128)S(1)}, f32[64,1024]{1,0:T(8,128)S(1)}, u32[]{:S(2)}, u32[]{:S(2)}) %collective-permute-start.19) | collective-permute-done | bytes 262176 | tf_op jit(solution)/shard_map/ppermute | solution.py:484
  81.2 9.5 %collective-permute-done.18 = f32[64,1024]{1,0:T(8,128)S(1)} collective-permute-done((f32[64,1024]{1,0:T(8,128)S(1)}, f32[64,1024]{1,0:T(8,128)S(1)}, u32[]{:S(2)}, u32[]{:S(2)}) %collective-permute-start.18) | collective-permute-done | bytes 262176 | tf_op jit(solution)/shard_map/ppermute | solution.py:484
  90.7 0.9 %fusion = f32[64,2048]{1,0:T(8,128)} fusion(f32[64,2048]{1,0:T(8,128)S(1)} %collective-permute-done.16, f32[64,1024]{1,0:T(8,128)S(1)} %collective-permute-done.19, f32[64,1024]{1,0:T(8,128)S(1)} %collective-permute-done.18, f32[64,2048]{1,0:T(8,128)S(1)} %get-tuple-element.84, f32[64,2048]{1,0:T(8,128)S(1)} %collective-permute-done.14), kind=kLoop, calls=%fused_computation.1 | loop fusion | flops 524288 | bytes 2621440 | tf_op jit(solution)/shard_map/add | solution.py:488
  (9 shorter events, 0.1 us)
Async XLA Ops:
  11.6 4.9 %collective-permute-start = (f32[128,256]{1,0:T(8,128)}, f32[128,256]{1,0:T(8,128)S(1)}, u32[]{:S(2)}, u32[]{:S(2)}) collective-permute-start(f32[128,256]{1,0:T(8,128)} %get-tuple-element.50), channel_id=1, source_target_pairs={{0,4},{4,0},{8,12},{12,8},{16,20},{20,16},{24,28},{28,24},{1,5},{5... | collective-permute-start | bytes 393224 | tf_op jit(solution)/shard_map/ppermute | solution.py:409
  12.1 7.1 %collective-permute-start.1 = (f32[128,256]{1,0:T(8,128)}, f32[128,256]{1,0:T(8,128)S(1)}, u32[]{:S(2)}, u32[]{:S(2)}) collective-permute-start(f32[128,256]{1,0:T(8,128)} %get-tuple-element.51), channel_id=1, source_target_pairs={{0,8},{4,12},{8,0},{12,4},{16,24},{20,28},{24,16},{28,20},{1,9},{5... | collective-permute-start | bytes 393224 | tf_op jit(solution)/shard_map/ppermute | solution.py:409
  14.6 12.3 %collective-permute-start.2 = (f32[128,256]{1,0:T(8,128)}, f32[128,256]{1,0:T(8,128)S(1)}, u32[]{:S(2)}, u32[]{:S(2)}) collective-permute-start(f32[128,256]{1,0:T(8,128)} %get-tuple-element.52), channel_id=1, source_target_pairs={{0,12},{4,8},{8,4},{12,0},{16,28},{20,24},{24,20},{28,16},{1,13},{... | collective-permute-start | bytes 393224 | tf_op jit(solution)/shard_map/ppermute | solution.py:409
  14.7 12.2 %collective-permute-start.3 = (f32[128,256]{1,0:T(8,128)}, f32[128,256]{1,0:T(8,128)S(1)}, u32[]{:S(2)}, u32[]{:S(2)}) collective-permute-start(f32[128,256]{1,0:T(8,128)} %get-tuple-element.53), channel_id=1, source_target_pairs={{0,16},{4,20},{8,24},{12,28},{16,0},{20,4},{24,8},{28,12},{1,17},{... | collective-permute-start | bytes 393224 | tf_op jit(solution)/shard_map/ppermute | solution.py:409
  16.5 12.0 %collective-permute-start.4 = (f32[128,256]{1,0:T(8,128)}, f32[128,256]{1,0:T(8,128)S(1)}, u32[]{:S(2)}, u32[]{:S(2)}) collective-permute-start(f32[128,256]{1,0:T(8,128)} %get-tuple-element.54), channel_id=1, source_target_pairs={{0,20},{4,16},{8,28},{12,24},{16,4},{20,0},{24,12},{28,8},{1,21},{... | collective-permute-start | bytes 393224 | tf_op jit(solution)/shard_map/ppermute | solution.py:409
  16.5 12.0 %collective-permute-start.5 = (f32[128,256]{1,0:T(8,128)}, f32[128,256]{1,0:T(8,128)S(1)}, u32[]{:S(2)}, u32[]{:S(2)}) collective-permute-start(f32[128,256]{1,0:T(8,128)} %get-tuple-element.55), channel_id=1, source_target_pairs={{0,24},{4,28},{8,16},{12,20},{16,8},{20,12},{24,0},{28,4},{1,25},{... | collective-permute-start | bytes 393224 | tf_op jit(solution)/shard_map/ppermute | solution.py:409
  19.2 9.3 %collective-permute-start.6 = (f32[128,256]{1,0:T(8,128)}, f32[128,256]{1,0:T(8,128)S(1)}, u32[]{:S(2)}, u32[]{:S(2)}) collective-permute-start(f32[128,256]{1,0:T(8,128)} %get-tuple-element.56), channel_id=1, source_target_pairs={{0,28},{4,24},{8,20},{12,16},{16,12},{20,8},{24,4},{28,0},{1,29},{... | collective-permute-start | bytes 393224 | tf_op jit(solution)/shard_map/ppermute | solution.py:409
  28.5 0.9 copy-start.2
  30.8 13.1 %copy-start = (f32[8,256,256]{2,1,0:T(8,128)S(1)}, f32[8,256,256]{2,1,0:T(8,128)}, u32[]{:S(2)}) copy-start(f32[8,256,256]{2,1,0:T(8,128)} %output_maps.1.map_hbm) | copy-start | bytes 6291460
  30.8 13.1 %copy-start.1 = (f32[256,1024]{1,0:T(8,128)S(1)}, f32[256,1024]{1,0:T(8,128)}, u32[]{:S(2)}) copy-start(f32[256,1024]{1,0:T(8,128)} %gate_hbm.3) | copy-start | bytes 3145732
  30.8 13.1 %copy-start.3 = (f32[128]{0:T(128)S(1)}, f32[128]{0:T(128)}, u32[]{:S(2)}) copy-start(f32[128]{0:T(128)} %param.14) | copy-start | bytes 1540
  30.8 4.0 %collective-permute-start.7 = (f32[128,128]{1,0:T(8,128)S(1)}, f32[128,128]{1,0:T(8,128)S(1)}, u32[]{:S(2)}, u32[]{:S(2)}) collective-permute-start(f32[128,128]{1,0:T(8,128)S(1)} %get-tuple-element.77), channel_id=1, source_target_pairs={{0,4},{4,0},{8,12},{12,8},{16,20},{20,16},{24,28},{28,24},{1,5},{5... | collective-permute-start | bytes 196616 | tf_op jit(solution)/shard_map/ppermute | solution.py:409
  31.3 6.2 %collective-permute-start.8 = (f32[128,128]{1,0:T(8,128)S(1)}, f32[128,128]{1,0:T(8,128)S(1)}, u32[]{:S(2)}, u32[]{:S(2)}) collective-permute-start(f32[128,128]{1,0:T(8,128)S(1)} %get-tuple-element.78), channel_id=1, source_target_pairs={{0,8},{4,12},{8,0},{12,4},{16,24},{20,28},{24,16},{28,20},{1,9},{5... | collective-permute-start | bytes 196616 | tf_op jit(solution)/shard_map/ppermute | solution.py:409
  33.0 10.8 %collective-permute-start.9 = (f32[128,128]{1,0:T(8,128)S(1)}, f32[128,128]{1,0:T(8,128)S(1)}, u32[]{:S(2)}, u32[]{:S(2)}) collective-permute-start(f32[128,128]{1,0:T(8,128)S(1)} %get-tuple-element.79), channel_id=1, source_target_pairs={{0,12},{4,8},{8,4},{12,0},{16,28},{20,24},{24,20},{28,16},{1,13},{... | collective-permute-start | bytes 196616 | tf_op jit(solution)/shard_map/ppermute | solution.py:409
  33.0 10.8 %collective-permute-start.10 = (f32[128,128]{1,0:T(8,128)S(1)}, f32[128,128]{1,0:T(8,128)S(1)}, u32[]{:S(2)}, u32[]{:S(2)}) collective-permute-start(f32[128,128]{1,0:T(8,128)S(1)} %get-tuple-element.80), channel_id=1, source_target_pairs={{0,16},{4,20},{8,24},{12,28},{16,0},{20,4},{24,8},{28,12},{1,17},{... | collective-permute-start | bytes 196616 | tf_op jit(solution)/shard_map/ppermute | solution.py:409
  34.6 9.3 %collective-permute-start.11 = (f32[128,128]{1,0:T(8,128)S(1)}, f32[128,128]{1,0:T(8,128)S(1)}, u32[]{:S(2)}, u32[]{:S(2)}) collective-permute-start(f32[128,128]{1,0:T(8,128)S(1)} %get-tuple-element.81), channel_id=1, source_target_pairs={{0,20},{4,16},{8,28},{12,24},{16,4},{20,0},{24,12},{28,8},{1,21},{... | collective-permute-start | bytes 196616 | tf_op jit(solution)/shard_map/ppermute | solution.py:409
  34.8 9.0 %collective-permute-start.12 = (f32[128,128]{1,0:T(8,128)S(1)}, f32[128,128]{1,0:T(8,128)S(1)}, u32[]{:S(2)}, u32[]{:S(2)}) collective-permute-start(f32[128,128]{1,0:T(8,128)S(1)} %get-tuple-element.82), channel_id=1, source_target_pairs={{0,24},{4,28},{8,16},{12,20},{16,8},{20,12},{24,0},{28,4},{1,25},{... | collective-permute-start | bytes 196616 | tf_op jit(solution)/shard_map/ppermute | solution.py:409
  37.5 6.4 %collective-permute-start.13 = (f32[128,128]{1,0:T(8,128)S(1)}, f32[128,128]{1,0:T(8,128)S(1)}, u32[]{:S(2)}, u32[]{:S(2)}) collective-permute-start(f32[128,128]{1,0:T(8,128)S(1)} %get-tuple-element.83), channel_id=1, source_target_pairs={{0,28},{4,24},{8,20},{12,16},{16,12},{20,8},{24,4},{28,0},{1,29},{... | collective-permute-start | bytes 196616 | tf_op jit(solution)/shard_map/ppermute | solution.py:409
  48.4 12.9 %collective-permute-start.15 = (f32[64,1024]{1,0:T(8,128)S(1)}, f32[64,1024]{1,0:T(8,128)S(1)}, u32[]{:S(2)}, u32[]{:S(2)}) collective-permute-start(f32[64,1024]{1,0:T(8,128)S(1)} %get-tuple-element.86), channel_id=1, source_target_pairs={{0,1},{3,2},{4,5},{7,6},{8,9},{11,10},{12,13},{15,14},{16,17},{19,... | collective-permute-start | bytes 786440 | tf_op jit(solution)/shard_map/ppermute | solution.py:477
  51.9 12.6 %collective-permute-start.17 = (f32[64,1024]{1,0:T(8,128)S(1)}, f32[64,1024]{1,0:T(8,128)S(1)}, u32[]{:S(2)}, u32[]{:S(2)}) collective-permute-start(f32[64,1024]{1,0:T(8,128)S(1)} %get-tuple-element.90), channel_id=1, source_target_pairs={{0,1},{3,2},{4,5},{7,6},{8,9},{11,10},{12,13},{15,14},{16,17},{19,... | collective-permute-start | bytes 786440 | tf_op jit(solution)/shard_map/ppermute | solution.py:477
  53.2 14.1 %collective-permute-start.14 = (f32[64,2048]{1,0:T(8,128)S(1)}, f32[64,2048]{1,0:T(8,128)S(1)}, u32[]{:S(2)}, u32[]{:S(2)}) collective-permute-start(f32[64,2048]{1,0:T(8,128)S(1)} %get-tuple-element.85), channel_id=1, source_target_pairs={{1,2},{2,1},{5,6},{6,5},{9,10},{10,9},{13,14},{14,13},{17,18},{18,... | collective-permute-start | bytes 1572872 | tf_op jit(solution)/shard_map/ppermute | solution.py:478
  61.3 29.4 %collective-permute-start.16 = (f32[64,2048]{1,0:T(8,128)S(1)}, f32[64,2048]{1,0:T(8,128)S(1)}, u32[]{:S(2)}, u32[]{:S(2)}) collective-permute-start(f32[64,2048]{1,0:T(8,128)S(1)} %get-tuple-element.88), channel_id=1, source_target_pairs={{0,1},{1,0},{2,3},{3,2},{4,5},{5,4},{6,7},{7,6},{8,9},{9,8},{10,11... | collective-permute-start | bytes 1572872 | tf_op jit(solution)/shard_map/ppermute | solution.py:487
  63.6 17.7 %collective-permute-start.19 = (f32[64,1024]{1,0:T(8,128)S(1)}, f32[64,1024]{1,0:T(8,128)S(1)}, u32[]{:S(2)}, u32[]{:S(2)}) collective-permute-start(f32[64,1024]{1,0:T(8,128)S(1)} %add.17), channel_id=1, source_target_pairs={{0,2},{1,3},{2,0},{3,1},{4,6},{5,7},{6,4},{7,5},{8,10},{9,11},{10,... | collective-permute-start | bytes 786440 | tf_op jit(solution)/shard_map/ppermute | solution.py:484
  64.6 26.2 %collective-permute-start.18 = (f32[64,1024]{1,0:T(8,128)S(1)}, f32[64,1024]{1,0:T(8,128)S(1)}, u32[]{:S(2)}, u32[]{:S(2)}) collective-permute-start(f32[64,1024]{1,0:T(8,128)S(1)} %add.16), channel_id=1, source_target_pairs={{0,2},{1,3},{2,0},{3,1},{4,6},{5,7},{6,4},{7,5},{8,10},{9,11},{10,... | collective-permute-start | bytes 786440 | tf_op jit(solution)/shard_map/ppermute | solution.py:484

commit v2 on v1

--- a/solution.py
+++ b/solution.py
@@ -15,11 +15,11 @@
 BAND = 256
 WEIGHT_ROWS = 128
 MOST_VMEM = 56
-SCAN_VMEM = 51
+SCAN_VMEM = 52.25
 WEIGHT_VMEM = 40
 FIRST_VMEM = 24
 LATER_VMEM = 24
-HEADS_AT_ONCE = 4
+HEADS_AT_ONCE = 8
 EPS = 1e-06
 
 
@@ -337,8 +337,12 @@
     return high, (value - high.astype(jnp.float32)).astype(jnp.bfloat16)
 
 
-def weight_kernel(weight_ref, parts_ref):
-    parts_ref[0], parts_ref[1] = split(weight_ref[...])
+def weight_kernel(weight_hbm, parts_ref, weight_ref, sems):
+    bands = [pl.ds(row, WEIGHT_ROWS) for row in range(0, weight_ref.shape[0], WEIGHT_ROWS)]
+    copies = fetch([(weight_hbm.at[band, :], weight_ref.at[band, :]) for band in bands], sems)
+    for copy, band in zip(copies, bands):
+        copy.wait()
+        parts_ref[0, band, :], parts_ref[1, band, :] = split(weight_ref[band, :])
 
 
 def projection_kernel(map_hbm, gate_hbm, gain_ref, parts_ref, own_hbm, *rest, pieces, swap):
@@ -394,7 +398,7 @@
 
 
 def params(mebibytes):
-    return pltpu.CompilerParams(vmem_limit_bytes=mebibytes * 1024 * 1024)
+    return pltpu.CompilerParams(vmem_limit_bytes=int(mebibytes * 1024 * 1024))
 
 
 def cost(flops, *arrays):
@@ -473,19 +477,23 @@
         return lax.psum_scatter(whole, axis, scatter_dimension=0, tiled=True)
     half = columns // 2
     halves = [(0, half), (half, half)]
-    *first, opposite = project([(3, *h) for h in halves] + [(3, 0, columns)], FIRST_VMEM)
-    from_end = [lax.ppermute(piece, axis, [(0, 1), (3, 2)]) for piece in first]
-    from_inner = lax.ppermute(opposite, axis, [(1, 2), (2, 1)])
+    outward = lax.axis_index(axis) == 1
+    opposite = project([(3, *h) for h in halves], FIRST_VMEM)
+    steps = [
+        (lax.ppermute(piece, axis, [(0, 1), (1, 2)]), lax.ppermute(piece, axis, [(3, 2), (2, 1)]))
+        for piece in opposite
+    ]
     *across, near, own = project(
         [(2, *h) for h in halves] + [(1, 0, columns), (0, 0, columns)], LATER_VMEM
     )
-    from_end[1], near = lax.optimization_barrier((from_end[1], near))
-    from_across = [
-        lax.ppermute(piece + came, axis, [(i, i ^ 2) for i in range(4)])
-        for piece, came in zip(across, from_end)
-    ]
+    from_end = [jnp.where(outward, up, down) for up, down in steps]
+    from_inner = [jnp.where(outward, down, up) for up, down in steps]
+    going = [piece + came for piece, came in zip(across, from_end)]
+    going[1], near = lax.optimization_barrier((going[1], near))
+    from_across = [lax.ppermute(piece, axis, [(i, i ^ 2) for i in range(4)]) for piece in going]
     from_near = lax.ppermute(near, axis, [(i, i ^ 1) for i in range(4)])
-    return (own + from_inner) + (from_near + jnp.concatenate(from_across, axis=1))
+    rest = [inner + far for inner, far in zip(from_inner, from_across)]
+    return (own + from_near) + jnp.concatenate(rest, axis=1)
 
 
 def per_device(queries, key_vectors, values, decays, strengths, out_gate, norm_gain, out_weight):
@@ -531,10 +539,12 @@
     states, maps, weights = entering_states(summaries, swap.heads, maps, out_weight)
     parts = pl.pallas_call(
         weight_kernel,
-        grid=(depth // WEIGHT_ROWS,),
-        in_specs=[pl.BlockSpec((WEIGHT_ROWS, columns), lambda i: (i, 0))],
-        out_specs=pl.BlockSpec((2, WEIGHT_ROWS, columns), lambda i: (0, i, 0)),
+        in_specs=[HBM],
         out_shape=jax.ShapeDtypeStruct((2, depth, columns), jnp.bfloat16),
+        scratch_shapes=[
+            pltpu.VMEM(out_weight.shape, jnp.float32),
+            pltpu.SemaphoreType.DMA((depth // WEIGHT_ROWS,)),
+        ],
         compiler_params=params(WEIGHT_VMEM),
         cost_estimate=cost(6 * weights.size, weights, weights),
         name="weight_parts",

time: 92 us -> 104 us (1.13)
  local copies, waits for them, and re-layouts: 0.92 us -> 9.93 us
  starting transfers between devices: 27.4 us -> 31.2 us
  Pallas kernels: 37.1 us -> 34.7 us
  other arithmetic: 1.03 us -> 2.96 us
    unnamed x8 -> x22, local copies, waits for them, and re-layouts: 0.92 us -> 9.93 us
    ppermute x5 -> x6, starting transfers between devices: 9.18 us -> 15.2 us  [the longest x2 6.9 us: project_and_sum(): lax.ppermute(piece, axis, [(0, 1), (1, 2)])]
    ppermute x5 -> x6, waiting for transfers between devices: 23.4 us -> 19.7 us  [the longest x2 19.6 us: project_and_sum(): lax.ppermute(piece, axis, [(i, i ^ 2) for i in range(4)])]
    pallas_call x1, Pallas kernels: 6.31 us -> 3.62 us  [per_device(): pl.pallas_call(weight_kernel, in_specs=[HBM], out_shape=jax.ShapeDtypeStr...]
    ppermute x1, starting transfers between devices: 2.21 us -> 0.01 us  [project_and_sum(): from_near = lax.ppermute(near, axis, [(i, i ^ 1) for i in range(4)])]
    add x3 -> x5, other arithmetic: 1.03 us -> 2.96 us  [the longest x2 1.05 us: project_and_sum(): going = [piece + came for piece, came in zip(across, from_end)]]
    ppermute x1, waiting for transfers between devices: 0.01 us -> 1.74 us  [project_and_sum(): from_near = lax.ppermute(near, axis, [(i, i ^ 1) for i in range(4)])]
    ppermute x14, waiting for transfers between devices: 1.66 us -> 3.25 us  [partners_swap(): lax.ppermute(arrays[i], axis, [(d, d ^ i) for d in range(count)])]
  transfers between devices with their start and end apart: 20 -> 21, of which waited for: 4 -> 6; matrix products, arithmetic and copies ran while one was open for 0% -> 2% of each run, Pallas kernels for 21% -> 16%
where the time goes in v2:
time: 104 us
  Pallas kernels  34.7 us (33%)
  starting transfers between devices  31.2 us (30%)
  waiting for transfers between devices  24.6 us (24%)
  local copies, waits for them, and re-layouts  9.93 us (10%)
  other arithmetic  2.96 us (3%)
    ppermute x2, waiting for transfers between devices, project_and_sum(): lax.ppermute(piece, axis, [(i, i ^ 2) for i in range(4)])  19.6 us
    ppermute x14, starting transfers between devices, partners_swap(): lax.ppermute(arrays[i], axis, [(d, d ^ i) for d in range(count)])  16 us
    pallas_call x2, Pallas kernels, project(): pl.pallas_call(functools.partial(projection_kernel, pieces=[(index, start...  12.5 us
    pallas_call x1, Pallas kernels, per_device(): pl.pallas_call(functools.partial(summary_kernel, swap=swap.heads), in_spe...  11.2 us
    unnamed x22, local copies, waits for them, and re-layouts  9.93 us
    ppermute x2, starting transfers between devices, project_and_sum(): lax.ppermute(piece, axis, [(0, 1), (1, 2)])  6.9 us
    ppermute x2, starting transfers between devices, project_and_sum(): lax.ppermute(piece, axis, [(i, i ^ 2) for i in range(4)])  6.29 us
    pallas_call x1, Pallas kernels, per_device(): pl.pallas_call(output_kernel, in_specs=[HBM] * 4, out_specs=HBM, out_shap...  6.01 us
  transfers between devices with their start and end apart: 21, of which 6 were waited for; matrix products, arithmetic and copies ran while one was open for 2% of the time, Pallas kernels for 16%

profile of v2, /device:TPU:0, one launch (start us, length us, event | category | flops | bytes accessed | tf_op | source)
XLA Modules:
  0.0 103.7 jit_solution(3831295298869993427)
XLA Ops:
  0.0 11.2 %state_summary.1 = (f32[8,256,256]{2,1,0:T(8,128)}, f32[128,256]{1,0:T(8,128)}, f32[128,256]{1,0:T(8,128)}, f32[128,256]{1,0:T(8,128)}, f32[128,256]{1,0:T(8,128...) custom-call(f32[8,256]{1,0:T(8,128)} %decay_hbm.3, ...), custom_call_target="tpu_custom_call" | custom-call | tf_op jit(solution)/shard_map/state_summary/pallas_call | solution.py:516
  11.2 0.5 collective-permute-start
  11.7 2.6 %collective-permute-start.1 = (f32[128,256]{1,0:T(8,128)}, f32[128,256]{1,0:T(8,128)S(1)}, u32[]{:S(2)}, u32[]{:S(2)}) collective-permute-start(f32[128,256]{1,0:T(8,128)} %get-tuple-element.50), channel_id=1, source_target_pairs={{0,8},{4,12},{8,0},{12,4},{16,24},{20,28},{24,16},{28,20},{1,9},{5... | collective-permute-start | bytes 393224 | tf_op jit(solution)/shard_map/ppermute | solution.py:413
  14.3 0.1 collective-permute-start.2
  14.4 1.8 %collective-permute-start.3 = (f32[128,256]{1,0:T(8,128)}, f32[128,256]{1,0:T(8,128)S(1)}, u32[]{:S(2)}, u32[]{:S(2)}) collective-permute-start(f32[128,256]{1,0:T(8,128)} %get-tuple-element.52), channel_id=1, source_target_pairs={{0,16},{4,20},{8,24},{12,28},{16,0},{20,4},{24,8},{28,12},{1,17},{... | collective-permute-start | bytes 393224 | tf_op jit(solution)/shard_map/ppermute | solution.py:413
  16.2 2.6 %collective-permute-start.5 = (f32[128,256]{1,0:T(8,128)}, f32[128,256]{1,0:T(8,128)S(1)}, u32[]{:S(2)}, u32[]{:S(2)}) collective-permute-start(f32[128,256]{1,0:T(8,128)} %get-tuple-element.54), channel_id=1, source_target_pairs={{0,24},{4,28},{8,16},{12,20},{16,8},{20,12},{24,0},{28,4},{1,25},{... | collective-permute-start | bytes 393224 | tf_op jit(solution)/shard_map/ppermute | solution.py:413
  18.8 0.1 collective-permute-done.1.rest_1_
  18.9 1.7 %collective-permute-start.6 = (f32[128,256]{1,0:T(8,128)}, f32[128,256]{1,0:T(8,128)S(1)}, u32[]{:S(2)}, u32[]{:S(2)}) collective-permute-start(f32[128,256]{1,0:T(8,128)} %get-tuple-element.55), channel_id=1, source_target_pairs={{0,28},{4,24},{8,20},{12,16},{16,12},{20,8},{24,4},{28,0},{1,29},{... | collective-permute-start | bytes 393224 | tf_op jit(solution)/shard_map/ppermute | solution.py:413
  20.6 6.0 %output_maps.1.map_hbm = f32[8,256,256]{2,1,0:T(8,128)} custom-call(f32[8,256]{1,0:T(8,128)} %decay_hbm.3, f32[256,512]{1,0:T(8,128)} %q_hbm.1, f32[256,512]{1,0:T(8,128)} %k_hbm.3, f32[8,256,256]{2,1,0:T(8,128)} %get-tuple-element.56.factor_hbm), custom_call_target="tpu_custom_call" | custom-call | flops 1207959552 | bytes 4718592 | tf_op jit(solution)/shard_map/output_maps/pallas_call | solution.py:527
  26.6 0.0 collective-permute-done.3.rest_3_
  26.6 1.5 %collective-permute-done.4.rest_4_ = f32[128,256]{1,0:T(8,128)S(1)} collective-permute-done((f32[128,256]{1,0:T(8,128)}, f32[128,256]{1,0:T(8,128)S(1)}, u32[]{:S(2)}, u32[]{:S(2)}) %collective-permute-start.4) | collective-permute-done | bytes 131104 | tf_op jit(solution)/shard_map/ppermute | solution.py:413
  28.1 0.0 collective-permute-done.5.rest_5_
  28.1 0.0 collective-permute-done.6.rest_6_
  28.1 0.9 copy-done.8
  29.1 1.4 %state_scan.1 = (f32[128,128]{1,0:T(8,128)S(1)}, f32[128,128]{1,0:T(8,128)S(1)}, f32[128,128]{1,0:T(8,128)S(1)}, f32[128,128]{1,0:T(8,128)S(1)}, f32[128,128]{1,...) custom-call(f32[128,256]{1,0:T(8,128)S(1)} %copy-done.8, ...), custom_call_target="tpu_custom_call" | custom-call | tf_op jit(solution)/shard_map/state_scan/pallas_call | solution.py:435
  30.4 0.0 copy-start.3
  30.4 0.0 copy-start.9
  30.5 0.5 collective-permute-start.7
  31.0 1.7 %collective-permute-start.8 = (f32[128,128]{1,0:T(8,128)S(1)}, f32[128,128]{1,0:T(8,128)S(1)}, u32[]{:S(2)}, u32[]{:S(2)}) collective-permute-start(f32[128,128]{1,0:T(8,128)S(1)} %get-tuple-element.77), channel_id=1, source_target_pairs={{0,8},{4,12},{8,0},{12,4},{16,24},{20,28},{24,16},{28,20},{1,9},{5... | collective-permute-start | bytes 196616 | tf_op jit(solution)/shard_map/ppermute | solution.py:413
  32.7 1.5 %collective-permute-start.10 = (f32[128,128]{1,0:T(8,128)S(1)}, f32[128,128]{1,0:T(8,128)S(1)}, u32[]{:S(2)}, u32[]{:S(2)}) collective-permute-start(f32[128,128]{1,0:T(8,128)S(1)} %get-tuple-element.79), channel_id=1, source_target_pairs={{0,16},{4,20},{8,24},{12,28},{16,0},{20,4},{24,8},{28,12},{1,17},{... | collective-permute-start | bytes 196616 | tf_op jit(solution)/shard_map/ppermute | solution.py:413
  34.2 0.3 collective-permute-start.11
  34.5 2.7 %collective-permute-start.12 = (f32[128,128]{1,0:T(8,128)S(1)}, f32[128,128]{1,0:T(8,128)S(1)}, u32[]{:S(2)}, u32[]{:S(2)}) collective-permute-start(f32[128,128]{1,0:T(8,128)S(1)} %get-tuple-element.81), channel_id=1, source_target_pairs={{0,24},{4,28},{8,16},{12,20},{16,8},{20,12},{24,0},{28,4},{1,25},{... | collective-permute-start | bytes 196616 | tf_op jit(solution)/shard_map/ppermute | solution.py:413
  37.2 0.0 collective-permute-done.8.rest_1_
  37.2 0.0 collective-permute-start.13
  37.2 3.6 %weight_parts.1.parts_ref = bf16[2,1024,2048]{2,1,0:T(8,128)(2,1)S(1)} custom-call(f32[1024,2048]{1,0:T(8,128)} %weight_hbm), custom_call_target="tpu_custom_call" | custom-call | flops 12582912 | bytes 16777216 | tf_op jit(solution)/shard_map/weight_parts/pallas_call | solution.py:540
  40.8 0.0 collective-permute-done.9.rest_2_
  40.8 0.0 collective-permute-done.10.rest_3_
  40.8 0.0 collective-permute-done.12.rest_5_
  40.9 1.6 %collective-permute-done.13.rest_6_ = f32[128,128]{1,0:T(8,128)S(1)} collective-permute-done((f32[128,128]{1,0:T(8,128)S(1)}, f32[128,128]{1,0:T(8,128)S(1)}, u32[]{:S(2)}, u32[]{:S(2)}) %collective-permute-start.13) | collective-permute-done | bytes 65568 | tf_op jit(solution)/shard_map/ppermute | solution.py:413
  42.5 5.1 %projection.3 = (f32[64,1024]{1,0:T(8,128)S(1)}, f32[64,1024]{1,0:T(8,128)}) custom-call(f32[8,256,256]{2,1,0:T(8,128)S(1)} %copy-done.2, f32[256,1024]{1,0:T(8,128)S(1)} %copy-done.3, f32[1,128]{1,0:T(1,128)S(1)} %bitcast.1, bf16[2,1024,2048]{2,1,0:T(8,128)(2,1)S(1)} %weight_parts.1.parts_ref, f32[128,128]{1,0:T(8,128)S(1)} %get-tuple-element.75.own_hbm, ...), custom_call_target="tpu_custom_call" | custom-call | flops 805306368 | bytes 8388608 | tf_op jit(solution)/shard_map/projection/pallas_call | solution.py:557
  47.6 3.3 %copy-done = bf16[2,1024,2048]{2,1,0:T(8,128)(2,1)} copy-done((bf16[2,1024,2048]{2,1,0:T(8,128)(2,1)}, bf16[2,1024,2048]{2,1,0:T(8,128)(2,1)S(1)}, u32[]{:S(2)}) %copy-start) | copy-done | bytes 8388632
  50.9 0.7 copy-done.10
  51.6 4.2 %collective-permute-start.14 = (f32[64,1024]{1,0:T(8,128)}, f32[64,1024]{1,0:T(8,128)}, u32[]{:S(2)}, u32[]{:S(2)}) collective-permute-start(f32[64,1024]{1,0:T(8,128)} %get-tuple-element.85), channel_id=1, source_target_pairs={{0,1},{1,2},{4,5},{5,6},{8,9},{9,10},{12,13},{13,14},{16,17},{17,1... | collective-permute-start | bytes 786440 | tf_op jit(solution)/shard_map/ppermute | solution.py:483
  55.8 1.4 %collective-permute-start.15 = (f32[64,1024]{1,0:T(8,128)}, f32[64,1024]{1,0:T(8,128)}, u32[]{:S(2)}, u32[]{:S(2)}) collective-permute-start(f32[64,1024]{1,0:T(8,128)} %get-tuple-element.85), channel_id=1, source_target_pairs={{3,2},{2,1},{7,6},{6,5},{11,10},{10,9},{15,14},{14,13},{19,18},{18... | collective-permute-start | bytes 786440 | tf_op jit(solution)/shard_map/ppermute | solution.py:483
  57.2 2.7 %collective-permute-start.18 = (f32[64,1024]{1,0:T(8,128)}, f32[64,1024]{1,0:T(8,128)S(1)}, u32[]{:S(2)}, u32[]{:S(2)}) collective-permute-start(f32[64,1024]{1,0:T(8,128)} %copy-done.10), channel_id=1, source_target_pairs={{0,1},{1,2},{4,5},{5,6},{8,9},{9,10},{12,13},{13,14},{16,17},{17,1... | collective-permute-start | bytes 786440 | tf_op jit(solution)/shard_map/ppermute | solution.py:483
  59.9 0.7 collective-permute-start.17
  60.6 3.4 %copy-done.1 = bf16[2,1024,2048]{2,1,0:T(8,128)(2,1)S(1)} copy-done((bf16[2,1024,2048]{2,1,0:T(8,128)(2,1)S(1)}, bf16[2,1024,2048]{2,1,0:T(8,128)(2,1)}, u32[]{:S(2)}) %copy-start.1) | copy-done | bytes 8388632
  63.9 0.8 copy-done.5
  64.8 0.8 copy-done.7
  65.6 7.3 %projection.2 = (f32[64,1024]{1,0:T(8,128)S(1)}, f32[64,1024]{1,0:T(8,128)S(1)}, f32[64,2048]{1,0:T(8,128)S(1)}, f32[64,2048]{1,0:T(8,128)S(1)}) custom-call(f32[8,256,256]{2,1,0:T(8,128)S(1)} %copy-done.2, f32[256,1024]{1,0:T(8,128)S(1)} %copy-done.3, f32[1,128]{1,0:T(1,128)S(1)} %bitcast.2, bf16[2,1024,2048]{2,1,0:T(8,128)(2,1)S(1)} %copy-done.1, ...), custom_call_target="tpu_custom_call" | custom-call | flops 2415919104 | bytes 8388608 | tf_op jit(solution)/shard_map/projection/pallas_call | solution.py:557
  73.0 1.0 select_add_fusion.3
  74.0 5.4 %collective-permute-start.20 = (f32[64,1024]{1,0:T(8,128)S(1)}, f32[64,1024]{1,0:T(8,128)S(1)}, u32[]{:S(2)}, u32[]{:S(2)}) collective-permute-start(f32[64,1024]{1,0:T(8,128)S(1)} %select_add_fusion.3), channel_id=1, source_target_pairs={{0,2},{1,3},{2,0},{3,1},{4,6},{5,7},{6,4},{7,5},{8,10},{9,11},{10,... | collective-permute-start | bytes 786440 | tf_op jit(solution)/shard_map/ppermute | solution.py:493
  79.5 0.9 collective-permute-start.19
  80.4 10.6 %collective-permute-done.20 = f32[64,1024]{1,0:T(8,128)S(1)} collective-permute-done((f32[64,1024]{1,0:T(8,128)S(1)}, f32[64,1024]{1,0:T(8,128)S(1)}, u32[]{:S(2)}, u32[]{:S(2)}) %collective-permute-start.20) | collective-permute-done | bytes 262176 | tf_op jit(solution)/shard_map/ppermute | solution.py:493
  91.0 1.0 select_add_fusion
  92.0 9.0 %collective-permute-done.19 = f32[64,1024]{1,0:T(8,128)S(1)} collective-permute-done((f32[64,1024]{1,0:T(8,128)S(1)}, f32[64,1024]{1,0:T(8,128)S(1)}, u32[]{:S(2)}, u32[]{:S(2)}) %collective-permute-start.19) | collective-permute-done | bytes 262176 | tf_op jit(solution)/shard_map/ppermute | solution.py:493
  101.0 1.7 %collective-permute-done.16 = f32[64,2048]{1,0:T(8,128)S(1)} collective-permute-done((f32[64,2048]{1,0:T(8,128)S(1)}, f32[64,2048]{1,0:T(8,128)S(1)}, u32[]{:S(2)}, u32[]{:S(2)}) %collective-permute-start.16) | collective-permute-done | bytes 524320 | tf_op jit(solution)/shard_map/ppermute | solution.py:494
  102.8 0.9 maximum_add_fusion
  (27 shorter events, 0.1 us)
Async XLA Ops:
  11.2 4.9 %collective-permute-start = (f32[128,256]{1,0:T(8,128)}, f32[128,256]{1,0:T(8,128)S(1)}, u32[]{:S(2)}, u32[]{:S(2)}) collective-permute-start(f32[128,256]{1,0:T(8,128)} %get-tuple-element.49), channel_id=1, source_target_pairs={{0,4},{4,0},{8,12},{12,8},{16,20},{20,16},{24,28},{28,24},{1,5},{5... | collective-permute-start | bytes 393224 | tf_op jit(solution)/shard_map/ppermute | solution.py:413
  11.7 7.1 %collective-permute-start.1 = (f32[128,256]{1,0:T(8,128)}, f32[128,256]{1,0:T(8,128)S(1)}, u32[]{:S(2)}, u32[]{:S(2)}) collective-permute-start(f32[128,256]{1,0:T(8,128)} %get-tuple-element.50), channel_id=1, source_target_pairs={{0,8},{4,12},{8,0},{12,4},{16,24},{20,28},{24,16},{28,20},{1,9},{5... | collective-permute-start | bytes 393224 | tf_op jit(solution)/shard_map/ppermute | solution.py:413
  14.3 12.3 %collective-permute-start.2 = (f32[128,256]{1,0:T(8,128)}, f32[128,256]{1,0:T(8,128)S(1)}, u32[]{:S(2)}, u32[]{:S(2)}) collective-permute-start(f32[128,256]{1,0:T(8,128)} %get-tuple-element.51), channel_id=1, source_target_pairs={{0,12},{4,8},{8,4},{12,0},{16,28},{20,24},{24,20},{28,16},{1,13},{... | collective-permute-start | bytes 393224 | tf_op jit(solution)/shard_map/ppermute | solution.py:413
  14.4 12.2 %collective-permute-start.3 = (f32[128,256]{1,0:T(8,128)}, f32[128,256]{1,0:T(8,128)S(1)}, u32[]{:S(2)}, u32[]{:S(2)}) collective-permute-start(f32[128,256]{1,0:T(8,128)} %get-tuple-element.52), channel_id=1, source_target_pairs={{0,16},{4,20},{8,24},{12,28},{16,0},{20,4},{24,8},{28,12},{1,17},{... | collective-permute-start | bytes 393224 | tf_op jit(solution)/shard_map/ppermute | solution.py:413
  16.1 12.0 %collective-permute-start.4 = (f32[128,256]{1,0:T(8,128)}, f32[128,256]{1,0:T(8,128)S(1)}, u32[]{:S(2)}, u32[]{:S(2)}) collective-permute-start(f32[128,256]{1,0:T(8,128)} %get-tuple-element.53), channel_id=1, source_target_pairs={{0,20},{4,16},{8,28},{12,24},{16,4},{20,0},{24,12},{28,8},{1,21},{... | collective-permute-start | bytes 393224 | tf_op jit(solution)/shard_map/ppermute | solution.py:413
  16.2 12.0 %collective-permute-start.5 = (f32[128,256]{1,0:T(8,128)}, f32[128,256]{1,0:T(8,128)S(1)}, u32[]{:S(2)}, u32[]{:S(2)}) collective-permute-start(f32[128,256]{1,0:T(8,128)} %get-tuple-element.54), channel_id=1, source_target_pairs={{0,24},{4,28},{8,16},{12,20},{16,8},{20,12},{24,0},{28,4},{1,25},{... | collective-permute-start | bytes 393224 | tf_op jit(solution)/shard_map/ppermute | solution.py:413
  18.9 9.3 %collective-permute-start.6 = (f32[128,256]{1,0:T(8,128)}, f32[128,256]{1,0:T(8,128)S(1)}, u32[]{:S(2)}, u32[]{:S(2)}) collective-permute-start(f32[128,256]{1,0:T(8,128)} %get-tuple-element.55), channel_id=1, source_target_pairs={{0,28},{4,24},{8,20},{12,16},{16,12},{20,8},{24,4},{28,0},{1,29},{... | collective-permute-start | bytes 393224 | tf_op jit(solution)/shard_map/ppermute | solution.py:413
  28.1 0.9 copy-start.8
  30.4 12.0 %copy-start.2 = (f32[8,256,256]{2,1,0:T(8,128)S(1)}, f32[8,256,256]{2,1,0:T(8,128)}, u32[]{:S(2)}) copy-start(f32[8,256,256]{2,1,0:T(8,128)} %output_maps.1.map_hbm) | copy-start | bytes 6291460
  30.4 12.0 %copy-start.3 = (f32[256,1024]{1,0:T(8,128)S(1)}, f32[256,1024]{1,0:T(8,128)}, u32[]{:S(2)}) copy-start(f32[256,1024]{1,0:T(8,128)} %gate_hbm.3) | copy-start | bytes 3145732
  30.4 12.0 %copy-start.9 = (f32[128]{0:T(128)S(1)}, f32[128]{0:T(128)}, u32[]{:S(2)}) copy-start(f32[128]{0:T(128)} %param.14) | copy-start | bytes 1540
  30.5 4.0 %collective-permute-start.7 = (f32[128,128]{1,0:T(8,128)S(1)}, f32[128,128]{1,0:T(8,128)S(1)}, u32[]{:S(2)}, u32[]{:S(2)}) collective-permute-start(f32[128,128]{1,0:T(8,128)S(1)} %get-tuple-element.76), channel_id=1, source_target_pairs={{0,4},{4,0},{8,12},{12,8},{16,20},{20,16},{24,28},{28,24},{1,5},{5... | collective-permute-start | bytes 196616 | tf_op jit(solution)/shard_map/ppermute | solution.py:413
  31.0 6.2 %collective-permute-start.8 = (f32[128,128]{1,0:T(8,128)S(1)}, f32[128,128]{1,0:T(8,128)S(1)}, u32[]{:S(2)}, u32[]{:S(2)}) collective-permute-start(f32[128,128]{1,0:T(8,128)S(1)} %get-tuple-element.77), channel_id=1, source_target_pairs={{0,8},{4,12},{8,0},{12,4},{16,24},{20,28},{24,16},{28,20},{1,9},{5... | collective-permute-start | bytes 196616 | tf_op jit(solution)/shard_map/ppermute | solution.py:413
  32.7 8.1 %collective-permute-start.9 = (f32[128,128]{1,0:T(8,128)S(1)}, f32[128,128]{1,0:T(8,128)S(1)}, u32[]{:S(2)}, u32[]{:S(2)}) collective-permute-start(f32[128,128]{1,0:T(8,128)S(1)} %get-tuple-element.78), channel_id=1, source_target_pairs={{0,12},{4,8},{8,4},{12,0},{16,28},{20,24},{24,20},{28,16},{1,13},{... | collective-permute-start | bytes 196616 | tf_op jit(solution)/shard_map/ppermute | solution.py:413
  32.7 8.1 %collective-permute-start.10 = (f32[128,128]{1,0:T(8,128)S(1)}, f32[128,128]{1,0:T(8,128)S(1)}, u32[]{:S(2)}, u32[]{:S(2)}) collective-permute-start(f32[128,128]{1,0:T(8,128)S(1)} %get-tuple-element.79), channel_id=1, source_target_pairs={{0,16},{4,20},{8,24},{12,28},{16,0},{20,4},{24,8},{28,12},{1,17},{... | collective-permute-start | bytes 196616 | tf_op jit(solution)/shard_map/ppermute | solution.py:413
  34.2 6.6 %collective-permute-start.11 = (f32[128,128]{1,0:T(8,128)S(1)}, f32[128,128]{1,0:T(8,128)S(1)}, u32[]{:S(2)}, u32[]{:S(2)}) collective-permute-start(f32[128,128]{1,0:T(8,128)S(1)} %get-tuple-element.80), channel_id=1, source_target_pairs={{0,20},{4,16},{8,28},{12,24},{16,4},{20,0},{24,12},{28,8},{1,21},{... | collective-permute-start | bytes 196616 | tf_op jit(solution)/shard_map/ppermute | solution.py:413
  34.5 6.3 %collective-permute-start.12 = (f32[128,128]{1,0:T(8,128)S(1)}, f32[128,128]{1,0:T(8,128)S(1)}, u32[]{:S(2)}, u32[]{:S(2)}) collective-permute-start(f32[128,128]{1,0:T(8,128)S(1)} %get-tuple-element.81), channel_id=1, source_target_pairs={{0,24},{4,28},{8,16},{12,20},{16,8},{20,12},{24,0},{28,4},{1,25},{... | collective-permute-start | bytes 196616 | tf_op jit(solution)/shard_map/ppermute | solution.py:413
  37.2 5.3 %collective-permute-start.13 = (f32[128,128]{1,0:T(8,128)S(1)}, f32[128,128]{1,0:T(8,128)S(1)}, u32[]{:S(2)}, u32[]{:S(2)}) collective-permute-start(f32[128,128]{1,0:T(8,128)S(1)} %get-tuple-element.82), channel_id=1, source_target_pairs={{0,28},{4,24},{8,20},{12,16},{16,12},{20,8},{24,4},{28,0},{1,29},{... | collective-permute-start | bytes 196616 | tf_op jit(solution)/shard_map/ppermute | solution.py:413
  40.8 6.8 %copy-start.4 = (f32[128,128]{1,0:T(8,128)}, f32[128,128]{1,0:T(8,128)S(1)}, u32[]{:S(2)}) copy-start(f32[128,128]{1,0:T(8,128)S(1)} %collective-permute-done.12.rest_5_) | copy-start | bytes 196612
  42.4 9.1 %copy-start.6 = (f32[128,128]{1,0:T(8,128)}, f32[128,128]{1,0:T(8,128)S(1)}, u32[]{:S(2)}) copy-start(f32[128,128]{1,0:T(8,128)S(1)} %collective-permute-done.13.rest_6_) | copy-start | bytes 196612
  47.6 3.3 %copy-start = (bf16[2,1024,2048]{2,1,0:T(8,128)(2,1)}, bf16[2,1024,2048]{2,1,0:T(8,128)(2,1)S(1)}, u32[]{:S(2)}) copy-start(bf16[2,1024,2048]{2,1,0:T(8,128)(2,1)S(1)} %weight_parts.1.parts_ref) | copy-start | bytes 25165828
  50.9 0.7 copy-start.10
  51.6 21.4 %collective-permute-start.14 = (f32[64,1024]{1,0:T(8,128)}, f32[64,1024]{1,0:T(8,128)}, u32[]{:S(2)}, u32[]{:S(2)}) collective-permute-start(f32[64,1024]{1,0:T(8,128)} %get-tuple-element.85), channel_id=1, source_target_pairs={{0,1},{1,2},{4,5},{5,6},{8,9},{9,10},{12,13},{13,14},{16,17},{17,1... | collective-permute-start | bytes 786440 | tf_op jit(solution)/shard_map/ppermute | solution.py:483
  55.8 17.2 %collective-permute-start.15 = (f32[64,1024]{1,0:T(8,128)}, f32[64,1024]{1,0:T(8,128)}, u32[]{:S(2)}, u32[]{:S(2)}) collective-permute-start(f32[64,1024]{1,0:T(8,128)} %get-tuple-element.85), channel_id=1, source_target_pairs={{3,2},{2,1},{7,6},{6,5},{11,10},{10,9},{15,14},{14,13},{19,18},{18... | collective-permute-start | bytes 786440 | tf_op jit(solution)/shard_map/ppermute | solution.py:483
  57.2 22.2 %collective-permute-start.18 = (f32[64,1024]{1,0:T(8,128)}, f32[64,1024]{1,0:T(8,128)S(1)}, u32[]{:S(2)}, u32[]{:S(2)}) collective-permute-start(f32[64,1024]{1,0:T(8,128)} %copy-done.10), channel_id=1, source_target_pairs={{0,1},{1,2},{4,5},{5,6},{8,9},{9,10},{12,13},{13,14},{16,17},{17,1... | collective-permute-start | bytes 786440 | tf_op jit(solution)/shard_map/ppermute | solution.py:483
  59.9 19.5 %collective-permute-start.17 = (f32[64,1024]{1,0:T(8,128)}, f32[64,1024]{1,0:T(8,128)S(1)}, u32[]{:S(2)}, u32[]{:S(2)}) collective-permute-start(f32[64,1024]{1,0:T(8,128)} %copy-done.10), channel_id=1, source_target_pairs={{3,2},{2,1},{7,6},{6,5},{11,10},{10,9},{15,14},{14,13},{19,18},{18... | collective-permute-start | bytes 786440 | tf_op jit(solution)/shard_map/ppermute | solution.py:483
  60.6 3.4 %copy-start.1 = (bf16[2,1024,2048]{2,1,0:T(8,128)(2,1)S(1)}, bf16[2,1024,2048]{2,1,0:T(8,128)(2,1)}, u32[]{:S(2)}) copy-start(bf16[2,1024,2048]{2,1,0:T(8,128)(2,1)} %copy-done) | copy-start | bytes 25165828
  63.9 0.8 copy-start.5
  64.8 0.8 copy-start.7
  74.0 17.0 %collective-permute-start.20 = (f32[64,1024]{1,0:T(8,128)S(1)}, f32[64,1024]{1,0:T(8,128)S(1)}, u32[]{:S(2)}, u32[]{:S(2)}) collective-permute-start(f32[64,1024]{1,0:T(8,128)S(1)} %select_add_fusion.3), channel_id=1, source_target_pairs={{0,2},{1,3},{2,0},{3,1},{4,6},{5,7},{6,4},{7,5},{8,10},{9,11},{10,... | collective-permute-start | bytes 786440 | tf_op jit(solution)/shard_map/ppermute | solution.py:493
  79.4 23.4 %collective-permute-start.16 = (f32[64,2048]{1,0:T(8,128)S(1)}, f32[64,2048]{1,0:T(8,128)S(1)}, u32[]{:S(2)}, u32[]{:S(2)}) collective-permute-start(f32[64,2048]{1,0:T(8,128)S(1)} %get-tuple-element.87), channel_id=1, source_target_pairs={{0,1},{1,0},{2,3},{3,2},{4,5},{5,4},{6,7},{7,6},{8,9},{9,8},{10,11... | collective-permute-start | bytes 1572872 | tf_op jit(solution)/shard_map/ppermute | solution.py:494
  79.5 21.5 %collective-permute-start.19 = (f32[64,1024]{1,0:T(8,128)S(1)}, f32[64,1024]{1,0:T(8,128)S(1)}, u32[]{:S(2)}, u32[]{:S(2)}) collective-permute-start(f32[64,1024]{1,0:T(8,128)S(1)} %select_add_fusion.1), channel_id=1, source_target_pairs={{0,2},{1,3},{2,0},{3,1},{4,6},{5,7},{6,4},{7,5},{8,10},{9,11},{10,... | collective-permute-start | bytes 786440 | tf_op jit(solution)/shard_map/ppermute | solution.py:493

commit v3 on v2

--- a/solution.py
+++ b/solution.py
@@ -13,6 +13,7 @@
 BLOCK = 128
 SMALL = 32
 BAND = 256
+SWAP_ORDER = (7, 6, 3, 5, 2, 4, 1)
 WEIGHT_ROWS = 128
 MOST_VMEM = 56
 SCAN_VMEM = 52.25
@@ -231,8 +232,14 @@
             )
         )
         leaving[-1].start()
+    if swap:
+        target = factor_hbm.at[value_heads, pl.ds(0, DK)]
+        leaving.append(
+            pltpu.make_async_copy(summary_ref.at[partner(0, swap)], target, out_sems.at[len(leaving)])
+        )
+        leaving[-1].start()
     for place, out_ref in enumerate(summaries):
-        out_ref[...] = summary_ref[partner(place, swap)]
+        out_ref[...] = summary_ref[partner(place + 1 if swap else place, swap)]
     for copy in leaving:
         copy.wait()
 
@@ -251,8 +258,12 @@
     map_ref,
     out_sems,
 ):
+    repeat = factor_ref.shape[0] // (k_hbm.shape[1] // DK)
+    groups = [pl.ds(head, repeat) for head in range(0, factor_ref.shape[0], repeat)]
     copies = fetch(
-        [(decay_hbm, decay_ref), (q_hbm, q_ref), (k_hbm, k_ref), (factor_hbm, factor_ref)], sems
+        [(decay_hbm, decay_ref), (q_hbm, q_ref), (k_hbm, k_ref)]
+        + [(factor_hbm.at[group], factor_ref.at[group]) for group in groups],
+        sems,
     )
     leaving = []
     for copy in copies[:3]:
@@ -270,8 +281,8 @@
         keys = unit(k_ref[:, lanes])
         for p in range(blocks):
             scores = [dot_transposed(queries[block(p)], keys[block(r)]) for r in range(p + 1)]
-            if key_head == 0 and p == 0:
-                copies[3].wait()
+            if p == 0:
+                copies[3 + key_head].wait()
             for head in range(key_head * repeat, (key_head + 1) * repeat):
                 at = columns[block(p), head : head + 1]
                 total = jnp.concatenate(
@@ -285,7 +296,7 @@
                         damp = jnp.exp(spread)
                     total = total + dot(scores[r] * damp, factor_ref[head, block(r), :])
                 map_ref[head, block(p), :] = total
-        group = pl.ds(key_head * repeat, repeat)
+        group = groups[key_head]
         leaving.append(
             pltpu.make_async_copy(map_ref.at[group], map_hbm.at[group], out_sems.at[key_head])
         )
@@ -307,12 +318,13 @@
             entry_ref[source + 1, head] = state
 
 
-def ordered_scan_kernel(own_hbm, *rest):
+def ordered_scan_kernel(factor_hbm, *rest):
     *arrays, held_ref, entry_ref, sems = rest
     count = entry_ref.shape[0]
     held, own_entry_hbm, entries = arrays[: count - 1], arrays[count - 1], arrays[count:]
     here = partner(0, True)
-    own = pltpu.make_async_copy(own_hbm, held_ref.at[here], sems.at[0])
+    own_summary = factor_hbm.at[factor_hbm.shape[0] - 1, pl.ds(0, DK)]
+    own = pltpu.make_async_copy(own_summary, held_ref.at[here], sems.at[0])
     own.start()
     for i, summary in enumerate(held):
         held_ref[partner(i + 1, True)] = summary[...]
@@ -393,6 +405,13 @@
                 out_ref[:, band - start : band - start + BAND] = result[at : at + rows]
 
 
+def forward_kernel(across_ref, own_ref, up_ref, down_ref, going_ref, staying_ref):
+    outward = lax.axis_index("tp") == 1
+    up, down = up_ref[...], down_ref[...]
+    going_ref[...] = across_ref[...] + jnp.where(outward, up, down)
+    staying_ref[...] = own_ref[...] + jnp.where(outward, down, up)
+
+
 def shape(*dims):
     return jax.ShapeDtypeStruct(dims, jnp.float32)
 
@@ -409,11 +428,10 @@
 
 def partners_swap(arrays, axis):
     count = len(arrays)
-    away = [
-        lax.ppermute(arrays[i], axis, [(d, d ^ i) for d in range(count)])
-        for i in range(count - 1, 0, -1)
-    ]
-    return [arrays[0]] + away[::-1]
+    arrays = list(arrays)
+    for i in [i for i in SWAP_ORDER if i < count]:
+        arrays[i] = lax.ppermute(arrays[i], axis, [(d, d ^ i) for d in range(count)])
+    return arrays
 
 
 class Swap(typing.NamedTuple):
@@ -425,11 +443,11 @@
     return heads == count and count & (count - 1) == 0 and count <= 8
 
 
-def entering_states(summaries, swap, beside, after):
-    heads = len(summaries)
+def entering_states(factors, summaries, swap, beside, after):
+    heads = factors.shape[0] - 1
     count = lax.axis_size("ctx")
     if swap:
-        held = partners_swap(summaries, "ctx")
+        held = partners_swap([factors, *summaries], "ctx")
         held, beside = lax.optimization_barrier((held, beside))
         entry = shape(DK, DV)
         entries = pl.pallas_call(
@@ -477,28 +495,31 @@
         return lax.psum_scatter(whole, axis, scatter_dimension=0, tiled=True)
     half = columns // 2
     halves = [(0, half), (half, half)]
-    outward = lax.axis_index(axis) == 1
     opposite = project([(3, *h) for h in halves], FIRST_VMEM)
     steps = [
         (lax.ppermute(piece, axis, [(0, 1), (1, 2)]), lax.ppermute(piece, axis, [(3, 2), (2, 1)]))
         for piece in opposite
     ]
-    *across, near, own = project(
-        [(2, *h) for h in halves] + [(1, 0, columns), (0, 0, columns)], LATER_VMEM
-    )
-    from_end = [jnp.where(outward, up, down) for up, down in steps]
-    from_inner = [jnp.where(outward, down, up) for up, down in steps]
-    going = [piece + came for piece, came in zip(across, from_end)]
-    going[1], near = lax.optimization_barrier((going[1], near))
-    from_across = [lax.ppermute(piece, axis, [(i, i ^ 2) for i in range(4)]) for piece in going]
+    *pieces, near = project(
+        [(2, *h) for h in halves] + [(0, *h) for h in halves] + [(1, 0, columns)], LATER_VMEM
+    )
     from_near = lax.ppermute(near, axis, [(i, i ^ 1) for i in range(4)])
-    rest = [inner + far for inner, far in zip(from_inner, from_across)]
-    return (own + from_near) + jnp.concatenate(rest, axis=1)
+    sums = []
+    for across, own, step in zip(pieces[:2], pieces[2:], steps):
+        going, staying = pl.pallas_call(
+            forward_kernel,
+            out_shape=[shape(*own.shape)] * 2,
+            compiler_params=params(LATER_VMEM),
+            name="forward",
+        )(across, own, *step)
+        sums.append(staying + lax.ppermute(going, axis, [(i, i ^ 2) for i in range(4)]))
+    return from_near + jnp.concatenate(sums, axis=1)
 
 
 def per_device(queries, key_vectors, values, decays, strengths, out_gate, norm_gain, out_weight):
     tokens = queries.shape[0]
     heads = values.shape[1] // DV
+    key_heads = queries.shape[1] // DK
     depth, columns = out_weight.shape
     rows = tokens // lax.axis_size("tp")
     gain = norm_gain.reshape(1, DV)
@@ -513,14 +534,15 @@
 
     factor_shape = shape(heads, tokens, DK + DV)
     groups = pl.cdiv(heads, HEADS_AT_ONCE)
+    sent = heads - 1 if swap.heads else heads
     factors, *summaries = pl.pallas_call(
         functools.partial(summary_kernel, swap=swap.heads),
         in_specs=[HBM] * 4,
-        out_specs=[HBM] + [VMEM] * heads,
-        out_shape=[factor_shape] + [shape(DK, DK + DV)] * heads,
+        out_specs=[HBM] + [VMEM] * sent,
+        out_shape=[shape(heads + 1, tokens, DK + DV)] + [shape(DK, DK + DV)] * sent,
         scratch_shapes=buffers(decays, strengths, key_vectors, values)
         + [pltpu.VMEM(factor_shape.shape, jnp.float32), pltpu.VMEM((heads, DK, DK + DV), jnp.float32)]
-        + [pltpu.SemaphoreType.DMA((groups,))],
+        + [pltpu.SemaphoreType.DMA((groups + 1,))],
         compiler_params=params(MOST_VMEM),
         name="state_summary",
     )(decays, strengths, key_vectors, values)
@@ -529,14 +551,14 @@
         in_specs=[HBM] * 4,
         out_specs=HBM,
         out_shape=factor_shape,
-        scratch_shapes=buffers(decays, queries, key_vectors, factors)
-        + [pltpu.VMEM(factor_shape.shape, jnp.float32)]
-        + [pltpu.SemaphoreType.DMA((queries.shape[1] // DK,))],
+        scratch_shapes=[pltpu.VMEM(a.shape, jnp.float32) for a in (decays, queries, key_vectors)]
+        + [pltpu.VMEM(factor_shape.shape, jnp.float32), pltpu.SemaphoreType.DMA((3 + key_heads,))]
+        + [pltpu.VMEM(factor_shape.shape, jnp.float32), pltpu.SemaphoreType.DMA((key_heads,))],
         compiler_params=params(MOST_VMEM),
         cost_estimate=cost(3 * 2 * heads * tokens * tokens * 384, factors, factors, queries),
         name="output_maps",
     )(decays, queries, key_vectors, factors)
-    states, maps, weights = entering_states(summaries, swap.heads, maps, out_weight)
+    states, maps, weights = entering_states(factors, summaries, swap.heads, maps, out_weight)
     parts = pl.pallas_call(
         weight_kernel,
         in_specs=[HBM],

time: 104 us -> 93.7 us (0.901)
  local copies, waits for them, and re-layouts: 9.93 us -> 0.02 us
  other arithmetic: 2.96 us -> 0.91 us
  starting transfers between devices: 31.2 us -> 32.3 us
    unnamed x22 -> x6, local copies, waits for them, and re-layouts: 9.93 us -> 0.02 us
    ppermute x2, starting transfers between devices: 6.29 us -> 3.03 us  [project_and_sum(): lax.ppermute(going, axis, [(i, i ^ 2) for i in range(4)])]
    ppermute x1, starting transfers between devices: 0.01 us -> 2.7 us  [project_and_sum(): from_near = lax.ppermute(near, axis, [(i, i ^ 1) for i in range(4)])]
    ppermute x2, starting transfers between devices: 6.9 us -> 9.28 us  [project_and_sum(): lax.ppermute(piece, axis, [(0, 1), (1, 2)])]
    add x5 -> x3, other arithmetic: 2.96 us -> 0.91 us  [the longest x1 0.85 us: project_and_sum(): return from_near + jnp.concatenate(sums, axis=1)]
    ppermute x2, waiting for transfers between devices: 19.6 us -> 21.6 us  [project_and_sum(): lax.ppermute(going, axis, [(i, i ^ 2) for i in range(4)])]
    ppermute x1, waiting for transfers between devices: 1.74 us -> 0.01 us  [project_and_sum(): from_near = lax.ppermute(near, axis, [(i, i ^ 1) for i in range(4)])]
  transfers between devices with their start and end apart: 21 -> 21, of which waited for: 6 -> 5; matrix products, arithmetic and copies ran while one was open for 2% -> 0% of each run, Pallas kernels for 16% -> 18%
where the time goes in v3:
time: 93.7 us; the launch traced here: 93.4 us
  Pallas kernels  34.9 us (37%)
  starting transfers between devices  32.3 us (34%)
  waiting for transfers between devices  25 us (27%)
    ppermute x2, waiting for transfers between devices, project_and_sum(): lax.ppermute(going, axis, [(i, i ^ 2) for i in range(4)])  21.6 us
    ppermute x14, starting transfers between devices, partners_swap(): lax.ppermute(arrays[i], axis, [(d, d ^ i) for d in range(count)])  16 us
    pallas_call x2, Pallas kernels, project(): pl.pallas_call(functools.partial(projection_kernel, pieces=[(index, start...  11.8 us
    pallas_call x1, Pallas kernels, per_device(): pl.pallas_call(functools.partial(summary_kernel, swap=swap.heads), in_spe...  11.3 us
    ppermute x2, starting transfers between devices, project_and_sum(): lax.ppermute(piece, axis, [(0, 1), (1, 2)])  9.28 us
    pallas_call x1, Pallas kernels, per_device(): pl.pallas_call(output_kernel, in_specs=[HBM] * 4, out_specs=HBM, out_shap...  5.89 us
    pallas_call x1, Pallas kernels, per_device(): pl.pallas_call(weight_kernel, in_specs=[HBM], out_shape=jax.ShapeDtypeStr...  3.62 us
    ppermute x14, waiting for transfers between devices, partners_swap(): lax.ppermute(arrays[i], axis, [(d, d ^ i) for d in range(count)])  3.38 us
  transfers between devices with their start and end apart: 21, of which 5 were waited for; matrix products, arithmetic and copies ran while one was open for 0% of the time, Pallas kernels for 18%

profile of v3, /device:TPU:0, one launch (start us, length us, event | category | flops | bytes accessed | tf_op | source)
XLA Modules:
  0.0 93.4 jit_solution(3764608925203343902)
XLA Ops:
  0.0 11.3 %state_summary.1 = (f32[9,256,256]{2,1,0:T(8,128)}, f32[128,256]{1,0:T(8,128)}, f32[128,256]{1,0:T(8,128)}, f32[128,256]{1,0:T(8,128)}, f32[128,256]{1,0:T(8,128...) custom-call(f32[8,256]{1,0:T(8,128)} %decay_hbm.3, f32[8,256]{1,0:T(8,128)} %strength_hbm.1, ...), custom_call_target="tpu_custom_call" | custom-call | tf_op jit(solution)/shard_map/state_summary/pallas_call | solution.py:538
  11.3 0.5 collective-permute-start
  11.9 2.6 %collective-permute-start.1 = (f32[128,256]{1,0:T(8,128)}, f32[128,256]{1,0:T(8,128)S(1)}, u32[]{:S(2)}, u32[]{:S(2)}) collective-permute-start(f32[128,256]{1,0:T(8,128)} %get-tuple-element.52), channel_id=1, source_target_pairs={{0,8},{4,12},{8,0},{12,4},{16,24},{20,28},{24,16},{28,20},{1,9},{5... | collective-permute-start | bytes 393224 | tf_op jit(solution)/shard_map/ppermute | solution.py:433
  14.4 0.1 collective-permute-start.2
  14.5 1.8 %collective-permute-start.3 = (f32[128,256]{1,0:T(8,128)}, f32[128,256]{1,0:T(8,128)S(1)}, u32[]{:S(2)}, u32[]{:S(2)}) collective-permute-start(f32[128,256]{1,0:T(8,128)} %get-tuple-element.54), channel_id=1, source_target_pairs={{0,16},{4,20},{8,24},{12,28},{16,0},{20,4},{24,8},{28,12},{1,17},{... | collective-permute-start | bytes 393224 | tf_op jit(solution)/shard_map/ppermute | solution.py:433
  16.3 0.0 collective-permute-start.4
  16.3 0.0 collective-permute-done.rest_0_
  16.3 2.6 %collective-permute-start.5 = (f32[128,256]{1,0:T(8,128)}, f32[128,256]{1,0:T(8,128)S(1)}, u32[]{:S(2)}, u32[]{:S(2)}) collective-permute-start(f32[128,256]{1,0:T(8,128)} %get-tuple-element.56), channel_id=1, source_target_pairs={{0,24},{4,28},{8,16},{12,20},{16,8},{20,12},{24,0},{28,4},{1,25},{... | collective-permute-start | bytes 393224 | tf_op jit(solution)/shard_map/ppermute | solution.py:433
  18.9 0.1 collective-permute-done.1.rest_1_
  19.0 1.7 %collective-permute-start.6 = (f32[128,256]{1,0:T(8,128)}, f32[128,256]{1,0:T(8,128)S(1)}, u32[]{:S(2)}, u32[]{:S(2)}) collective-permute-start(f32[128,256]{1,0:T(8,128)} %get-tuple-element.57), channel_id=1, source_target_pairs={{0,28},{4,24},{8,20},{12,16},{16,12},{20,8},{24,4},{28,0},{1,29},{... | collective-permute-start | bytes 393224 | tf_op jit(solution)/shard_map/ppermute | solution.py:433
  20.7 5.9 %output_maps.1.map_hbm = f32[8,256,256]{2,1,0:T(8,128)} custom-call(f32[8,256]{1,0:T(8,128)} %decay_hbm.3, f32[256,512]{1,0:T(8,128)} %q_hbm.1, f32[256,512]{1,0:T(8,128)} %k_hbm.3, f32[9,256,256]{2,1,0:T(8,128)} %get-tuple-element.59.factor_hbm), custom_call_target="tpu_custom_call" | custom-call | flops 1207959552 | bytes 5242880 | tf_op jit(solution)/shard_map/output_maps/pallas_call | solution.py:549
  26.6 0.0 collective-permute-done.2.rest_2_
  26.6 0.0 collective-permute-done.3.rest_3_
  26.6 1.6 %collective-permute-done.4.rest_4_ = f32[128,256]{1,0:T(8,128)S(1)} collective-permute-done((f32[128,256]{1,0:T(8,128)}, f32[128,256]{1,0:T(8,128)S(1)}, u32[]{:S(2)}, u32[]{:S(2)}) %collective-permute-start.4) | collective-permute-done | bytes 131104 | tf_op jit(solution)/shard_map/ppermute | solution.py:433
  28.3 0.0 collective-permute-done.5.rest_5_
  28.3 0.0 collective-permute-done.6.rest_6_
  28.3 2.1 %state_scan.1 = (f32[128,128]{1,0:T(8,128)S(1)}, f32[128,128]{1,0:T(8,128)S(1)}, f32[128,128]{1,0:T(8,128)S(1)}, f32[128,128]{1,0:T(8,128)S(1)}, f32[128,128]{1,...) custom-call(f32[9,256,256]{2,1,0:T(8,128)} %get-tuple-element.59.factor_hbm, ...), custom_call_target="tpu_custom_call" | custom-call | tf_op jit(solution)/shard_map/state_scan/pallas_call | solution.py:453
  30.4 0.0 copy-start.1
  30.4 0.0 copy-start.2
  30.4 0.5 collective-permute-start.7
  30.9 1.7 %collective-permute-start.8 = (f32[128,128]{1,0:T(8,128)S(1)}, f32[128,128]{1,0:T(8,128)S(1)}, u32[]{:S(2)}, u32[]{:S(2)}) collective-permute-start(f32[128,128]{1,0:T(8,128)S(1)} %get-tuple-element.78), channel_id=1, source_target_pairs={{0,8},{4,12},{8,0},{12,4},{16,24},{20,28},{24,16},{28,20},{1,9},{5... | collective-permute-start | bytes 196616 | tf_op jit(solution)/shard_map/ppermute | solution.py:433
  32.6 0.0 collective-permute-start.9
  32.6 1.5 %collective-permute-start.10 = (f32[128,128]{1,0:T(8,128)S(1)}, f32[128,128]{1,0:T(8,128)S(1)}, u32[]{:S(2)}, u32[]{:S(2)}) collective-permute-start(f32[128,128]{1,0:T(8,128)S(1)} %get-tuple-element.80), channel_id=1, source_target_pairs={{0,16},{4,20},{8,24},{12,28},{16,0},{20,4},{24,8},{28,12},{1,17},{... | collective-permute-start | bytes 196616 | tf_op jit(solution)/shard_map/ppermute | solution.py:433
  34.1 0.3 collective-permute-start.11
  34.4 0.0 collective-permute-done.7.rest_0_
  34.4 2.7 %collective-permute-start.12 = (f32[128,128]{1,0:T(8,128)S(1)}, f32[128,128]{1,0:T(8,128)S(1)}, u32[]{:S(2)}, u32[]{:S(2)}) collective-permute-start(f32[128,128]{1,0:T(8,128)S(1)} %get-tuple-element.82), channel_id=1, source_target_pairs={{0,24},{4,28},{8,16},{12,20},{16,8},{20,12},{24,0},{28,4},{1,25},{... | collective-permute-start | bytes 196616 | tf_op jit(solution)/shard_map/ppermute | solution.py:433
  37.1 0.0 collective-permute-done.8.rest_1_
  37.1 0.0 collective-permute-start.13
  37.1 3.6 %weight_parts.1.parts_ref = bf16[2,1024,2048]{2,1,0:T(8,128)(2,1)S(1)} custom-call(f32[1024,2048]{1,0:T(8,128)} %weight_hbm), custom_call_target="tpu_custom_call" | custom-call | flops 12582912 | bytes 16777216 | tf_op jit(solution)/shard_map/weight_parts/pallas_call | solution.py:562
  40.7 0.0 collective-permute-done.10.rest_3_
  40.8 1.6 %collective-permute-done.13.rest_6_ = f32[128,128]{1,0:T(8,128)S(1)} collective-permute-done((f32[128,128]{1,0:T(8,128)S(1)}, f32[128,128]{1,0:T(8,128)S(1)}, u32[]{:S(2)}, u32[]{:S(2)}) %collective-permute-start.13) | collective-permute-done | bytes 65568 | tf_op jit(solution)/shard_map/ppermute | solution.py:433
  42.4 4.4 %projection.3 = (f32[64,1024]{1,0:T(8,128)S(1)}, f32[64,1024]{1,0:T(8,128)S(1)}) custom-call(f32[8,256,256]{2,1,0:T(8,128)S(1)} %copy-done, f32[256,1024]{1,0:T(8,128)S(1)} %copy-done.1, f32[1,128]{1,0:T(1,128)S(1)} %bitcast.1, bf16[2,1024,2048]{2,1,0:T(8,128)(2,1)S(1)} %weight_parts.1.parts_ref, f32[128,128]{1,0:T(8,128)S(1)} %get-tuple-element.76.own_hbm, ...), custom_call_target="tpu_custom_call" | custom-call | flops 805306368 | bytes 8388608 | tf_op jit(solution)/shard_map/projection/pallas_call | solution.py:579
  46.8 0.7 collective-permute-start.16
  47.5 4.1 %collective-permute-start.15 = (f32[64,1024]{1,0:T(8,128)S(1)}, f32[64,1024]{1,0:T(8,128)S(1)}, u32[]{:S(2)}, u32[]{:S(2)}) collective-permute-start(f32[64,1024]{1,0:T(8,128)S(1)} %get-tuple-element.87), channel_id=1, source_target_pairs={{0,1},{1,2},{4,5},{5,6},{8,9},{9,10},{12,13},{13,14},{16,17},{17,1... | collective-permute-start | bytes 786440 | tf_op jit(solution)/shard_map/ppermute | solution.py:500
  51.6 0.7 collective-permute-start.19
  52.3 5.2 %collective-permute-start.18 = (f32[64,1024]{1,0:T(8,128)S(1)}, f32[64,1024]{1,0:T(8,128)S(1)}, u32[]{:S(2)}, u32[]{:S(2)}) collective-permute-start(f32[64,1024]{1,0:T(8,128)S(1)} %get-tuple-element.92), channel_id=1, source_target_pairs={{0,1},{1,2},{4,5},{5,6},{8,9},{9,10},{12,13},{13,14},{16,17},{17,1... | collective-permute-start | bytes 786440 | tf_op jit(solution)/shard_map/ppermute | solution.py:500
  57.5 7.4 %projection.2 = (f32[64,1024]{1,0:T(8,128)S(1)}, f32[64,1024]{1,0:T(8,128)S(1)}, f32[64,1024]{1,0:T(8,128)S(1)}, f32[64,1024]{1,0:T(8,128)S(1)}, f32[64,2048]{1,0:T(8,128)S(1)}) custom-call(f32[8,256,256]{2,1,0:T(8,128)S(1)} %copy-done, f32[256,1024]{1,0:T(8,128)S(1)} %copy-done.1, f32[1,128]{1,0:T(1,128)S(1)} %bitcast.2, ...), custom_call_target="tpu_custom_call" | custom-call | flops 2415919104 | bytes 8388608 | tf_op jit(solution)/shard_map/projection/pallas_call | solution.py:579
  64.9 2.7 %collective-permute-start.14 = (f32[64,2048]{1,0:T(8,128)S(1)}, f32[64,2048]{1,0:T(8,128)S(1)}, u32[]{:S(2)}, u32[]{:S(2)}) collective-permute-start(f32[64,2048]{1,0:T(8,128)S(1)} %get-tuple-element.84), channel_id=1, source_target_pairs={{0,1},{1,0},{2,3},{3,2},{4,5},{5,4},{6,7},{7,6},{8,9},{9,8},{10,11... | collective-permute-start | bytes 1572872 | tf_op jit(solution)/shard_map/ppermute | solution.py:506
  67.6 0.0 collective-permute-done.16.down_ref
  67.6 0.0 collective-permute-done.15.up_ref
  67.6 0.1 forward.2
  67.7 0.1 collective-permute-start.17
  67.8 0.1 forward.3
  67.9 3.0 %collective-permute-start.20 = (f32[64,1024]{1,0:T(8,128)S(1)}, f32[64,1024]{1,0:T(8,128)S(1)}, u32[]{:S(2)}, u32[]{:S(2)}) collective-permute-start(f32[64,1024]{1,0:T(8,128)S(1)} %get-tuple-element.94), channel_id=1, source_target_pairs={{0,2},{1,3},{2,0},{3,1},{4,6},{5,7},{6,4},{7,5},{8,10},{9,11},{10,... | collective-permute-start | bytes 786440 | tf_op jit(solution)/shard_map/ppermute | solution.py:515
  70.9 14.7 %collective-permute-done.17 = f32[64,1024]{1,0:T(8,128)S(1)} collective-permute-done((f32[64,1024]{1,0:T(8,128)S(1)}, f32[64,1024]{1,0:T(8,128)S(1)}, u32[]{:S(2)}, u32[]{:S(2)}) %collective-permute-start.17) | collective-permute-done | bytes 262176 | tf_op jit(solution)/shard_map/ppermute | solution.py:515
  85.6 6.8 %collective-permute-done.20 = f32[64,1024]{1,0:T(8,128)S(1)} collective-permute-done((f32[64,1024]{1,0:T(8,128)S(1)}, f32[64,1024]{1,0:T(8,128)S(1)}, u32[]{:S(2)}, u32[]{:S(2)}) %collective-permute-start.20) | collective-permute-done | bytes 262176 | tf_op jit(solution)/shard_map/ppermute | solution.py:515
  92.5 0.0 collective-permute-done.14
  92.5 0.9 maximum_add_fusion
  (11 shorter events, 0.1 us)
Async XLA Ops:
  11.3 4.9 %collective-permute-start = (f32[128,256]{1,0:T(8,128)}, f32[128,256]{1,0:T(8,128)S(1)}, u32[]{:S(2)}, u32[]{:S(2)}) collective-permute-start(f32[128,256]{1,0:T(8,128)} %get-tuple-element.51), channel_id=1, source_target_pairs={{0,4},{4,0},{8,12},{12,8},{16,20},{20,16},{24,28},{28,24},{1,5},{5... | collective-permute-start | bytes 393224 | tf_op jit(solution)/shard_map/ppermute | solution.py:433
  11.9 7.1 %collective-permute-start.1 = (f32[128,256]{1,0:T(8,128)}, f32[128,256]{1,0:T(8,128)S(1)}, u32[]{:S(2)}, u32[]{:S(2)}) collective-permute-start(f32[128,256]{1,0:T(8,128)} %get-tuple-element.52), channel_id=1, source_target_pairs={{0,8},{4,12},{8,0},{12,4},{16,24},{20,28},{24,16},{28,20},{1,9},{5... | collective-permute-start | bytes 393224 | tf_op jit(solution)/shard_map/ppermute | solution.py:433
  14.4 12.2 %collective-permute-start.2 = (f32[128,256]{1,0:T(8,128)}, f32[128,256]{1,0:T(8,128)S(1)}, u32[]{:S(2)}, u32[]{:S(2)}) collective-permute-start(f32[128,256]{1,0:T(8,128)} %get-tuple-element.53), channel_id=1, source_target_pairs={{0,12},{4,8},{8,4},{12,0},{16,28},{20,24},{24,20},{28,16},{1,13},{... | collective-permute-start | bytes 393224 | tf_op jit(solution)/shard_map/ppermute | solution.py:433
  14.5 12.1 %collective-permute-start.3 = (f32[128,256]{1,0:T(8,128)}, f32[128,256]{1,0:T(8,128)S(1)}, u32[]{:S(2)}, u32[]{:S(2)}) collective-permute-start(f32[128,256]{1,0:T(8,128)} %get-tuple-element.54), channel_id=1, source_target_pairs={{0,16},{4,20},{8,24},{12,28},{16,0},{20,4},{24,8},{28,12},{1,17},{... | collective-permute-start | bytes 393224 | tf_op jit(solution)/shard_map/ppermute | solution.py:433
  16.3 12.0 %collective-permute-start.4 = (f32[128,256]{1,0:T(8,128)}, f32[128,256]{1,0:T(8,128)S(1)}, u32[]{:S(2)}, u32[]{:S(2)}) collective-permute-start(f32[128,256]{1,0:T(8,128)} %get-tuple-element.55), channel_id=1, source_target_pairs={{0,20},{4,16},{8,28},{12,24},{16,4},{20,0},{24,12},{28,8},{1,21},{... | collective-permute-start | bytes 393224 | tf_op jit(solution)/shard_map/ppermute | solution.py:433
  16.3 12.0 %collective-permute-start.5 = (f32[128,256]{1,0:T(8,128)}, f32[128,256]{1,0:T(8,128)S(1)}, u32[]{:S(2)}, u32[]{:S(2)}) collective-permute-start(f32[128,256]{1,0:T(8,128)} %get-tuple-element.56), channel_id=1, source_target_pairs={{0,24},{4,28},{8,16},{12,20},{16,8},{20,12},{24,0},{28,4},{1,25},{... | collective-permute-start | bytes 393224 | tf_op jit(solution)/shard_map/ppermute | solution.py:433
  19.0 9.3 %collective-permute-start.6 = (f32[128,256]{1,0:T(8,128)}, f32[128,256]{1,0:T(8,128)S(1)}, u32[]{:S(2)}, u32[]{:S(2)}) collective-permute-start(f32[128,256]{1,0:T(8,128)} %get-tuple-element.57), channel_id=1, source_target_pairs={{0,28},{4,24},{8,20},{12,16},{16,12},{20,8},{24,4},{28,0},{1,29},{... | collective-permute-start | bytes 393224 | tf_op jit(solution)/shard_map/ppermute | solution.py:433
  30.3 12.0 %copy-start = (f32[8,256,256]{2,1,0:T(8,128)S(1)}, f32[8,256,256]{2,1,0:T(8,128)}, u32[]{:S(2)}) copy-start(f32[8,256,256]{2,1,0:T(8,128)} %output_maps.1.map_hbm) | copy-start | bytes 6291460
  30.4 12.0 %copy-start.1 = (f32[256,1024]{1,0:T(8,128)S(1)}, f32[256,1024]{1,0:T(8,128)}, u32[]{:S(2)}) copy-start(f32[256,1024]{1,0:T(8,128)} %gate_hbm.3) | copy-start | bytes 3145732
  30.4 12.0 %copy-start.2 = (f32[128]{0:T(128)S(1)}, f32[128]{0:T(128)}, u32[]{:S(2)}) copy-start(f32[128]{0:T(128)} %param.14) | copy-start | bytes 1540
  30.4 4.0 %collective-permute-start.7 = (f32[128,128]{1,0:T(8,128)S(1)}, f32[128,128]{1,0:T(8,128)S(1)}, u32[]{:S(2)}, u32[]{:S(2)}) collective-permute-start(f32[128,128]{1,0:T(8,128)S(1)} %get-tuple-element.77), channel_id=1, source_target_pairs={{0,4},{4,0},{8,12},{12,8},{16,20},{20,16},{24,28},{28,24},{1,5},{5... | collective-permute-start | bytes 196616 | tf_op jit(solution)/shard_map/ppermute | solution.py:433
  30.9 6.2 %collective-permute-start.8 = (f32[128,128]{1,0:T(8,128)S(1)}, f32[128,128]{1,0:T(8,128)S(1)}, u32[]{:S(2)}, u32[]{:S(2)}) collective-permute-start(f32[128,128]{1,0:T(8,128)S(1)} %get-tuple-element.78), channel_id=1, source_target_pairs={{0,8},{4,12},{8,0},{12,4},{16,24},{20,28},{24,16},{28,20},{1,9},{5... | collective-permute-start | bytes 196616 | tf_op jit(solution)/shard_map/ppermute | solution.py:433
  32.6 8.1 %collective-permute-start.9 = (f32[128,128]{1,0:T(8,128)S(1)}, f32[128,128]{1,0:T(8,128)S(1)}, u32[]{:S(2)}, u32[]{:S(2)}) collective-permute-start(f32[128,128]{1,0:T(8,128)S(1)} %get-tuple-element.79), channel_id=1, source_target_pairs={{0,12},{4,8},{8,4},{12,0},{16,28},{20,24},{24,20},{28,16},{1,13},{... | collective-permute-start | bytes 196616 | tf_op jit(solution)/shard_map/ppermute | solution.py:433
  32.6 8.1 %collective-permute-start.10 = (f32[128,128]{1,0:T(8,128)S(1)}, f32[128,128]{1,0:T(8,128)S(1)}, u32[]{:S(2)}, u32[]{:S(2)}) collective-permute-start(f32[128,128]{1,0:T(8,128)S(1)} %get-tuple-element.80), channel_id=1, source_target_pairs={{0,16},{4,20},{8,24},{12,28},{16,0},{20,4},{24,8},{28,12},{1,17},{... | collective-permute-start | bytes 196616 | tf_op jit(solution)/shard_map/ppermute | solution.py:433
  34.1 6.6 %collective-permute-start.11 = (f32[128,128]{1,0:T(8,128)S(1)}, f32[128,128]{1,0:T(8,128)S(1)}, u32[]{:S(2)}, u32[]{:S(2)}) collective-permute-start(f32[128,128]{1,0:T(8,128)S(1)} %get-tuple-element.81), channel_id=1, source_target_pairs={{0,20},{4,16},{8,28},{12,24},{16,4},{20,0},{24,12},{28,8},{1,21},{... | collective-permute-start | bytes 196616 | tf_op jit(solution)/shard_map/ppermute | solution.py:433
  34.4 6.3 %collective-permute-start.12 = (f32[128,128]{1,0:T(8,128)S(1)}, f32[128,128]{1,0:T(8,128)S(1)}, u32[]{:S(2)}, u32[]{:S(2)}) collective-permute-start(f32[128,128]{1,0:T(8,128)S(1)} %get-tuple-element.82), channel_id=1, source_target_pairs={{0,24},{4,28},{8,16},{12,20},{16,8},{20,12},{24,0},{28,4},{1,25},{... | collective-permute-start | bytes 196616 | tf_op jit(solution)/shard_map/ppermute | solution.py:433
  37.1 5.3 %collective-permute-start.13 = (f32[128,128]{1,0:T(8,128)S(1)}, f32[128,128]{1,0:T(8,128)S(1)}, u32[]{:S(2)}, u32[]{:S(2)}) collective-permute-start(f32[128,128]{1,0:T(8,128)S(1)} %get-tuple-element.83), channel_id=1, source_target_pairs={{0,28},{4,24},{8,20},{12,16},{16,12},{20,8},{24,4},{28,0},{1,29},{... | collective-permute-start | bytes 196616 | tf_op jit(solution)/shard_map/ppermute | solution.py:433
  46.8 20.8 %collective-permute-start.16 = (f32[64,1024]{1,0:T(8,128)S(1)}, f32[64,1024]{1,0:T(8,128)S(1)}, u32[]{:S(2)}, u32[]{:S(2)}) collective-permute-start(f32[64,1024]{1,0:T(8,128)S(1)} %get-tuple-element.87), channel_id=1, source_target_pairs={{3,2},{2,1},{7,6},{6,5},{11,10},{10,9},{15,14},{14,13},{19,18},{18... | collective-permute-start | bytes 786440 | tf_op jit(solution)/shard_map/ppermute | solution.py:500
  47.5 20.1 %collective-permute-start.15 = (f32[64,1024]{1,0:T(8,128)S(1)}, f32[64,1024]{1,0:T(8,128)S(1)}, u32[]{:S(2)}, u32[]{:S(2)}) collective-permute-start(f32[64,1024]{1,0:T(8,128)S(1)} %get-tuple-element.87), channel_id=1, source_target_pairs={{0,1},{1,2},{4,5},{5,6},{8,9},{9,10},{12,13},{13,14},{16,17},{17,1... | collective-permute-start | bytes 786440 | tf_op jit(solution)/shard_map/ppermute | solution.py:500
  51.6 16.1 %collective-permute-start.19 = (f32[64,1024]{1,0:T(8,128)S(1)}, f32[64,1024]{1,0:T(8,128)S(1)}, u32[]{:S(2)}, u32[]{:S(2)}) collective-permute-start(f32[64,1024]{1,0:T(8,128)S(1)} %get-tuple-element.92), channel_id=1, source_target_pairs={{3,2},{2,1},{7,6},{6,5},{11,10},{10,9},{15,14},{14,13},{19,18},{18... | collective-permute-start | bytes 786440 | tf_op jit(solution)/shard_map/ppermute | solution.py:500
  52.3 15.5 %collective-permute-start.18 = (f32[64,1024]{1,0:T(8,128)S(1)}, f32[64,1024]{1,0:T(8,128)S(1)}, u32[]{:S(2)}, u32[]{:S(2)}) collective-permute-start(f32[64,1024]{1,0:T(8,128)S(1)} %get-tuple-element.92), channel_id=1, source_target_pairs={{0,1},{1,2},{4,5},{5,6},{8,9},{9,10},{12,13},{13,14},{16,17},{17,1... | collective-permute-start | bytes 786440 | tf_op jit(solution)/shard_map/ppermute | solution.py:500
  64.9 27.6 %collective-permute-start.14 = (f32[64,2048]{1,0:T(8,128)S(1)}, f32[64,2048]{1,0:T(8,128)S(1)}, u32[]{:S(2)}, u32[]{:S(2)}) collective-permute-start(f32[64,2048]{1,0:T(8,128)S(1)} %get-tuple-element.84), channel_id=1, source_target_pairs={{0,1},{1,0},{2,3},{3,2},{4,5},{5,4},{6,7},{7,6},{8,9},{9,8},{10,11... | collective-permute-start | bytes 1572872 | tf_op jit(solution)/shard_map/ppermute | solution.py:506
  67.7 17.9 %collective-permute-start.17 = (f32[64,1024]{1,0:T(8,128)S(1)}, f32[64,1024]{1,0:T(8,128)S(1)}, u32[]{:S(2)}, u32[]{:S(2)}) collective-permute-start(f32[64,1024]{1,0:T(8,128)S(1)} %get-tuple-element.89), channel_id=1, source_target_pairs={{0,2},{1,3},{2,0},{3,1},{4,6},{5,7},{6,4},{7,5},{8,10},{9,11},{10,... | collective-permute-start | bytes 786440 | tf_op jit(solution)/shard_map/ppermute | solution.py:515
  67.9 24.6 %collective-permute-start.20 = (f32[64,1024]{1,0:T(8,128)S(1)}, f32[64,1024]{1,0:T(8,128)S(1)}, u32[]{:S(2)}, u32[]{:S(2)}) collective-permute-start(f32[64,1024]{1,0:T(8,128)S(1)} %get-tuple-element.94), channel_id=1, source_target_pairs={{0,2},{1,3},{2,0},{3,1},{4,6},{5,7},{6,4},{7,5},{8,10},{9,11},{10,... | collective-permute-start | bytes 786440 | tf_op jit(solution)/shard_map/ppermute | solution.py:515

commit v4 on v3

--- a/solution.py
+++ b/solution.py
@@ -493,27 +493,19 @@
     if count != 4:
         whole = jnp.concatenate(project([(i, 0, columns) for i in range(count)], LATER_VMEM), axis=0)
         return lax.psum_scatter(whole, axis, scatter_dimension=0, tiled=True)
-    half = columns // 2
-    halves = [(0, half), (half, half)]
-    opposite = project([(3, *h) for h in halves], FIRST_VMEM)
-    steps = [
-        (lax.ppermute(piece, axis, [(0, 1), (1, 2)]), lax.ppermute(piece, axis, [(3, 2), (2, 1)]))
-        for piece in opposite
-    ]
-    *pieces, near = project(
-        [(2, *h) for h in halves] + [(0, *h) for h in halves] + [(1, 0, columns)], LATER_VMEM
-    )
+    (opposite,) = project([(3, 0, columns)], FIRST_VMEM)
+    up = lax.ppermute(opposite, axis, [(0, 1), (1, 2)])
+    down = lax.ppermute(opposite, axis, [(3, 2), (2, 1)])
+    across, own, near = project([(i, 0, columns) for i in (2, 0, 1)], LATER_VMEM)
     from_near = lax.ppermute(near, axis, [(i, i ^ 1) for i in range(4)])
-    sums = []
-    for across, own, step in zip(pieces[:2], pieces[2:], steps):
-        going, staying = pl.pallas_call(
-            forward_kernel,
-            out_shape=[shape(*own.shape)] * 2,
-            compiler_params=params(LATER_VMEM),
-            name="forward",
-        )(across, own, *step)
-        sums.append(staying + lax.ppermute(going, axis, [(i, i ^ 2) for i in range(4)]))
-    return from_near + jnp.concatenate(sums, axis=1)
+    going, staying = pl.pallas_call(
+        forward_kernel,
+        out_shape=[shape(*own.shape)] * 2,
+        compiler_params=params(LATER_VMEM),
+        name="forward",
+    )(across, own, up, down)
+    from_across = lax.ppermute(going, axis, [(i, i ^ 2) for i in range(4)])
+    return (staying + from_near) + from_across
 
 
 def per_device(queries, key_vectors, values, decays, strengths, out_gate, norm_gain, out_weight):

time: 93.7 us -> 91.1 us (0.972)
  starting transfers between devices: 32.3 us -> 26.9 us
  waiting for transfers between devices: 25 us -> 27.8 us
    ppermute x1, waiting for transfers between devices: 0.01 us -> 14.4 us  [project_and_sum(): from_near = lax.ppermute(near, axis, [(i, i ^ 1) for i in range(4)])]
    ppermute x6 -> x3, waiting for transfers between devices: 21.6 us -> 10 us  [the longest x1 7.87 us: project_and_sum(): from_across = lax.ppermute(going, axis, [(i, i ^ 2) for i in range(4)])]
    ppermute x6 -> x3, starting transfers between devices: 13.7 us -> 8.3 us  [the longest x1 4.11 us: project_and_sum(): up = lax.ppermute(opposite, axis, [(0, 1), (1, 2)])]
  transfers between devices with their start and end apart: 21 -> 18, of which waited for: 5 -> 6; matrix products, arithmetic and copies ran while one was open for 0% -> 0% of each run, Pallas kernels for 18% -> 19%
where the time goes in v4:
time: 91.1 us; the launch traced here: 90.8 us
  Pallas kernels  35 us (38%)
  waiting for transfers between devices  27.8 us (31%)
  starting transfers between devices  26.9 us (30%)
    ppermute x14, starting transfers between devices, partners_swap(): lax.ppermute(arrays[i], axis, [(d, d ^ i) for d in range(count)])  16 us
    ppermute x1, waiting for transfers between devices, project_and_sum(): from_near = lax.ppermute(near, axis, [(i, i ^ 1) for i in range(4)])  14.4 us
    pallas_call x2, Pallas kernels, project(): pl.pallas_call(functools.partial(projection_kernel, pieces=[(index, start...  11.8 us
    pallas_call x1, Pallas kernels, per_device(): pl.pallas_call(functools.partial(summary_kernel, swap=swap.heads), in_spe...  11.4 us
    ppermute x1, waiting for transfers between devices, project_and_sum(): from_across = lax.ppermute(going, axis, [(i, i ^ 2) for i in range(4)])  7.87 us
    pallas_call x1, Pallas kernels, per_device(): pl.pallas_call(output_kernel, in_specs=[HBM] * 4, out_specs=HBM, out_shap...  5.91 us
    ppermute x1, starting transfers between devices, project_and_sum(): up = lax.ppermute(opposite, axis, [(0, 1), (1, 2)])  4.11 us
    pallas_call x1, Pallas kernels, per_device(): pl.pallas_call(weight_kernel, in_specs=[HBM], out_shape=jax.ShapeDtypeStr...  3.62 us
  transfers between devices with their start and end apart: 18, of which 6 were waited for; matrix products, arithmetic and copies ran while one was open for 0% of the time, Pallas kernels for 19%

profile of v4, /device:TPU:0, one launch (start us, length us, event | category | flops | bytes accessed | tf_op | source)
XLA Modules:
  0.0 90.8 jit_solution(6300490090388713190)
XLA Ops:
  0.0 11.4 %state_summary.1 = (f32[9,256,256]{2,1,0:T(8,128)}, f32[128,256]{1,0:T(8,128)}, f32[128,256]{1,0:T(8,128)}, f32[128,256]{1,0:T(8,128)}, f32[128,256]{1,0:T(8,128...) custom-call(f32[8,256]{1,0:T(8,128)} %decay_hbm.3, f32[8,256]{1,0:T(8,128)} %strength_hbm.1, ...), custom_call_target="tpu_custom_call" | custom-call | tf_op jit(solution)/shard_map/state_summary/pallas_call | solution.py:530
  11.4 0.5 collective-permute-start
  11.9 2.6 %collective-permute-start.1 = (f32[128,256]{1,0:T(8,128)}, f32[128,256]{1,0:T(8,128)S(1)}, u32[]{:S(2)}, u32[]{:S(2)}) collective-permute-start(f32[128,256]{1,0:T(8,128)} %get-tuple-element.46), channel_id=1, source_target_pairs={{0,8},{4,12},{8,0},{12,4},{16,24},{20,28},{24,16},{28,20},{1,9},{5... | collective-permute-start | bytes 393224 | tf_op jit(solution)/shard_map/ppermute | solution.py:433
  14.5 0.1 collective-permute-start.2
  14.5 1.8 %collective-permute-start.3 = (f32[128,256]{1,0:T(8,128)}, f32[128,256]{1,0:T(8,128)S(1)}, u32[]{:S(2)}, u32[]{:S(2)}) collective-permute-start(f32[128,256]{1,0:T(8,128)} %get-tuple-element.48), channel_id=1, source_target_pairs={{0,16},{4,20},{8,24},{12,28},{16,0},{20,4},{24,8},{28,12},{1,17},{... | collective-permute-start | bytes 393224 | tf_op jit(solution)/shard_map/ppermute | solution.py:433
  16.3 0.0 collective-permute-start.4
  16.3 0.0 collective-permute-done.rest_0_
  16.3 2.6 %collective-permute-start.5 = (f32[128,256]{1,0:T(8,128)}, f32[128,256]{1,0:T(8,128)S(1)}, u32[]{:S(2)}, u32[]{:S(2)}) collective-permute-start(f32[128,256]{1,0:T(8,128)} %get-tuple-element.50), channel_id=1, source_target_pairs={{0,24},{4,28},{8,16},{12,20},{16,8},{20,12},{24,0},{28,4},{1,25},{... | collective-permute-start | bytes 393224 | tf_op jit(solution)/shard_map/ppermute | solution.py:433
  18.9 0.1 collective-permute-done.1.rest_1_
  19.0 1.7 %collective-permute-start.6 = (f32[128,256]{1,0:T(8,128)}, f32[128,256]{1,0:T(8,128)S(1)}, u32[]{:S(2)}, u32[]{:S(2)}) collective-permute-start(f32[128,256]{1,0:T(8,128)} %get-tuple-element.51), channel_id=1, source_target_pairs={{0,28},{4,24},{8,20},{12,16},{16,12},{20,8},{24,4},{28,0},{1,29},{... | collective-permute-start | bytes 393224 | tf_op jit(solution)/shard_map/ppermute | solution.py:433
  20.7 5.9 %output_maps.1.map_hbm = f32[8,256,256]{2,1,0:T(8,128)} custom-call(f32[8,256]{1,0:T(8,128)} %decay_hbm.3, f32[256,512]{1,0:T(8,128)} %q_hbm.1, f32[256,512]{1,0:T(8,128)} %k_hbm.3, f32[9,256,256]{2,1,0:T(8,128)} %get-tuple-element.53.factor_hbm), custom_call_target="tpu_custom_call" | custom-call | flops 1207959552 | bytes 5242880 | tf_op jit(solution)/shard_map/output_maps/pallas_call | solution.py:541
  26.7 0.0 collective-permute-done.2.rest_2_
  26.7 0.0 collective-permute-done.3.rest_3_
  26.7 1.6 %collective-permute-done.4.rest_4_ = f32[128,256]{1,0:T(8,128)S(1)} collective-permute-done((f32[128,256]{1,0:T(8,128)}, f32[128,256]{1,0:T(8,128)S(1)}, u32[]{:S(2)}, u32[]{:S(2)}) %collective-permute-start.4) | collective-permute-done | bytes 131104 | tf_op jit(solution)/shard_map/ppermute | solution.py:433
  28.3 0.0 collective-permute-done.5.rest_5_
  28.3 0.0 collective-permute-done.6.rest_6_
  28.3 2.1 %state_scan.1 = (f32[128,128]{1,0:T(8,128)S(1)}, f32[128,128]{1,0:T(8,128)S(1)}, f32[128,128]{1,0:T(8,128)S(1)}, f32[128,128]{1,0:T(8,128)S(1)}, f32[128,128]{1,...) custom-call(f32[9,256,256]{2,1,0:T(8,128)} %get-tuple-element.53.factor_hbm, ...), custom_call_target="tpu_custom_call" | custom-call | tf_op jit(solution)/shard_map/state_scan/pallas_call | solution.py:453
  30.4 0.0 copy-start
  30.4 0.0 copy-start.1
  30.4 0.0 copy-start.2
  30.4 0.5 collective-permute-start.7
  30.9 1.7 %collective-permute-start.8 = (f32[128,128]{1,0:T(8,128)S(1)}, f32[128,128]{1,0:T(8,128)S(1)}, u32[]{:S(2)}, u32[]{:S(2)}) collective-permute-start(f32[128,128]{1,0:T(8,128)S(1)} %get-tuple-element.72), channel_id=1, source_target_pairs={{0,8},{4,12},{8,0},{12,4},{16,24},{20,28},{24,16},{28,20},{1,9},{5... | collective-permute-start | bytes 196616 | tf_op jit(solution)/shard_map/ppermute | solution.py:433
  32.6 0.0 collective-permute-start.9
  32.6 1.5 %collective-permute-start.10 = (f32[128,128]{1,0:T(8,128)S(1)}, f32[128,128]{1,0:T(8,128)S(1)}, u32[]{:S(2)}, u32[]{:S(2)}) collective-permute-start(f32[128,128]{1,0:T(8,128)S(1)} %get-tuple-element.74), channel_id=1, source_target_pairs={{0,16},{4,20},{8,24},{12,28},{16,0},{20,4},{24,8},{28,12},{1,17},{... | collective-permute-start | bytes 196616 | tf_op jit(solution)/shard_map/ppermute | solution.py:433
  34.2 0.3 collective-permute-start.11
  34.5 0.0 collective-permute-done.7.rest_0_
  34.5 2.7 %collective-permute-start.12 = (f32[128,128]{1,0:T(8,128)S(1)}, f32[128,128]{1,0:T(8,128)S(1)}, u32[]{:S(2)}, u32[]{:S(2)}) collective-permute-start(f32[128,128]{1,0:T(8,128)S(1)} %get-tuple-element.76), channel_id=1, source_target_pairs={{0,24},{4,28},{8,16},{12,20},{16,8},{20,12},{24,0},{28,4},{1,25},{... | collective-permute-start | bytes 196616 | tf_op jit(solution)/shard_map/ppermute | solution.py:433
  37.1 0.0 collective-permute-done.8.rest_1_
  37.1 0.0 collective-permute-start.13
  37.1 3.6 %weight_parts.1.parts_ref = bf16[2,1024,2048]{2,1,0:T(8,128)(2,1)S(1)} custom-call(f32[1024,2048]{1,0:T(8,128)} %weight_hbm), custom_call_target="tpu_custom_call" | custom-call | flops 12582912 | bytes 16777216 | tf_op jit(solution)/shard_map/weight_parts/pallas_call | solution.py:554
  40.8 0.0 collective-permute-done.9.rest_2_
  40.8 0.0 collective-permute-done.10.rest_3_
  40.8 0.0 collective-permute-done.11.rest_4_
  40.8 0.0 collective-permute-done.12.rest_5_
  40.8 1.6 %collective-permute-done.13.rest_6_ = f32[128,128]{1,0:T(8,128)S(1)} collective-permute-done((f32[128,128]{1,0:T(8,128)S(1)}, f32[128,128]{1,0:T(8,128)S(1)}, u32[]{:S(2)}, u32[]{:S(2)}) %collective-permute-start.13) | collective-permute-done | bytes 65568 | tf_op jit(solution)/shard_map/ppermute | solution.py:433
  42.4 0.0 copy-done
  42.4 4.4 %projection.3 = f32[64,2048]{1,0:T(8,128)S(1)} custom-call(f32[8,256,256]{2,1,0:T(8,128)S(1)} %copy-done, f32[256,1024]{1,0:T(8,128)S(1)} %copy-done.1, f32[1,128]{1,0:T(1,128)S(1)} %bitcast.1, bf16[2,1024,2048]{2,1,0:T(8,128)(2,1)S(1)} %weight_parts.1.parts_ref, f32[128,128]{1,0:T(8,128)S(1)} %get-tuple-element.70.own_hbm, ...), custom_call_target="tpu_custom_call" | custom-call | flops 805306368 | bytes 8388608 | tf_op jit(solution)/shard_map/projection/pallas_call | solution.py:571
  46.9 0.7 collective-permute-start.15
  47.6 4.1 %collective-permute-start.14 = (f32[64,2048]{1,0:T(8,128)S(1)}, f32[64,2048]{1,0:T(8,128)S(1)}, u32[]{:S(2)}, u32[]{:S(2)}) collective-permute-start(f32[64,2048]{1,0:T(8,128)S(1)} %projection.3), channel_id=1, source_target_pairs={{0,1},{1,2},{4,5},{5,6},{8,9},{9,10},{12,13},{13,14},{16,17},{17,1... | collective-permute-start | bytes 1572872 | tf_op jit(solution)/shard_map/ppermute | solution.py:497
  51.7 7.4 %projection.2 = (f32[64,2048]{1,0:T(8,128)S(1)}, f32[64,2048]{1,0:T(8,128)S(1)}, f32[64,2048]{1,0:T(8,128)S(1)}) custom-call(f32[8,256,256]{2,1,0:T(8,128)S(1)} %copy-done, f32[256,1024]{1,0:T(8,128)S(1)} %copy-done.1, f32[1,128]{1,0:T(1,128)S(1)} %bitcast.2, bf16[2,1024,2048]{2,1,0:T(8,128)(2,1)S(1)} %weight_parts.1.parts_ref, ...), custom_call_target="tpu_custom_call" | custom-call | flops 2415919104 | bytes 8388608 | tf_op jit(solution)/shard_map/projection/pallas_call | solution.py:571
  59.1 2.7 %collective-permute-start.16 = (f32[64,2048]{1,0:T(8,128)S(1)}, f32[64,2048]{1,0:T(8,128)S(1)}, u32[]{:S(2)}, u32[]{:S(2)}) collective-permute-start(f32[64,2048]{1,0:T(8,128)S(1)} %get-tuple-element.81), channel_id=1, source_target_pairs={{0,1},{1,0},{2,3},{3,2},{4,5},{5,4},{6,7},{7,6},{8,9},{9,8},{10,11... | collective-permute-start | bytes 1572872 | tf_op jit(solution)/shard_map/ppermute | solution.py:500
  61.8 0.0 collective-permute-done.15.down_ref
  61.8 2.1 %collective-permute-done.14.up_ref = f32[64,2048]{1,0:T(8,128)S(1)} collective-permute-done((f32[64,2048]{1,0:T(8,128)S(1)}, f32[64,2048]{1,0:T(8,128)S(1)}, u32[]{:S(2)}, u32[]{:S(2)}) %collective-permute-start.14) | collective-permute-done | bytes 524320 | tf_op jit(solution)/shard_map/ppermute | solution.py:497
  63.9 0.2 forward.1
  64.1 3.5 %collective-permute-start.17 = (f32[64,2048]{1,0:T(8,128)S(1)}, f32[64,2048]{1,0:T(8,128)S(1)}, u32[]{:S(2)}, u32[]{:S(2)}) collective-permute-start(f32[64,2048]{1,0:T(8,128)S(1)} %get-tuple-element.82), channel_id=1, source_target_pairs={{0,2},{1,3},{2,0},{3,1},{4,6},{5,7},{6,4},{7,5},{8,10},{9,11},{10,... | collective-permute-start | bytes 1572872 | tf_op jit(solution)/shard_map/ppermute | solution.py:507
  67.6 14.4 %collective-permute-done.16 = f32[64,2048]{1,0:T(8,128)S(1)} collective-permute-done((f32[64,2048]{1,0:T(8,128)S(1)}, f32[64,2048]{1,0:T(8,128)S(1)}, u32[]{:S(2)}, u32[]{:S(2)}) %collective-permute-start.16) | collective-permute-done | bytes 524320 | tf_op jit(solution)/shard_map/ppermute | solution.py:500
  82.0 7.9 %collective-permute-done.17 = f32[64,2048]{1,0:T(8,128)S(1)} collective-permute-done((f32[64,2048]{1,0:T(8,128)S(1)}, f32[64,2048]{1,0:T(8,128)S(1)}, u32[]{:S(2)}, u32[]{:S(2)}) %collective-permute-start.17) | collective-permute-done | bytes 524320 | tf_op jit(solution)/shard_map/ppermute | solution.py:507
  89.9 0.9 add_add_fusion
  (2 shorter events, 0.0 us)
Async XLA Ops:
  11.4 4.9 %collective-permute-start = (f32[128,256]{1,0:T(8,128)}, f32[128,256]{1,0:T(8,128)S(1)}, u32[]{:S(2)}, u32[]{:S(2)}) collective-permute-start(f32[128,256]{1,0:T(8,128)} %get-tuple-element.45), channel_id=1, source_target_pairs={{0,4},{4,0},{8,12},{12,8},{16,20},{20,16},{24,28},{28,24},{1,5},{5... | collective-permute-start | bytes 393224 | tf_op jit(solution)/shard_map/ppermute | solution.py:433
  11.9 7.1 %collective-permute-start.1 = (f32[128,256]{1,0:T(8,128)}, f32[128,256]{1,0:T(8,128)S(1)}, u32[]{:S(2)}, u32[]{:S(2)}) collective-permute-start(f32[128,256]{1,0:T(8,128)} %get-tuple-element.46), channel_id=1, source_target_pairs={{0,8},{4,12},{8,0},{12,4},{16,24},{20,28},{24,16},{28,20},{1,9},{5... | collective-permute-start | bytes 393224 | tf_op jit(solution)/shard_map/ppermute | solution.py:433
  14.5 12.2 %collective-permute-start.2 = (f32[128,256]{1,0:T(8,128)}, f32[128,256]{1,0:T(8,128)S(1)}, u32[]{:S(2)}, u32[]{:S(2)}) collective-permute-start(f32[128,256]{1,0:T(8,128)} %get-tuple-element.47), channel_id=1, source_target_pairs={{0,12},{4,8},{8,4},{12,0},{16,28},{20,24},{24,20},{28,16},{1,13},{... | collective-permute-start | bytes 393224 | tf_op jit(solution)/shard_map/ppermute | solution.py:433
  14.5 12.1 %collective-permute-start.3 = (f32[128,256]{1,0:T(8,128)}, f32[128,256]{1,0:T(8,128)S(1)}, u32[]{:S(2)}, u32[]{:S(2)}) collective-permute-start(f32[128,256]{1,0:T(8,128)} %get-tuple-element.48), channel_id=1, source_target_pairs={{0,16},{4,20},{8,24},{12,28},{16,0},{20,4},{24,8},{28,12},{1,17},{... | collective-permute-start | bytes 393224 | tf_op jit(solution)/shard_map/ppermute | solution.py:433
  16.3 12.0 %collective-permute-start.4 = (f32[128,256]{1,0:T(8,128)}, f32[128,256]{1,0:T(8,128)S(1)}, u32[]{:S(2)}, u32[]{:S(2)}) collective-permute-start(f32[128,256]{1,0:T(8,128)} %get-tuple-element.49), channel_id=1, source_target_pairs={{0,20},{4,16},{8,28},{12,24},{16,4},{20,0},{24,12},{28,8},{1,21},{... | collective-permute-start | bytes 393224 | tf_op jit(solution)/shard_map/ppermute | solution.py:433
  16.3 12.0 %collective-permute-start.5 = (f32[128,256]{1,0:T(8,128)}, f32[128,256]{1,0:T(8,128)S(1)}, u32[]{:S(2)}, u32[]{:S(2)}) collective-permute-start(f32[128,256]{1,0:T(8,128)} %get-tuple-element.50), channel_id=1, source_target_pairs={{0,24},{4,28},{8,16},{12,20},{16,8},{20,12},{24,0},{28,4},{1,25},{... | collective-permute-start | bytes 393224 | tf_op jit(solution)/shard_map/ppermute | solution.py:433
  19.0 9.3 %collective-permute-start.6 = (f32[128,256]{1,0:T(8,128)}, f32[128,256]{1,0:T(8,128)S(1)}, u32[]{:S(2)}, u32[]{:S(2)}) collective-permute-start(f32[128,256]{1,0:T(8,128)} %get-tuple-element.51), channel_id=1, source_target_pairs={{0,28},{4,24},{8,20},{12,16},{16,12},{20,8},{24,4},{28,0},{1,29},{... | collective-permute-start | bytes 393224 | tf_op jit(solution)/shard_map/ppermute | solution.py:433
  30.4 12.0 %copy-start = (f32[8,256,256]{2,1,0:T(8,128)S(1)}, f32[8,256,256]{2,1,0:T(8,128)}, u32[]{:S(2)}) copy-start(f32[8,256,256]{2,1,0:T(8,128)} %output_maps.1.map_hbm) | copy-start | bytes 6291460
  30.4 12.0 %copy-start.1 = (f32[256,1024]{1,0:T(8,128)S(1)}, f32[256,1024]{1,0:T(8,128)}, u32[]{:S(2)}) copy-start(f32[256,1024]{1,0:T(8,128)} %gate_hbm.3) | copy-start | bytes 3145732
  30.4 12.0 %copy-start.2 = (f32[128]{0:T(128)S(1)}, f32[128]{0:T(128)}, u32[]{:S(2)}) copy-start(f32[128]{0:T(128)} %param.14) | copy-start | bytes 1540
  30.4 4.0 %collective-permute-start.7 = (f32[128,128]{1,0:T(8,128)S(1)}, f32[128,128]{1,0:T(8,128)S(1)}, u32[]{:S(2)}, u32[]{:S(2)}) collective-permute-start(f32[128,128]{1,0:T(8,128)S(1)} %get-tuple-element.71), channel_id=1, source_target_pairs={{0,4},{4,0},{8,12},{12,8},{16,20},{20,16},{24,28},{28,24},{1,5},{5... | collective-permute-start | bytes 196616 | tf_op jit(solution)/shard_map/ppermute | solution.py:433
  30.9 6.2 %collective-permute-start.8 = (f32[128,128]{1,0:T(8,128)S(1)}, f32[128,128]{1,0:T(8,128)S(1)}, u32[]{:S(2)}, u32[]{:S(2)}) collective-permute-start(f32[128,128]{1,0:T(8,128)S(1)} %get-tuple-element.72), channel_id=1, source_target_pairs={{0,8},{4,12},{8,0},{12,4},{16,24},{20,28},{24,16},{28,20},{1,9},{5... | collective-permute-start | bytes 196616 | tf_op jit(solution)/shard_map/ppermute | solution.py:433
  32.6 8.1 %collective-permute-start.9 = (f32[128,128]{1,0:T(8,128)S(1)}, f32[128,128]{1,0:T(8,128)S(1)}, u32[]{:S(2)}, u32[]{:S(2)}) collective-permute-start(f32[128,128]{1,0:T(8,128)S(1)} %get-tuple-element.73), channel_id=1, source_target_pairs={{0,12},{4,8},{8,4},{12,0},{16,28},{20,24},{24,20},{28,16},{1,13},{... | collective-permute-start | bytes 196616 | tf_op jit(solution)/shard_map/ppermute | solution.py:433
  32.6 8.1 %collective-permute-start.10 = (f32[128,128]{1,0:T(8,128)S(1)}, f32[128,128]{1,0:T(8,128)S(1)}, u32[]{:S(2)}, u32[]{:S(2)}) collective-permute-start(f32[128,128]{1,0:T(8,128)S(1)} %get-tuple-element.74), channel_id=1, source_target_pairs={{0,16},{4,20},{8,24},{12,28},{16,0},{20,4},{24,8},{28,12},{1,17},{... | collective-permute-start | bytes 196616 | tf_op jit(solution)/shard_map/ppermute | solution.py:433
  34.2 6.6 %collective-permute-start.11 = (f32[128,128]{1,0:T(8,128)S(1)}, f32[128,128]{1,0:T(8,128)S(1)}, u32[]{:S(2)}, u32[]{:S(2)}) collective-permute-start(f32[128,128]{1,0:T(8,128)S(1)} %get-tuple-element.75), channel_id=1, source_target_pairs={{0,20},{4,16},{8,28},{12,24},{16,4},{20,0},{24,12},{28,8},{1,21},{... | collective-permute-start | bytes 196616 | tf_op jit(solution)/shard_map/ppermute | solution.py:433
  34.5 6.3 %collective-permute-start.12 = (f32[128,128]{1,0:T(8,128)S(1)}, f32[128,128]{1,0:T(8,128)S(1)}, u32[]{:S(2)}, u32[]{:S(2)}) collective-permute-start(f32[128,128]{1,0:T(8,128)S(1)} %get-tuple-element.76), channel_id=1, source_target_pairs={{0,24},{4,28},{8,16},{12,20},{16,8},{20,12},{24,0},{28,4},{1,25},{... | collective-permute-start | bytes 196616 | tf_op jit(solution)/shard_map/ppermute | solution.py:433
  37.1 5.3 %collective-permute-start.13 = (f32[128,128]{1,0:T(8,128)S(1)}, f32[128,128]{1,0:T(8,128)S(1)}, u32[]{:S(2)}, u32[]{:S(2)}) collective-permute-start(f32[128,128]{1,0:T(8,128)S(1)} %get-tuple-element.77), channel_id=1, source_target_pairs={{0,28},{4,24},{8,20},{12,16},{16,12},{20,8},{24,4},{28,0},{1,29},{... | collective-permute-start | bytes 196616 | tf_op jit(solution)/shard_map/ppermute | solution.py:433
  46.9 14.9 %collective-permute-start.15 = (f32[64,2048]{1,0:T(8,128)S(1)}, f32[64,2048]{1,0:T(8,128)S(1)}, u32[]{:S(2)}, u32[]{:S(2)}) collective-permute-start(f32[64,2048]{1,0:T(8,128)S(1)} %projection.3), channel_id=1, source_target_pairs={{3,2},{2,1},{7,6},{6,5},{11,10},{10,9},{15,14},{14,13},{19,18},{18... | collective-permute-start | bytes 1572872 | tf_op jit(solution)/shard_map/ppermute | solution.py:498
  47.6 16.4 %collective-permute-start.14 = (f32[64,2048]{1,0:T(8,128)S(1)}, f32[64,2048]{1,0:T(8,128)S(1)}, u32[]{:S(2)}, u32[]{:S(2)}) collective-permute-start(f32[64,2048]{1,0:T(8,128)S(1)} %projection.3), channel_id=1, source_target_pairs={{0,1},{1,2},{4,5},{5,6},{8,9},{9,10},{12,13},{13,14},{16,17},{17,1... | collective-permute-start | bytes 1572872 | tf_op jit(solution)/shard_map/ppermute | solution.py:497
  59.1 22.9 %collective-permute-start.16 = (f32[64,2048]{1,0:T(8,128)S(1)}, f32[64,2048]{1,0:T(8,128)S(1)}, u32[]{:S(2)}, u32[]{:S(2)}) collective-permute-start(f32[64,2048]{1,0:T(8,128)S(1)} %get-tuple-element.81), channel_id=1, source_target_pairs={{0,1},{1,0},{2,3},{3,2},{4,5},{5,4},{6,7},{7,6},{8,9},{9,8},{10,11... | collective-permute-start | bytes 1572872 | tf_op jit(solution)/shard_map/ppermute | solution.py:500
  64.1 25.8 %collective-permute-start.17 = (f32[64,2048]{1,0:T(8,128)S(1)}, f32[64,2048]{1,0:T(8,128)S(1)}, u32[]{:S(2)}, u32[]{:S(2)}) collective-permute-start(f32[64,2048]{1,0:T(8,128)S(1)} %get-tuple-element.82), channel_id=1, source_target_pairs={{0,2},{1,3},{2,0},{3,1},{4,6},{5,7},{6,4},{7,5},{8,10},{9,11},{10,... | collective-permute-start | bytes 1572872 | tf_op jit(solution)/shard_map/ppermute | solution.py:507

commit v5 on v4

--- a/solution.py
+++ b/solution.py
@@ -59,12 +59,25 @@
     return rows, rows.T
 
 
-def spread_diagonal(packed):
-    size = packed.shape[0]
-    place = iota(packed.shape, 1) // size
-    return jnp.concatenate(
-        [jnp.where(place == block, packed, 0.0) for block in range(BLOCK // size)], axis=0
-    )
+def split(value):
+    high = value.astype(jnp.bfloat16)
+    return high, (value - high.astype(jnp.float32)).astype(jnp.bfloat16)
+
+
+def dot_parts(left, right):
+    rows = left[0].shape[0]
+    both = jnp.concatenate(left, axis=0)
+    sums = jnp.dot(both, right[0], preferred_element_type=jnp.float32)
+    rest = jnp.dot(left[0], right[1], preferred_element_type=jnp.float32)
+    return sums[:rows] + (sums[rows:] + rest)
+
+
+def stack_parts(*values):
+    return tuple(jnp.concatenate(pieces, axis=0) for pieces in zip(*values))
+
+
+def spread_parts(parts, masks):
+    return tuple(jnp.concatenate([part * mask for mask in masks], axis=0) for part in parts)
 
 
 def lower_inverses(lowers):
@@ -75,68 +88,77 @@
     eye = jnp.where(row == column, 1.0, 0.0)
     in_8 = row // 8 == column // 8
     in_16 = row // 16 == column // 16
+    odd = place % 2 == 1
+    masks = [
+        jnp.where(place == index, 1.0, 0.0).astype(jnp.bfloat16) for index in range(BLOCK // SMALL)
+    ]
     packed = []
     for lower in lowers:
         blocks = jnp.zeros((SMALL, BLOCK), jnp.float32)
-        for block in range(BLOCK // SMALL):
-            blocks = jnp.where(place == block, lower[block * SMALL : (block + 1) * SMALL], blocks)
+        for index in range(BLOCK // SMALL):
+            blocks = jnp.where(place == index, lower[index * SMALL : (index + 1) * SMALL], blocks)
         packed.append(blocks)
     nil = [jnp.where(in_8, blocks, 0.0) for blocks in packed]
-    nil_2 = [dot(n, spread_diagonal(n)) for n in nil]
-    wide_2 = [spread_diagonal(n) for n in nil_2]
+    parts = [split(n) for n in nil]
+    nil_2 = [split(dot_parts(n, spread_parts(n, masks))) for n in parts]
     start = [eye - n for n in nil]
-    nil_4 = [dot(n, w) for n, w in zip(nil_2, wide_2)]
-    start = [s + dot(s, w) for s, w in zip(start, wide_2)]
-    inv = [s + dot(s, spread_diagonal(n)) for s, n in zip(start, nil_4)]
-    step_16 = [spread_diagonal(jnp.where(in_16 & ~in_8, blocks, 0.0)) for blocks in packed]
+    pairs = [
+        dot_parts(stack_parts(n, split(s)), spread_parts(n, masks)) for n, s in zip(nil_2, start)
+    ]
+    start = [s + pair[SMALL:] for s, pair in zip(start, pairs)]
+    nil_4 = [spread_parts(split(pair[:SMALL]), masks) for pair in pairs]
+    inv = [s + dot_parts(split(s), n) for s, n in zip(start, nil_4)]
+    step_16 = [
+        spread_parts(split(jnp.where(in_16 & ~in_8, blocks, 0.0)), masks) for blocks in packed
+    ]
     half = [jnp.concatenate([d[8:16], d[24:32]], axis=0) for d in inv]
-    half = [dot(h, w) for h, w in zip(half, step_16)]
-    half = [dot(h, spread_diagonal(d)) for h, d in zip(half, inv)]
+    half = [dot_parts(split(h), w) for h, w in zip(half, step_16)]
+    half = [dot_parts(split(h), spread_parts(split(d), masks)) for h, d in zip(half, inv)]
     inv = [
         jnp.concatenate([d[:8], d[8:16] - h[:8], d[16:24], d[24:] - h[8:]], axis=0)
         for d, h in zip(inv, half)
     ]
-    step_32 = [spread_diagonal(jnp.where(in_16, 0.0, blocks)) for blocks in packed]
-    half = [dot(d[16:], w) for d, w in zip(inv, step_32)]
-    half = [dot(h, spread_diagonal(d)) for h, d in zip(half, inv)]
+    step_32 = [spread_parts(split(jnp.where(in_16, 0.0, blocks)), masks) for blocks in packed]
+    half = [dot_parts(split(d[16:]), w) for d, w in zip(inv, step_32)]
+    half = [dot_parts(split(h), spread_parts(split(d), masks)) for h, d in zip(half, inv)]
     inv = [jnp.concatenate([d[:16], d[16:] - h], axis=0) for d, h in zip(inv, half)]
-    odd = place % 2 == 1
-    zeros = jnp.zeros((SMALL, BLOCK), jnp.float32)
+    wide = [spread_parts(split(d), masks) for d in inv]
     low = [jnp.where(odd, d, 0.0) for d in inv]
-    wide = [
-        spread_diagonal(jnp.concatenate([jnp.where(odd, 0.0, d), l], axis=0)) for d, l in zip(inv, low)
-    ]
-    step_64 = [
-        spread_diagonal(
-            jnp.concatenate(
-                [
-                    zeros,
-                    jnp.where(
-                        place == 0, lower[32:64], jnp.where(place == 2, lower[96:128], 0.0)
-                    ),
-                ],
-                axis=0,
+    zeros = jnp.zeros((SMALL, BLOCK), jnp.bfloat16)
+    step_64 = []
+    for lower in lowers:
+        below = jnp.where(place == 0, lower[32:64], jnp.where(place == 2, lower[96:128], 0.0))
+        step_64.append(
+            tuple(
+                jnp.concatenate([zeros, part * masks[0], zeros, part * masks[2]], axis=0)
+                for part in split(below)
             )
         )
-        for lower in lowers
-    ]
-    half = [dot(l, w) for l, w in zip(low, step_64)]
-    half = [dot(h, w) for h, w in zip(half, wide)]
+    half = [dot_parts(split(l), w) for l, w in zip(low, step_64)]
+    half = [dot_parts(split(h), w) for h, w in zip(half, wide)]
     inv = [
         jnp.concatenate([jnp.where(odd, 0.0, d), l - h], axis=0) for d, l, h in zip(inv, low, half)
     ]
     left = iota((64, BLOCK), 1) < 64
     low = [jnp.where(left, 0.0, d) for d in inv]
     wide = [jnp.concatenate([jnp.where(left, d, 0.0), l], axis=0) for d, l in zip(inv, low)]
+    wide_parts = [split(w) for w in wide]
+    zeros = jnp.zeros((64, BLOCK), jnp.bfloat16)
     step_128 = [
-        jnp.concatenate(
-            [jnp.zeros((64, BLOCK), jnp.float32), jnp.where(left, lower[64:], 0.0)], axis=0
+        tuple(
+            jnp.concatenate([zeros, part], axis=0) for part in split(jnp.where(left, lower[64:], 0.0))
         )
         for lower in lowers
     ]
-    half = [dot(l, w) for l, w in zip(low, step_128)]
-    half = [dot(h, w) for h, w in zip(half, wide)]
-    return [jnp.concatenate([w[:64], w[64:] - h], axis=0) for w, h in zip(wide, half)]
+    half = [dot_parts(tuple(part[64:] for part in l), w) for l, w in zip(wide_parts, step_128)]
+    half = [dot_parts(split(h), w) for h, w in zip(half, wide_parts)]
+    return [
+        tuple(
+            jnp.concatenate([high, low], axis=0)
+            for high, low in zip((part[:64] for part in parts), split(w[64:] - h))
+        )
+        for parts, w, h in zip(wide_parts, wide, half)
+    ]
 
 
 def block(index):
@@ -214,16 +236,16 @@
                     axis=1,
                 )
                 for r in range(p):
-                    right = right - dot(lower[head, p, r], factors[head, r])
-                factors[head, p] = dot(inverse[head, p], right)
+                    right = right - dot_parts(split(lower[head, p, r]), split(factors[head, r]))
+                factors[head, p] = dot_parts(inverse[head, p], split(right))
                 factor_ref[head, block(p), :] = factors[head, p]
-        flipped = {key_head: [k.T for k in keys[key_head]] for key_head in keys}
+        flipped = {key_head: [split(k.T) for k in keys[key_head]] for key_head in keys}
         for head in heads:
             last = rows[head : head + 1, tokens - 1 : tokens]
             total = jnp.exp(last) * eye
             for p in range(blocks):
                 ending = jnp.exp(last - columns[block(p), head : head + 1])
-                total = total + dot(flipped[head // repeat][p], factors[head, p] * ending)
+                total = total + dot_parts(flipped[head // repeat][p], split(factors[head, p] * ending))
             summary_ref[head] = total
         group = pl.ds(first, len(heads))
         leaving.append(
@@ -321,7 +343,7 @@
 def ordered_scan_kernel(factor_hbm, *rest):
     *arrays, held_ref, entry_ref, sems = rest
     count = entry_ref.shape[0]
-    held, own_entry_hbm, entries = arrays[: count - 1], arrays[count - 1], arrays[count:]
+    held, entries = arrays[: count - 1], arrays[count - 1 :]
     here = partner(0, True)
     own_summary = factor_hbm.at[factor_hbm.shape[0] - 1, pl.ds(0, DK)]
     own = pltpu.make_async_copy(own_summary, held_ref.at[here], sems.at[0])
@@ -337,16 +359,8 @@
             added = added + dot(held_ref[source, :, :DK], state)
         state = added
         entry_ref[source + 1] = state
-    own = pltpu.make_async_copy(entry_ref.at[here], own_entry_hbm, sems.at[1])
-    own.start()
     for i, entry in enumerate(entries):
-        entry[...] = entry_ref[partner(i + 1, True)]
-    own.wait()
-
-
-def split(value):
-    high = value.astype(jnp.bfloat16)
-    return high, (value - high.astype(jnp.float32)).astype(jnp.bfloat16)
+        entry[...] = entry_ref[partner(i, True)]
 
 
 def weight_kernel(weight_hbm, parts_ref, weight_ref, sems):
@@ -357,14 +371,13 @@
         parts_ref[0, band, :], parts_ref[1, band, :] = split(weight_ref[band, :])
 
 
-def projection_kernel(map_hbm, gate_hbm, gain_ref, parts_ref, own_hbm, *rest, pieces, swap):
-    *arrays, map_ref, gate_ref, state_ref, high_ref, low_ref, gate_sems, map_sems, state_sems = rest
+def projection_kernel(map_hbm, gate_hbm, gain_ref, parts_ref, *rest, pieces, swap):
+    *arrays, map_ref, gate_ref, state_ref, high_ref, low_ref, gate_sems, map_sems = rest
     outs = arrays[-len(pieces) :]
     states = arrays[: -len(pieces)]
     heads = state_ref.shape[0]
     rows = outs[0].shape[0]
     blocks = sorted({index for index, _ in pieces})
-    own = fetch([(own_hbm, state_ref.at[partner(0, swap.heads)])], state_sems)
     places = []
     for i, index in enumerate(blocks):
         start = (lax.axis_index("tp") ^ index) * rows if swap.rows else index * rows
@@ -379,8 +392,8 @@
         map_sems,
     )
     for i, state in enumerate(states):
-        state_ref[partner(i + 1, swap.heads)] = state[...]
-    for copy in own + gates:
+        state_ref[partner(i, swap.heads)] = state[...]
+    for copy in gates:
         copy.wait()
     gain = gain_ref[...]
     for head in range(heads):
@@ -405,7 +418,7 @@
                 out_ref[:, band - start : band - start + BAND] = result[at : at + rows]
 
 
-def forward_kernel(across_ref, own_ref, up_ref, down_ref, going_ref, staying_ref):
+def forward_kernel(across_ref, own_ref, up_ref, down_ref, _, going_ref, staying_ref, __):
     outward = lax.axis_index("tp") == 1
     up, down = up_ref[...], down_ref[...]
     going_ref[...] = across_ref[...] + jnp.where(outward, up, down)
@@ -453,12 +466,12 @@
         entries = pl.pallas_call(
             ordered_scan_kernel,
             in_specs=[HBM] + [VMEM] * (count - 1),
-            out_specs=[HBM] + [VMEM] * (count - 1),
+            out_specs=[VMEM] * count,
             out_shape=[entry] * count,
             scratch_shapes=[
                 pltpu.VMEM((count, DK, DK + DV), jnp.float32),
                 pltpu.VMEM((count, DK, DV), jnp.float32),
-                pltpu.SemaphoreType.DMA((2,)),
+                pltpu.SemaphoreType.DMA((1,)),
             ],
             compiler_params=params(SCAN_VMEM),
             name="state_scan",
@@ -497,14 +510,18 @@
     up = lax.ppermute(opposite, axis, [(0, 1), (1, 2)])
     down = lax.ppermute(opposite, axis, [(3, 2), (2, 1)])
     across, own, near = project([(i, 0, columns) for i in (2, 0, 1)], LATER_VMEM)
-    from_near = lax.ppermute(near, axis, [(i, i ^ 1) for i in range(4)])
-    going, staying = pl.pallas_call(
+    anywhere = pl.BlockSpec(memory_space=pl.ANY)
+    going, staying, near = pl.pallas_call(
         forward_kernel,
-        out_shape=[shape(*own.shape)] * 2,
+        in_specs=[VMEM] * 4 + [anywhere],
+        out_specs=[VMEM] * 2 + [anywhere],
+        out_shape=[shape(*own.shape)] * 3,
+        input_output_aliases={4: 2},
         compiler_params=params(LATER_VMEM),
         name="forward",
-    )(across, own, up, down)
+    )(across, own, up, down, near)
     from_across = lax.ppermute(going, axis, [(i, i ^ 2) for i in range(4)])
+    from_near = lax.ppermute(near, axis, [(i, i ^ 1) for i in range(4)])
     return (staying + from_near) + from_across
 
 
@@ -567,12 +584,12 @@
     def project(pieces, vmem):
         total = len({piece[0] for piece in pieces}) * rows
         normed = pltpu.VMEM((total, depth), jnp.bfloat16)
-        counts = (total // rows, heads * total // rows, 1)
+        counts = (total // rows, heads * total // rows)
         return pl.pallas_call(
             functools.partial(
                 projection_kernel, pieces=[(index, start) for index, start, _ in pieces], swap=swap
             ),
-            in_specs=[HBM] * 2 + [VMEM] * 2 + [HBM] + [VMEM] * (heads - 1),
+            in_specs=[HBM] * 2 + [VMEM] * (2 + heads),
             out_shape=[shape(rows, width) for _, _, width in pieces],
             scratch_shapes=[
                 pltpu.VMEM((heads, total, DK + DV), jnp.float32),

time: 91.1 us -> 87.7 us (0.963)
  Pallas kernels: 35 us -> 32.7 us
  starting transfers between devices: 26.9 us -> 25.2 us
    ppermute x1, waiting for transfers between devices: 7.87 us -> 0.01 us  [project_and_sum(): from_across = lax.ppermute(going, axis, [(i, i ^ 2) for i in range(4)])]
    ppermute x1, waiting for transfers between devices: 14.4 us -> 20.7 us  [project_and_sum(): from_near = lax.ppermute(near, axis, [(i, i ^ 1) for i in range(4)])]
    pallas_call x1, Pallas kernels: 11.4 us -> 9.4 us  [per_device(): pl.pallas_call(functools.partial(summary_kernel, swap=swap.heads), in_spe...]
    ppermute x1, waiting for transfers between devices: 2.14 us -> 4.07 us  [project_and_sum(): up = lax.ppermute(opposite, axis, [(0, 1), (1, 2)])]
    ppermute x1, starting transfers between devices: 3.5 us -> 1.88 us  [project_and_sum(): from_across = lax.ppermute(going, axis, [(i, i ^ 2) for i in range(4)])]
  transfers between devices with their start and end apart: 18 -> 18, of which waited for: 6 -> 5; matrix products, arithmetic and copies ran while one was open for 0% -> 0% of each run, Pallas kernels for 19% -> 19%
where the time goes in v5:
time: 87.7 us; the launch traced here: 87.1 us
  Pallas kernels  32.7 us (37%)
  waiting for transfers between devices  28.2 us (32%)
  starting transfers between devices  25.2 us (29%)
  other arithmetic  0.88 us (1%)
    ppermute x1, waiting for transfers between devices, project_and_sum(): from_near = lax.ppermute(near, axis, [(i, i ^ 1) for i in range(4)])  20.7 us
    ppermute x14, starting transfers between devices, partners_swap(): lax.ppermute(arrays[i], axis, [(d, d ^ i) for d in range(count)])  16 us
    pallas_call x2, Pallas kernels, project(): pl.pallas_call(functools.partial(projection_kernel, pieces=[(index, start...  11.7 us
    pallas_call x1, Pallas kernels, per_device(): pl.pallas_call(functools.partial(summary_kernel, swap=swap.heads), in_spe...  9.4 us
    pallas_call x1, Pallas kernels, per_device(): pl.pallas_call(output_kernel, in_specs=[HBM] * 4, out_specs=HBM, out_shap...  5.71 us
    ppermute x1, starting transfers between devices, project_and_sum(): up = lax.ppermute(opposite, axis, [(0, 1), (1, 2)])  4.11 us
    ppermute x1, waiting for transfers between devices, project_and_sum(): up = lax.ppermute(opposite, axis, [(0, 1), (1, 2)])  4.07 us
    pallas_call x1, Pallas kernels, per_device(): pl.pallas_call(weight_kernel, in_specs=[HBM], out_shape=jax.ShapeDtypeStr...  3.79 us
  transfers between devices with their start and end apart: 18, of which 5 were waited for; matrix products, arithmetic and copies ran while one was open for 0% of the time, Pallas kernels for 19%

profile of v5, /device:TPU:0, one launch (start us, length us, event | category | flops | bytes accessed | tf_op | source)
XLA Modules:
  0.0 87.1 jit_solution(16841235293751002029)
XLA Ops:
  0.0 9.4 %state_summary.1 = (f32[9,256,256]{2,1,0:T(8,128)}, f32[128,256]{1,0:T(8,128)}, f32[128,256]{1,0:T(8,128)}, f32[128,256]{1,0:T(8,128)}, f32[128,256]{1,0:T(8,128...) custom-call(f32[8,256]{1,0:T(8,128)} %decay_hbm.3, f32[8,256]{1,0:T(8,128)} %strength_hbm.1, ...), custom_call_target="tpu_custom_call" | custom-call | tf_op jit(solution)/shard_map/state_summary/pallas_call | solution.py:547
  9.4 0.5 collective-permute-start
  9.9 2.6 %collective-permute-start.1 = (f32[128,256]{1,0:T(8,128)}, f32[128,256]{1,0:T(8,128)S(1)}, u32[]{:S(2)}, u32[]{:S(2)}) collective-permute-start(f32[128,256]{1,0:T(8,128)} %get-tuple-element.47), channel_id=1, source_target_pairs={{0,8},{4,12},{8,0},{12,4},{16,24},{20,28},{24,16},{28,20},{1,9},{5... | collective-permute-start | bytes 393224 | tf_op jit(solution)/shard_map/ppermute | solution.py:446
  12.5 0.1 collective-permute-start.2
  12.6 1.8 %collective-permute-start.3 = (f32[128,256]{1,0:T(8,128)}, f32[128,256]{1,0:T(8,128)S(1)}, u32[]{:S(2)}, u32[]{:S(2)}) collective-permute-start(f32[128,256]{1,0:T(8,128)} %get-tuple-element.49), channel_id=1, source_target_pairs={{0,16},{4,20},{8,24},{12,28},{16,0},{20,4},{24,8},{28,12},{1,17},{... | collective-permute-start | bytes 393224 | tf_op jit(solution)/shard_map/ppermute | solution.py:446
  14.3 0.0 collective-permute-start.4
  14.3 0.0 collective-permute-done.rest_0_
  14.3 2.6 %collective-permute-start.5 = (f32[128,256]{1,0:T(8,128)}, f32[128,256]{1,0:T(8,128)S(1)}, u32[]{:S(2)}, u32[]{:S(2)}) collective-permute-start(f32[128,256]{1,0:T(8,128)} %get-tuple-element.51), channel_id=1, source_target_pairs={{0,24},{4,28},{8,16},{12,20},{16,8},{20,12},{24,0},{28,4},{1,25},{... | collective-permute-start | bytes 393224 | tf_op jit(solution)/shard_map/ppermute | solution.py:446
  16.9 0.1 collective-permute-done.1.rest_1_
  17.0 1.7 %collective-permute-start.6 = (f32[128,256]{1,0:T(8,128)}, f32[128,256]{1,0:T(8,128)S(1)}, u32[]{:S(2)}, u32[]{:S(2)}) collective-permute-start(f32[128,256]{1,0:T(8,128)} %get-tuple-element.52), channel_id=1, source_target_pairs={{0,28},{4,24},{8,20},{12,16},{16,12},{20,8},{24,4},{28,0},{1,29},{... | collective-permute-start | bytes 393224 | tf_op jit(solution)/shard_map/ppermute | solution.py:446
  18.8 5.7 %output_maps.1.map_hbm = f32[8,256,256]{2,1,0:T(8,128)} custom-call(f32[8,256]{1,0:T(8,128)} %decay_hbm.3, f32[256,512]{1,0:T(8,128)} %q_hbm.1, f32[256,512]{1,0:T(8,128)} %k_hbm.3, f32[9,256,256]{2,1,0:T(8,128)} %get-tuple-element.54.factor_hbm), custom_call_target="tpu_custom_call" | custom-call | flops 1207959552 | bytes 5242880 | tf_op jit(solution)/shard_map/output_maps/pallas_call | solution.py:558
  24.5 0.0 collective-permute-done.2.rest_2_
  24.5 0.0 collective-permute-done.3.rest_3_
  24.5 1.8 %collective-permute-done.4.rest_4_ = f32[128,256]{1,0:T(8,128)S(1)} collective-permute-done((f32[128,256]{1,0:T(8,128)}, f32[128,256]{1,0:T(8,128)S(1)}, u32[]{:S(2)}, u32[]{:S(2)}) %collective-permute-start.4) | collective-permute-done | bytes 131104 | tf_op jit(solution)/shard_map/ppermute | solution.py:446
  26.3 0.0 collective-permute-done.5.rest_5_
  26.3 0.0 collective-permute-done.6.rest_6_
  26.3 2.0 %state_scan.1 = (f32[128,128]{1,0:T(8,128)S(1)}, f32[128,128]{1,0:T(8,128)S(1)}, f32[128,128]{1,0:T(8,128)S(1)}, f32[128,128]{1,0:T(8,128)S(1)}, f32[128,128]{1,...) custom-call(f32[9,256,256]{2,1,0:T(8,128)} %get-tuple-element.54.factor_hbm, ...), custom_call_target="tpu_custom_call" | custom-call | tf_op jit(solution)/shard_map/state_scan/pallas_call | solution.py:466
  28.3 0.0 copy-start
  28.3 0.0 copy-start.1
  28.3 0.0 copy-start.2
  28.4 0.5 collective-permute-start.7
  28.9 1.7 %collective-permute-start.8 = (f32[128,128]{1,0:T(8,128)S(1)}, f32[128,128]{1,0:T(8,128)S(1)}, u32[]{:S(2)}, u32[]{:S(2)}) collective-permute-start(f32[128,128]{1,0:T(8,128)S(1)} %get-tuple-element.73), channel_id=1, source_target_pairs={{0,8},{4,12},{8,0},{12,4},{16,24},{20,28},{24,16},{28,20},{1,9},{5... | collective-permute-start | bytes 196616 | tf_op jit(solution)/shard_map/ppermute | solution.py:446
  30.6 0.0 collective-permute-start.9
  30.6 1.5 %collective-permute-start.10 = (f32[128,128]{1,0:T(8,128)S(1)}, f32[128,128]{1,0:T(8,128)S(1)}, u32[]{:S(2)}, u32[]{:S(2)}) collective-permute-start(f32[128,128]{1,0:T(8,128)S(1)} %get-tuple-element.75), channel_id=1, source_target_pairs={{0,16},{4,20},{8,24},{12,28},{16,0},{20,4},{24,8},{28,12},{1,17},{... | collective-permute-start | bytes 196616 | tf_op jit(solution)/shard_map/ppermute | solution.py:446
  32.1 0.3 collective-permute-start.11
  32.4 0.0 collective-permute-done.7.rest_1_
  32.4 2.7 %collective-permute-start.12 = (f32[128,128]{1,0:T(8,128)S(1)}, f32[128,128]{1,0:T(8,128)S(1)}, u32[]{:S(2)}, u32[]{:S(2)}) collective-permute-start(f32[128,128]{1,0:T(8,128)S(1)} %get-tuple-element.77), channel_id=1, source_target_pairs={{0,24},{4,28},{8,16},{12,20},{16,8},{20,12},{24,0},{28,4},{1,25},{... | collective-permute-start | bytes 196616 | tf_op jit(solution)/shard_map/ppermute | solution.py:446
  35.1 0.0 collective-permute-done.8.rest_2_
  35.1 0.0 collective-permute-start.13
  35.1 3.8 %weight_parts.1.parts_ref = bf16[2,1024,2048]{2,1,0:T(8,128)(2,1)S(1)} custom-call(f32[1024,2048]{1,0:T(8,128)} %weight_hbm), custom_call_target="tpu_custom_call" | custom-call | flops 12582912 | bytes 16777216 | tf_op jit(solution)/shard_map/weight_parts/pallas_call | solution.py:571
  38.9 0.0 collective-permute-done.9.rest_3_
  38.9 0.0 collective-permute-done.10.rest_4_
  38.9 0.0 collective-permute-done.11.rest_5_
  38.9 0.0 collective-permute-done.12.rest_6_
  38.9 1.4 %collective-permute-done.13.rest_7_ = f32[128,128]{1,0:T(8,128)S(1)} collective-permute-done((f32[128,128]{1,0:T(8,128)S(1)}, f32[128,128]{1,0:T(8,128)S(1)}, u32[]{:S(2)}, u32[]{:S(2)}) %collective-permute-start.13) | collective-permute-done | bytes 65568 | tf_op jit(solution)/shard_map/ppermute | solution.py:446
  40.4 0.0 copy-done
  40.4 4.3 %projection.3 = f32[64,2048]{1,0:T(8,128)S(1)} custom-call(f32[8,256,256]{2,1,0:T(8,128)S(1)} %copy-done, f32[256,1024]{1,0:T(8,128)S(1)} %copy-done.1, f32[1,128]{1,0:T(1,128)S(1)} %bitcast.1, bf16[2,1024,2048]{2,1,0:T(8,128)(2,1)S(1)} %weight_parts.1.parts_ref, f32[128,128]{1,0:T(8,128)S(1)} %get-tuple-element.71.rest_0_, ...), custom_call_target="tpu_custom_call" | custom-call | flops 805306368 | bytes 8388608 | tf_op jit(solution)/shard_map/projection/pallas_call | solution.py:588
  44.7 0.7 collective-permute-start.15
  45.4 4.1 %collective-permute-start.14 = (f32[64,2048]{1,0:T(8,128)S(1)}, f32[64,2048]{1,0:T(8,128)S(1)}, u32[]{:S(2)}, u32[]{:S(2)}) collective-permute-start(f32[64,2048]{1,0:T(8,128)S(1)} %projection.3), channel_id=1, source_target_pairs={{0,1},{1,2},{4,5},{5,6},{8,9},{9,10},{12,13},{13,14},{16,17},{17,1... | collective-permute-start | bytes 1572872 | tf_op jit(solution)/shard_map/ppermute | solution.py:510
  49.5 7.3 %projection.2 = (f32[64,2048]{1,0:T(8,128)S(1)}, f32[64,2048]{1,0:T(8,128)S(1)}, f32[64,2048]{1,0:T(8,128)S(1)}) custom-call(f32[8,256,256]{2,1,0:T(8,128)S(1)} %copy-done, f32[256,1024]{1,0:T(8,128)S(1)} %copy-done.1, f32[1,128]{1,0:T(1,128)S(1)} %bitcast.2, bf16[2,1024,2048]{2,1,0:T(8,128)(2,1)S(1)} %weight_parts.1.parts_ref, ...), custom_call_target="tpu_custom_call" | custom-call | flops 2415919104 | bytes 8388608 | tf_op jit(solution)/shard_map/projection/pallas_call | solution.py:588
  56.9 0.0 collective-permute-done.15.down_ref
  56.9 4.1 %collective-permute-done.14.up_ref = f32[64,2048]{1,0:T(8,128)S(1)} collective-permute-done((f32[64,2048]{1,0:T(8,128)S(1)}, f32[64,2048]{1,0:T(8,128)S(1)}, u32[]{:S(2)}, u32[]{:S(2)}) %collective-permute-start.14) | collective-permute-done | bytes 524320 | tf_op jit(solution)/shard_map/ppermute | solution.py:510
  60.9 0.2 forward.1
  61.1 2.5 %collective-permute-start.16 = (f32[64,2048]{1,0:T(8,128)S(1)}, f32[64,2048]{1,0:T(8,128)S(1)}, u32[]{:S(2)}, u32[]{:S(2)}) collective-permute-start(f32[64,2048]{1,0:T(8,128)S(1)} %get-tuple-element.83), channel_id=1, source_target_pairs={{0,1},{1,0},{2,3},{3,2},{4,5},{5,4},{6,7},{7,6},{8,9},{9,8},{10,11... | collective-permute-start | bytes 1572872 | tf_op jit(solution)/shard_map/ppermute | solution.py:524
  63.7 1.9 %collective-permute-start.17 = (f32[64,2048]{1,0:T(8,128)S(1)}, f32[64,2048]{1,0:T(8,128)S(1)}, u32[]{:S(2)}, u32[]{:S(2)}) collective-permute-start(f32[64,2048]{1,0:T(8,128)S(1)} %get-tuple-element.84), channel_id=1, source_target_pairs={{0,2},{1,3},{2,0},{3,1},{4,6},{5,7},{6,4},{7,5},{8,10},{9,11},{10,... | collective-permute-start | bytes 1572872 | tf_op jit(solution)/shard_map/ppermute | solution.py:523
  65.5 20.7 %collective-permute-done.16 = f32[64,2048]{1,0:T(8,128)S(1)} collective-permute-done((f32[64,2048]{1,0:T(8,128)S(1)}, f32[64,2048]{1,0:T(8,128)S(1)}, u32[]{:S(2)}, u32[]{:S(2)}) %collective-permute-start.16) | collective-permute-done | bytes 524320 | tf_op jit(solution)/shard_map/ppermute | solution.py:524
  86.3 0.0 collective-permute-done.17
  86.3 0.9 %add_add_fusion = f32[64,2048]{1,0:T(8,128)} fusion(f32[64,2048]{1,0:T(8,128)S(1)} %collective-permute-done.17, f32[64,2048]{1,0:T(8,128)S(1)} %get-tuple-element.82, f32[64,2048]{1,0:T(8,128)S(1)} %collective-permute-done.16), kind=kLoop, calls=%fused_computation | loop fusion | flops 262144 | bytes 2097152 | tf_op jit(solution)/shard_map/add | solution.py:525
  (2 shorter events, 0.0 us)
Async XLA Ops:
  9.4 4.9 %collective-permute-start = (f32[128,256]{1,0:T(8,128)}, f32[128,256]{1,0:T(8,128)S(1)}, u32[]{:S(2)}, u32[]{:S(2)}) collective-permute-start(f32[128,256]{1,0:T(8,128)} %get-tuple-element.46), channel_id=1, source_target_pairs={{0,4},{4,0},{8,12},{12,8},{16,20},{20,16},{24,28},{28,24},{1,5},{5... | collective-permute-start | bytes 393224 | tf_op jit(solution)/shard_map/ppermute | solution.py:446
  9.9 7.1 %collective-permute-start.1 = (f32[128,256]{1,0:T(8,128)}, f32[128,256]{1,0:T(8,128)S(1)}, u32[]{:S(2)}, u32[]{:S(2)}) collective-permute-start(f32[128,256]{1,0:T(8,128)} %get-tuple-element.47), channel_id=1, source_target_pairs={{0,8},{4,12},{8,0},{12,4},{16,24},{20,28},{24,16},{28,20},{1,9},{5... | collective-permute-start | bytes 393224 | tf_op jit(solution)/shard_map/ppermute | solution.py:446
  12.5 12.0 %collective-permute-start.2 = (f32[128,256]{1,0:T(8,128)}, f32[128,256]{1,0:T(8,128)S(1)}, u32[]{:S(2)}, u32[]{:S(2)}) collective-permute-start(f32[128,256]{1,0:T(8,128)} %get-tuple-element.48), channel_id=1, source_target_pairs={{0,12},{4,8},{8,4},{12,0},{16,28},{20,24},{24,20},{28,16},{1,13},{... | collective-permute-start | bytes 393224 | tf_op jit(solution)/shard_map/ppermute | solution.py:446
  12.6 11.9 %collective-permute-start.3 = (f32[128,256]{1,0:T(8,128)}, f32[128,256]{1,0:T(8,128)S(1)}, u32[]{:S(2)}, u32[]{:S(2)}) collective-permute-start(f32[128,256]{1,0:T(8,128)} %get-tuple-element.49), channel_id=1, source_target_pairs={{0,16},{4,20},{8,24},{12,28},{16,0},{20,4},{24,8},{28,12},{1,17},{... | collective-permute-start | bytes 393224 | tf_op jit(solution)/shard_map/ppermute | solution.py:446
  14.3 12.0 %collective-permute-start.4 = (f32[128,256]{1,0:T(8,128)}, f32[128,256]{1,0:T(8,128)S(1)}, u32[]{:S(2)}, u32[]{:S(2)}) collective-permute-start(f32[128,256]{1,0:T(8,128)} %get-tuple-element.50), channel_id=1, source_target_pairs={{0,20},{4,16},{8,28},{12,24},{16,4},{20,0},{24,12},{28,8},{1,21},{... | collective-permute-start | bytes 393224 | tf_op jit(solution)/shard_map/ppermute | solution.py:446
  14.3 12.0 %collective-permute-start.5 = (f32[128,256]{1,0:T(8,128)}, f32[128,256]{1,0:T(8,128)S(1)}, u32[]{:S(2)}, u32[]{:S(2)}) collective-permute-start(f32[128,256]{1,0:T(8,128)} %get-tuple-element.51), channel_id=1, source_target_pairs={{0,24},{4,28},{8,16},{12,20},{16,8},{20,12},{24,0},{28,4},{1,25},{... | collective-permute-start | bytes 393224 | tf_op jit(solution)/shard_map/ppermute | solution.py:446
  17.0 9.3 %collective-permute-start.6 = (f32[128,256]{1,0:T(8,128)}, f32[128,256]{1,0:T(8,128)S(1)}, u32[]{:S(2)}, u32[]{:S(2)}) collective-permute-start(f32[128,256]{1,0:T(8,128)} %get-tuple-element.52), channel_id=1, source_target_pairs={{0,28},{4,24},{8,20},{12,16},{16,12},{20,8},{24,4},{28,0},{1,29},{... | collective-permute-start | bytes 393224 | tf_op jit(solution)/shard_map/ppermute | solution.py:446
  28.3 12.0 %copy-start = (f32[8,256,256]{2,1,0:T(8,128)S(1)}, f32[8,256,256]{2,1,0:T(8,128)}, u32[]{:S(2)}) copy-start(f32[8,256,256]{2,1,0:T(8,128)} %output_maps.1.map_hbm) | copy-start | bytes 6291460
  28.3 12.0 %copy-start.1 = (f32[256,1024]{1,0:T(8,128)S(1)}, f32[256,1024]{1,0:T(8,128)}, u32[]{:S(2)}) copy-start(f32[256,1024]{1,0:T(8,128)} %gate_hbm.3) | copy-start | bytes 3145732
  28.3 12.0 %copy-start.2 = (f32[128]{0:T(128)S(1)}, f32[128]{0:T(128)}, u32[]{:S(2)}) copy-start(f32[128]{0:T(128)} %param.14) | copy-start | bytes 1540
  28.4 4.0 %collective-permute-start.7 = (f32[128,128]{1,0:T(8,128)S(1)}, f32[128,128]{1,0:T(8,128)S(1)}, u32[]{:S(2)}, u32[]{:S(2)}) collective-permute-start(f32[128,128]{1,0:T(8,128)S(1)} %get-tuple-element.72), channel_id=1, source_target_pairs={{0,4},{4,0},{8,12},{12,8},{16,20},{20,16},{24,28},{28,24},{1,5},{5... | collective-permute-start | bytes 196616 | tf_op jit(solution)/shard_map/ppermute | solution.py:446
  28.9 6.2 %collective-permute-start.8 = (f32[128,128]{1,0:T(8,128)S(1)}, f32[128,128]{1,0:T(8,128)S(1)}, u32[]{:S(2)}, u32[]{:S(2)}) collective-permute-start(f32[128,128]{1,0:T(8,128)S(1)} %get-tuple-element.73), channel_id=1, source_target_pairs={{0,8},{4,12},{8,0},{12,4},{16,24},{20,28},{24,16},{28,20},{1,9},{5... | collective-permute-start | bytes 196616 | tf_op jit(solution)/shard_map/ppermute | solution.py:446
  30.6 8.3 %collective-permute-start.9 = (f32[128,128]{1,0:T(8,128)S(1)}, f32[128,128]{1,0:T(8,128)S(1)}, u32[]{:S(2)}, u32[]{:S(2)}) collective-permute-start(f32[128,128]{1,0:T(8,128)S(1)} %get-tuple-element.74), channel_id=1, source_target_pairs={{0,12},{4,8},{8,4},{12,0},{16,28},{20,24},{24,20},{28,16},{1,13},{... | collective-permute-start | bytes 196616 | tf_op jit(solution)/shard_map/ppermute | solution.py:446
  30.6 8.3 %collective-permute-start.10 = (f32[128,128]{1,0:T(8,128)S(1)}, f32[128,128]{1,0:T(8,128)S(1)}, u32[]{:S(2)}, u32[]{:S(2)}) collective-permute-start(f32[128,128]{1,0:T(8,128)S(1)} %get-tuple-element.75), channel_id=1, source_target_pairs={{0,16},{4,20},{8,24},{12,28},{16,0},{20,4},{24,8},{28,12},{1,17},{... | collective-permute-start | bytes 196616 | tf_op jit(solution)/shard_map/ppermute | solution.py:446
  32.1 6.8 %collective-permute-start.11 = (f32[128,128]{1,0:T(8,128)S(1)}, f32[128,128]{1,0:T(8,128)S(1)}, u32[]{:S(2)}, u32[]{:S(2)}) collective-permute-start(f32[128,128]{1,0:T(8,128)S(1)} %get-tuple-element.76), channel_id=1, source_target_pairs={{0,20},{4,16},{8,28},{12,24},{16,4},{20,0},{24,12},{28,8},{1,21},{... | collective-permute-start | bytes 196616 | tf_op jit(solution)/shard_map/ppermute | solution.py:446
  32.4 6.5 %collective-permute-start.12 = (f32[128,128]{1,0:T(8,128)S(1)}, f32[128,128]{1,0:T(8,128)S(1)}, u32[]{:S(2)}, u32[]{:S(2)}) collective-permute-start(f32[128,128]{1,0:T(8,128)S(1)} %get-tuple-element.77), channel_id=1, source_target_pairs={{0,24},{4,28},{8,16},{12,20},{16,8},{20,12},{24,0},{28,4},{1,25},{... | collective-permute-start | bytes 196616 | tf_op jit(solution)/shard_map/ppermute | solution.py:446
  35.1 5.3 %collective-permute-start.13 = (f32[128,128]{1,0:T(8,128)S(1)}, f32[128,128]{1,0:T(8,128)S(1)}, u32[]{:S(2)}, u32[]{:S(2)}) collective-permute-start(f32[128,128]{1,0:T(8,128)S(1)} %get-tuple-element.78), channel_id=1, source_target_pairs={{0,28},{4,24},{8,20},{12,16},{16,12},{20,8},{24,4},{28,0},{1,29},{... | collective-permute-start | bytes 196616 | tf_op jit(solution)/shard_map/ppermute | solution.py:446
  44.7 12.2 %collective-permute-start.15 = (f32[64,2048]{1,0:T(8,128)S(1)}, f32[64,2048]{1,0:T(8,128)S(1)}, u32[]{:S(2)}, u32[]{:S(2)}) collective-permute-start(f32[64,2048]{1,0:T(8,128)S(1)} %projection.3), channel_id=1, source_target_pairs={{3,2},{2,1},{7,6},{6,5},{11,10},{10,9},{15,14},{14,13},{19,18},{18... | collective-permute-start | bytes 1572872 | tf_op jit(solution)/shard_map/ppermute | solution.py:511
  45.4 15.5 %collective-permute-start.14 = (f32[64,2048]{1,0:T(8,128)S(1)}, f32[64,2048]{1,0:T(8,128)S(1)}, u32[]{:S(2)}, u32[]{:S(2)}) collective-permute-start(f32[64,2048]{1,0:T(8,128)S(1)} %projection.3), channel_id=1, source_target_pairs={{0,1},{1,2},{4,5},{5,6},{8,9},{9,10},{12,13},{13,14},{16,17},{17,1... | collective-permute-start | bytes 1572872 | tf_op jit(solution)/shard_map/ppermute | solution.py:510
  61.1 25.1 %collective-permute-start.16 = (f32[64,2048]{1,0:T(8,128)S(1)}, f32[64,2048]{1,0:T(8,128)S(1)}, u32[]{:S(2)}, u32[]{:S(2)}) collective-permute-start(f32[64,2048]{1,0:T(8,128)S(1)} %get-tuple-element.83), channel_id=1, source_target_pairs={{0,1},{1,0},{2,3},{3,2},{4,5},{5,4},{6,7},{7,6},{8,9},{9,8},{10,11... | collective-permute-start | bytes 1572872 | tf_op jit(solution)/shard_map/ppermute | solution.py:524
  63.7 22.6 %collective-permute-start.17 = (f32[64,2048]{1,0:T(8,128)S(1)}, f32[64,2048]{1,0:T(8,128)S(1)}, u32[]{:S(2)}, u32[]{:S(2)}) collective-permute-start(f32[64,2048]{1,0:T(8,128)S(1)} %get-tuple-element.84), channel_id=1, source_target_pairs={{0,2},{1,3},{2,0},{3,1},{4,6},{5,7},{6,4},{7,5},{8,10},{9,11},{10,... | collective-permute-start | bytes 1572872 | tf_op jit(solution)/shard_map/ppermute | solution.py:523

commit v6 on v5

--- a/solution.py
+++ b/solution.py
@@ -13,7 +13,7 @@
 BLOCK = 128
 SMALL = 32
 BAND = 256
-SWAP_ORDER = (7, 6, 3, 5, 2, 4, 1)
+SWAP_ORDER = (7, 6, 5, 4, 3, 2, 1)
 WEIGHT_ROWS = 128
 MOST_VMEM = 56
 SCAN_VMEM = 52.25
@@ -173,7 +173,7 @@
 
 
 def partner(place, swap):
-    return lax.axis_index("ctx") ^ place if swap else place
+    return lax.axis_index("ctx") ^ (0, *SWAP_ORDER)[place] if swap else place
 
 
 def summary_kernel(decay_hbm, strength_hbm, k_hbm, v_hbm, factor_hbm, *rest, swap):
@@ -418,11 +418,12 @@
                 out_ref[:, band - start : band - start + BAND] = result[at : at + rows]
 
 
-def forward_kernel(across_ref, own_ref, up_ref, down_ref, _, going_ref, staying_ref, __):
-    outward = lax.axis_index("tp") == 1
-    up, down = up_ref[...], down_ref[...]
-    going_ref[...] = across_ref[...] + jnp.where(outward, up, down)
-    staying_ref[...] = own_ref[...] + jnp.where(outward, down, up)
+def forward_kernel(across_ref, end_ref, going_ref):
+    going_ref[...] = across_ref[...] + end_ref[...]
+
+
+def hand_on_kernel(_, __, ___):
+    pass
 
 
 def shape(*dims):
@@ -441,10 +442,10 @@
 
 def partners_swap(arrays, axis):
     count = len(arrays)
-    arrays = list(arrays)
-    for i in [i for i in SWAP_ORDER if i < count]:
-        arrays[i] = lax.ppermute(arrays[i], axis, [(d, d ^ i) for d in range(count)])
-    return arrays
+    return [arrays[0]] + [
+        lax.ppermute(array, axis, [(d, d ^ i) for d in range(count)])
+        for array, i in zip(arrays[1:], SWAP_ORDER)
+    ]
 
 
 class Swap(typing.NamedTuple):
@@ -453,7 +454,7 @@
 
 
 def swap_is_possible(heads, count):
-    return heads == count and count & (count - 1) == 0 and count <= 8
+    return heads == count == 1 + len(SWAP_ORDER)
 
 
 def entering_states(factors, summaries, swap, beside, after):
@@ -507,22 +508,28 @@
         whole = jnp.concatenate(project([(i, 0, columns) for i in range(count)], LATER_VMEM), axis=0)
         return lax.psum_scatter(whole, axis, scatter_dimension=0, tiled=True)
     (opposite,) = project([(3, 0, columns)], FIRST_VMEM)
-    up = lax.ppermute(opposite, axis, [(0, 1), (1, 2)])
-    down = lax.ppermute(opposite, axis, [(3, 2), (2, 1)])
+    from_end = lax.ppermute(opposite, axis, [(0, 1), (3, 2)])
+    from_inner = lax.ppermute(opposite, axis, [(1, 2), (2, 1)])
     across, own, near = project([(i, 0, columns) for i in (2, 0, 1)], LATER_VMEM)
-    anywhere = pl.BlockSpec(memory_space=pl.ANY)
-    going, staying, near = pl.pallas_call(
+    going = pl.pallas_call(
         forward_kernel,
-        in_specs=[VMEM] * 4 + [anywhere],
-        out_specs=[VMEM] * 2 + [anywhere],
-        out_shape=[shape(*own.shape)] * 3,
-        input_output_aliases={4: 2},
+        out_shape=shape(*own.shape),
         compiler_params=params(LATER_VMEM),
         name="forward",
-    )(across, own, up, down, near)
+    )(across, from_end)
+    anywhere = pl.BlockSpec(memory_space=pl.ANY)
+    near = pl.pallas_call(
+        hand_on_kernel,
+        in_specs=[anywhere] * 2,
+        out_specs=anywhere,
+        out_shape=shape(*near.shape),
+        input_output_aliases={0: 0},
+        compiler_params=params(LATER_VMEM),
+        name="hand_on",
+    )(near, going)
+    from_near = lax.ppermute(near, axis, [(i, i ^ 1) for i in range(4)])
     from_across = lax.ppermute(going, axis, [(i, i ^ 2) for i in range(4)])
-    from_near = lax.ppermute(near, axis, [(i, i ^ 1) for i in range(4)])
-    return (staying + from_near) + from_across
+    return ((own + from_inner) + from_near) + from_across
 
 
 def per_device(queries, key_vectors, values, decays, strengths, out_gate, norm_gain, out_weight):

time: 87.7 us -> 89.2 us (1.017)
  waiting for transfers between devices: 28.2 us -> 31.6 us
  starting transfers between devices: 25.2 us -> 23.6 us
    ppermute x1, waiting for transfers between devices: 0.01 us -> 2.52 us  [project_and_sum(): from_across = lax.ppermute(going, axis, [(i, i ^ 2) for i in range(4)])]
    ppermute x1, waiting for transfers between devices: 20.7 us -> 21.8 us  [project_and_sum(): from_near = lax.ppermute(near, axis, [(i, i ^ 1) for i in range(4)])]
  transfers between devices with their start and end apart: 18 -> 18, of which waited for: 5 -> 7; matrix products, arithmetic and copies ran while one was open for 0% -> 0% of each run, Pallas kernels for 19% -> 19%
where the time goes in v6:
time: 89.2 us; the launch traced here: 88.9 us
  Pallas kernels  32.6 us (37%)
  waiting for transfers between devices  31.6 us (35%)
  starting transfers between devices  23.6 us (26%)
  other arithmetic  0.92 us (1%)
    ppermute x1, waiting for transfers between devices, project_and_sum(): from_near = lax.ppermute(near, axis, [(i, i ^ 1) for i in range(4)])  21.8 us
    ppermute x14, starting transfers between devices, partners_swap(): lax.ppermute(array, axis, [(d, d ^ i) for d in range(count)])  15.8 us
    pallas_call x2, Pallas kernels, project(): pl.pallas_call(functools.partial(projection_kernel, pieces=[(index, start...  11.7 us
    pallas_call x1, Pallas kernels, per_device(): pl.pallas_call(functools.partial(summary_kernel, swap=swap.heads), in_spe...  9.37 us
    pallas_call x1, Pallas kernels, per_device(): pl.pallas_call(output_kernel, in_specs=[HBM] * 4, out_specs=HBM, out_shap...  5.7 us
    pallas_call x1, Pallas kernels, per_device(): pl.pallas_call(weight_kernel, in_specs=[HBM], out_shape=jax.ShapeDtypeStr...  3.79 us
    ppermute x1, waiting for transfers between devices, project_and_sum(): from_end = lax.ppermute(opposite, axis, [(0, 1), (3, 2)])  3.77 us
    ppermute x1, starting transfers between devices, project_and_sum(): from_end = lax.ppermute(opposite, axis, [(0, 1), (3, 2)])  3.51 us
  transfers between devices with their start and end apart: 18, of which 7 were waited for; matrix products, arithmetic and copies ran while one was open for 0% of the time, Pallas kernels for 19%

profile of v6, /device:TPU:0, one launch (start us, length us, event | category | flops | bytes accessed | tf_op | source)
XLA Modules:
  0.0 88.9 jit_solution(3189609578818655870)
XLA Ops:
  0.0 9.4 %state_summary.1 = (f32[9,256,256]{2,1,0:T(8,128)}, f32[128,256]{1,0:T(8,128)}, f32[128,256]{1,0:T(8,128)}, f32[128,256]{1,0:T(8,128)}, f32[128,256]{1,0:T(8,128...) custom-call(f32[8,256]{1,0:T(8,128)} %decay_hbm.3, f32[8,256]{1,0:T(8,128)} %strength_hbm.1, ...), custom_call_target="tpu_custom_call" | custom-call | tf_op jit(solution)/shard_map/state_summary/pallas_call | solution.py:554
  9.4 3.4 %collective-permute-start = (f32[128,256]{1,0:T(8,128)}, f32[128,256]{1,0:T(8,128)S(1)}, u32[]{:S(2)}, u32[]{:S(2)}) collective-permute-start(f32[128,256]{1,0:T(8,128)} %get-tuple-element.43), channel_id=1, source_target_pairs={{0,28},{4,24},{8,20},{12,16},{16,12},{20,8},{24,4},{28,0},{1,29},{... | collective-permute-start | bytes 393224 | tf_op jit(solution)/shard_map/ppermute | solution.py:446
  12.8 0.6 collective-permute-start.1
  13.4 1.4 %collective-permute-start.2 = (f32[128,256]{1,0:T(8,128)}, f32[128,256]{1,0:T(8,128)S(1)}, u32[]{:S(2)}, u32[]{:S(2)}) collective-permute-start(f32[128,256]{1,0:T(8,128)} %get-tuple-element.45), channel_id=1, source_target_pairs={{0,20},{4,16},{8,28},{12,24},{16,4},{20,0},{24,12},{28,8},{1,21},{... | collective-permute-start | bytes 393224 | tf_op jit(solution)/shard_map/ppermute | solution.py:446
  14.8 0.3 collective-permute-start.3
  15.1 1.2 %collective-permute-start.4 = (f32[128,256]{1,0:T(8,128)}, f32[128,256]{1,0:T(8,128)S(1)}, u32[]{:S(2)}, u32[]{:S(2)}) collective-permute-start(f32[128,256]{1,0:T(8,128)} %get-tuple-element.47), channel_id=1, source_target_pairs={{0,12},{4,8},{8,4},{12,0},{16,28},{20,24},{24,20},{28,16},{1,13},{... | collective-permute-start | bytes 393224 | tf_op jit(solution)/shard_map/ppermute | solution.py:446
  16.2 0.7 collective-permute-done.rest_0_
  17.0 2.4 %collective-permute-start.5 = (f32[128,256]{1,0:T(8,128)}, f32[128,256]{1,0:T(8,128)S(1)}, u32[]{:S(2)}, u32[]{:S(2)}) collective-permute-start(f32[128,256]{1,0:T(8,128)} %get-tuple-element.48), channel_id=1, source_target_pairs={{0,8},{4,12},{8,0},{12,4},{16,24},{20,28},{24,16},{28,20},{1,9},{5... | collective-permute-start | bytes 393224 | tf_op jit(solution)/shard_map/ppermute | solution.py:446
  19.4 0.9 collective-permute-done.1.rest_1_
  20.3 0.0 collective-permute-start.6
  20.3 5.7 %output_maps.1.map_hbm = f32[8,256,256]{2,1,0:T(8,128)} custom-call(f32[8,256]{1,0:T(8,128)} %decay_hbm.3, f32[256,512]{1,0:T(8,128)} %q_hbm.1, f32[256,512]{1,0:T(8,128)} %k_hbm.3, f32[9,256,256]{2,1,0:T(8,128)} %get-tuple-element.51.factor_hbm), custom_call_target="tpu_custom_call" | custom-call | flops 1207959552 | bytes 5242880 | tf_op jit(solution)/shard_map/output_maps/pallas_call | solution.py:565
  26.0 0.0 collective-permute-done.2.rest_2_
  26.0 0.0 collective-permute-done.3.rest_3_
  26.0 0.0 collective-permute-done.4.rest_4_
  26.0 0.3 collective-permute-done.5.rest_5_
  26.3 0.0 collective-permute-done.6.rest_6_
  26.3 2.0 %state_scan.1 = (f32[128,128]{1,0:T(8,128)S(1)}, f32[128,128]{1,0:T(8,128)S(1)}, f32[128,128]{1,0:T(8,128)S(1)}, f32[128,128]{1,0:T(8,128)S(1)}, f32[128,128]{1,...) custom-call(f32[9,256,256]{2,1,0:T(8,128)} %get-tuple-element.51.factor_hbm, ...), custom_call_target="tpu_custom_call" | custom-call | tf_op jit(solution)/shard_map/state_scan/pallas_call | solution.py:467
  28.3 0.0 copy-start
  28.3 0.0 copy-start.1
  28.3 0.0 copy-start.2
  28.4 2.8 %collective-permute-start.7 = (f32[128,128]{1,0:T(8,128)S(1)}, f32[128,128]{1,0:T(8,128)S(1)}, u32[]{:S(2)}, u32[]{:S(2)}) collective-permute-start(f32[128,128]{1,0:T(8,128)S(1)} %get-tuple-element.69), channel_id=1, source_target_pairs={{0,28},{4,24},{8,20},{12,16},{16,12},{20,8},{24,4},{28,0},{1,29},{... | collective-permute-start | bytes 196616 | tf_op jit(solution)/shard_map/ppermute | solution.py:446
  31.1 0.0 collective-permute-start.8
  31.2 1.3 %collective-permute-start.9 = (f32[128,128]{1,0:T(8,128)S(1)}, f32[128,128]{1,0:T(8,128)S(1)}, u32[]{:S(2)}, u32[]{:S(2)}) collective-permute-start(f32[128,128]{1,0:T(8,128)S(1)} %get-tuple-element.71), channel_id=1, source_target_pairs={{0,20},{4,16},{8,28},{12,24},{16,4},{20,0},{24,12},{28,8},{1,21},{... | collective-permute-start | bytes 196616 | tf_op jit(solution)/shard_map/ppermute | solution.py:446
  32.5 0.7 collective-permute-start.10
  33.2 1.4 %collective-permute-start.11 = (f32[128,128]{1,0:T(8,128)S(1)}, f32[128,128]{1,0:T(8,128)S(1)}, u32[]{:S(2)}, u32[]{:S(2)}) collective-permute-start(f32[128,128]{1,0:T(8,128)S(1)} %get-tuple-element.73), channel_id=1, source_target_pairs={{0,12},{4,8},{8,4},{12,0},{16,28},{20,24},{24,20},{28,16},{1,13},{... | collective-permute-start | bytes 196616 | tf_op jit(solution)/shard_map/ppermute | solution.py:446
  34.6 0.0 collective-permute-done.7.rest_1_
  34.6 0.3 collective-permute-start.12
  34.9 1.5 %collective-permute-done.8.rest_2_ = f32[128,128]{1,0:T(8,128)S(1)} collective-permute-done((f32[128,128]{1,0:T(8,128)S(1)}, f32[128,128]{1,0:T(8,128)S(1)}, u32[]{:S(2)}, u32[]{:S(2)}) %collective-permute-start.8) | collective-permute-done | bytes 65568 | tf_op jit(solution)/shard_map/ppermute | solution.py:446
  36.4 0.0 collective-permute-start.13
  36.4 3.8 %weight_parts.1.parts_ref = bf16[2,1024,2048]{2,1,0:T(8,128)(2,1)S(1)} custom-call(f32[1024,2048]{1,0:T(8,128)} %weight_hbm), custom_call_target="tpu_custom_call" | custom-call | flops 12582912 | bytes 16777216 | tf_op jit(solution)/shard_map/weight_parts/pallas_call | solution.py:578
  40.2 0.0 collective-permute-done.9.rest_3_
  40.2 0.0 collective-permute-done.10.rest_4_
  40.2 0.0 collective-permute-done.11.rest_5_
  40.2 0.0 collective-permute-done.12.rest_6_
  40.2 0.0 collective-permute-done.13.rest_7_
  40.2 0.0 copy-done
  40.2 4.3 %projection.3 = f32[64,2048]{1,0:T(8,128)S(1)} custom-call(f32[8,256,256]{2,1,0:T(8,128)S(1)} %copy-done, f32[256,1024]{1,0:T(8,128)S(1)} %copy-done.1, f32[1,128]{1,0:T(1,128)S(1)} %bitcast.1, bf16[2,1024,2048]{2,1,0:T(8,128)(2,1)S(1)} %weight_parts.1.parts_ref, f32[128,128]{1,0:T(8,128)S(1)} %get-tuple-element.68.rest_0_, ...), custom_call_target="tpu_custom_call" | custom-call | flops 805306368 | bytes 8388608 | tf_op jit(solution)/shard_map/projection/pallas_call | solution.py:595
  44.6 3.5 %collective-permute-start.15 = (f32[64,2048]{1,0:T(8,128)S(1)}, f32[64,2048]{1,0:T(8,128)S(1)}, u32[]{:S(2)}, u32[]{:S(2)}) collective-permute-start(f32[64,2048]{1,0:T(8,128)S(1)} %projection.3), channel_id=1, source_target_pairs={{0,1},{3,2},{4,5},{7,6},{8,9},{11,10},{12,13},{15,14},{16,17},{19,... | collective-permute-start | bytes 1572872 | tf_op jit(solution)/shard_map/ppermute | solution.py:511
  48.1 0.7 collective-permute-start.14
  48.8 7.3 %projection.2 = (f32[64,2048]{1,0:T(8,128)S(1)}, f32[64,2048]{1,0:T(8,128)S(1)}, f32[64,2048]{1,0:T(8,128)S(1)}) custom-call(f32[8,256,256]{2,1,0:T(8,128)S(1)} %copy-done, f32[256,1024]{1,0:T(8,128)S(1)} %copy-done.1, f32[1,128]{1,0:T(1,128)S(1)} %bitcast.2, bf16[2,1024,2048]{2,1,0:T(8,128)(2,1)S(1)} %weight_parts.1.parts_ref, ...), custom_call_target="tpu_custom_call" | custom-call | flops 2415919104 | bytes 8388608 | tf_op jit(solution)/shard_map/projection/pallas_call | solution.py:595
  56.1 3.8 %collective-permute-done.15.end_ref = f32[64,2048]{1,0:T(8,128)S(1)} collective-permute-done((f32[64,2048]{1,0:T(8,128)S(1)}, f32[64,2048]{1,0:T(8,128)S(1)}, u32[]{:S(2)}, u32[]{:S(2)}) %collective-permute-start.15) | collective-permute-done | bytes 524320 | tf_op jit(solution)/shard_map/ppermute | solution.py:511
  59.9 0.1 forward.1.__
  60.0 2.5 %collective-permute-start.16 = (f32[64,2048]{1,0:T(8,128)S(1)}, f32[64,2048]{1,0:T(8,128)S(1)}, u32[]{:S(2)}, u32[]{:S(2)}) collective-permute-start(f32[64,2048]{1,0:T(8,128)S(1)} %hand_on.1), channel_id=1, source_target_pairs={{0,1},{1,0},{2,3},{3,2},{4,5},{5,4},{6,7},{7,6},{8,9},{9,8},{10,11... | collective-permute-start | bytes 1572872 | tf_op jit(solution)/shard_map/ppermute | solution.py:530
  62.5 1.1 %collective-permute-start.17 = (f32[64,2048]{1,0:T(8,128)S(1)}, f32[64,2048]{1,0:T(8,128)S(1)}, u32[]{:S(2)}, u32[]{:S(2)}) collective-permute-start(f32[64,2048]{1,0:T(8,128)S(1)} %forward.1.__), channel_id=1, source_target_pairs={{0,2},{1,3},{2,0},{3,1},{4,6},{5,7},{6,4},{7,5},{8,10},{9,11},{10,... | collective-permute-start | bytes 1572872 | tf_op jit(solution)/shard_map/ppermute | solution.py:531
  63.6 0.0 collective-permute-done.14
  63.6 21.8 %collective-permute-done.16 = f32[64,2048]{1,0:T(8,128)S(1)} collective-permute-done((f32[64,2048]{1,0:T(8,128)S(1)}, f32[64,2048]{1,0:T(8,128)S(1)}, u32[]{:S(2)}, u32[]{:S(2)}) %collective-permute-start.16) | collective-permute-done | bytes 524320 | tf_op jit(solution)/shard_map/ppermute | solution.py:530
  85.5 2.5 %collective-permute-done.17 = f32[64,2048]{1,0:T(8,128)S(1)} collective-permute-done((f32[64,2048]{1,0:T(8,128)S(1)}, f32[64,2048]{1,0:T(8,128)S(1)}, u32[]{:S(2)}, u32[]{:S(2)}) %collective-permute-start.17) | collective-permute-done | bytes 524320 | tf_op jit(solution)/shard_map/ppermute | solution.py:531
  88.0 0.9 %add_add_fusion = f32[64,2048]{1,0:T(8,128)} fusion(f32[64,2048]{1,0:T(8,128)S(1)} %collective-permute-done.17, f32[64,2048]{1,0:T(8,128)S(1)} %collective-permute-done.16, f32[64,2048]{1,0:T(8,128)S(1)} %get-tuple-element.76, f32[64,2048]{1,0:T(8,128)S(1)} %collective-permute-done.14), kind=kLoop, calls=%fused_computation | loop fusion | flops 393216 | bytes 2621440 | tf_op jit(solution)/shard_map/add | solution.py:532
  (3 shorter events, 0.0 us)
Async XLA Ops:
  9.4 7.6 %collective-permute-start = (f32[128,256]{1,0:T(8,128)}, f32[128,256]{1,0:T(8,128)S(1)}, u32[]{:S(2)}, u32[]{:S(2)}) collective-permute-start(f32[128,256]{1,0:T(8,128)} %get-tuple-element.43), channel_id=1, source_target_pairs={{0,28},{4,24},{8,20},{12,16},{16,12},{20,8},{24,4},{28,0},{1,29},{... | collective-permute-start | bytes 393224 | tf_op jit(solution)/shard_map/ppermute | solution.py:446
  12.8 7.5 %collective-permute-start.1 = (f32[128,256]{1,0:T(8,128)}, f32[128,256]{1,0:T(8,128)S(1)}, u32[]{:S(2)}, u32[]{:S(2)}) collective-permute-start(f32[128,256]{1,0:T(8,128)} %get-tuple-element.44), channel_id=1, source_target_pairs={{0,24},{4,28},{8,16},{12,20},{16,8},{20,12},{24,0},{28,4},{1,25},{... | collective-permute-start | bytes 393224 | tf_op jit(solution)/shard_map/ppermute | solution.py:446
  13.4 12.6 %collective-permute-start.2 = (f32[128,256]{1,0:T(8,128)}, f32[128,256]{1,0:T(8,128)S(1)}, u32[]{:S(2)}, u32[]{:S(2)}) collective-permute-start(f32[128,256]{1,0:T(8,128)} %get-tuple-element.45), channel_id=1, source_target_pairs={{0,20},{4,16},{8,28},{12,24},{16,4},{20,0},{24,12},{28,8},{1,21},{... | collective-permute-start | bytes 393224 | tf_op jit(solution)/shard_map/ppermute | solution.py:446
  14.8 11.2 %collective-permute-start.3 = (f32[128,256]{1,0:T(8,128)}, f32[128,256]{1,0:T(8,128)S(1)}, u32[]{:S(2)}, u32[]{:S(2)}) collective-permute-start(f32[128,256]{1,0:T(8,128)} %get-tuple-element.46), channel_id=1, source_target_pairs={{0,16},{4,20},{8,24},{12,28},{16,0},{20,4},{24,8},{28,12},{1,17},{... | collective-permute-start | bytes 393224 | tf_op jit(solution)/shard_map/ppermute | solution.py:446
  15.1 10.9 %collective-permute-start.4 = (f32[128,256]{1,0:T(8,128)}, f32[128,256]{1,0:T(8,128)S(1)}, u32[]{:S(2)}, u32[]{:S(2)}) collective-permute-start(f32[128,256]{1,0:T(8,128)} %get-tuple-element.47), channel_id=1, source_target_pairs={{0,12},{4,8},{8,4},{12,0},{16,28},{20,24},{24,20},{28,16},{1,13},{... | collective-permute-start | bytes 393224 | tf_op jit(solution)/shard_map/ppermute | solution.py:446
  17.0 9.3 %collective-permute-start.5 = (f32[128,256]{1,0:T(8,128)}, f32[128,256]{1,0:T(8,128)S(1)}, u32[]{:S(2)}, u32[]{:S(2)}) collective-permute-start(f32[128,256]{1,0:T(8,128)} %get-tuple-element.48), channel_id=1, source_target_pairs={{0,8},{4,12},{8,0},{12,4},{16,24},{20,28},{24,16},{28,20},{1,9},{5... | collective-permute-start | bytes 393224 | tf_op jit(solution)/shard_map/ppermute | solution.py:446
  20.3 6.1 %collective-permute-start.6 = (f32[128,256]{1,0:T(8,128)}, f32[128,256]{1,0:T(8,128)S(1)}, u32[]{:S(2)}, u32[]{:S(2)}) collective-permute-start(f32[128,256]{1,0:T(8,128)} %get-tuple-element.49), channel_id=1, source_target_pairs={{0,4},{4,0},{8,12},{12,8},{16,20},{20,16},{24,28},{28,24},{1,5},{5... | collective-permute-start | bytes 393224 | tf_op jit(solution)/shard_map/ppermute | solution.py:446
  28.3 11.9 %copy-start = (f32[8,256,256]{2,1,0:T(8,128)S(1)}, f32[8,256,256]{2,1,0:T(8,128)}, u32[]{:S(2)}) copy-start(f32[8,256,256]{2,1,0:T(8,128)} %output_maps.1.map_hbm) | copy-start | bytes 6291460
  28.3 11.9 %copy-start.1 = (f32[256,1024]{1,0:T(8,128)S(1)}, f32[256,1024]{1,0:T(8,128)}, u32[]{:S(2)}) copy-start(f32[256,1024]{1,0:T(8,128)} %gate_hbm.3) | copy-start | bytes 3145732
  28.3 11.9 %copy-start.2 = (f32[128]{0:T(128)S(1)}, f32[128]{0:T(128)}, u32[]{:S(2)}) copy-start(f32[128]{0:T(128)} %param.14) | copy-start | bytes 1540
  28.4 6.2 %collective-permute-start.7 = (f32[128,128]{1,0:T(8,128)S(1)}, f32[128,128]{1,0:T(8,128)S(1)}, u32[]{:S(2)}, u32[]{:S(2)}) collective-permute-start(f32[128,128]{1,0:T(8,128)S(1)} %get-tuple-element.69), channel_id=1, source_target_pairs={{0,28},{4,24},{8,20},{12,16},{16,12},{20,8},{24,4},{28,0},{1,29},{... | collective-permute-start | bytes 196616 | tf_op jit(solution)/shard_map/ppermute | solution.py:446
  31.1 5.2 %collective-permute-start.8 = (f32[128,128]{1,0:T(8,128)S(1)}, f32[128,128]{1,0:T(8,128)S(1)}, u32[]{:S(2)}, u32[]{:S(2)}) collective-permute-start(f32[128,128]{1,0:T(8,128)S(1)} %get-tuple-element.70), channel_id=1, source_target_pairs={{0,24},{4,28},{8,16},{12,20},{16,8},{20,12},{24,0},{28,4},{1,25},{... | collective-permute-start | bytes 196616 | tf_op jit(solution)/shard_map/ppermute | solution.py:446
  31.2 9.0 %collective-permute-start.9 = (f32[128,128]{1,0:T(8,128)S(1)}, f32[128,128]{1,0:T(8,128)S(1)}, u32[]{:S(2)}, u32[]{:S(2)}) collective-permute-start(f32[128,128]{1,0:T(8,128)S(1)} %get-tuple-element.71), channel_id=1, source_target_pairs={{0,20},{4,16},{8,28},{12,24},{16,4},{20,0},{24,12},{28,8},{1,21},{... | collective-permute-start | bytes 196616 | tf_op jit(solution)/shard_map/ppermute | solution.py:446
  32.5 7.7 %collective-permute-start.10 = (f32[128,128]{1,0:T(8,128)S(1)}, f32[128,128]{1,0:T(8,128)S(1)}, u32[]{:S(2)}, u32[]{:S(2)}) collective-permute-start(f32[128,128]{1,0:T(8,128)S(1)} %get-tuple-element.72), channel_id=1, source_target_pairs={{0,16},{4,20},{8,24},{12,28},{16,0},{20,4},{24,8},{28,12},{1,17},{... | collective-permute-start | bytes 196616 | tf_op jit(solution)/shard_map/ppermute | solution.py:446
  33.2 7.0 %collective-permute-start.11 = (f32[128,128]{1,0:T(8,128)S(1)}, f32[128,128]{1,0:T(8,128)S(1)}, u32[]{:S(2)}, u32[]{:S(2)}) collective-permute-start(f32[128,128]{1,0:T(8,128)S(1)} %get-tuple-element.73), channel_id=1, source_target_pairs={{0,12},{4,8},{8,4},{12,0},{16,28},{20,24},{24,20},{28,16},{1,13},{... | collective-permute-start | bytes 196616 | tf_op jit(solution)/shard_map/ppermute | solution.py:446
  34.6 5.6 %collective-permute-start.12 = (f32[128,128]{1,0:T(8,128)S(1)}, f32[128,128]{1,0:T(8,128)S(1)}, u32[]{:S(2)}, u32[]{:S(2)}) collective-permute-start(f32[128,128]{1,0:T(8,128)S(1)} %get-tuple-element.74), channel_id=1, source_target_pairs={{0,8},{4,12},{8,0},{12,4},{16,24},{20,28},{24,16},{28,20},{1,9},{5... | collective-permute-start | bytes 196616 | tf_op jit(solution)/shard_map/ppermute | solution.py:446
  36.4 3.8 %collective-permute-start.13 = (f32[128,128]{1,0:T(8,128)S(1)}, f32[128,128]{1,0:T(8,128)S(1)}, u32[]{:S(2)}, u32[]{:S(2)}) collective-permute-start(f32[128,128]{1,0:T(8,128)S(1)} %get-tuple-element.75), channel_id=1, source_target_pairs={{0,4},{4,0},{8,12},{12,8},{16,20},{20,16},{24,28},{28,24},{1,5},{5... | collective-permute-start | bytes 196616 | tf_op jit(solution)/shard_map/ppermute | solution.py:446
  44.6 15.3 %collective-permute-start.15 = (f32[64,2048]{1,0:T(8,128)S(1)}, f32[64,2048]{1,0:T(8,128)S(1)}, u32[]{:S(2)}, u32[]{:S(2)}) collective-permute-start(f32[64,2048]{1,0:T(8,128)S(1)} %projection.3), channel_id=1, source_target_pairs={{0,1},{3,2},{4,5},{7,6},{8,9},{11,10},{12,13},{15,14},{16,17},{19,... | collective-permute-start | bytes 1572872 | tf_op jit(solution)/shard_map/ppermute | solution.py:511
  48.1 15.5 %collective-permute-start.14 = (f32[64,2048]{1,0:T(8,128)S(1)}, f32[64,2048]{1,0:T(8,128)S(1)}, u32[]{:S(2)}, u32[]{:S(2)}) collective-permute-start(f32[64,2048]{1,0:T(8,128)S(1)} %projection.3), channel_id=1, source_target_pairs={{1,2},{2,1},{5,6},{6,5},{9,10},{10,9},{13,14},{14,13},{17,18},{18,... | collective-permute-start | bytes 1572872 | tf_op jit(solution)/shard_map/ppermute | solution.py:512
  60.0 25.5 %collective-permute-start.16 = (f32[64,2048]{1,0:T(8,128)S(1)}, f32[64,2048]{1,0:T(8,128)S(1)}, u32[]{:S(2)}, u32[]{:S(2)}) collective-permute-start(f32[64,2048]{1,0:T(8,128)S(1)} %hand_on.1), channel_id=1, source_target_pairs={{0,1},{1,0},{2,3},{3,2},{4,5},{5,4},{6,7},{7,6},{8,9},{9,8},{10,11... | collective-permute-start | bytes 1572872 | tf_op jit(solution)/shard_map/ppermute | solution.py:530
  62.5 25.5 %collective-permute-start.17 = (f32[64,2048]{1,0:T(8,128)S(1)}, f32[64,2048]{1,0:T(8,128)S(1)}, u32[]{:S(2)}, u32[]{:S(2)}) collective-permute-start(f32[64,2048]{1,0:T(8,128)S(1)} %forward.1.__), channel_id=1, source_target_pairs={{0,2},{1,3},{2,0},{3,1},{4,6},{5,7},{6,4},{7,5},{8,10},{9,11},{10,... | collective-permute-start | bytes 1572872 | tf_op jit(solution)/shard_map/ppermute | solution.py:531

commit v7 on v6

--- a/solution.py
+++ b/solution.py
@@ -14,12 +14,11 @@
 SMALL = 32
 BAND = 256
 SWAP_ORDER = (7, 6, 5, 4, 3, 2, 1)
-WEIGHT_ROWS = 128
+WEIGHT_ROWS = 256
 MOST_VMEM = 56
 SCAN_VMEM = 52.25
-WEIGHT_VMEM = 40
-FIRST_VMEM = 24
-LATER_VMEM = 24
+FIRST_VMEM = 40
+LATER_VMEM = 32
 HEADS_AT_ONCE = 8
 EPS = 1e-06
 
@@ -363,15 +362,12 @@
         entry[...] = entry_ref[partner(i, True)]
 
 
-def weight_kernel(weight_hbm, parts_ref, weight_ref, sems):
-    bands = [pl.ds(row, WEIGHT_ROWS) for row in range(0, weight_ref.shape[0], WEIGHT_ROWS)]
-    copies = fetch([(weight_hbm.at[band, :], weight_ref.at[band, :]) for band in bands], sems)
-    for copy, band in zip(copies, bands):
-        copy.wait()
-        parts_ref[0, band, :], parts_ref[1, band, :] = split(weight_ref[band, :])
-
-
-def projection_kernel(map_hbm, gate_hbm, gain_ref, parts_ref, *rest, pieces, swap):
+def projection_kernel(map_hbm, gate_hbm, gain_ref, weight_ref, *rest, pieces, split_here, swap):
+    if split_here:
+        *rest, whole_ref, weight_sems = rest
+        parts_ref = rest.pop(-8)
+    else:
+        parts_ref = weight_ref
     *arrays, map_ref, gate_ref, state_ref, high_ref, low_ref, gate_sems, map_sems = rest
     outs = arrays[-len(pieces) :]
     states = arrays[: -len(pieces)]
@@ -391,6 +387,11 @@
         ],
         map_sems,
     )
+    if split_here:
+        bands = [pl.ds(row, WEIGHT_ROWS) for row in range(0, weight_ref.shape[0], WEIGHT_ROWS)]
+        weights = fetch(
+            [(weight_ref.at[band, :], whole_ref.at[band, :]) for band in bands], weight_sems
+        )
     for i, state in enumerate(states):
         state_ref[partner(i, swap.heads)] = state[...]
     for copy in gates:
@@ -406,16 +407,27 @@
         scale = lax.rsqrt(jnp.mean(core * core, axis=-1, keepdims=True) + EPS)
         high_ref[:, lanes], low_ref[:, lanes] = split(core * scale * factor)
     total = len(blocks) * rows
-    for band in range(0, parts_ref.shape[2], BAND):
-        lanes = slice(band, band + BAND)
-        both = jnp.concatenate([high_ref[...], low_ref[...]], axis=0)
-        sums = jnp.dot(both, parts_ref[0, :, lanes], preferred_element_type=jnp.float32)
-        last = jnp.dot(high_ref[...], parts_ref[1, :, lanes], preferred_element_type=jnp.float32)
-        result = sums[:total] + (sums[total:] + last)
-        for (index, start), out_ref in zip(pieces, outs):
-            if start <= band < start + out_ref.shape[1]:
-                at = blocks.index(index) * rows
-                out_ref[:, band - start : band - start + BAND] = result[at : at + rows]
+    depth, columns = parts_ref.shape[1:]
+    step = WEIGHT_ROWS if split_here else depth
+    for index, row in enumerate(range(0, depth, step)):
+        band = slice(row, row + step)
+        if split_here:
+            weights[index].wait()
+            parts_ref[0, band, :], parts_ref[1, band, :] = split(whole_ref[band, :])
+        for column in range(0, columns, BAND):
+            lanes = slice(column, column + BAND)
+            both = jnp.concatenate([high_ref[:, band], low_ref[:, band]], axis=0)
+            sums = jnp.dot(both, parts_ref[0, band, lanes], preferred_element_type=jnp.float32)
+            last = jnp.dot(
+                high_ref[:, band], parts_ref[1, band, lanes], preferred_element_type=jnp.float32
+            )
+            result = sums[:total] + (sums[total:] + last)
+            for (piece, start), out_ref in zip(pieces, outs):
+                if start <= column < start + out_ref.shape[1]:
+                    at = blocks.index(piece) * rows
+                    target = slice(column - start, column - start + BAND)
+                    part = result[at : at + rows]
+                    out_ref[:, target] = part if index == 0 else out_ref[:, target] + part
 
 
 def forward_kernel(across_ref, end_ref, going_ref):
@@ -505,12 +517,13 @@
 def project_and_sum(project, columns, axis):
     count = lax.axis_size(axis)
     if count != 4:
-        whole = jnp.concatenate(project([(i, 0, columns) for i in range(count)], LATER_VMEM), axis=0)
+        *pieces, _ = project([(i, 0, columns) for i in range(count)], FIRST_VMEM)
+        whole = jnp.concatenate(pieces, axis=0)
         return lax.psum_scatter(whole, axis, scatter_dimension=0, tiled=True)
-    (opposite,) = project([(3, 0, columns)], FIRST_VMEM)
+    opposite, parts = project([(3, 0, columns)], FIRST_VMEM)
     from_end = lax.ppermute(opposite, axis, [(0, 1), (3, 2)])
     from_inner = lax.ppermute(opposite, axis, [(1, 2), (2, 1)])
-    across, own, near = project([(i, 0, columns) for i in (2, 0, 1)], LATER_VMEM)
+    across, own, near = project([(i, 0, columns) for i in (2, 0, 1)], LATER_VMEM, parts)
     going = pl.pallas_call(
         forward_kernel,
         out_shape=shape(*own.shape),
@@ -566,7 +579,7 @@
         output_kernel,
         in_specs=[HBM] * 4,
         out_specs=HBM,
-        out_shape=factor_shape,
+        out_shape=shape(8 * heads, tokens, DK + DV),
         scratch_shapes=[pltpu.VMEM(a.shape, jnp.float32) for a in (decays, queries, key_vectors)]
         + [pltpu.VMEM(factor_shape.shape, jnp.float32), pltpu.SemaphoreType.DMA((3 + key_heads,))]
         + [pltpu.VMEM(factor_shape.shape, jnp.float32), pltpu.SemaphoreType.DMA((key_heads,))],
@@ -575,29 +588,27 @@
         name="output_maps",
     )(decays, queries, key_vectors, factors)
     states, maps, weights = entering_states(factors, summaries, swap.heads, maps, out_weight)
-    parts = pl.pallas_call(
-        weight_kernel,
-        in_specs=[HBM],
-        out_shape=jax.ShapeDtypeStruct((2, depth, columns), jnp.bfloat16),
-        scratch_shapes=[
-            pltpu.VMEM(out_weight.shape, jnp.float32),
-            pltpu.SemaphoreType.DMA((depth // WEIGHT_ROWS,)),
-        ],
-        compiler_params=params(WEIGHT_VMEM),
-        cost_estimate=cost(6 * weights.size, weights, weights),
-        name="weight_parts",
-    )(weights)
-
-    def project(pieces, vmem):
+    parts_shape = jax.ShapeDtypeStruct((2, depth, columns), jnp.bfloat16)
+
+    fetched = [
+        pltpu.VMEM(out_weight.shape, jnp.float32),
+        pltpu.SemaphoreType.DMA((depth // WEIGHT_ROWS,)),
+    ]
+
+    def project(pieces, vmem, parts=None):
         total = len({piece[0] for piece in pieces}) * rows
         normed = pltpu.VMEM((total, depth), jnp.bfloat16)
         counts = (total // rows, heads * total // rows)
         return pl.pallas_call(
             functools.partial(
-                projection_kernel, pieces=[(index, start) for index, start, _ in pieces], swap=swap
+                projection_kernel,
+                pieces=[(index, start) for index, start, _ in pieces],
+                split_here=parts is None,
+                swap=swap,
             ),
-            in_specs=[HBM] * 2 + [VMEM] * (2 + heads),
-            out_shape=[shape(rows, width) for _, _, width in pieces],
+            in_specs=[HBM] * 2 + [VMEM, HBM if parts is None else VMEM] + [VMEM] * heads,
+            out_shape=[shape(rows, width) for _, _, width in pieces]
+            + [parts_shape] * (parts is None),
             scratch_shapes=[
                 pltpu.VMEM((heads, total, DK + DV), jnp.float32),
                 pltpu.VMEM((total, heads * DV), jnp.float32),
@@ -605,11 +616,12 @@
                 normed,
                 normed,
             ]
-            + [pltpu.SemaphoreType.DMA((n,)) for n in counts],
+            + [pltpu.SemaphoreType.DMA((n,)) for n in counts]
+            + fetched * (parts is None),
             compiler_params=params(vmem),
             cost_estimate=cost(3 * 2 * total * depth * columns, out_weight),
             name="projection",
-        )(maps, out_gate, gain, parts, *states)
+        )(maps, out_gate, gain, weights if parts is None else parts, *states)
 
     return project_and_sum(project, columns, "tp")
 

time: 89.2 us -> 87.8 us (0.984)
  Pallas kernels: 32.6 us -> 28.6 us
  waiting for transfers between devices: 31.6 us -> 34.1 us
    pallas_call x1 -> x0, Pallas kernels: 3.79 us -> none  [per_device(): pl.pallas_call(weight_kernel, in_specs=[HBM], out_shape=jax.ShapeDtypeStr...]
    ppermute x14, waiting for transfers between devices: 3.44 us -> 5.93 us  [partners_swap(): lax.ppermute(array, axis, [(d, d ^ i) for d in range(count)])]
  transfers between devices with their start and end apart: 18 -> 18, of which waited for: 7 -> 10; matrix products, arithmetic and copies ran while one was open for 0% -> 0% of each run, Pallas kernels for 19% -> 14%
where the time goes in v7:
time: 87.8 us; the launch traced here: 87.5 us
  waiting for transfers between devices  34.1 us (39%)
  Pallas kernels  28.6 us (33%)
  starting transfers between devices  23.7 us (27%)
  other arithmetic  0.92 us (1%)
    ppermute x1, waiting for transfers between devices, project_and_sum(): from_near = lax.ppermute(near, axis, [(i, i ^ 1) for i in range(4)])  21.2 us
    ppermute x14, starting transfers between devices, partners_swap(): lax.ppermute(array, axis, [(d, d ^ i) for d in range(count)])  15.9 us
    pallas_call x2, Pallas kernels, project(): pl.pallas_call(functools.partial(projection_kernel, pieces=[(index, start...  11.4 us
    pallas_call x1, Pallas kernels, per_device(): pl.pallas_call(functools.partial(summary_kernel, swap=swap.heads), in_spe...  9.36 us
    ppermute x14, waiting for transfers between devices, partners_swap(): lax.ppermute(array, axis, [(d, d ^ i) for d in range(count)])  5.93 us
    pallas_call x1, Pallas kernels, per_device(): pl.pallas_call(output_kernel, in_specs=[HBM] * 4, out_specs=HBM, out_shap...  5.8 us
    ppermute x1, waiting for transfers between devices, project_and_sum(): from_end = lax.ppermute(opposite, axis, [(0, 1), (3, 2)])  4.43 us
    ppermute x1, starting transfers between devices, project_and_sum(): from_end = lax.ppermute(opposite, axis, [(0, 1), (3, 2)])  3.51 us
  transfers between devices with their start and end apart: 18, of which 10 were waited for; matrix products, arithmetic and copies ran while one was open for 0% of the time, Pallas kernels for 14%

profile of v7, /device:TPU:0, one launch (start us, length us, event | category | flops | bytes accessed | tf_op | source)
XLA Modules:
  0.0 87.5 jit_solution(3513590299549366279)
XLA Ops:
  0.0 9.4 %state_summary.1 = (f32[9,256,256]{2,1,0:T(8,128)}, f32[128,256]{1,0:T(8,128)}, f32[128,256]{1,0:T(8,128)}, f32[128,256]{1,0:T(8,128)}, f32[128,256]{1,0:T(8,128...) custom-call(f32[8,256]{1,0:T(8,128)} %decay_hbm.3, f32[8,256]{1,0:T(8,128)} %strength_hbm.1, ...), custom_call_target="tpu_custom_call" | custom-call | tf_op jit(solution)/shard_map/state_summary/pallas_call | solution.py:567
  9.4 3.4 %collective-permute-start = (f32[128,256]{1,0:T(8,128)}, f32[128,256]{1,0:T(8,128)S(1)}, u32[]{:S(2)}, u32[]{:S(2)}) collective-permute-start(f32[128,256]{1,0:T(8,128)} %get-tuple-element.45), channel_id=1, source_target_pairs={{0,28},{4,24},{8,20},{12,16},{16,12},{20,8},{24,4},{28,0},{1,29},{... | collective-permute-start | bytes 393224 | tf_op jit(solution)/shard_map/ppermute | solution.py:458
  12.8 0.6 collective-permute-start.1
  13.4 1.4 %collective-permute-start.2 = (f32[128,256]{1,0:T(8,128)}, f32[128,256]{1,0:T(8,128)S(1)}, u32[]{:S(2)}, u32[]{:S(2)}) collective-permute-start(f32[128,256]{1,0:T(8,128)} %get-tuple-element.47), channel_id=1, source_target_pairs={{0,20},{4,16},{8,28},{12,24},{16,4},{20,0},{24,12},{28,8},{1,21},{... | collective-permute-start | bytes 393224 | tf_op jit(solution)/shard_map/ppermute | solution.py:458
  14.8 0.3 collective-permute-start.3
  15.1 1.2 %collective-permute-start.4 = (f32[128,256]{1,0:T(8,128)}, f32[128,256]{1,0:T(8,128)S(1)}, u32[]{:S(2)}, u32[]{:S(2)}) collective-permute-start(f32[128,256]{1,0:T(8,128)} %get-tuple-element.49), channel_id=1, source_target_pairs={{0,12},{4,8},{8,4},{12,0},{16,28},{20,24},{24,20},{28,16},{1,13},{... | collective-permute-start | bytes 393224 | tf_op jit(solution)/shard_map/ppermute | solution.py:458
  16.2 0.7 collective-permute-done.rest_0_
  17.0 2.4 %collective-permute-start.5 = (f32[128,256]{1,0:T(8,128)}, f32[128,256]{1,0:T(8,128)S(1)}, u32[]{:S(2)}, u32[]{:S(2)}) collective-permute-start(f32[128,256]{1,0:T(8,128)} %get-tuple-element.50), channel_id=1, source_target_pairs={{0,8},{4,12},{8,0},{12,4},{16,24},{20,28},{24,16},{28,20},{1,9},{5... | collective-permute-start | bytes 393224 | tf_op jit(solution)/shard_map/ppermute | solution.py:458
  19.4 0.9 %collective-permute-done.1.rest_1_ = f32[128,256]{1,0:T(8,128)S(1)} collective-permute-done((f32[128,256]{1,0:T(8,128)}, f32[128,256]{1,0:T(8,128)S(1)}, u32[]{:S(2)}, u32[]{:S(2)}) %collective-permute-start.1) | collective-permute-done | bytes 131104 | tf_op jit(solution)/shard_map/ppermute | solution.py:458
  20.3 0.0 collective-permute-start.6
  20.3 0.0 copy-start
  20.3 0.0 copy-start.1
  20.3 5.8 %output_maps.1.map_hbm = f32[64,256,256]{2,1,0:T(8,128)} custom-call(f32[8,256]{1,0:T(8,128)} %decay_hbm.3, f32[256,512]{1,0:T(8,128)} %q_hbm.1, f32[256,512]{1,0:T(8,128)} %k_hbm.3, f32[9,256,256]{2,1,0:T(8,128)} %get-tuple-element.53.factor_hbm), custom_call_target="tpu_custom_call" | custom-call | flops 1207959552 | bytes 5242880 | tf_op jit(solution)/shard_map/output_maps/pallas_call | solution.py:578
  26.1 0.0 collective-permute-done.2.rest_2_
  26.1 0.0 collective-permute-done.3.rest_3_
  26.1 0.0 collective-permute-done.4.rest_4_
  26.1 0.2 collective-permute-done.5.rest_5_
  26.3 0.0 collective-permute-done.6.rest_6_
  26.3 2.0 %state_scan.1 = (f32[128,128]{1,0:T(8,128)S(1)}, f32[128,128]{1,0:T(8,128)S(1)}, f32[128,128]{1,0:T(8,128)S(1)}, f32[128,128]{1,0:T(8,128)S(1)}, f32[128,128]{1,...) custom-call(f32[9,256,256]{2,1,0:T(8,128)} %get-tuple-element.53.factor_hbm, ...), custom_call_target="tpu_custom_call" | custom-call | tf_op jit(solution)/shard_map/state_scan/pallas_call | solution.py:479
  28.3 2.9 %collective-permute-start.7 = (f32[128,128]{1,0:T(8,128)S(1)}, f32[128,128]{1,0:T(8,128)S(1)}, u32[]{:S(2)}, u32[]{:S(2)}) collective-permute-start(f32[128,128]{1,0:T(8,128)S(1)} %get-tuple-element.71), channel_id=1, source_target_pairs={{0,28},{4,24},{8,20},{12,16},{16,12},{20,8},{24,4},{28,0},{1,29},{... | collective-permute-start | bytes 196616 | tf_op jit(solution)/shard_map/ppermute | solution.py:458
  31.2 0.0 collective-permute-start.8
  31.2 1.3 %collective-permute-start.9 = (f32[128,128]{1,0:T(8,128)S(1)}, f32[128,128]{1,0:T(8,128)S(1)}, u32[]{:S(2)}, u32[]{:S(2)}) collective-permute-start(f32[128,128]{1,0:T(8,128)S(1)} %get-tuple-element.73), channel_id=1, source_target_pairs={{0,20},{4,16},{8,28},{12,24},{16,4},{20,0},{24,12},{28,8},{1,21},{... | collective-permute-start | bytes 196616 | tf_op jit(solution)/shard_map/ppermute | solution.py:458
  32.6 0.7 collective-permute-start.10
  33.2 1.4 %collective-permute-start.11 = (f32[128,128]{1,0:T(8,128)S(1)}, f32[128,128]{1,0:T(8,128)S(1)}, u32[]{:S(2)}, u32[]{:S(2)}) collective-permute-start(f32[128,128]{1,0:T(8,128)S(1)} %get-tuple-element.75), channel_id=1, source_target_pairs={{0,12},{4,8},{8,4},{12,0},{16,28},{20,24},{24,20},{28,16},{1,13},{... | collective-permute-start | bytes 196616 | tf_op jit(solution)/shard_map/ppermute | solution.py:458
  34.6 0.0 collective-permute-done.7.rest_1_
  34.6 0.3 collective-permute-start.12
  34.9 1.5 %collective-permute-done.8.rest_2_ = f32[128,128]{1,0:T(8,128)S(1)} collective-permute-done((f32[128,128]{1,0:T(8,128)S(1)}, f32[128,128]{1,0:T(8,128)S(1)}, u32[]{:S(2)}, u32[]{:S(2)}) %collective-permute-start.8) | collective-permute-done | bytes 65568 | tf_op jit(solution)/shard_map/ppermute | solution.py:458
  36.4 0.0 collective-permute-start.13
  36.4 0.2 collective-permute-done.9.rest_3_
  36.6 1.8 %collective-permute-done.10.rest_4_ = f32[128,128]{1,0:T(8,128)S(1)} collective-permute-done((f32[128,128]{1,0:T(8,128)S(1)}, f32[128,128]{1,0:T(8,128)S(1)}, u32[]{:S(2)}, u32[]{:S(2)}) %collective-permute-start.10) | collective-permute-done | bytes 65568 | tf_op jit(solution)/shard_map/ppermute | solution.py:458
  38.4 0.0 collective-permute-done.11.rest_5_
  38.4 0.6 collective-permute-done.12.rest_6_
  39.0 0.0 collective-permute-done.13.rest_7_
  39.0 0.0 copy-done
  39.0 0.0 copy-done.1
  39.0 5.3 %projection.2 = (f32[64,2048]{1,0:T(8,128)S(1)}, bf16[2,1024,2048]{2,1,0:T(8,128)(2,1)S(1)}) custom-call(f32[64,256,256]{2,1,0:T(8,128)} %output_maps.1.map_hbm, f32[256,1024]{1,0:T(8,128)S(1)} %copy-done, f32[1,128]{1,0:T(1,128)S(1)} %bitcast.1, f32[1024,2048]{1,0:T(8,128)} %weight_ref, f32[128,128]{1,0:T(8,128)S(1)} %get-tuple-element.70.rest_0_, ...), custom_call_target="tpu_custom_call" | custom-call | flops 805306368 | bytes 8388608 | tf_op jit(solution)/shard_map/projection/pallas_call | solution.py:602
  44.3 3.5 %collective-permute-start.15 = (f32[64,2048]{1,0:T(8,128)S(1)}, f32[64,2048]{1,0:T(8,128)S(1)}, u32[]{:S(2)}, u32[]{:S(2)}) collective-permute-start(f32[64,2048]{1,0:T(8,128)S(1)} %get-tuple-element.80), channel_id=1, source_target_pairs={{0,1},{3,2},{4,5},{7,6},{8,9},{11,10},{12,13},{15,14},{16,17},{19,... | collective-permute-start | bytes 1572872 | tf_op jit(solution)/shard_map/ppermute | solution.py:524
  47.8 0.7 collective-permute-start.14
  48.5 6.2 %projection.3 = (f32[64,2048]{1,0:T(8,128)S(1)}, f32[64,2048]{1,0:T(8,128)S(1)}, f32[64,2048]{1,0:T(8,128)S(1)}) custom-call(f32[64,256,256]{2,1,0:T(8,128)} %output_maps.1.map_hbm, f32[256,1024]{1,0:T(8,128)S(1)} %copy-done, f32[1,128]{1,0:T(1,128)S(1)} %bitcast.2, bf16[2,1024,2048]{2,1,0:T(8,128)(2,1)S(1)} %get-tuple-element.78.weight_ref, ...), custom_call_target="tpu_custom_call" | custom-call | flops 2415919104 | bytes 8388608 | tf_op jit(solution)/shard_map/projection/pallas_call | solution.py:602
  54.7 4.4 %collective-permute-done.15.end_ref = f32[64,2048]{1,0:T(8,128)S(1)} collective-permute-done((f32[64,2048]{1,0:T(8,128)S(1)}, f32[64,2048]{1,0:T(8,128)S(1)}, u32[]{:S(2)}, u32[]{:S(2)}) %collective-permute-start.15) | collective-permute-done | bytes 524320 | tf_op jit(solution)/shard_map/ppermute | solution.py:524
  59.1 0.1 forward.1.__
  59.2 2.5 %collective-permute-start.16 = (f32[64,2048]{1,0:T(8,128)S(1)}, f32[64,2048]{1,0:T(8,128)S(1)}, u32[]{:S(2)}, u32[]{:S(2)}) collective-permute-start(f32[64,2048]{1,0:T(8,128)S(1)} %hand_on.1), channel_id=1, source_target_pairs={{0,1},{1,0},{2,3},{3,2},{4,5},{5,4},{6,7},{7,6},{8,9},{9,8},{10,11... | collective-permute-start | bytes 1572872 | tf_op jit(solution)/shard_map/ppermute | solution.py:543
  61.7 1.1 %collective-permute-start.17 = (f32[64,2048]{1,0:T(8,128)S(1)}, f32[64,2048]{1,0:T(8,128)S(1)}, u32[]{:S(2)}, u32[]{:S(2)}) collective-permute-start(f32[64,2048]{1,0:T(8,128)S(1)} %forward.1.__), channel_id=1, source_target_pairs={{0,2},{1,3},{2,0},{3,1},{4,6},{5,7},{6,4},{7,5},{8,10},{9,11},{10,... | collective-permute-start | bytes 1572872 | tf_op jit(solution)/shard_map/ppermute | solution.py:544
  62.8 0.0 collective-permute-done.14
  62.8 21.2 %collective-permute-done.16 = f32[64,2048]{1,0:T(8,128)S(1)} collective-permute-done((f32[64,2048]{1,0:T(8,128)S(1)}, f32[64,2048]{1,0:T(8,128)S(1)}, u32[]{:S(2)}, u32[]{:S(2)}) %collective-permute-start.16) | collective-permute-done | bytes 524320 | tf_op jit(solution)/shard_map/ppermute | solution.py:543
  84.1 2.5 %collective-permute-done.17 = f32[64,2048]{1,0:T(8,128)S(1)} collective-permute-done((f32[64,2048]{1,0:T(8,128)S(1)}, f32[64,2048]{1,0:T(8,128)S(1)}, u32[]{:S(2)}, u32[]{:S(2)}) %collective-permute-start.17) | collective-permute-done | bytes 524320 | tf_op jit(solution)/shard_map/ppermute | solution.py:544
  86.6 0.9 %add_add_fusion = f32[64,2048]{1,0:T(8,128)} fusion(f32[64,2048]{1,0:T(8,128)S(1)} %collective-permute-done.17, f32[64,2048]{1,0:T(8,128)S(1)} %collective-permute-done.16, f32[64,2048]{1,0:T(8,128)S(1)} %get-tuple-element.79, f32[64,2048]{1,0:T(8,128)S(1)} %collective-permute-done.14), kind=kLoop, calls=%fused_computation | loop fusion | flops 393216 | bytes 2621440 | tf_op jit(solution)/shard_map/add | solution.py:545
  (1 shorter events, 0.0 us)
Async XLA Ops:
  9.4 7.6 %collective-permute-start = (f32[128,256]{1,0:T(8,128)}, f32[128,256]{1,0:T(8,128)S(1)}, u32[]{:S(2)}, u32[]{:S(2)}) collective-permute-start(f32[128,256]{1,0:T(8,128)} %get-tuple-element.45), channel_id=1, source_target_pairs={{0,28},{4,24},{8,20},{12,16},{16,12},{20,8},{24,4},{28,0},{1,29},{... | collective-permute-start | bytes 393224 | tf_op jit(solution)/shard_map/ppermute | solution.py:458
  12.8 7.5 %collective-permute-start.1 = (f32[128,256]{1,0:T(8,128)}, f32[128,256]{1,0:T(8,128)S(1)}, u32[]{:S(2)}, u32[]{:S(2)}) collective-permute-start(f32[128,256]{1,0:T(8,128)} %get-tuple-element.46), channel_id=1, source_target_pairs={{0,24},{4,28},{8,16},{12,20},{16,8},{20,12},{24,0},{28,4},{1,25},{... | collective-permute-start | bytes 393224 | tf_op jit(solution)/shard_map/ppermute | solution.py:458
  13.4 12.7 %collective-permute-start.2 = (f32[128,256]{1,0:T(8,128)}, f32[128,256]{1,0:T(8,128)S(1)}, u32[]{:S(2)}, u32[]{:S(2)}) collective-permute-start(f32[128,256]{1,0:T(8,128)} %get-tuple-element.47), channel_id=1, source_target_pairs={{0,20},{4,16},{8,28},{12,24},{16,4},{20,0},{24,12},{28,8},{1,21},{... | collective-permute-start | bytes 393224 | tf_op jit(solution)/shard_map/ppermute | solution.py:458
  14.8 11.3 %collective-permute-start.3 = (f32[128,256]{1,0:T(8,128)}, f32[128,256]{1,0:T(8,128)S(1)}, u32[]{:S(2)}, u32[]{:S(2)}) collective-permute-start(f32[128,256]{1,0:T(8,128)} %get-tuple-element.48), channel_id=1, source_target_pairs={{0,16},{4,20},{8,24},{12,28},{16,0},{20,4},{24,8},{28,12},{1,17},{... | collective-permute-start | bytes 393224 | tf_op jit(solution)/shard_map/ppermute | solution.py:458
  15.1 11.0 %collective-permute-start.4 = (f32[128,256]{1,0:T(8,128)}, f32[128,256]{1,0:T(8,128)S(1)}, u32[]{:S(2)}, u32[]{:S(2)}) collective-permute-start(f32[128,256]{1,0:T(8,128)} %get-tuple-element.49), channel_id=1, source_target_pairs={{0,12},{4,8},{8,4},{12,0},{16,28},{20,24},{24,20},{28,16},{1,13},{... | collective-permute-start | bytes 393224 | tf_op jit(solution)/shard_map/ppermute | solution.py:458
  17.0 9.3 %collective-permute-start.5 = (f32[128,256]{1,0:T(8,128)}, f32[128,256]{1,0:T(8,128)S(1)}, u32[]{:S(2)}, u32[]{:S(2)}) collective-permute-start(f32[128,256]{1,0:T(8,128)} %get-tuple-element.50), channel_id=1, source_target_pairs={{0,8},{4,12},{8,0},{12,4},{16,24},{20,28},{24,16},{28,20},{1,9},{5... | collective-permute-start | bytes 393224 | tf_op jit(solution)/shard_map/ppermute | solution.py:458
  20.3 6.1 %collective-permute-start.6 = (f32[128,256]{1,0:T(8,128)}, f32[128,256]{1,0:T(8,128)S(1)}, u32[]{:S(2)}, u32[]{:S(2)}) collective-permute-start(f32[128,256]{1,0:T(8,128)} %get-tuple-element.51), channel_id=1, source_target_pairs={{0,4},{4,0},{8,12},{12,8},{16,20},{20,16},{24,28},{28,24},{1,5},{5... | collective-permute-start | bytes 393224 | tf_op jit(solution)/shard_map/ppermute | solution.py:458
  20.3 18.8 %copy-start = (f32[256,1024]{1,0:T(8,128)S(1)}, f32[256,1024]{1,0:T(8,128)}, u32[]{:S(2)}) copy-start(f32[256,1024]{1,0:T(8,128)} %gate_hbm.3) | copy-start | bytes 3145732
  20.3 18.8 %copy-start.1 = (f32[128]{0:T(128)S(1)}, f32[128]{0:T(128)}, u32[]{:S(2)}) copy-start(f32[128]{0:T(128)} %param.14) | copy-start | bytes 1540
  28.3 6.3 %collective-permute-start.7 = (f32[128,128]{1,0:T(8,128)S(1)}, f32[128,128]{1,0:T(8,128)S(1)}, u32[]{:S(2)}, u32[]{:S(2)}) collective-permute-start(f32[128,128]{1,0:T(8,128)S(1)} %get-tuple-element.71), channel_id=1, source_target_pairs={{0,28},{4,24},{8,20},{12,16},{16,12},{20,8},{24,4},{28,0},{1,29},{... | collective-permute-start | bytes 196616 | tf_op jit(solution)/shard_map/ppermute | solution.py:458
  31.2 5.2 %collective-permute-start.8 = (f32[128,128]{1,0:T(8,128)S(1)}, f32[128,128]{1,0:T(8,128)S(1)}, u32[]{:S(2)}, u32[]{:S(2)}) collective-permute-start(f32[128,128]{1,0:T(8,128)S(1)} %get-tuple-element.72), channel_id=1, source_target_pairs={{0,24},{4,28},{8,16},{12,20},{16,8},{20,12},{24,0},{28,4},{1,25},{... | collective-permute-start | bytes 196616 | tf_op jit(solution)/shard_map/ppermute | solution.py:458
  31.2 5.4 %collective-permute-start.9 = (f32[128,128]{1,0:T(8,128)S(1)}, f32[128,128]{1,0:T(8,128)S(1)}, u32[]{:S(2)}, u32[]{:S(2)}) collective-permute-start(f32[128,128]{1,0:T(8,128)S(1)} %get-tuple-element.73), channel_id=1, source_target_pairs={{0,20},{4,16},{8,28},{12,24},{16,4},{20,0},{24,12},{28,8},{1,21},{... | collective-permute-start | bytes 196616 | tf_op jit(solution)/shard_map/ppermute | solution.py:458
  32.6 5.9 %collective-permute-start.10 = (f32[128,128]{1,0:T(8,128)S(1)}, f32[128,128]{1,0:T(8,128)S(1)}, u32[]{:S(2)}, u32[]{:S(2)}) collective-permute-start(f32[128,128]{1,0:T(8,128)S(1)} %get-tuple-element.74), channel_id=1, source_target_pairs={{0,16},{4,20},{8,24},{12,28},{16,0},{20,4},{24,8},{28,12},{1,17},{... | collective-permute-start | bytes 196616 | tf_op jit(solution)/shard_map/ppermute | solution.py:458
  33.2 5.2 %collective-permute-start.11 = (f32[128,128]{1,0:T(8,128)S(1)}, f32[128,128]{1,0:T(8,128)S(1)}, u32[]{:S(2)}, u32[]{:S(2)}) collective-permute-start(f32[128,128]{1,0:T(8,128)S(1)} %get-tuple-element.75), channel_id=1, source_target_pairs={{0,12},{4,8},{8,4},{12,0},{16,28},{20,24},{24,20},{28,16},{1,13},{... | collective-permute-start | bytes 196616 | tf_op jit(solution)/shard_map/ppermute | solution.py:458
  34.6 4.4 %collective-permute-start.12 = (f32[128,128]{1,0:T(8,128)S(1)}, f32[128,128]{1,0:T(8,128)S(1)}, u32[]{:S(2)}, u32[]{:S(2)}) collective-permute-start(f32[128,128]{1,0:T(8,128)S(1)} %get-tuple-element.76), channel_id=1, source_target_pairs={{0,8},{4,12},{8,0},{12,4},{16,24},{20,28},{24,16},{28,20},{1,9},{5... | collective-permute-start | bytes 196616 | tf_op jit(solution)/shard_map/ppermute | solution.py:458
  36.4 2.6 %collective-permute-start.13 = (f32[128,128]{1,0:T(8,128)S(1)}, f32[128,128]{1,0:T(8,128)S(1)}, u32[]{:S(2)}, u32[]{:S(2)}) collective-permute-start(f32[128,128]{1,0:T(8,128)S(1)} %get-tuple-element.77), channel_id=1, source_target_pairs={{0,4},{4,0},{8,12},{12,8},{16,20},{20,16},{24,28},{28,24},{1,5},{5... | collective-permute-start | bytes 196616 | tf_op jit(solution)/shard_map/ppermute | solution.py:458
  44.3 14.8 %collective-permute-start.15 = (f32[64,2048]{1,0:T(8,128)S(1)}, f32[64,2048]{1,0:T(8,128)S(1)}, u32[]{:S(2)}, u32[]{:S(2)}) collective-permute-start(f32[64,2048]{1,0:T(8,128)S(1)} %get-tuple-element.80), channel_id=1, source_target_pairs={{0,1},{3,2},{4,5},{7,6},{8,9},{11,10},{12,13},{15,14},{16,17},{19,... | collective-permute-start | bytes 1572872 | tf_op jit(solution)/shard_map/ppermute | solution.py:524
  47.8 15.0 %collective-permute-start.14 = (f32[64,2048]{1,0:T(8,128)S(1)}, f32[64,2048]{1,0:T(8,128)S(1)}, u32[]{:S(2)}, u32[]{:S(2)}) collective-permute-start(f32[64,2048]{1,0:T(8,128)S(1)} %get-tuple-element.80), channel_id=1, source_target_pairs={{1,2},{2,1},{5,6},{6,5},{9,10},{10,9},{13,14},{14,13},{17,18},{18,... | collective-permute-start | bytes 1572872 | tf_op jit(solution)/shard_map/ppermute | solution.py:525
  59.2 24.9 %collective-permute-start.16 = (f32[64,2048]{1,0:T(8,128)S(1)}, f32[64,2048]{1,0:T(8,128)S(1)}, u32[]{:S(2)}, u32[]{:S(2)}) collective-permute-start(f32[64,2048]{1,0:T(8,128)S(1)} %hand_on.1), channel_id=1, source_target_pairs={{0,1},{1,0},{2,3},{3,2},{4,5},{5,4},{6,7},{7,6},{8,9},{9,8},{10,11... | collective-permute-start | bytes 1572872 | tf_op jit(solution)/shard_map/ppermute | solution.py:543
  61.7 24.9 %collective-permute-start.17 = (f32[64,2048]{1,0:T(8,128)S(1)}, f32[64,2048]{1,0:T(8,128)S(1)}, u32[]{:S(2)}, u32[]{:S(2)}) collective-permute-start(f32[64,2048]{1,0:T(8,128)S(1)} %forward.1.__), channel_id=1, source_target_pairs={{0,2},{1,3},{2,0},{3,1},{4,6},{5,7},{6,4},{7,5},{8,10},{9,11},{10,... | collective-permute-start | bytes 1572872 | tf_op jit(solution)/shard_map/ppermute | solution.py:544

commit v8 on v7

--- a/solution.py
+++ b/solution.py
@@ -13,9 +13,10 @@
 BLOCK = 128
 SMALL = 32
 BAND = 256
-SWAP_ORDER = (7, 6, 5, 4, 3, 2, 1)
+SWAP_ORDER = (1, 2, 7, 6, 5, 4, 3)
 WEIGHT_ROWS = 256
 MOST_VMEM = 56
+MAP_VMEM = 56
 SCAN_VMEM = 52.25
 FIRST_VMEM = 40
 LATER_VMEM = 32
@@ -68,6 +69,15 @@
     both = jnp.concatenate(left, axis=0)
     sums = jnp.dot(both, right[0], preferred_element_type=jnp.float32)
     rest = jnp.dot(left[0], right[1], preferred_element_type=jnp.float32)
+    return sums[:rows] + (sums[rows:] + rest)
+
+
+def dot_parts_transposed(left, right):
+    rows = left[0].shape[0]
+    dims = (((1,), (1,)), ((), ()))
+    both = jnp.concatenate(left, axis=0)
+    sums = lax.dot_general(both, right[0], dims, preferred_element_type=jnp.float32)
+    rest = lax.dot_general(left[0], right[1], dims, preferred_element_type=jnp.float32)
     return sums[:rows] + (sums[rows:] + rest)
 
 
@@ -299,13 +309,20 @@
     for key_head in range(key_heads):
         lanes = slice(key_head * DK, (key_head + 1) * DK)
         queries = unit(q_ref[:, lanes]) * DK**-0.5
-        keys = unit(k_ref[:, lanes])
+        keys = split(unit(k_ref[:, lanes]))
+        heads = range(key_head * repeat, (key_head + 1) * repeat)
+        parts = {}
         for p in range(blocks):
-            scores = [dot_transposed(queries[block(p)], keys[block(r)]) for r in range(p + 1)]
+            query_parts = split(queries[block(p)])
+            scores = [
+                dot_parts_transposed(query_parts, tuple(part[block(r)] for part in keys))
+                for r in range(p + 1)
+            ]
             if p == 0:
                 copies[3 + key_head].wait()
-            for head in range(key_head * repeat, (key_head + 1) * repeat):
+            for head in heads:
                 at = columns[block(p), head : head + 1]
+                parts[head, p] = split(factor_ref[head, block(p), :])
                 total = jnp.concatenate(
                     [queries[block(p)] * jnp.exp(at), jnp.zeros((BLOCK, DV), jnp.float32)], axis=1
                 )
@@ -315,7 +332,7 @@
                         damp = jnp.where(inclusive, jnp.exp(jnp.where(inclusive, spread, 0.0)), 0.0)
                     else:
                         damp = jnp.exp(spread)
-                    total = total + dot(scores[r] * damp, factor_ref[head, block(r), :])
+                    total = total + dot_parts(split(scores[r] * damp), parts[head, r])
                 map_ref[head, block(p), :] = total
         group = groups[key_head]
         leaving.append(
@@ -583,7 +600,7 @@
         scratch_shapes=[pltpu.VMEM(a.shape, jnp.float32) for a in (decays, queries, key_vectors)]
         + [pltpu.VMEM(factor_shape.shape, jnp.float32), pltpu.SemaphoreType.DMA((3 + key_heads,))]
         + [pltpu.VMEM(factor_shape.shape, jnp.float32), pltpu.SemaphoreType.DMA((key_heads,))],
-        compiler_params=params(MOST_VMEM),
+        compiler_params=params(MAP_VMEM),
         cost_estimate=cost(3 * 2 * heads * tokens * tokens * 384, factors, factors, queries),
         name="output_maps",
     )(decays, queries, key_vectors, factors)

time: 87.8 us -> 90.7 us (1.033)
  waiting for transfers between devices: 34.1 us -> 38.2 us
    ppermute x14, waiting for transfers between devices: 5.93 us -> 9.81 us  [partners_swap(): lax.ppermute(array, axis, [(d, d ^ i) for d in range(count)])]
    ppermute x14, starting transfers between devices: 15.9 us -> 14.7 us  [partners_swap(): lax.ppermute(array, axis, [(d, d ^ i) for d in range(count)])]
  transfers between devices with their start and end apart: 18 -> 18, of which waited for: 10 -> 9; matrix products, arithmetic and copies ran while one was open for 0% -> 0% of each run, Pallas kernels for 14% -> 13%
where the time goes in v8:
time: 90.7 us; the launch traced here: 90.5 us
  waiting for transfers between devices  38.2 us (42%)
  Pallas kernels  28.4 us (31%)
  starting transfers between devices  22.8 us (25%)
  other arithmetic  0.92 us (1%)
    ppermute x1, waiting for transfers between devices, project_and_sum(): from_near = lax.ppermute(near, axis, [(i, i ^ 1) for i in range(4)])  21.4 us
    ppermute x14, starting transfers between devices, partners_swap(): lax.ppermute(array, axis, [(d, d ^ i) for d in range(count)])  14.7 us
    pallas_call x2, Pallas kernels, project(): pl.pallas_call(functools.partial(projection_kernel, pieces=[(index, start...  11.4 us
    ppermute x14, waiting for transfers between devices, partners_swap(): lax.ppermute(array, axis, [(d, d ^ i) for d in range(count)])  9.81 us
    pallas_call x1, Pallas kernels, per_device(): pl.pallas_call(functools.partial(summary_kernel, swap=swap.heads), in_spe...  9.36 us
    pallas_call x1, Pallas kernels, per_device(): pl.pallas_call(output_kernel, in_specs=[HBM] * 4, out_specs=HBM, out_shap...  5.62 us
    ppermute x1, waiting for transfers between devices, project_and_sum(): from_end = lax.ppermute(opposite, axis, [(0, 1), (3, 2)])  4.53 us
    ppermute x1, starting transfers between devices, project_and_sum(): from_end = lax.ppermute(opposite, axis, [(0, 1), (3, 2)])  3.73 us
  transfers between devices with their start and end apart: 18, of which 9 were waited for; matrix products, arithmetic and copies ran while one was open for 0% of the time, Pallas kernels for 13%

profile of v8, /device:TPU:0, one launch (start us, length us, event | category | flops | bytes accessed | tf_op | source)
XLA Modules:
  0.0 90.5 jit_solution(6738790043025483556)
XLA Ops:
  0.0 9.4 %state_summary.1 = (f32[9,256,256]{2,1,0:T(8,128)}, f32[128,256]{1,0:T(8,128)}, f32[128,256]{1,0:T(8,128)}, f32[128,256]{1,0:T(8,128)}, f32[128,256]{1,0:T(8,128...) custom-call(f32[8,256]{1,0:T(8,128)} %decay_hbm.3, f32[8,256]{1,0:T(8,128)} %strength_hbm.1, ...), custom_call_target="tpu_custom_call" | custom-call | tf_op jit(solution)/shard_map/state_summary/pallas_call | solution.py:584
  9.4 0.5 collective-permute-start
  9.9 2.6 %collective-permute-start.1 = (f32[128,256]{1,0:T(8,128)}, f32[128,256]{1,0:T(8,128)S(1)}, u32[]{:S(2)}, u32[]{:S(2)}) collective-permute-start(f32[128,256]{1,0:T(8,128)} %get-tuple-element.46), channel_id=1, source_target_pairs={{0,8},{4,12},{8,0},{12,4},{16,24},{20,28},{24,16},{28,20},{1,9},{5... | collective-permute-start | bytes 393224 | tf_op jit(solution)/shard_map/ppermute | solution.py:475
  12.5 1.3 %collective-permute-start.2 = (f32[128,256]{1,0:T(8,128)}, f32[128,256]{1,0:T(8,128)S(1)}, u32[]{:S(2)}, u32[]{:S(2)}) collective-permute-start(f32[128,256]{1,0:T(8,128)} %get-tuple-element.47), channel_id=1, source_target_pairs={{0,28},{4,24},{8,20},{12,16},{16,12},{20,8},{24,4},{28,0},{1,29},{... | collective-permute-start | bytes 393224 | tf_op jit(solution)/shard_map/ppermute | solution.py:475
  13.7 1.4 %collective-permute-start.3 = (f32[128,256]{1,0:T(8,128)}, f32[128,256]{1,0:T(8,128)S(1)}, u32[]{:S(2)}, u32[]{:S(2)}) collective-permute-start(f32[128,256]{1,0:T(8,128)} %get-tuple-element.48), channel_id=1, source_target_pairs={{0,24},{4,28},{8,16},{12,20},{16,8},{20,12},{24,0},{28,4},{1,25},{... | collective-permute-start | bytes 393224 | tf_op jit(solution)/shard_map/ppermute | solution.py:475
  15.2 1.2 %collective-permute-start.4 = (f32[128,256]{1,0:T(8,128)}, f32[128,256]{1,0:T(8,128)S(1)}, u32[]{:S(2)}, u32[]{:S(2)}) collective-permute-start(f32[128,256]{1,0:T(8,128)} %get-tuple-element.49), channel_id=1, source_target_pairs={{0,20},{4,16},{8,28},{12,24},{16,4},{20,0},{24,12},{28,8},{1,21},{... | collective-permute-start | bytes 393224 | tf_op jit(solution)/shard_map/ppermute | solution.py:475
  16.3 0.0 collective-permute-done.rest_0_
  16.3 0.5 collective-permute-start.5
  16.9 0.0 collective-permute-done.1.rest_1_
  16.9 0.9 %collective-permute-start.6 = (f32[128,256]{1,0:T(8,128)}, f32[128,256]{1,0:T(8,128)S(1)}, u32[]{:S(2)}, u32[]{:S(2)}) collective-permute-start(f32[128,256]{1,0:T(8,128)} %get-tuple-element.51), channel_id=1, source_target_pairs={{0,12},{4,8},{8,4},{12,0},{16,28},{20,24},{24,20},{28,16},{1,13},{... | collective-permute-start | bytes 393224 | tf_op jit(solution)/shard_map/ppermute | solution.py:475
  17.8 0.0 copy-start
  17.8 0.0 copy-start.1
  17.8 5.6 %output_maps.1.map_hbm = f32[64,256,256]{2,1,0:T(8,128)} custom-call(f32[8,256]{1,0:T(8,128)} %decay_hbm.3, f32[256,512]{1,0:T(8,128)} %q_hbm.1, f32[256,512]{1,0:T(8,128)} %k_hbm.3, f32[9,256,256]{2,1,0:T(8,128)} %get-tuple-element.53.factor_hbm), custom_call_target="tpu_custom_call" | custom-call | flops 1207959552 | bytes 5242880 | tf_op jit(solution)/shard_map/output_maps/pallas_call | solution.py:595
  23.4 0.0 collective-permute-done.2.rest_2_
  23.4 0.7 collective-permute-done.3.rest_3_
  24.1 2.1 %collective-permute-done.4.rest_4_ = f32[128,256]{1,0:T(8,128)S(1)} collective-permute-done((f32[128,256]{1,0:T(8,128)}, f32[128,256]{1,0:T(8,128)S(1)}, u32[]{:S(2)}, u32[]{:S(2)}) %collective-permute-start.4) | collective-permute-done | bytes 131104 | tf_op jit(solution)/shard_map/ppermute | solution.py:475
  26.2 3.0 %collective-permute-done.5.rest_5_ = f32[128,256]{1,0:T(8,128)S(1)} collective-permute-done((f32[128,256]{1,0:T(8,128)}, f32[128,256]{1,0:T(8,128)S(1)}, u32[]{:S(2)}, u32[]{:S(2)}) %collective-permute-start.5) | collective-permute-done | bytes 131104 | tf_op jit(solution)/shard_map/ppermute | solution.py:475
  29.2 0.0 collective-permute-done.6.rest_6_
  29.2 2.0 %state_scan.1 = (f32[128,128]{1,0:T(8,128)S(1)}, f32[128,128]{1,0:T(8,128)S(1)}, f32[128,128]{1,0:T(8,128)S(1)}, f32[128,128]{1,0:T(8,128)S(1)}, f32[128,128]{1,...) custom-call(f32[9,256,256]{2,1,0:T(8,128)} %get-tuple-element.53.factor_hbm, ...), custom_call_target="tpu_custom_call" | custom-call | tf_op jit(solution)/shard_map/state_scan/pallas_call | solution.py:496
  31.2 0.1 collective-permute-start.7
  31.3 0.8 collective-permute-start.8
  32.0 0.8 collective-permute-start.9
  32.8 1.9 %collective-permute-start.10 = (f32[128,128]{1,0:T(8,128)S(1)}, f32[128,128]{1,0:T(8,128)S(1)}, u32[]{:S(2)}, u32[]{:S(2)}) collective-permute-start(f32[128,128]{1,0:T(8,128)S(1)} %get-tuple-element.74), channel_id=1, source_target_pairs={{0,24},{4,28},{8,16},{12,20},{16,8},{20,12},{24,0},{28,4},{1,25},{... | collective-permute-start | bytes 196616 | tf_op jit(solution)/shard_map/ppermute | solution.py:475
  34.7 1.0 %collective-permute-start.11 = (f32[128,128]{1,0:T(8,128)S(1)}, f32[128,128]{1,0:T(8,128)S(1)}, u32[]{:S(2)}, u32[]{:S(2)}) collective-permute-start(f32[128,128]{1,0:T(8,128)S(1)} %get-tuple-element.75), channel_id=1, source_target_pairs={{0,20},{4,16},{8,28},{12,24},{16,4},{20,0},{24,12},{28,8},{1,21},{... | collective-permute-start | bytes 196616 | tf_op jit(solution)/shard_map/ppermute | solution.py:475
  35.7 0.0 collective-permute-done.7.rest_1_
  35.7 0.7 collective-permute-start.12
  36.4 0.0 collective-permute-done.8.rest_2_
  36.4 1.1 %collective-permute-start.13 = (f32[128,128]{1,0:T(8,128)S(1)}, f32[128,128]{1,0:T(8,128)S(1)}, u32[]{:S(2)}, u32[]{:S(2)}) collective-permute-start(f32[128,128]{1,0:T(8,128)S(1)} %get-tuple-element.77), channel_id=1, source_target_pairs={{0,12},{4,8},{8,4},{12,0},{16,28},{20,24},{24,20},{28,16},{1,13},{... | collective-permute-start | bytes 196616 | tf_op jit(solution)/shard_map/ppermute | solution.py:475
  37.5 0.0 collective-permute-done.9.rest_3_
  37.5 1.3 %collective-permute-done.10.rest_4_ = f32[128,128]{1,0:T(8,128)S(1)} collective-permute-done((f32[128,128]{1,0:T(8,128)S(1)}, f32[128,128]{1,0:T(8,128)S(1)}, u32[]{:S(2)}, u32[]{:S(2)}) %collective-permute-start.10) | collective-permute-done | bytes 65568 | tf_op jit(solution)/shard_map/ppermute | solution.py:475
  38.9 1.3 %collective-permute-done.11.rest_5_ = f32[128,128]{1,0:T(8,128)S(1)} collective-permute-done((f32[128,128]{1,0:T(8,128)S(1)}, f32[128,128]{1,0:T(8,128)S(1)}, u32[]{:S(2)}, u32[]{:S(2)}) %collective-permute-start.11) | collective-permute-done | bytes 65568 | tf_op jit(solution)/shard_map/ppermute | solution.py:475
  40.1 1.4 %collective-permute-done.12.rest_6_ = f32[128,128]{1,0:T(8,128)S(1)} collective-permute-done((f32[128,128]{1,0:T(8,128)S(1)}, f32[128,128]{1,0:T(8,128)S(1)}, u32[]{:S(2)}, u32[]{:S(2)}) %collective-permute-start.12) | collective-permute-done | bytes 65568 | tf_op jit(solution)/shard_map/ppermute | solution.py:475
  41.6 0.0 collective-permute-done.13.rest_7_
  41.6 0.0 copy-done
  41.6 0.0 copy-done.1
  41.6 5.3 %projection.2 = (f32[64,2048]{1,0:T(8,128)S(1)}, bf16[2,1024,2048]{2,1,0:T(8,128)(2,1)S(1)}) custom-call(f32[64,256,256]{2,1,0:T(8,128)} %output_maps.1.map_hbm, f32[256,1024]{1,0:T(8,128)S(1)} %copy-done, f32[1,128]{1,0:T(1,128)S(1)} %bitcast.1, f32[1024,2048]{1,0:T(8,128)} %weight_ref, f32[128,128]{1,0:T(8,128)S(1)} %get-tuple-element.70.rest_0_, ...), custom_call_target="tpu_custom_call" | custom-call | flops 805306368 | bytes 8388608 | tf_op jit(solution)/shard_map/projection/pallas_call | solution.py:619
  46.8 3.7 %collective-permute-start.15 = (f32[64,2048]{1,0:T(8,128)S(1)}, f32[64,2048]{1,0:T(8,128)S(1)}, u32[]{:S(2)}, u32[]{:S(2)}) collective-permute-start(f32[64,2048]{1,0:T(8,128)S(1)} %get-tuple-element.80), channel_id=1, source_target_pairs={{0,1},{3,2},{4,5},{7,6},{8,9},{11,10},{12,13},{15,14},{16,17},{19,... | collective-permute-start | bytes 1572872 | tf_op jit(solution)/shard_map/ppermute | solution.py:541
  50.6 0.7 collective-permute-start.14
  51.3 6.2 %projection.3 = (f32[64,2048]{1,0:T(8,128)S(1)}, f32[64,2048]{1,0:T(8,128)S(1)}, f32[64,2048]{1,0:T(8,128)S(1)}) custom-call(f32[64,256,256]{2,1,0:T(8,128)} %output_maps.1.map_hbm, f32[256,1024]{1,0:T(8,128)S(1)} %copy-done, f32[1,128]{1,0:T(1,128)S(1)} %bitcast.2, bf16[2,1024,2048]{2,1,0:T(8,128)(2,1)S(1)} %get-tuple-element.78.weight_ref, ...), custom_call_target="tpu_custom_call" | custom-call | flops 2415919104 | bytes 8388608 | tf_op jit(solution)/shard_map/projection/pallas_call | solution.py:619
  57.4 4.5 %collective-permute-done.15.end_ref = f32[64,2048]{1,0:T(8,128)S(1)} collective-permute-done((f32[64,2048]{1,0:T(8,128)S(1)}, f32[64,2048]{1,0:T(8,128)S(1)}, u32[]{:S(2)}, u32[]{:S(2)}) %collective-permute-start.15) | collective-permute-done | bytes 524320 | tf_op jit(solution)/shard_map/ppermute | solution.py:541
  62.0 0.1 forward.1.__
  62.0 2.5 %collective-permute-start.16 = (f32[64,2048]{1,0:T(8,128)S(1)}, f32[64,2048]{1,0:T(8,128)S(1)}, u32[]{:S(2)}, u32[]{:S(2)}) collective-permute-start(f32[64,2048]{1,0:T(8,128)S(1)} %hand_on.1), channel_id=1, source_target_pairs={{0,1},{1,0},{2,3},{3,2},{4,5},{5,4},{6,7},{7,6},{8,9},{9,8},{10,11... | collective-permute-start | bytes 1572872 | tf_op jit(solution)/shard_map/ppermute | solution.py:560
  64.6 1.1 %collective-permute-start.17 = (f32[64,2048]{1,0:T(8,128)S(1)}, f32[64,2048]{1,0:T(8,128)S(1)}, u32[]{:S(2)}, u32[]{:S(2)}) collective-permute-start(f32[64,2048]{1,0:T(8,128)S(1)} %forward.1.__), channel_id=1, source_target_pairs={{0,2},{1,3},{2,0},{3,1},{4,6},{5,7},{6,4},{7,5},{8,10},{9,11},{10,... | collective-permute-start | bytes 1572872 | tf_op jit(solution)/shard_map/ppermute | solution.py:561
  65.7 0.0 collective-permute-done.14
  65.7 21.4 %collective-permute-done.16 = f32[64,2048]{1,0:T(8,128)S(1)} collective-permute-done((f32[64,2048]{1,0:T(8,128)S(1)}, f32[64,2048]{1,0:T(8,128)S(1)}, u32[]{:S(2)}, u32[]{:S(2)}) %collective-permute-start.16) | collective-permute-done | bytes 524320 | tf_op jit(solution)/shard_map/ppermute | solution.py:560
  87.1 2.5 %collective-permute-done.17 = f32[64,2048]{1,0:T(8,128)S(1)} collective-permute-done((f32[64,2048]{1,0:T(8,128)S(1)}, f32[64,2048]{1,0:T(8,128)S(1)}, u32[]{:S(2)}, u32[]{:S(2)}) %collective-permute-start.17) | collective-permute-done | bytes 524320 | tf_op jit(solution)/shard_map/ppermute | solution.py:561
  89.6 0.9 %add_add_fusion = f32[64,2048]{1,0:T(8,128)} fusion(f32[64,2048]{1,0:T(8,128)S(1)} %collective-permute-done.17, f32[64,2048]{1,0:T(8,128)S(1)} %collective-permute-done.16, f32[64,2048]{1,0:T(8,128)S(1)} %get-tuple-element.79, f32[64,2048]{1,0:T(8,128)S(1)} %collective-permute-done.14), kind=kLoop, calls=%fused_computation | loop fusion | flops 393216 | bytes 2621440 | tf_op jit(solution)/shard_map/add | solution.py:562
  (1 shorter events, 0.0 us)
Async XLA Ops:
  9.4 7.0 %collective-permute-start = (f32[128,256]{1,0:T(8,128)}, f32[128,256]{1,0:T(8,128)S(1)}, u32[]{:S(2)}, u32[]{:S(2)}) collective-permute-start(f32[128,256]{1,0:T(8,128)} %get-tuple-element.45), channel_id=1, source_target_pairs={{0,4},{4,0},{8,12},{12,8},{16,20},{20,16},{24,28},{28,24},{1,5},{5... | collective-permute-start | bytes 393224 | tf_op jit(solution)/shard_map/ppermute | solution.py:475
  9.9 7.0 %collective-permute-start.1 = (f32[128,256]{1,0:T(8,128)}, f32[128,256]{1,0:T(8,128)S(1)}, u32[]{:S(2)}, u32[]{:S(2)}) collective-permute-start(f32[128,256]{1,0:T(8,128)} %get-tuple-element.46), channel_id=1, source_target_pairs={{0,8},{4,12},{8,0},{12,4},{16,24},{20,28},{24,16},{28,20},{1,9},{5... | collective-permute-start | bytes 393224 | tf_op jit(solution)/shard_map/ppermute | solution.py:475
  12.5 11.0 %collective-permute-start.2 = (f32[128,256]{1,0:T(8,128)}, f32[128,256]{1,0:T(8,128)S(1)}, u32[]{:S(2)}, u32[]{:S(2)}) collective-permute-start(f32[128,256]{1,0:T(8,128)} %get-tuple-element.47), channel_id=1, source_target_pairs={{0,28},{4,24},{8,20},{12,16},{16,12},{20,8},{24,4},{28,0},{1,29},{... | collective-permute-start | bytes 393224 | tf_op jit(solution)/shard_map/ppermute | solution.py:475
  13.7 10.4 %collective-permute-start.3 = (f32[128,256]{1,0:T(8,128)}, f32[128,256]{1,0:T(8,128)S(1)}, u32[]{:S(2)}, u32[]{:S(2)}) collective-permute-start(f32[128,256]{1,0:T(8,128)} %get-tuple-element.48), channel_id=1, source_target_pairs={{0,24},{4,28},{8,16},{12,20},{16,8},{20,12},{24,0},{28,4},{1,25},{... | collective-permute-start | bytes 393224 | tf_op jit(solution)/shard_map/ppermute | solution.py:475
  15.2 11.1 %collective-permute-start.4 = (f32[128,256]{1,0:T(8,128)}, f32[128,256]{1,0:T(8,128)S(1)}, u32[]{:S(2)}, u32[]{:S(2)}) collective-permute-start(f32[128,256]{1,0:T(8,128)} %get-tuple-element.49), channel_id=1, source_target_pairs={{0,20},{4,16},{8,28},{12,24},{16,4},{20,0},{24,12},{28,8},{1,21},{... | collective-permute-start | bytes 393224 | tf_op jit(solution)/shard_map/ppermute | solution.py:475
  16.3 12.8 %collective-permute-start.5 = (f32[128,256]{1,0:T(8,128)}, f32[128,256]{1,0:T(8,128)S(1)}, u32[]{:S(2)}, u32[]{:S(2)}) collective-permute-start(f32[128,256]{1,0:T(8,128)} %get-tuple-element.50), channel_id=1, source_target_pairs={{0,16},{4,20},{8,24},{12,28},{16,0},{20,4},{24,8},{28,12},{1,17},{... | collective-permute-start | bytes 393224 | tf_op jit(solution)/shard_map/ppermute | solution.py:475
  16.9 12.3 %collective-permute-start.6 = (f32[128,256]{1,0:T(8,128)}, f32[128,256]{1,0:T(8,128)S(1)}, u32[]{:S(2)}, u32[]{:S(2)}) collective-permute-start(f32[128,256]{1,0:T(8,128)} %get-tuple-element.51), channel_id=1, source_target_pairs={{0,12},{4,8},{8,4},{12,0},{16,28},{20,24},{24,20},{28,16},{1,13},{... | collective-permute-start | bytes 393224 | tf_op jit(solution)/shard_map/ppermute | solution.py:475
  17.8 23.8 %copy-start = (f32[256,1024]{1,0:T(8,128)S(1)}, f32[256,1024]{1,0:T(8,128)}, u32[]{:S(2)}) copy-start(f32[256,1024]{1,0:T(8,128)} %gate_hbm.3) | copy-start | bytes 3145732
  17.8 23.8 %copy-start.1 = (f32[128]{0:T(128)S(1)}, f32[128]{0:T(128)}, u32[]{:S(2)}) copy-start(f32[128]{0:T(128)} %param.14) | copy-start | bytes 1540
  31.2 4.5 %collective-permute-start.7 = (f32[128,128]{1,0:T(8,128)S(1)}, f32[128,128]{1,0:T(8,128)S(1)}, u32[]{:S(2)}, u32[]{:S(2)}) collective-permute-start(f32[128,128]{1,0:T(8,128)S(1)} %get-tuple-element.71), channel_id=1, source_target_pairs={{0,4},{4,0},{8,12},{12,8},{16,20},{20,16},{24,28},{28,24},{1,5},{5... | collective-permute-start | bytes 196616 | tf_op jit(solution)/shard_map/ppermute | solution.py:475
  31.3 5.2 %collective-permute-start.8 = (f32[128,128]{1,0:T(8,128)S(1)}, f32[128,128]{1,0:T(8,128)S(1)}, u32[]{:S(2)}, u32[]{:S(2)}) collective-permute-start(f32[128,128]{1,0:T(8,128)S(1)} %get-tuple-element.72), channel_id=1, source_target_pairs={{0,8},{4,12},{8,0},{12,4},{16,24},{20,28},{24,16},{28,20},{1,9},{5... | collective-permute-start | bytes 196616 | tf_op jit(solution)/shard_map/ppermute | solution.py:475
  32.0 5.5 %collective-permute-start.9 = (f32[128,128]{1,0:T(8,128)S(1)}, f32[128,128]{1,0:T(8,128)S(1)}, u32[]{:S(2)}, u32[]{:S(2)}) collective-permute-start(f32[128,128]{1,0:T(8,128)S(1)} %get-tuple-element.73), channel_id=1, source_target_pairs={{0,28},{4,24},{8,20},{12,16},{16,12},{20,8},{24,4},{28,0},{1,29},{... | collective-permute-start | bytes 196616 | tf_op jit(solution)/shard_map/ppermute | solution.py:475
  32.8 6.0 %collective-permute-start.10 = (f32[128,128]{1,0:T(8,128)S(1)}, f32[128,128]{1,0:T(8,128)S(1)}, u32[]{:S(2)}, u32[]{:S(2)}) collective-permute-start(f32[128,128]{1,0:T(8,128)S(1)} %get-tuple-element.74), channel_id=1, source_target_pairs={{0,24},{4,28},{8,16},{12,20},{16,8},{20,12},{24,0},{28,4},{1,25},{... | collective-permute-start | bytes 196616 | tf_op jit(solution)/shard_map/ppermute | solution.py:475
  34.7 5.4 %collective-permute-start.11 = (f32[128,128]{1,0:T(8,128)S(1)}, f32[128,128]{1,0:T(8,128)S(1)}, u32[]{:S(2)}, u32[]{:S(2)}) collective-permute-start(f32[128,128]{1,0:T(8,128)S(1)} %get-tuple-element.75), channel_id=1, source_target_pairs={{0,20},{4,16},{8,28},{12,24},{16,4},{20,0},{24,12},{28,8},{1,21},{... | collective-permute-start | bytes 196616 | tf_op jit(solution)/shard_map/ppermute | solution.py:475
  35.7 5.8 %collective-permute-start.12 = (f32[128,128]{1,0:T(8,128)S(1)}, f32[128,128]{1,0:T(8,128)S(1)}, u32[]{:S(2)}, u32[]{:S(2)}) collective-permute-start(f32[128,128]{1,0:T(8,128)S(1)} %get-tuple-element.76), channel_id=1, source_target_pairs={{0,16},{4,20},{8,24},{12,28},{16,0},{20,4},{24,8},{28,12},{1,17},{... | collective-permute-start | bytes 196616 | tf_op jit(solution)/shard_map/ppermute | solution.py:475
  36.4 5.1 %collective-permute-start.13 = (f32[128,128]{1,0:T(8,128)S(1)}, f32[128,128]{1,0:T(8,128)S(1)}, u32[]{:S(2)}, u32[]{:S(2)}) collective-permute-start(f32[128,128]{1,0:T(8,128)S(1)} %get-tuple-element.77), channel_id=1, source_target_pairs={{0,12},{4,8},{8,4},{12,0},{16,28},{20,24},{24,20},{28,16},{1,13},{... | collective-permute-start | bytes 196616 | tf_op jit(solution)/shard_map/ppermute | solution.py:475
  46.8 15.1 %collective-permute-start.15 = (f32[64,2048]{1,0:T(8,128)S(1)}, f32[64,2048]{1,0:T(8,128)S(1)}, u32[]{:S(2)}, u32[]{:S(2)}) collective-permute-start(f32[64,2048]{1,0:T(8,128)S(1)} %get-tuple-element.80), channel_id=1, source_target_pairs={{0,1},{3,2},{4,5},{7,6},{8,9},{11,10},{12,13},{15,14},{16,17},{19,... | collective-permute-start | bytes 1572872 | tf_op jit(solution)/shard_map/ppermute | solution.py:541
  50.6 15.1 %collective-permute-start.14 = (f32[64,2048]{1,0:T(8,128)S(1)}, f32[64,2048]{1,0:T(8,128)S(1)}, u32[]{:S(2)}, u32[]{:S(2)}) collective-permute-start(f32[64,2048]{1,0:T(8,128)S(1)} %get-tuple-element.80), channel_id=1, source_target_pairs={{1,2},{2,1},{5,6},{6,5},{9,10},{10,9},{13,14},{14,13},{17,18},{18,... | collective-permute-start | bytes 1572872 | tf_op jit(solution)/shard_map/ppermute | solution.py:542
  62.0 25.0 %collective-permute-start.16 = (f32[64,2048]{1,0:T(8,128)S(1)}, f32[64,2048]{1,0:T(8,128)S(1)}, u32[]{:S(2)}, u32[]{:S(2)}) collective-permute-start(f32[64,2048]{1,0:T(8,128)S(1)} %hand_on.1), channel_id=1, source_target_pairs={{0,1},{1,0},{2,3},{3,2},{4,5},{5,4},{6,7},{7,6},{8,9},{9,8},{10,11... | collective-permute-start | bytes 1572872 | tf_op jit(solution)/shard_map/ppermute | solution.py:560
  64.6 25.0 %collective-permute-start.17 = (f32[64,2048]{1,0:T(8,128)S(1)}, f32[64,2048]{1,0:T(8,128)S(1)}, u32[]{:S(2)}, u32[]{:S(2)}) collective-permute-start(f32[64,2048]{1,0:T(8,128)S(1)} %forward.1.__), channel_id=1, source_target_pairs={{0,2},{1,3},{2,0},{3,1},{4,6},{5,7},{6,4},{7,5},{8,10},{9,11},{10,... | collective-permute-start | bytes 1572872 | tf_op jit(solution)/shard_map/ppermute | solution.py:561

commit v9 on v8

--- a/solution.py
+++ b/solution.py
@@ -13,7 +13,7 @@
 BLOCK = 128
 SMALL = 32
 BAND = 256
-SWAP_ORDER = (1, 2, 7, 6, 5, 4, 3)
+SWAP_ORDER = (7, 6, 5, 4, 3, 2, 1)
 WEIGHT_ROWS = 256
 MOST_VMEM = 56
 MAP_VMEM = 56
@@ -190,17 +190,18 @@
     copies = fetch(
         [(decay_hbm, decay_ref), (strength_hbm, strength_ref), (k_hbm, k_ref), (v_hbm, v_ref)], sems
     )
-    for copy in copies[:3]:
-        copy.wait()
     tokens = k_ref.shape[0]
     key_heads = k_ref.shape[1] // DK
     value_heads = v_ref.shape[1] // DV
     repeat = value_heads // key_heads
     blocks = tokens // BLOCK
+    for copy in copies[:2]:
+        copy.wait()
     rows, columns = cumulative_logs(decay_ref[...])
     strengths = strength_ref[...].T
     strict = iota((BLOCK, BLOCK), 0) > iota((BLOCK, BLOCK), 1)
     eye = jnp.where(iota((BLOCK, DK + DV), 0) == iota((BLOCK, DK + DV), 1), 1.0, 0.0)
+    copies[2].wait()
     leaving = []
     for first in range(0, value_heads, HEADS_AT_ONCE):
         heads = range(first, min(first + HEADS_AT_ONCE, value_heads))
@@ -297,14 +298,15 @@
         sems,
     )
     leaving = []
-    for copy in copies[:3]:
-        copy.wait()
     tokens = q_ref.shape[0]
     key_heads = q_ref.shape[1] // DK
     value_heads = factor_ref.shape[0]
     repeat = value_heads // key_heads
     blocks = tokens // BLOCK
+    copies[0].wait()
     rows, columns = cumulative_logs(decay_ref[...])
+    for copy in copies[1:3]:
+        copy.wait()
     inclusive = iota((BLOCK, BLOCK), 0) >= iota((BLOCK, BLOCK), 1)
     for key_head in range(key_heads):
         lanes = slice(key_head * DK, (key_head + 1) * DK)
@@ -367,13 +369,12 @@
     for i, summary in enumerate(held):
         held_ref[partner(i + 1, True)] = summary[...]
     own.wait()
-    state = jnp.zeros(entry_ref.shape[1:], jnp.float32)
-    entry_ref[0] = state
-    for source in range(count - 1):
-        added = held_ref[source, :, DK:]
-        if source:
-            added = added + dot(held_ref[source, :, :DK], state)
-        state = added
+    maps = [split(held_ref[source, :, :DK]) for source in range(1, count - 1)]
+    state = held_ref[0, :, DK:]
+    entry_ref[0] = jnp.zeros_like(state)
+    entry_ref[1] = state
+    for source in range(1, count - 1):
+        state = held_ref[source, :, DK:] + dot_parts(maps[source - 1], split(state))
         entry_ref[source + 1] = state
     for i, entry in enumerate(entries):
         entry[...] = entry_ref[partner(i, True)]

time: 90.7 us -> 87.6 us (0.966)
  waiting for transfers between devices: 38.2 us -> 34.6 us
    ppermute x14, waiting for transfers between devices: 9.81 us -> 6.3 us  [partners_swap(): lax.ppermute(array, axis, [(d, d ^ i) for d in range(count)])]
  transfers between devices with their start and end apart: 18 -> 18, of which waited for: 9 -> 10; matrix products, arithmetic and copies ran while one was open for 0% -> 0% of each run, Pallas kernels for 13% -> 13%
where the time goes in v9:
time: 87.6 us; the launch traced here: 87.4 us
  waiting for transfers between devices  34.6 us (39%)
  Pallas kernels  28.4 us (32%)
  starting transfers between devices  23.3 us (27%)
  other arithmetic  0.92 us (1%)
    ppermute x1, waiting for transfers between devices, project_and_sum(): from_near = lax.ppermute(near, axis, [(i, i ^ 1) for i in range(4)])  21.3 us
    ppermute x14, starting transfers between devices, partners_swap(): lax.ppermute(array, axis, [(d, d ^ i) for d in range(count)])  15.5 us
    pallas_call x2, Pallas kernels, project(): pl.pallas_call(functools.partial(projection_kernel, pieces=[(index, start...  11.4 us
    pallas_call x1, Pallas kernels, per_device(): pl.pallas_call(functools.partial(summary_kernel, swap=swap.heads), in_spe...  9.5 us
    ppermute x14, waiting for transfers between devices, partners_swap(): lax.ppermute(array, axis, [(d, d ^ i) for d in range(count)])  6.3 us
    pallas_call x1, Pallas kernels, per_device(): pl.pallas_call(output_kernel, in_specs=[HBM] * 4, out_specs=HBM, out_shap...  5.44 us
    ppermute x1, waiting for transfers between devices, project_and_sum(): from_end = lax.ppermute(opposite, axis, [(0, 1), (3, 2)])  4.45 us
    ppermute x1, starting transfers between devices, project_and_sum(): from_end = lax.ppermute(opposite, axis, [(0, 1), (3, 2)])  3.51 us
  transfers between devices with their start and end apart: 18, of which 10 were waited for; matrix products, arithmetic and copies ran while one was open for 0% of the time, Pallas kernels for 13%

profile of v9, /device:TPU:0, one launch (start us, length us, event | category | flops | bytes accessed | tf_op | source)
XLA Modules:
  0.0 87.4 jit_solution(6805851347560807136)
XLA Ops:
  0.0 9.5 %state_summary.1 = (f32[9,256,256]{2,1,0:T(8,128)}, f32[128,256]{1,0:T(8,128)}, f32[128,256]{1,0:T(8,128)}, f32[128,256]{1,0:T(8,128)}, f32[128,256]{1,0:T(8,128...) custom-call(f32[8,256]{1,0:T(8,128)} %decay_hbm.3, f32[8,256]{1,0:T(8,128)} %strength_hbm.1, ...), custom_call_target="tpu_custom_call" | custom-call | tf_op jit(solution)/shard_map/state_summary/pallas_call | solution.py:585
  9.5 3.4 %collective-permute-start = (f32[128,256]{1,0:T(8,128)}, f32[128,256]{1,0:T(8,128)S(1)}, u32[]{:S(2)}, u32[]{:S(2)}) collective-permute-start(f32[128,256]{1,0:T(8,128)} %get-tuple-element.45), channel_id=1, source_target_pairs={{0,28},{4,24},{8,20},{12,16},{16,12},{20,8},{24,4},{28,0},{1,29},{... | collective-permute-start | bytes 393224 | tf_op jit(solution)/shard_map/ppermute | solution.py:476
  12.9 0.6 collective-permute-start.1
  13.5 1.4 %collective-permute-start.2 = (f32[128,256]{1,0:T(8,128)}, f32[128,256]{1,0:T(8,128)S(1)}, u32[]{:S(2)}, u32[]{:S(2)}) collective-permute-start(f32[128,256]{1,0:T(8,128)} %get-tuple-element.47), channel_id=1, source_target_pairs={{0,20},{4,16},{8,28},{12,24},{16,4},{20,0},{24,12},{28,8},{1,21},{... | collective-permute-start | bytes 393224 | tf_op jit(solution)/shard_map/ppermute | solution.py:476
  14.9 0.3 collective-permute-start.3
  15.2 1.1 %collective-permute-start.4 = (f32[128,256]{1,0:T(8,128)}, f32[128,256]{1,0:T(8,128)S(1)}, u32[]{:S(2)}, u32[]{:S(2)}) collective-permute-start(f32[128,256]{1,0:T(8,128)} %get-tuple-element.49), channel_id=1, source_target_pairs={{0,12},{4,8},{8,4},{12,0},{16,28},{20,24},{24,20},{28,16},{1,13},{... | collective-permute-start | bytes 393224 | tf_op jit(solution)/shard_map/ppermute | solution.py:476
  16.3 0.8 collective-permute-done.rest_0_
  17.1 2.4 %collective-permute-start.5 = (f32[128,256]{1,0:T(8,128)}, f32[128,256]{1,0:T(8,128)S(1)}, u32[]{:S(2)}, u32[]{:S(2)}) collective-permute-start(f32[128,256]{1,0:T(8,128)} %get-tuple-element.50), channel_id=1, source_target_pairs={{0,8},{4,12},{8,0},{12,4},{16,24},{20,28},{24,16},{28,20},{1,9},{5... | collective-permute-start | bytes 393224 | tf_op jit(solution)/shard_map/ppermute | solution.py:476
  19.5 0.9 %collective-permute-done.1.rest_1_ = f32[128,256]{1,0:T(8,128)S(1)} collective-permute-done((f32[128,256]{1,0:T(8,128)}, f32[128,256]{1,0:T(8,128)S(1)}, u32[]{:S(2)}, u32[]{:S(2)}) %collective-permute-start.1) | collective-permute-done | bytes 131104 | tf_op jit(solution)/shard_map/ppermute | solution.py:476
  20.4 0.0 collective-permute-start.6
  20.4 0.0 copy-start
  20.4 0.0 copy-start.1
  20.4 5.4 %output_maps.1.map_hbm = f32[64,256,256]{2,1,0:T(8,128)} custom-call(f32[8,256]{1,0:T(8,128)} %decay_hbm.3, f32[256,512]{1,0:T(8,128)} %q_hbm.1, f32[256,512]{1,0:T(8,128)} %k_hbm.3, f32[9,256,256]{2,1,0:T(8,128)} %get-tuple-element.53.factor_hbm), custom_call_target="tpu_custom_call" | custom-call | flops 1207959552 | bytes 5242880 | tf_op jit(solution)/shard_map/output_maps/pallas_call | solution.py:596
  25.8 0.0 collective-permute-done.2.rest_2_
  25.9 0.0 collective-permute-done.3.rest_3_
  25.9 0.0 collective-permute-done.4.rest_4_
  25.9 0.6 collective-permute-done.5.rest_5_
  26.5 0.0 collective-permute-done.6.rest_6_
  26.5 2.0 %state_scan.1 = (f32[128,128]{1,0:T(8,128)S(1)}, f32[128,128]{1,0:T(8,128)S(1)}, f32[128,128]{1,0:T(8,128)S(1)}, f32[128,128]{1,0:T(8,128)S(1)}, f32[128,128]{1,...) custom-call(f32[9,256,256]{2,1,0:T(8,128)} %get-tuple-element.53.factor_hbm, ...), custom_call_target="tpu_custom_call" | custom-call | tf_op jit(solution)/shard_map/state_scan/pallas_call | solution.py:497
  28.5 2.5 %collective-permute-start.7 = (f32[128,128]{1,0:T(8,128)S(1)}, f32[128,128]{1,0:T(8,128)S(1)}, u32[]{:S(2)}, u32[]{:S(2)}) collective-permute-start(f32[128,128]{1,0:T(8,128)S(1)} %get-tuple-element.71), channel_id=1, source_target_pairs={{0,28},{4,24},{8,20},{12,16},{16,12},{20,8},{24,4},{28,0},{1,29},{... | collective-permute-start | bytes 196616 | tf_op jit(solution)/shard_map/ppermute | solution.py:476
  31.0 0.2 collective-permute-start.8
  31.1 1.2 %collective-permute-start.9 = (f32[128,128]{1,0:T(8,128)S(1)}, f32[128,128]{1,0:T(8,128)S(1)}, u32[]{:S(2)}, u32[]{:S(2)}) collective-permute-start(f32[128,128]{1,0:T(8,128)S(1)} %get-tuple-element.73), channel_id=1, source_target_pairs={{0,20},{4,16},{8,28},{12,24},{16,4},{20,0},{24,12},{28,8},{1,21},{... | collective-permute-start | bytes 196616 | tf_op jit(solution)/shard_map/ppermute | solution.py:476
  32.3 0.7 collective-permute-start.10
  33.0 1.4 %collective-permute-start.11 = (f32[128,128]{1,0:T(8,128)S(1)}, f32[128,128]{1,0:T(8,128)S(1)}, u32[]{:S(2)}, u32[]{:S(2)}) collective-permute-start(f32[128,128]{1,0:T(8,128)S(1)} %get-tuple-element.75), channel_id=1, source_target_pairs={{0,12},{4,8},{8,4},{12,0},{16,28},{20,24},{24,20},{28,16},{1,13},{... | collective-permute-start | bytes 196616 | tf_op jit(solution)/shard_map/ppermute | solution.py:476
  34.4 0.0 collective-permute-done.7.rest_1_
  34.4 0.3 collective-permute-start.12
  34.7 1.5 %collective-permute-done.8.rest_2_ = f32[128,128]{1,0:T(8,128)S(1)} collective-permute-done((f32[128,128]{1,0:T(8,128)S(1)}, f32[128,128]{1,0:T(8,128)S(1)}, u32[]{:S(2)}, u32[]{:S(2)}) %collective-permute-start.8) | collective-permute-done | bytes 65568 | tf_op jit(solution)/shard_map/ppermute | solution.py:476
  36.2 0.0 collective-permute-start.13
  36.2 0.5 collective-permute-done.9.rest_3_
  36.7 1.7 %collective-permute-done.10.rest_4_ = f32[128,128]{1,0:T(8,128)S(1)} collective-permute-done((f32[128,128]{1,0:T(8,128)S(1)}, f32[128,128]{1,0:T(8,128)S(1)}, u32[]{:S(2)}, u32[]{:S(2)}) %collective-permute-start.10) | collective-permute-done | bytes 65568 | tf_op jit(solution)/shard_map/ppermute | solution.py:476
  38.3 0.0 collective-permute-done.11.rest_5_
  38.4 0.4 collective-permute-done.12.rest_6_
  38.8 0.0 collective-permute-done.13.rest_7_
  38.8 0.0 copy-done
  38.8 0.0 copy-done.1
  38.8 5.3 %projection.2 = (f32[64,2048]{1,0:T(8,128)S(1)}, bf16[2,1024,2048]{2,1,0:T(8,128)(2,1)S(1)}) custom-call(f32[64,256,256]{2,1,0:T(8,128)} %output_maps.1.map_hbm, f32[256,1024]{1,0:T(8,128)S(1)} %copy-done, f32[1,128]{1,0:T(1,128)S(1)} %bitcast.1, f32[1024,2048]{1,0:T(8,128)} %weight_ref, f32[128,128]{1,0:T(8,128)S(1)} %get-tuple-element.70.rest_0_, ...), custom_call_target="tpu_custom_call" | custom-call | flops 805306368 | bytes 8388608 | tf_op jit(solution)/shard_map/projection/pallas_call | solution.py:620
  44.1 3.5 %collective-permute-start.15 = (f32[64,2048]{1,0:T(8,128)S(1)}, f32[64,2048]{1,0:T(8,128)S(1)}, u32[]{:S(2)}, u32[]{:S(2)}) collective-permute-start(f32[64,2048]{1,0:T(8,128)S(1)} %get-tuple-element.80), channel_id=1, source_target_pairs={{0,1},{3,2},{4,5},{7,6},{8,9},{11,10},{12,13},{15,14},{16,17},{19,... | collective-permute-start | bytes 1572872 | tf_op jit(solution)/shard_map/ppermute | solution.py:542
  47.6 0.7 collective-permute-start.14
  48.3 6.2 %projection.3 = (f32[64,2048]{1,0:T(8,128)S(1)}, f32[64,2048]{1,0:T(8,128)S(1)}, f32[64,2048]{1,0:T(8,128)S(1)}) custom-call(f32[64,256,256]{2,1,0:T(8,128)} %output_maps.1.map_hbm, f32[256,1024]{1,0:T(8,128)S(1)} %copy-done, f32[1,128]{1,0:T(1,128)S(1)} %bitcast.2, bf16[2,1024,2048]{2,1,0:T(8,128)(2,1)S(1)} %get-tuple-element.78.weight_ref, ...), custom_call_target="tpu_custom_call" | custom-call | flops 2415919104 | bytes 8388608 | tf_op jit(solution)/shard_map/projection/pallas_call | solution.py:620
  54.5 4.5 %collective-permute-done.15.end_ref = f32[64,2048]{1,0:T(8,128)S(1)} collective-permute-done((f32[64,2048]{1,0:T(8,128)S(1)}, f32[64,2048]{1,0:T(8,128)S(1)}, u32[]{:S(2)}, u32[]{:S(2)}) %collective-permute-start.15) | collective-permute-done | bytes 524320 | tf_op jit(solution)/shard_map/ppermute | solution.py:542
  58.9 0.1 forward.1.__
  59.0 2.5 %collective-permute-start.16 = (f32[64,2048]{1,0:T(8,128)S(1)}, f32[64,2048]{1,0:T(8,128)S(1)}, u32[]{:S(2)}, u32[]{:S(2)}) collective-permute-start(f32[64,2048]{1,0:T(8,128)S(1)} %hand_on.1), channel_id=1, source_target_pairs={{0,1},{1,0},{2,3},{3,2},{4,5},{5,4},{6,7},{7,6},{8,9},{9,8},{10,11... | collective-permute-start | bytes 1572872 | tf_op jit(solution)/shard_map/ppermute | solution.py:561
  61.5 1.1 %collective-permute-start.17 = (f32[64,2048]{1,0:T(8,128)S(1)}, f32[64,2048]{1,0:T(8,128)S(1)}, u32[]{:S(2)}, u32[]{:S(2)}) collective-permute-start(f32[64,2048]{1,0:T(8,128)S(1)} %forward.1.__), channel_id=1, source_target_pairs={{0,2},{1,3},{2,0},{3,1},{4,6},{5,7},{6,4},{7,5},{8,10},{9,11},{10,... | collective-permute-start | bytes 1572872 | tf_op jit(solution)/shard_map/ppermute | solution.py:562
  62.6 0.0 collective-permute-done.14
  62.6 21.3 %collective-permute-done.16 = f32[64,2048]{1,0:T(8,128)S(1)} collective-permute-done((f32[64,2048]{1,0:T(8,128)S(1)}, f32[64,2048]{1,0:T(8,128)S(1)}, u32[]{:S(2)}, u32[]{:S(2)}) %collective-permute-start.16) | collective-permute-done | bytes 524320 | tf_op jit(solution)/shard_map/ppermute | solution.py:561
  83.9 2.6 %collective-permute-done.17 = f32[64,2048]{1,0:T(8,128)S(1)} collective-permute-done((f32[64,2048]{1,0:T(8,128)S(1)}, f32[64,2048]{1,0:T(8,128)S(1)}, u32[]{:S(2)}, u32[]{:S(2)}) %collective-permute-start.17) | collective-permute-done | bytes 524320 | tf_op jit(solution)/shard_map/ppermute | solution.py:562
  86.4 0.9 %add_add_fusion = f32[64,2048]{1,0:T(8,128)} fusion(f32[64,2048]{1,0:T(8,128)S(1)} %collective-permute-done.17, f32[64,2048]{1,0:T(8,128)S(1)} %collective-permute-done.16, f32[64,2048]{1,0:T(8,128)S(1)} %get-tuple-element.79, f32[64,2048]{1,0:T(8,128)S(1)} %collective-permute-done.14), kind=kLoop, calls=%fused_computation | loop fusion | flops 393216 | bytes 2621440 | tf_op jit(solution)/shard_map/add | solution.py:563
  (1 shorter events, 0.0 us)
Async XLA Ops:
  9.5 7.6 %collective-permute-start = (f32[128,256]{1,0:T(8,128)}, f32[128,256]{1,0:T(8,128)S(1)}, u32[]{:S(2)}, u32[]{:S(2)}) collective-permute-start(f32[128,256]{1,0:T(8,128)} %get-tuple-element.45), channel_id=1, source_target_pairs={{0,28},{4,24},{8,20},{12,16},{16,12},{20,8},{24,4},{28,0},{1,29},{... | collective-permute-start | bytes 393224 | tf_op jit(solution)/shard_map/ppermute | solution.py:476
  12.9 7.5 %collective-permute-start.1 = (f32[128,256]{1,0:T(8,128)}, f32[128,256]{1,0:T(8,128)S(1)}, u32[]{:S(2)}, u32[]{:S(2)}) collective-permute-start(f32[128,256]{1,0:T(8,128)} %get-tuple-element.46), channel_id=1, source_target_pairs={{0,24},{4,28},{8,16},{12,20},{16,8},{20,12},{24,0},{28,4},{1,25},{... | collective-permute-start | bytes 393224 | tf_op jit(solution)/shard_map/ppermute | solution.py:476
  13.5 12.3 %collective-permute-start.2 = (f32[128,256]{1,0:T(8,128)}, f32[128,256]{1,0:T(8,128)S(1)}, u32[]{:S(2)}, u32[]{:S(2)}) collective-permute-start(f32[128,256]{1,0:T(8,128)} %get-tuple-element.47), channel_id=1, source_target_pairs={{0,20},{4,16},{8,28},{12,24},{16,4},{20,0},{24,12},{28,8},{1,21},{... | collective-permute-start | bytes 393224 | tf_op jit(solution)/shard_map/ppermute | solution.py:476
  14.9 10.9 %collective-permute-start.3 = (f32[128,256]{1,0:T(8,128)}, f32[128,256]{1,0:T(8,128)S(1)}, u32[]{:S(2)}, u32[]{:S(2)}) collective-permute-start(f32[128,256]{1,0:T(8,128)} %get-tuple-element.48), channel_id=1, source_target_pairs={{0,16},{4,20},{8,24},{12,28},{16,0},{20,4},{24,8},{28,12},{1,17},{... | collective-permute-start | bytes 393224 | tf_op jit(solution)/shard_map/ppermute | solution.py:476
  15.2 10.6 %collective-permute-start.4 = (f32[128,256]{1,0:T(8,128)}, f32[128,256]{1,0:T(8,128)S(1)}, u32[]{:S(2)}, u32[]{:S(2)}) collective-permute-start(f32[128,256]{1,0:T(8,128)} %get-tuple-element.49), channel_id=1, source_target_pairs={{0,12},{4,8},{8,4},{12,0},{16,28},{20,24},{24,20},{28,16},{1,13},{... | collective-permute-start | bytes 393224 | tf_op jit(solution)/shard_map/ppermute | solution.py:476
  17.1 9.3 %collective-permute-start.5 = (f32[128,256]{1,0:T(8,128)}, f32[128,256]{1,0:T(8,128)S(1)}, u32[]{:S(2)}, u32[]{:S(2)}) collective-permute-start(f32[128,256]{1,0:T(8,128)} %get-tuple-element.50), channel_id=1, source_target_pairs={{0,8},{4,12},{8,0},{12,4},{16,24},{20,28},{24,16},{28,20},{1,9},{5... | collective-permute-start | bytes 393224 | tf_op jit(solution)/shard_map/ppermute | solution.py:476
  20.4 6.1 %collective-permute-start.6 = (f32[128,256]{1,0:T(8,128)}, f32[128,256]{1,0:T(8,128)S(1)}, u32[]{:S(2)}, u32[]{:S(2)}) collective-permute-start(f32[128,256]{1,0:T(8,128)} %get-tuple-element.51), channel_id=1, source_target_pairs={{0,4},{4,0},{8,12},{12,8},{16,20},{20,16},{24,28},{28,24},{1,5},{5... | collective-permute-start | bytes 393224 | tf_op jit(solution)/shard_map/ppermute | solution.py:476
  20.4 18.4 %copy-start = (f32[256,1024]{1,0:T(8,128)S(1)}, f32[256,1024]{1,0:T(8,128)}, u32[]{:S(2)}) copy-start(f32[256,1024]{1,0:T(8,128)} %gate_hbm.3) | copy-start | bytes 3145732
  20.4 18.4 %copy-start.1 = (f32[128]{0:T(128)S(1)}, f32[128]{0:T(128)}, u32[]{:S(2)}) copy-start(f32[128]{0:T(128)} %param.14) | copy-start | bytes 1540
  28.5 6.0 %collective-permute-start.7 = (f32[128,128]{1,0:T(8,128)S(1)}, f32[128,128]{1,0:T(8,128)S(1)}, u32[]{:S(2)}, u32[]{:S(2)}) collective-permute-start(f32[128,128]{1,0:T(8,128)S(1)} %get-tuple-element.71), channel_id=1, source_target_pairs={{0,28},{4,24},{8,20},{12,16},{16,12},{20,8},{24,4},{28,0},{1,29},{... | collective-permute-start | bytes 196616 | tf_op jit(solution)/shard_map/ppermute | solution.py:476
  31.0 5.2 %collective-permute-start.8 = (f32[128,128]{1,0:T(8,128)S(1)}, f32[128,128]{1,0:T(8,128)S(1)}, u32[]{:S(2)}, u32[]{:S(2)}) collective-permute-start(f32[128,128]{1,0:T(8,128)S(1)} %get-tuple-element.72), channel_id=1, source_target_pairs={{0,24},{4,28},{8,16},{12,20},{16,8},{20,12},{24,0},{28,4},{1,25},{... | collective-permute-start | bytes 196616 | tf_op jit(solution)/shard_map/ppermute | solution.py:476
  31.1 5.5 %collective-permute-start.9 = (f32[128,128]{1,0:T(8,128)S(1)}, f32[128,128]{1,0:T(8,128)S(1)}, u32[]{:S(2)}, u32[]{:S(2)}) collective-permute-start(f32[128,128]{1,0:T(8,128)S(1)} %get-tuple-element.73), channel_id=1, source_target_pairs={{0,20},{4,16},{8,28},{12,24},{16,4},{20,0},{24,12},{28,8},{1,21},{... | collective-permute-start | bytes 196616 | tf_op jit(solution)/shard_map/ppermute | solution.py:476
  32.3 6.0 %collective-permute-start.10 = (f32[128,128]{1,0:T(8,128)S(1)}, f32[128,128]{1,0:T(8,128)S(1)}, u32[]{:S(2)}, u32[]{:S(2)}) collective-permute-start(f32[128,128]{1,0:T(8,128)S(1)} %get-tuple-element.74), channel_id=1, source_target_pairs={{0,16},{4,20},{8,24},{12,28},{16,0},{20,4},{24,8},{28,12},{1,17},{... | collective-permute-start | bytes 196616 | tf_op jit(solution)/shard_map/ppermute | solution.py:476
  33.0 5.3 %collective-permute-start.11 = (f32[128,128]{1,0:T(8,128)S(1)}, f32[128,128]{1,0:T(8,128)S(1)}, u32[]{:S(2)}, u32[]{:S(2)}) collective-permute-start(f32[128,128]{1,0:T(8,128)S(1)} %get-tuple-element.75), channel_id=1, source_target_pairs={{0,12},{4,8},{8,4},{12,0},{16,28},{20,24},{24,20},{28,16},{1,13},{... | collective-permute-start | bytes 196616 | tf_op jit(solution)/shard_map/ppermute | solution.py:476
  34.4 4.4 %collective-permute-start.12 = (f32[128,128]{1,0:T(8,128)S(1)}, f32[128,128]{1,0:T(8,128)S(1)}, u32[]{:S(2)}, u32[]{:S(2)}) collective-permute-start(f32[128,128]{1,0:T(8,128)S(1)} %get-tuple-element.76), channel_id=1, source_target_pairs={{0,8},{4,12},{8,0},{12,4},{16,24},{20,28},{24,16},{28,20},{1,9},{5... | collective-permute-start | bytes 196616 | tf_op jit(solution)/shard_map/ppermute | solution.py:476
  36.2 2.6 %collective-permute-start.13 = (f32[128,128]{1,0:T(8,128)S(1)}, f32[128,128]{1,0:T(8,128)S(1)}, u32[]{:S(2)}, u32[]{:S(2)}) collective-permute-start(f32[128,128]{1,0:T(8,128)S(1)} %get-tuple-element.77), channel_id=1, source_target_pairs={{0,4},{4,0},{8,12},{12,8},{16,20},{20,16},{24,28},{28,24},{1,5},{5... | collective-permute-start | bytes 196616 | tf_op jit(solution)/shard_map/ppermute | solution.py:476
  44.1 14.8 %collective-permute-start.15 = (f32[64,2048]{1,0:T(8,128)S(1)}, f32[64,2048]{1,0:T(8,128)S(1)}, u32[]{:S(2)}, u32[]{:S(2)}) collective-permute-start(f32[64,2048]{1,0:T(8,128)S(1)} %get-tuple-element.80), channel_id=1, source_target_pairs={{0,1},{3,2},{4,5},{7,6},{8,9},{11,10},{12,13},{15,14},{16,17},{19,... | collective-permute-start | bytes 1572872 | tf_op jit(solution)/shard_map/ppermute | solution.py:542
  47.6 15.0 %collective-permute-start.14 = (f32[64,2048]{1,0:T(8,128)S(1)}, f32[64,2048]{1,0:T(8,128)S(1)}, u32[]{:S(2)}, u32[]{:S(2)}) collective-permute-start(f32[64,2048]{1,0:T(8,128)S(1)} %get-tuple-element.80), channel_id=1, source_target_pairs={{1,2},{2,1},{5,6},{6,5},{9,10},{10,9},{13,14},{14,13},{17,18},{18,... | collective-permute-start | bytes 1572872 | tf_op jit(solution)/shard_map/ppermute | solution.py:543
  59.0 24.9 %collective-permute-start.16 = (f32[64,2048]{1,0:T(8,128)S(1)}, f32[64,2048]{1,0:T(8,128)S(1)}, u32[]{:S(2)}, u32[]{:S(2)}) collective-permute-start(f32[64,2048]{1,0:T(8,128)S(1)} %hand_on.1), channel_id=1, source_target_pairs={{0,1},{1,0},{2,3},{3,2},{4,5},{5,4},{6,7},{7,6},{8,9},{9,8},{10,11... | collective-permute-start | bytes 1572872 | tf_op jit(solution)/shard_map/ppermute | solution.py:561
  61.5 24.9 %collective-permute-start.17 = (f32[64,2048]{1,0:T(8,128)S(1)}, f32[64,2048]{1,0:T(8,128)S(1)}, u32[]{:S(2)}, u32[]{:S(2)}) collective-permute-start(f32[64,2048]{1,0:T(8,128)S(1)} %forward.1.__), channel_id=1, source_target_pairs={{0,2},{1,3},{2,0},{3,1},{4,6},{5,7},{6,4},{7,5},{8,10},{9,11},{10,... | collective-permute-start | bytes 1572872 | tf_op jit(solution)/shard_map/ppermute | solution.py:562

commit v10 on v9

--- a/solution.py
+++ b/solution.py
@@ -16,11 +16,11 @@
 SWAP_ORDER = (7, 6, 5, 4, 3, 2, 1)
 WEIGHT_ROWS = 256
 MOST_VMEM = 56
-MAP_VMEM = 56
+MAP_VMEM = 53.75
 SCAN_VMEM = 52.25
 FIRST_VMEM = 40
 LATER_VMEM = 32
-HEADS_AT_ONCE = 8
+HEADS_AT_ONCE = 4
 EPS = 1e-06
 
 
@@ -186,7 +186,8 @@
 
 
 def summary_kernel(decay_hbm, strength_hbm, k_hbm, v_hbm, factor_hbm, *rest, swap):
-    *summaries, decay_ref, strength_ref, k_ref, v_ref, sems, factor_ref, summary_ref, out_sems = rest
+    *summaries, decay_ref, strength_ref, k_ref, v_ref, sems = rest[:-4]
+    factor_ref, summary_ref, log_ref, out_sems = rest[-4:]
     copies = fetch(
         [(decay_hbm, decay_ref), (strength_hbm, strength_ref), (k_hbm, k_ref), (v_hbm, v_ref)], sems
     )
@@ -201,8 +202,11 @@
     strengths = strength_ref[...].T
     strict = iota((BLOCK, BLOCK), 0) > iota((BLOCK, BLOCK), 1)
     eye = jnp.where(iota((BLOCK, DK + DV), 0) == iota((BLOCK, DK + DV), 1), 1.0, 0.0)
+    log_ref[:value_heads] = rows
+    target = factor_hbm.at[value_heads, pl.ds(DK, log_ref.shape[0])]
+    leaving = [pltpu.make_async_copy(log_ref, target, out_sems.at[0])]
+    leaving[0].start()
     copies[2].wait()
-    leaving = []
     for first in range(0, value_heads, HEADS_AT_ONCE):
         heads = range(first, min(first + HEADS_AT_ONCE, value_heads))
         keys = {}
@@ -277,12 +281,12 @@
 
 
 def output_kernel(
-    decay_hbm,
     q_hbm,
     k_hbm,
     factor_hbm,
     map_hbm,
-    decay_ref,
+    own_ref,
+    log_ref,
     q_ref,
     k_ref,
     factor_ref,
@@ -293,20 +297,22 @@
     repeat = factor_ref.shape[0] // (k_hbm.shape[1] // DK)
     groups = [pl.ds(head, repeat) for head in range(0, factor_ref.shape[0], repeat)]
     copies = fetch(
-        [(decay_hbm, decay_ref), (q_hbm, q_ref), (k_hbm, k_ref)]
-        + [(factor_hbm.at[group], factor_ref.at[group]) for group in groups],
+        [(factor_hbm.at[factor_ref.shape[0], pl.ds(DK, log_ref.shape[0])], log_ref)]
+        + [(q_hbm, q_ref), (k_hbm, k_ref)]
+        + [(factor_hbm.at[group], factor_ref.at[group]) for group in groups]
+        + [(factor_hbm.at[factor_ref.shape[0], pl.ds(0, DK)], own_ref)],
         sems,
     )
-    leaving = []
+    leaving = [copies.pop()]
     tokens = q_ref.shape[0]
     key_heads = q_ref.shape[1] // DK
     value_heads = factor_ref.shape[0]
     repeat = value_heads // key_heads
     blocks = tokens // BLOCK
-    copies[0].wait()
-    rows, columns = cumulative_logs(decay_ref[...])
-    for copy in copies[1:3]:
+    for copy in copies[:3]:
         copy.wait()
+    rows = log_ref[:value_heads]
+    columns = log_ref[...].T
     inclusive = iota((BLOCK, BLOCK), 0) >= iota((BLOCK, BLOCK), 1)
     for key_head in range(key_heads):
         lanes = slice(key_head * DK, (key_head + 1) * DK)
@@ -358,17 +364,12 @@
             entry_ref[source + 1, head] = state
 
 
-def ordered_scan_kernel(factor_hbm, *rest):
-    *arrays, held_ref, entry_ref, sems = rest
+def ordered_scan_kernel(*rest):
+    *arrays, held_ref, entry_ref = rest
     count = entry_ref.shape[0]
-    held, entries = arrays[: count - 1], arrays[count - 1 :]
-    here = partner(0, True)
-    own_summary = factor_hbm.at[factor_hbm.shape[0] - 1, pl.ds(0, DK)]
-    own = pltpu.make_async_copy(own_summary, held_ref.at[here], sems.at[0])
-    own.start()
+    held, entries = arrays[:count], arrays[count:]
     for i, summary in enumerate(held):
-        held_ref[partner(i + 1, True)] = summary[...]
-    own.wait()
+        held_ref[partner(i, True)] = summary[...]
     maps = [split(held_ref[source, :, :DK]) for source in range(1, count - 1)]
     state = held_ref[0, :, DK:]
     entry_ref[0] = jnp.zeros_like(state)
@@ -487,22 +488,21 @@
     return heads == count == 1 + len(SWAP_ORDER)
 
 
-def entering_states(factors, summaries, swap, beside, after):
-    heads = factors.shape[0] - 1
+def entering_states(own, summaries, swap, beside, after):
+    heads = len(summaries) + swap
     count = lax.axis_size("ctx")
     if swap:
-        held = partners_swap([factors, *summaries], "ctx")
+        held = partners_swap([own, *summaries], "ctx")
         held, beside = lax.optimization_barrier((held, beside))
         entry = shape(DK, DV)
         entries = pl.pallas_call(
             ordered_scan_kernel,
-            in_specs=[HBM] + [VMEM] * (count - 1),
+            in_specs=[VMEM] * count,
             out_specs=[VMEM] * count,
             out_shape=[entry] * count,
             scratch_shapes=[
                 pltpu.VMEM((count, DK, DK + DV), jnp.float32),
                 pltpu.VMEM((count, DK, DV), jnp.float32),
-                pltpu.SemaphoreType.DMA((1,)),
             ],
             compiler_params=params(SCAN_VMEM),
             name="state_scan",
@@ -582,6 +582,7 @@
     factor_shape = shape(heads, tokens, DK + DV)
     groups = pl.cdiv(heads, HEADS_AT_ONCE)
     sent = heads - 1 if swap.heads else heads
+    log_shape = shape(8 * pl.cdiv(heads, 8), tokens)
     factors, *summaries = pl.pallas_call(
         functools.partial(summary_kernel, swap=swap.heads),
         in_specs=[HBM] * 4,
@@ -589,23 +590,23 @@
         out_shape=[shape(heads + 1, tokens, DK + DV)] + [shape(DK, DK + DV)] * sent,
         scratch_shapes=buffers(decays, strengths, key_vectors, values)
         + [pltpu.VMEM(factor_shape.shape, jnp.float32), pltpu.VMEM((heads, DK, DK + DV), jnp.float32)]
-        + [pltpu.SemaphoreType.DMA((groups + 1,))],
+        + [pltpu.VMEM(log_shape.shape, jnp.float32), pltpu.SemaphoreType.DMA((groups + 2,))],
         compiler_params=params(MOST_VMEM),
         name="state_summary",
     )(decays, strengths, key_vectors, values)
-    maps = pl.pallas_call(
+    maps, own = pl.pallas_call(
         output_kernel,
-        in_specs=[HBM] * 4,
-        out_specs=HBM,
-        out_shape=shape(8 * heads, tokens, DK + DV),
-        scratch_shapes=[pltpu.VMEM(a.shape, jnp.float32) for a in (decays, queries, key_vectors)]
-        + [pltpu.VMEM(factor_shape.shape, jnp.float32), pltpu.SemaphoreType.DMA((3 + key_heads,))]
+        in_specs=[HBM] * 3,
+        out_specs=[HBM, VMEM],
+        out_shape=[shape(8 * heads, tokens, DK + DV), shape(DK, DK + DV)],
+        scratch_shapes=[pltpu.VMEM(a.shape, jnp.float32) for a in (log_shape, queries, key_vectors)]
+        + [pltpu.VMEM(factor_shape.shape, jnp.float32), pltpu.SemaphoreType.DMA((4 + key_heads,))]
         + [pltpu.VMEM(factor_shape.shape, jnp.float32), pltpu.SemaphoreType.DMA((key_heads,))],
         compiler_params=params(MAP_VMEM),
         cost_estimate=cost(3 * 2 * heads * tokens * tokens * 384, factors, factors, queries),
         name="output_maps",
-    )(decays, queries, key_vectors, factors)
-    states, maps, weights = entering_states(factors, summaries, swap.heads, maps, out_weight)
+    )(queries, key_vectors, factors)
+    states, maps, weights = entering_states(own, summaries, swap.heads, maps, out_weight)
     parts_shape = jax.ShapeDtypeStruct((2, depth, columns), jnp.bfloat16)
 
     fetched = [

time: 87.6 us -> 88.5 us (1.010)
  local copies, waits for them, and re-layouts: 0.01 us -> 1.88 us
    unnamed x4, local copies, waits for them, and re-layouts: 0.01 us -> 1.88 us
    pallas_call x2, Pallas kernels: 7.43 us -> 6.45 us  [the longest x1 5.31 us: per_device(): pl.pallas_call(output_kernel, in_specs=[HBM] * 3, out_specs=[HBM, VMEM],...]
where the time goes in v10:
time: 88.5 us; the launch traced here: 88.2 us
  waiting for transfers between devices  34.1 us (39%)
  Pallas kernels  27.6 us (31%)
  starting transfers between devices  23.5 us (27%)
  local copies, waits for them, and re-layouts  1.88 us (2%)
  other arithmetic  0.92 us (1%)
    ppermute x1, waiting for transfers between devices, project_and_sum(): from_near = lax.ppermute(near, axis, [(i, i ^ 1) for i in range(4)])  21.1 us
    ppermute x14, starting transfers between devices, partners_swap(): lax.ppermute(array, axis, [(d, d ^ i) for d in range(count)])  15.7 us
    pallas_call x2, Pallas kernels, project(): pl.pallas_call(functools.partial(projection_kernel, pieces=[(index, start...  11.2 us
    pallas_call x1, Pallas kernels, per_device(): pl.pallas_call(functools.partial(summary_kernel, swap=swap.heads), in_spe...  9.92 us
    ppermute x14, waiting for transfers between devices, partners_swap(): lax.ppermute(array, axis, [(d, d ^ i) for d in range(count)])  6.16 us
    pallas_call x1, Pallas kernels, per_device(): pl.pallas_call(output_kernel, in_specs=[HBM] * 3, out_specs=[HBM, VMEM],...  5.31 us
    ppermute x1, waiting for transfers between devices, project_and_sum(): from_end = lax.ppermute(opposite, axis, [(0, 1), (3, 2)])  4.3 us
    ppermute x1, starting transfers between devices, project_and_sum(): from_end = lax.ppermute(opposite, axis, [(0, 1), (3, 2)])  3.5 us
  transfers between devices with their start and end apart: 18, of which 10 were waited for; matrix products, arithmetic and copies ran while one was open for 0% of the time, Pallas kernels for 13%

profile of v10, /device:TPU:0, one launch (start us, length us, event | category | flops | bytes accessed | tf_op | source)
XLA Modules:
  0.0 88.2 jit_solution(11302920380995499704)
XLA Ops:
  0.0 9.9 %state_summary.1 = (f32[9,256,256]{2,1,0:T(8,128)}, f32[128,256]{1,0:T(8,128)}, f32[128,256]{1,0:T(8,128)}, f32[128,256]{1,0:T(8,128)}, f32[128,256]{1,0:T(8,128...) custom-call(f32[8,256]{1,0:T(8,128)} %decay_hbm.1, f32[8,256]{1,0:T(8,128)} %strength_hbm.1, ...), custom_call_target="tpu_custom_call" | custom-call | tf_op jit(solution)/shard_map/state_summary/pallas_call | solution.py:586
  9.9 3.4 %collective-permute-start = (f32[128,256]{1,0:T(8,128)}, f32[128,256]{1,0:T(8,128)S(1)}, u32[]{:S(2)}, u32[]{:S(2)}) collective-permute-start(f32[128,256]{1,0:T(8,128)} %get-tuple-element.48), channel_id=1, source_target_pairs={{0,28},{4,24},{8,20},{12,16},{16,12},{20,8},{24,4},{28,0},{1,29},{... | collective-permute-start | bytes 393224 | tf_op jit(solution)/shard_map/ppermute | solution.py:477
  13.3 0.6 collective-permute-start.1
  14.0 1.4 %collective-permute-start.2 = (f32[128,256]{1,0:T(8,128)}, f32[128,256]{1,0:T(8,128)S(1)}, u32[]{:S(2)}, u32[]{:S(2)}) collective-permute-start(f32[128,256]{1,0:T(8,128)} %get-tuple-element.50), channel_id=1, source_target_pairs={{0,20},{4,16},{8,28},{12,24},{16,4},{20,0},{24,12},{28,8},{1,21},{... | collective-permute-start | bytes 393224 | tf_op jit(solution)/shard_map/ppermute | solution.py:477
  15.3 0.3 collective-permute-start.3
  15.6 1.1 %collective-permute-start.4 = (f32[128,256]{1,0:T(8,128)}, f32[128,256]{1,0:T(8,128)S(1)}, u32[]{:S(2)}, u32[]{:S(2)}) collective-permute-start(f32[128,256]{1,0:T(8,128)} %get-tuple-element.52), channel_id=1, source_target_pairs={{0,12},{4,8},{8,4},{12,0},{16,28},{20,24},{24,20},{28,16},{1,13},{... | collective-permute-start | bytes 393224 | tf_op jit(solution)/shard_map/ppermute | solution.py:477
  16.8 0.8 collective-permute-done.rest_1_
  17.5 2.4 %collective-permute-start.5 = (f32[128,256]{1,0:T(8,128)}, f32[128,256]{1,0:T(8,128)S(1)}, u32[]{:S(2)}, u32[]{:S(2)}) collective-permute-start(f32[128,256]{1,0:T(8,128)} %get-tuple-element.53), channel_id=1, source_target_pairs={{0,8},{4,12},{8,0},{12,4},{16,24},{20,28},{24,16},{28,20},{1,9},{5... | collective-permute-start | bytes 393224 | tf_op jit(solution)/shard_map/ppermute | solution.py:477
  19.9 0.9 collective-permute-done.1.rest_2_
  20.8 0.0 collective-permute-start.6
  20.8 5.3 %output_maps.1 = (f32[64,256,256]{2,1,0:T(8,128)}, f32[128,256]{1,0:T(8,128)S(1)}) custom-call(f32[256,512]{1,0:T(8,128)} %q_hbm.1, f32[256,512]{1,0:T(8,128)} %k_hbm.3, f32[9,256,256]{2,1,0:T(8,128)} %get-tuple-element.46.factor_hbm), custom_call_target="tpu_custom_call" | custom-call | flops 1207959552 | bytes 5242880 | tf_op jit(solution)/shard_map/output_maps/pallas_call | solution.py:597
  26.1 0.0 collective-permute-done.2.rest_3_
  26.1 0.0 collective-permute-done.3.rest_4_
  26.2 0.0 collective-permute-done.4.rest_5_
  26.2 0.7 collective-permute-done.5.rest_6_
  26.9 0.0 collective-permute-done.6.rest_7_
  26.9 1.1 %state_scan.1 = (f32[128,128]{1,0:T(8,128)S(1)}, f32[128,128]{1,0:T(8,128)S(1)}, f32[128,128]{1,0:T(8,128)S(1)}, f32[128,128]{1,0:T(8,128)S(1)}, f32[128,128]{1,...) custom-call(f32[128,256]{1,0:T(8,128)S(1)} %get-tuple-element.57.rest_0_, ...), custom_call_target="tpu_custom_call" | custom-call | tf_op jit(solution)/shard_map/state_scan/pallas_call | solution.py:498
  28.0 2.4 %collective-permute-start.7 = (f32[128,128]{1,0:T(8,128)S(1)}, f32[128,128]{1,0:T(8,128)S(1)}, u32[]{:S(2)}, u32[]{:S(2)}) collective-permute-start(f32[128,128]{1,0:T(8,128)S(1)} %get-tuple-element.75), channel_id=1, source_target_pairs={{0,28},{4,24},{8,20},{12,16},{16,12},{20,8},{24,4},{28,0},{1,29},{... | collective-permute-start | bytes 196616 | tf_op jit(solution)/shard_map/ppermute | solution.py:477
  30.4 0.3 collective-permute-start.8
  30.7 1.2 %collective-permute-start.9 = (f32[128,128]{1,0:T(8,128)S(1)}, f32[128,128]{1,0:T(8,128)S(1)}, u32[]{:S(2)}, u32[]{:S(2)}) collective-permute-start(f32[128,128]{1,0:T(8,128)S(1)} %get-tuple-element.77), channel_id=1, source_target_pairs={{0,20},{4,16},{8,28},{12,24},{16,4},{20,0},{24,12},{28,8},{1,21},{... | collective-permute-start | bytes 196616 | tf_op jit(solution)/shard_map/ppermute | solution.py:477
  31.9 0.6 collective-permute-start.10
  32.5 1.3 %collective-permute-start.11 = (f32[128,128]{1,0:T(8,128)S(1)}, f32[128,128]{1,0:T(8,128)S(1)}, u32[]{:S(2)}, u32[]{:S(2)}) collective-permute-start(f32[128,128]{1,0:T(8,128)S(1)} %get-tuple-element.79), channel_id=1, source_target_pairs={{0,12},{4,8},{8,4},{12,0},{16,28},{20,24},{24,20},{28,16},{1,13},{... | collective-permute-start | bytes 196616 | tf_op jit(solution)/shard_map/ppermute | solution.py:477
  33.9 0.0 collective-permute-done.7.rest_1_
  33.9 0.7 collective-permute-start.12
  34.5 1.1 %collective-permute-done.8.rest_2_ = f32[128,128]{1,0:T(8,128)S(1)} collective-permute-done((f32[128,128]{1,0:T(8,128)S(1)}, f32[128,128]{1,0:T(8,128)S(1)}, u32[]{:S(2)}, u32[]{:S(2)}) %collective-permute-start.8) | collective-permute-done | bytes 65568 | tf_op jit(solution)/shard_map/ppermute | solution.py:477
  35.6 0.0 collective-permute-start.13
  35.6 0.5 collective-permute-done.9.rest_3_
  36.2 1.7 %collective-permute-done.10.rest_4_ = f32[128,128]{1,0:T(8,128)S(1)} collective-permute-done((f32[128,128]{1,0:T(8,128)S(1)}, f32[128,128]{1,0:T(8,128)S(1)}, u32[]{:S(2)}, u32[]{:S(2)}) %collective-permute-start.10) | collective-permute-done | bytes 65568 | tf_op jit(solution)/shard_map/ppermute | solution.py:477
  37.9 0.0 collective-permute-done.11.rest_5_
  37.9 0.4 collective-permute-done.12.rest_6_
  38.3 0.0 collective-permute-done.13.rest_7_
  38.3 0.0 copy-start
  38.3 1.2 %copy-done = f32[256,1024]{1,0:T(8,128)S(1)} copy-done((f32[256,1024]{1,0:T(8,128)S(1)}, f32[256,1024]{1,0:T(8,128)}, u32[]{:S(2)}) %copy-start) | copy-done | bytes 1048600
  39.5 0.0 copy-start.1
  39.5 0.7 copy-done.1
  40.2 5.1 %projection.2 = (f32[64,2048]{1,0:T(8,128)S(1)}, bf16[2,1024,2048]{2,1,0:T(8,128)(2,1)S(1)}) custom-call(f32[64,256,256]{2,1,0:T(8,128)} %get-tuple-element.56.map_hbm, f32[256,1024]{1,0:T(8,128)S(1)} %copy-done, f32[1,128]{1,0:T(1,128)S(1)} %bitcast.1, f32[1024,2048]{1,0:T(8,128)} %weight_ref, f32[128,128]{1,0:T(8,128)S(1)} %get-tuple-element.74.rest_0_, ...), custom_call_target="tpu_custom_call" | custom-call | flops 805306368 | bytes 8388608 | tf_op jit(solution)/shard_map/projection/pallas_call | solution.py:621
  45.3 3.5 %collective-permute-start.15 = (f32[64,2048]{1,0:T(8,128)S(1)}, f32[64,2048]{1,0:T(8,128)S(1)}, u32[]{:S(2)}, u32[]{:S(2)}) collective-permute-start(f32[64,2048]{1,0:T(8,128)S(1)} %get-tuple-element.84), channel_id=1, source_target_pairs={{0,1},{3,2},{4,5},{7,6},{8,9},{11,10},{12,13},{15,14},{16,17},{19,... | collective-permute-start | bytes 1572872 | tf_op jit(solution)/shard_map/ppermute | solution.py:542
  48.8 0.7 collective-permute-start.14
  49.5 6.2 %projection.3 = (f32[64,2048]{1,0:T(8,128)S(1)}, f32[64,2048]{1,0:T(8,128)S(1)}, f32[64,2048]{1,0:T(8,128)S(1)}) custom-call(f32[64,256,256]{2,1,0:T(8,128)} %get-tuple-element.56.map_hbm, f32[256,1024]{1,0:T(8,128)S(1)} %copy-done, f32[1,128]{1,0:T(1,128)S(1)} %bitcast.2, bf16[2,1024,2048]{2,1,0:T(8,128)(2,1)S(1)} %get-tuple-element.82.weight_ref, ...), custom_call_target="tpu_custom_call" | custom-call | flops 2415919104 | bytes 8388608 | tf_op jit(solution)/shard_map/projection/pallas_call | solution.py:621
  55.6 4.3 %collective-permute-done.15.end_ref = f32[64,2048]{1,0:T(8,128)S(1)} collective-permute-done((f32[64,2048]{1,0:T(8,128)S(1)}, f32[64,2048]{1,0:T(8,128)S(1)}, u32[]{:S(2)}, u32[]{:S(2)}) %collective-permute-start.15) | collective-permute-done | bytes 524320 | tf_op jit(solution)/shard_map/ppermute | solution.py:542
  59.9 0.1 forward.1.__
  60.0 2.5 %collective-permute-start.16 = (f32[64,2048]{1,0:T(8,128)S(1)}, f32[64,2048]{1,0:T(8,128)S(1)}, u32[]{:S(2)}, u32[]{:S(2)}) collective-permute-start(f32[64,2048]{1,0:T(8,128)S(1)} %hand_on.1), channel_id=1, source_target_pairs={{0,1},{1,0},{2,3},{3,2},{4,5},{5,4},{6,7},{7,6},{8,9},{9,8},{10,11... | collective-permute-start | bytes 1572872 | tf_op jit(solution)/shard_map/ppermute | solution.py:561
  62.6 1.1 %collective-permute-start.17 = (f32[64,2048]{1,0:T(8,128)S(1)}, f32[64,2048]{1,0:T(8,128)S(1)}, u32[]{:S(2)}, u32[]{:S(2)}) collective-permute-start(f32[64,2048]{1,0:T(8,128)S(1)} %forward.1.__), channel_id=1, source_target_pairs={{0,2},{1,3},{2,0},{3,1},{4,6},{5,7},{6,4},{7,5},{8,10},{9,11},{10,... | collective-permute-start | bytes 1572872 | tf_op jit(solution)/shard_map/ppermute | solution.py:562
  63.6 0.0 collective-permute-done.14
  63.6 21.1 %collective-permute-done.16 = f32[64,2048]{1,0:T(8,128)S(1)} collective-permute-done((f32[64,2048]{1,0:T(8,128)S(1)}, f32[64,2048]{1,0:T(8,128)S(1)}, u32[]{:S(2)}, u32[]{:S(2)}) %collective-permute-start.16) | collective-permute-done | bytes 524320 | tf_op jit(solution)/shard_map/ppermute | solution.py:561
  84.8 2.5 %collective-permute-done.17 = f32[64,2048]{1,0:T(8,128)S(1)} collective-permute-done((f32[64,2048]{1,0:T(8,128)S(1)}, f32[64,2048]{1,0:T(8,128)S(1)}, u32[]{:S(2)}, u32[]{:S(2)}) %collective-permute-start.17) | collective-permute-done | bytes 524320 | tf_op jit(solution)/shard_map/ppermute | solution.py:562
  87.3 0.9 %add_add_fusion = f32[64,2048]{1,0:T(8,128)} fusion(f32[64,2048]{1,0:T(8,128)S(1)} %collective-permute-done.17, f32[64,2048]{1,0:T(8,128)S(1)} %collective-permute-done.16, f32[64,2048]{1,0:T(8,128)S(1)} %get-tuple-element.83, f32[64,2048]{1,0:T(8,128)S(1)} %collective-permute-done.14), kind=kLoop, calls=%fused_computation | loop fusion | flops 393216 | bytes 2621440 | tf_op jit(solution)/shard_map/add | solution.py:563
  (1 shorter events, 0.0 us)
Async XLA Ops:
  9.9 7.6 %collective-permute-start = (f32[128,256]{1,0:T(8,128)}, f32[128,256]{1,0:T(8,128)S(1)}, u32[]{:S(2)}, u32[]{:S(2)}) collective-permute-start(f32[128,256]{1,0:T(8,128)} %get-tuple-element.48), channel_id=1, source_target_pairs={{0,28},{4,24},{8,20},{12,16},{16,12},{20,8},{24,4},{28,0},{1,29},{... | collective-permute-start | bytes 393224 | tf_op jit(solution)/shard_map/ppermute | solution.py:477
  13.3 7.5 %collective-permute-start.1 = (f32[128,256]{1,0:T(8,128)}, f32[128,256]{1,0:T(8,128)S(1)}, u32[]{:S(2)}, u32[]{:S(2)}) collective-permute-start(f32[128,256]{1,0:T(8,128)} %get-tuple-element.49), channel_id=1, source_target_pairs={{0,24},{4,28},{8,16},{12,20},{16,8},{20,12},{24,0},{28,4},{1,25},{... | collective-permute-start | bytes 393224 | tf_op jit(solution)/shard_map/ppermute | solution.py:477
  14.0 12.2 %collective-permute-start.2 = (f32[128,256]{1,0:T(8,128)}, f32[128,256]{1,0:T(8,128)S(1)}, u32[]{:S(2)}, u32[]{:S(2)}) collective-permute-start(f32[128,256]{1,0:T(8,128)} %get-tuple-element.50), channel_id=1, source_target_pairs={{0,20},{4,16},{8,28},{12,24},{16,4},{20,0},{24,12},{28,8},{1,21},{... | collective-permute-start | bytes 393224 | tf_op jit(solution)/shard_map/ppermute | solution.py:477
  15.3 10.8 %collective-permute-start.3 = (f32[128,256]{1,0:T(8,128)}, f32[128,256]{1,0:T(8,128)S(1)}, u32[]{:S(2)}, u32[]{:S(2)}) collective-permute-start(f32[128,256]{1,0:T(8,128)} %get-tuple-element.51), channel_id=1, source_target_pairs={{0,16},{4,20},{8,24},{12,28},{16,0},{20,4},{24,8},{28,12},{1,17},{... | collective-permute-start | bytes 393224 | tf_op jit(solution)/shard_map/ppermute | solution.py:477
  15.6 10.5 %collective-permute-start.4 = (f32[128,256]{1,0:T(8,128)}, f32[128,256]{1,0:T(8,128)S(1)}, u32[]{:S(2)}, u32[]{:S(2)}) collective-permute-start(f32[128,256]{1,0:T(8,128)} %get-tuple-element.52), channel_id=1, source_target_pairs={{0,12},{4,8},{8,4},{12,0},{16,28},{20,24},{24,20},{28,16},{1,13},{... | collective-permute-start | bytes 393224 | tf_op jit(solution)/shard_map/ppermute | solution.py:477
  17.5 9.3 %collective-permute-start.5 = (f32[128,256]{1,0:T(8,128)}, f32[128,256]{1,0:T(8,128)S(1)}, u32[]{:S(2)}, u32[]{:S(2)}) collective-permute-start(f32[128,256]{1,0:T(8,128)} %get-tuple-element.53), channel_id=1, source_target_pairs={{0,8},{4,12},{8,0},{12,4},{16,24},{20,28},{24,16},{28,20},{1,9},{5... | collective-permute-start | bytes 393224 | tf_op jit(solution)/shard_map/ppermute | solution.py:477
  20.8 6.1 %collective-permute-start.6 = (f32[128,256]{1,0:T(8,128)}, f32[128,256]{1,0:T(8,128)S(1)}, u32[]{:S(2)}, u32[]{:S(2)}) collective-permute-start(f32[128,256]{1,0:T(8,128)} %get-tuple-element.54), channel_id=1, source_target_pairs={{0,4},{4,0},{8,12},{12,8},{16,20},{20,16},{24,28},{28,24},{1,5},{5... | collective-permute-start | bytes 393224 | tf_op jit(solution)/shard_map/ppermute | solution.py:477
  28.0 5.8 %collective-permute-start.7 = (f32[128,128]{1,0:T(8,128)S(1)}, f32[128,128]{1,0:T(8,128)S(1)}, u32[]{:S(2)}, u32[]{:S(2)}) collective-permute-start(f32[128,128]{1,0:T(8,128)S(1)} %get-tuple-element.75), channel_id=1, source_target_pairs={{0,28},{4,24},{8,20},{12,16},{16,12},{20,8},{24,4},{28,0},{1,29},{... | collective-permute-start | bytes 196616 | tf_op jit(solution)/shard_map/ppermute | solution.py:477
  30.4 5.2 %collective-permute-start.8 = (f32[128,128]{1,0:T(8,128)S(1)}, f32[128,128]{1,0:T(8,128)S(1)}, u32[]{:S(2)}, u32[]{:S(2)}) collective-permute-start(f32[128,128]{1,0:T(8,128)S(1)} %get-tuple-element.76), channel_id=1, source_target_pairs={{0,24},{4,28},{8,16},{12,20},{16,8},{20,12},{24,0},{28,4},{1,25},{... | collective-permute-start | bytes 196616 | tf_op jit(solution)/shard_map/ppermute | solution.py:477
  30.7 5.5 %collective-permute-start.9 = (f32[128,128]{1,0:T(8,128)S(1)}, f32[128,128]{1,0:T(8,128)S(1)}, u32[]{:S(2)}, u32[]{:S(2)}) collective-permute-start(f32[128,128]{1,0:T(8,128)S(1)} %get-tuple-element.77), channel_id=1, source_target_pairs={{0,20},{4,16},{8,28},{12,24},{16,4},{20,0},{24,12},{28,8},{1,21},{... | collective-permute-start | bytes 196616 | tf_op jit(solution)/shard_map/ppermute | solution.py:477
  31.9 6.0 %collective-permute-start.10 = (f32[128,128]{1,0:T(8,128)S(1)}, f32[128,128]{1,0:T(8,128)S(1)}, u32[]{:S(2)}, u32[]{:S(2)}) collective-permute-start(f32[128,128]{1,0:T(8,128)S(1)} %get-tuple-element.78), channel_id=1, source_target_pairs={{0,16},{4,20},{8,24},{12,28},{16,0},{20,4},{24,8},{28,12},{1,17},{... | collective-permute-start | bytes 196616 | tf_op jit(solution)/shard_map/ppermute | solution.py:477
  32.5 5.4 %collective-permute-start.11 = (f32[128,128]{1,0:T(8,128)S(1)}, f32[128,128]{1,0:T(8,128)S(1)}, u32[]{:S(2)}, u32[]{:S(2)}) collective-permute-start(f32[128,128]{1,0:T(8,128)S(1)} %get-tuple-element.79), channel_id=1, source_target_pairs={{0,12},{4,8},{8,4},{12,0},{16,28},{20,24},{24,20},{28,16},{1,13},{... | collective-permute-start | bytes 196616 | tf_op jit(solution)/shard_map/ppermute | solution.py:477
  33.9 4.5 %collective-permute-start.12 = (f32[128,128]{1,0:T(8,128)S(1)}, f32[128,128]{1,0:T(8,128)S(1)}, u32[]{:S(2)}, u32[]{:S(2)}) collective-permute-start(f32[128,128]{1,0:T(8,128)S(1)} %get-tuple-element.80), channel_id=1, source_target_pairs={{0,8},{4,12},{8,0},{12,4},{16,24},{20,28},{24,16},{28,20},{1,9},{5... | collective-permute-start | bytes 196616 | tf_op jit(solution)/shard_map/ppermute | solution.py:477
  35.6 2.7 %collective-permute-start.13 = (f32[128,128]{1,0:T(8,128)S(1)}, f32[128,128]{1,0:T(8,128)S(1)}, u32[]{:S(2)}, u32[]{:S(2)}) collective-permute-start(f32[128,128]{1,0:T(8,128)S(1)} %get-tuple-element.81), channel_id=1, source_target_pairs={{0,4},{4,0},{8,12},{12,8},{16,20},{20,16},{24,28},{28,24},{1,5},{5... | collective-permute-start | bytes 196616 | tf_op jit(solution)/shard_map/ppermute | solution.py:477
  38.3 1.2 %copy-start = (f32[256,1024]{1,0:T(8,128)S(1)}, f32[256,1024]{1,0:T(8,128)}, u32[]{:S(2)}) copy-start(f32[256,1024]{1,0:T(8,128)} %gate_hbm.3) | copy-start | bytes 3145732
  39.5 0.7 copy-start.1
  45.3 14.7 %collective-permute-start.15 = (f32[64,2048]{1,0:T(8,128)S(1)}, f32[64,2048]{1,0:T(8,128)S(1)}, u32[]{:S(2)}, u32[]{:S(2)}) collective-permute-start(f32[64,2048]{1,0:T(8,128)S(1)} %get-tuple-element.84), channel_id=1, source_target_pairs={{0,1},{3,2},{4,5},{7,6},{8,9},{11,10},{12,13},{15,14},{16,17},{19,... | collective-permute-start | bytes 1572872 | tf_op jit(solution)/shard_map/ppermute | solution.py:542
  48.8 14.9 %collective-permute-start.14 = (f32[64,2048]{1,0:T(8,128)S(1)}, f32[64,2048]{1,0:T(8,128)S(1)}, u32[]{:S(2)}, u32[]{:S(2)}) collective-permute-start(f32[64,2048]{1,0:T(8,128)S(1)} %get-tuple-element.84), channel_id=1, source_target_pairs={{1,2},{2,1},{5,6},{6,5},{9,10},{10,9},{13,14},{14,13},{17,18},{18,... | collective-permute-start | bytes 1572872 | tf_op jit(solution)/shard_map/ppermute | solution.py:543
  60.0 24.7 %collective-permute-start.16 = (f32[64,2048]{1,0:T(8,128)S(1)}, f32[64,2048]{1,0:T(8,128)S(1)}, u32[]{:S(2)}, u32[]{:S(2)}) collective-permute-start(f32[64,2048]{1,0:T(8,128)S(1)} %hand_on.1), channel_id=1, source_target_pairs={{0,1},{1,0},{2,3},{3,2},{4,5},{5,4},{6,7},{7,6},{8,9},{9,8},{10,11... | collective-permute-start | bytes 1572872 | tf_op jit(solution)/shard_map/ppermute | solution.py:561
  62.6 24.7 %collective-permute-start.17 = (f32[64,2048]{1,0:T(8,128)S(1)}, f32[64,2048]{1,0:T(8,128)S(1)}, u32[]{:S(2)}, u32[]{:S(2)}) collective-permute-start(f32[64,2048]{1,0:T(8,128)S(1)} %forward.1.__), channel_id=1, source_target_pairs={{0,2},{1,3},{2,0},{3,1},{4,6},{5,7},{6,4},{7,5},{8,10},{9,11},{10,... | collective-permute-start | bytes 1572872 | tf_op jit(solution)/shard_map/ppermute | solution.py:562

commit v11 on v10

--- a/solution.py
+++ b/solution.py
@@ -20,7 +20,7 @@
 SCAN_VMEM = 52.25
 FIRST_VMEM = 40
 LATER_VMEM = 32
-HEADS_AT_ONCE = 4
+HEADS_AT_ONCE = 8
 EPS = 1e-06
 
 
@@ -364,7 +364,7 @@
             entry_ref[source + 1, head] = state
 
 
-def ordered_scan_kernel(*rest):
+def ordered_scan_kernel(_, *rest):
     *arrays, held_ref, entry_ref = rest
     count = entry_ref.shape[0]
     held, entries = arrays[:count], arrays[count:]
@@ -497,7 +497,7 @@
         entry = shape(DK, DV)
         entries = pl.pallas_call(
             ordered_scan_kernel,
-            in_specs=[VMEM] * count,
+            in_specs=[HBM] + [VMEM] * count,
             out_specs=[VMEM] * count,
             out_shape=[entry] * count,
             scratch_shapes=[
@@ -506,7 +506,7 @@
             ],
             compiler_params=params(SCAN_VMEM),
             name="state_scan",
-        )(*held)
+        )(beside, *held)
         entries, after = lax.optimization_barrier((entries, after))
         return partners_swap(entries, "ctx"), beside, after
     parts = max(1, count // heads)

time: 88.5 us -> 86.5 us (0.977)
  local copies, waits for them, and re-layouts: 1.88 us -> 0.01 us
    unnamed x4, local copies, waits for them, and re-layouts: 1.88 us -> 0.01 us
where the time goes in v11:
time: 86.5 us; the launch traced here: 86.2 us
  waiting for transfers between devices  34.2 us (40%)
  Pallas kernels  27.4 us (32%)
  starting transfers between devices  23.5 us (27%)
  other arithmetic  0.92 us (1%)
    ppermute x1, waiting for transfers between devices, project_and_sum(): from_near = lax.ppermute(near, axis, [(i, i ^ 1) for i in range(4)])  21.2 us
    ppermute x14, starting transfers between devices, partners_swap(): lax.ppermute(array, axis, [(d, d ^ i) for d in range(count)])  15.7 us
    pallas_call x2, Pallas kernels, project(): pl.pallas_call(functools.partial(projection_kernel, pieces=[(index, start...  11.4 us
    pallas_call x1, Pallas kernels, per_device(): pl.pallas_call(functools.partial(summary_kernel, swap=swap.heads), in_spe...  9.52 us
    ppermute x14, waiting for transfers between devices, partners_swap(): lax.ppermute(array, axis, [(d, d ^ i) for d in range(count)])  6.17 us
    pallas_call x1, Pallas kernels, per_device(): pl.pallas_call(output_kernel, in_specs=[HBM] * 3, out_specs=[HBM, VMEM],...  5.31 us
    ppermute x1, waiting for transfers between devices, project_and_sum(): from_end = lax.ppermute(opposite, axis, [(0, 1), (3, 2)])  4.35 us
    ppermute x1, starting transfers between devices, project_and_sum(): from_end = lax.ppermute(opposite, axis, [(0, 1), (3, 2)])  3.47 us
  transfers between devices with their start and end apart: 18, of which 10 were waited for; matrix products, arithmetic and copies ran while one was open for 0% of the time, Pallas kernels for 13%

profile of v11, /device:TPU:0, one launch (start us, length us, event | category | flops | bytes accessed | tf_op | source)
XLA Modules:
  0.0 86.2 jit_solution(10267478338518569162)
XLA Ops:
  0.0 9.5 %state_summary.1 = (f32[9,256,256]{2,1,0:T(8,128)}, f32[128,256]{1,0:T(8,128)}, f32[128,256]{1,0:T(8,128)}, f32[128,256]{1,0:T(8,128)}, f32[128,256]{1,0:T(8,128...) custom-call(f32[8,256]{1,0:T(8,128)} %decay_hbm.1, f32[8,256]{1,0:T(8,128)} %strength_hbm.1, ...), custom_call_target="tpu_custom_call" | custom-call | tf_op jit(solution)/shard_map/state_summary/pallas_call | solution.py:586
  9.5 3.4 %collective-permute-start = (f32[128,256]{1,0:T(8,128)}, f32[128,256]{1,0:T(8,128)S(1)}, u32[]{:S(2)}, u32[]{:S(2)}) collective-permute-start(f32[128,256]{1,0:T(8,128)} %get-tuple-element.48), channel_id=1, source_target_pairs={{0,28},{4,24},{8,20},{12,16},{16,12},{20,8},{24,4},{28,0},{1,29},{... | collective-permute-start | bytes 393224 | tf_op jit(solution)/shard_map/ppermute | solution.py:477
  12.9 0.6 collective-permute-start.1
  13.6 1.4 %collective-permute-start.2 = (f32[128,256]{1,0:T(8,128)}, f32[128,256]{1,0:T(8,128)S(1)}, u32[]{:S(2)}, u32[]{:S(2)}) collective-permute-start(f32[128,256]{1,0:T(8,128)} %get-tuple-element.50), channel_id=1, source_target_pairs={{0,20},{4,16},{8,28},{12,24},{16,4},{20,0},{24,12},{28,8},{1,21},{... | collective-permute-start | bytes 393224 | tf_op jit(solution)/shard_map/ppermute | solution.py:477
  15.0 0.3 collective-permute-start.3
  15.2 1.2 %collective-permute-start.4 = (f32[128,256]{1,0:T(8,128)}, f32[128,256]{1,0:T(8,128)S(1)}, u32[]{:S(2)}, u32[]{:S(2)}) collective-permute-start(f32[128,256]{1,0:T(8,128)} %get-tuple-element.52), channel_id=1, source_target_pairs={{0,12},{4,8},{8,4},{12,0},{16,28},{20,24},{24,20},{28,16},{1,13},{... | collective-permute-start | bytes 393224 | tf_op jit(solution)/shard_map/ppermute | solution.py:477
  16.4 0.7 collective-permute-done.rest_1_
  17.1 2.4 %collective-permute-start.5 = (f32[128,256]{1,0:T(8,128)}, f32[128,256]{1,0:T(8,128)S(1)}, u32[]{:S(2)}, u32[]{:S(2)}) collective-permute-start(f32[128,256]{1,0:T(8,128)} %get-tuple-element.53), channel_id=1, source_target_pairs={{0,8},{4,12},{8,0},{12,4},{16,24},{20,28},{24,16},{28,20},{1,9},{5... | collective-permute-start | bytes 393224 | tf_op jit(solution)/shard_map/ppermute | solution.py:477
  19.5 0.9 %collective-permute-done.1.rest_2_ = f32[128,256]{1,0:T(8,128)S(1)} collective-permute-done((f32[128,256]{1,0:T(8,128)}, f32[128,256]{1,0:T(8,128)S(1)}, u32[]{:S(2)}, u32[]{:S(2)}) %collective-permute-start.1) | collective-permute-done | bytes 131104 | tf_op jit(solution)/shard_map/ppermute | solution.py:477
  20.4 0.0 collective-permute-start.6
  20.4 5.3 %output_maps.1 = (f32[64,256,256]{2,1,0:T(8,128)}, f32[128,256]{1,0:T(8,128)S(1)}) custom-call(f32[256,512]{1,0:T(8,128)} %q_hbm.1, f32[256,512]{1,0:T(8,128)} %k_hbm.3, f32[9,256,256]{2,1,0:T(8,128)} %get-tuple-element.46.factor_hbm), custom_call_target="tpu_custom_call" | custom-call | flops 1207959552 | bytes 5242880 | tf_op jit(solution)/shard_map/output_maps/pallas_call | solution.py:597
  25.7 0.0 collective-permute-done.2.rest_3_
  25.7 0.0 collective-permute-done.3.rest_4_
  25.7 0.0 collective-permute-done.4.rest_5_
  25.8 0.7 collective-permute-done.5.rest_6_
  26.5 0.0 collective-permute-done.6.rest_7_
  26.5 0.0 copy-start
  26.5 0.0 copy-start.1
  26.5 1.1 %state_scan.1 = (f32[128,128]{1,0:T(8,128)S(1)}, f32[128,128]{1,0:T(8,128)S(1)}, f32[128,128]{1,0:T(8,128)S(1)}, f32[128,128]{1,0:T(8,128)S(1)}, f32[128,128]{1,...) custom-call(f32[64,256,256]{2,1,0:T(8,128)} %get-tuple-element.56._.map_hbm, ...), custom_call_target="tpu_custom_call" | custom-call | tf_op jit(solution)/shard_map/state_scan/pallas_call | solution.py:498
  27.6 2.4 %collective-permute-start.7 = (f32[128,128]{1,0:T(8,128)S(1)}, f32[128,128]{1,0:T(8,128)S(1)}, u32[]{:S(2)}, u32[]{:S(2)}) collective-permute-start(f32[128,128]{1,0:T(8,128)S(1)} %get-tuple-element.75), channel_id=1, source_target_pairs={{0,28},{4,24},{8,20},{12,16},{16,12},{20,8},{24,4},{28,0},{1,29},{... | collective-permute-start | bytes 196616 | tf_op jit(solution)/shard_map/ppermute | solution.py:477
  30.0 0.3 collective-permute-start.8
  30.3 1.2 %collective-permute-start.9 = (f32[128,128]{1,0:T(8,128)S(1)}, f32[128,128]{1,0:T(8,128)S(1)}, u32[]{:S(2)}, u32[]{:S(2)}) collective-permute-start(f32[128,128]{1,0:T(8,128)S(1)} %get-tuple-element.77), channel_id=1, source_target_pairs={{0,20},{4,16},{8,28},{12,24},{16,4},{20,0},{24,12},{28,8},{1,21},{... | collective-permute-start | bytes 196616 | tf_op jit(solution)/shard_map/ppermute | solution.py:477
  31.5 0.6 collective-permute-start.10
  32.1 1.3 %collective-permute-start.11 = (f32[128,128]{1,0:T(8,128)S(1)}, f32[128,128]{1,0:T(8,128)S(1)}, u32[]{:S(2)}, u32[]{:S(2)}) collective-permute-start(f32[128,128]{1,0:T(8,128)S(1)} %get-tuple-element.79), channel_id=1, source_target_pairs={{0,12},{4,8},{8,4},{12,0},{16,28},{20,24},{24,20},{28,16},{1,13},{... | collective-permute-start | bytes 196616 | tf_op jit(solution)/shard_map/ppermute | solution.py:477
  33.5 0.0 collective-permute-done.7.rest_1_
  33.5 0.6 collective-permute-start.12
  34.1 1.2 %collective-permute-done.8.rest_2_ = f32[128,128]{1,0:T(8,128)S(1)} collective-permute-done((f32[128,128]{1,0:T(8,128)S(1)}, f32[128,128]{1,0:T(8,128)S(1)}, u32[]{:S(2)}, u32[]{:S(2)}) %collective-permute-start.8) | collective-permute-done | bytes 65568 | tf_op jit(solution)/shard_map/ppermute | solution.py:477
  35.3 0.0 collective-permute-start.13
  35.3 0.5 collective-permute-done.9.rest_3_
  35.8 1.7 %collective-permute-done.10.rest_4_ = f32[128,128]{1,0:T(8,128)S(1)} collective-permute-done((f32[128,128]{1,0:T(8,128)S(1)}, f32[128,128]{1,0:T(8,128)S(1)}, u32[]{:S(2)}, u32[]{:S(2)}) %collective-permute-start.10) | collective-permute-done | bytes 65568 | tf_op jit(solution)/shard_map/ppermute | solution.py:477
  37.5 0.0 collective-permute-done.11.rest_5_
  37.5 0.4 collective-permute-done.12.rest_6_
  37.9 0.0 collective-permute-done.13.rest_7_
  37.9 0.0 copy-done
  37.9 0.0 copy-done.1
  37.9 5.3 %projection.2 = (f32[64,2048]{1,0:T(8,128)S(1)}, bf16[2,1024,2048]{2,1,0:T(8,128)(2,1)S(1)}) custom-call(f32[64,256,256]{2,1,0:T(8,128)} %get-tuple-element.56._.map_hbm, f32[256,1024]{1,0:T(8,128)S(1)} %copy-done, f32[1,128]{1,0:T(1,128)S(1)} %bitcast.1, f32[1024,2048]{1,0:T(8,128)} %weight_ref, f32[128,128]{1,0:T(8,128)S(1)} %get-tuple-element.74.rest_0_, ...), custom_call_target="tpu_custom_call" | custom-call | flops 805306368 | bytes 8388608 | tf_op jit(solution)/shard_map/projection/pallas_call | solution.py:621
  43.2 3.5 %collective-permute-start.15 = (f32[64,2048]{1,0:T(8,128)S(1)}, f32[64,2048]{1,0:T(8,128)S(1)}, u32[]{:S(2)}, u32[]{:S(2)}) collective-permute-start(f32[64,2048]{1,0:T(8,128)S(1)} %get-tuple-element.84), channel_id=1, source_target_pairs={{0,1},{3,2},{4,5},{7,6},{8,9},{11,10},{12,13},{15,14},{16,17},{19,... | collective-permute-start | bytes 1572872 | tf_op jit(solution)/shard_map/ppermute | solution.py:542
  46.7 0.7 collective-permute-start.14
  47.4 6.2 %projection.3 = (f32[64,2048]{1,0:T(8,128)S(1)}, f32[64,2048]{1,0:T(8,128)S(1)}, f32[64,2048]{1,0:T(8,128)S(1)}) custom-call(f32[64,256,256]{2,1,0:T(8,128)} %get-tuple-element.56._.map_hbm, f32[256,1024]{1,0:T(8,128)S(1)} %copy-done, f32[1,128]{1,0:T(1,128)S(1)} %bitcast.2, bf16[2,1024,2048]{2,1,0:T(8,128)(2,1)S(1)} %get-tuple-element.82.weight_ref, ...), custom_call_target="tpu_custom_call" | custom-call | flops 2415919104 | bytes 8388608 | tf_op jit(solution)/shard_map/projection/pallas_call | solution.py:621
  53.5 4.4 %collective-permute-done.15.end_ref = f32[64,2048]{1,0:T(8,128)S(1)} collective-permute-done((f32[64,2048]{1,0:T(8,128)S(1)}, f32[64,2048]{1,0:T(8,128)S(1)}, u32[]{:S(2)}, u32[]{:S(2)}) %collective-permute-start.15) | collective-permute-done | bytes 524320 | tf_op jit(solution)/shard_map/ppermute | solution.py:542
  57.9 0.1 forward.1.__
  58.0 2.5 %collective-permute-start.16 = (f32[64,2048]{1,0:T(8,128)S(1)}, f32[64,2048]{1,0:T(8,128)S(1)}, u32[]{:S(2)}, u32[]{:S(2)}) collective-permute-start(f32[64,2048]{1,0:T(8,128)S(1)} %hand_on.1), channel_id=1, source_target_pairs={{0,1},{1,0},{2,3},{3,2},{4,5},{5,4},{6,7},{7,6},{8,9},{9,8},{10,11... | collective-permute-start | bytes 1572872 | tf_op jit(solution)/shard_map/ppermute | solution.py:561
  60.5 1.1 %collective-permute-start.17 = (f32[64,2048]{1,0:T(8,128)S(1)}, f32[64,2048]{1,0:T(8,128)S(1)}, u32[]{:S(2)}, u32[]{:S(2)}) collective-permute-start(f32[64,2048]{1,0:T(8,128)S(1)} %forward.1.__), channel_id=1, source_target_pairs={{0,2},{1,3},{2,0},{3,1},{4,6},{5,7},{6,4},{7,5},{8,10},{9,11},{10,... | collective-permute-start | bytes 1572872 | tf_op jit(solution)/shard_map/ppermute | solution.py:562
  61.6 0.0 collective-permute-done.14
  61.6 21.2 %collective-permute-done.16 = f32[64,2048]{1,0:T(8,128)S(1)} collective-permute-done((f32[64,2048]{1,0:T(8,128)S(1)}, f32[64,2048]{1,0:T(8,128)S(1)}, u32[]{:S(2)}, u32[]{:S(2)}) %collective-permute-start.16) | collective-permute-done | bytes 524320 | tf_op jit(solution)/shard_map/ppermute | solution.py:561
  82.8 2.5 %collective-permute-done.17 = f32[64,2048]{1,0:T(8,128)S(1)} collective-permute-done((f32[64,2048]{1,0:T(8,128)S(1)}, f32[64,2048]{1,0:T(8,128)S(1)}, u32[]{:S(2)}, u32[]{:S(2)}) %collective-permute-start.17) | collective-permute-done | bytes 524320 | tf_op jit(solution)/shard_map/ppermute | solution.py:562
  85.3 0.9 %add_add_fusion = f32[64,2048]{1,0:T(8,128)} fusion(f32[64,2048]{1,0:T(8,128)S(1)} %collective-permute-done.17, f32[64,2048]{1,0:T(8,128)S(1)} %collective-permute-done.16, f32[64,2048]{1,0:T(8,128)S(1)} %get-tuple-element.83, f32[64,2048]{1,0:T(8,128)S(1)} %collective-permute-done.14), kind=kLoop, calls=%fused_computation | loop fusion | flops 393216 | bytes 2621440 | tf_op jit(solution)/shard_map/add | solution.py:563
  (1 shorter events, 0.0 us)
Async XLA Ops:
  9.5 7.6 %collective-permute-start = (f32[128,256]{1,0:T(8,128)}, f32[128,256]{1,0:T(8,128)S(1)}, u32[]{:S(2)}, u32[]{:S(2)}) collective-permute-start(f32[128,256]{1,0:T(8,128)} %get-tuple-element.48), channel_id=1, source_target_pairs={{0,28},{4,24},{8,20},{12,16},{16,12},{20,8},{24,4},{28,0},{1,29},{... | collective-permute-start | bytes 393224 | tf_op jit(solution)/shard_map/ppermute | solution.py:477
  12.9 7.5 %collective-permute-start.1 = (f32[128,256]{1,0:T(8,128)}, f32[128,256]{1,0:T(8,128)S(1)}, u32[]{:S(2)}, u32[]{:S(2)}) collective-permute-start(f32[128,256]{1,0:T(8,128)} %get-tuple-element.49), channel_id=1, source_target_pairs={{0,24},{4,28},{8,16},{12,20},{16,8},{20,12},{24,0},{28,4},{1,25},{... | collective-permute-start | bytes 393224 | tf_op jit(solution)/shard_map/ppermute | solution.py:477
  13.6 12.2 %collective-permute-start.2 = (f32[128,256]{1,0:T(8,128)}, f32[128,256]{1,0:T(8,128)S(1)}, u32[]{:S(2)}, u32[]{:S(2)}) collective-permute-start(f32[128,256]{1,0:T(8,128)} %get-tuple-element.50), channel_id=1, source_target_pairs={{0,20},{4,16},{8,28},{12,24},{16,4},{20,0},{24,12},{28,8},{1,21},{... | collective-permute-start | bytes 393224 | tf_op jit(solution)/shard_map/ppermute | solution.py:477
  15.0 10.8 %collective-permute-start.3 = (f32[128,256]{1,0:T(8,128)}, f32[128,256]{1,0:T(8,128)S(1)}, u32[]{:S(2)}, u32[]{:S(2)}) collective-permute-start(f32[128,256]{1,0:T(8,128)} %get-tuple-element.51), channel_id=1, source_target_pairs={{0,16},{4,20},{8,24},{12,28},{16,0},{20,4},{24,8},{28,12},{1,17},{... | collective-permute-start | bytes 393224 | tf_op jit(solution)/shard_map/ppermute | solution.py:477
  15.2 10.5 %collective-permute-start.4 = (f32[128,256]{1,0:T(8,128)}, f32[128,256]{1,0:T(8,128)S(1)}, u32[]{:S(2)}, u32[]{:S(2)}) collective-permute-start(f32[128,256]{1,0:T(8,128)} %get-tuple-element.52), channel_id=1, source_target_pairs={{0,12},{4,8},{8,4},{12,0},{16,28},{20,24},{24,20},{28,16},{1,13},{... | collective-permute-start | bytes 393224 | tf_op jit(solution)/shard_map/ppermute | solution.py:477
  17.1 9.3 %collective-permute-start.5 = (f32[128,256]{1,0:T(8,128)}, f32[128,256]{1,0:T(8,128)S(1)}, u32[]{:S(2)}, u32[]{:S(2)}) collective-permute-start(f32[128,256]{1,0:T(8,128)} %get-tuple-element.53), channel_id=1, source_target_pairs={{0,8},{4,12},{8,0},{12,4},{16,24},{20,28},{24,16},{28,20},{1,9},{5... | collective-permute-start | bytes 393224 | tf_op jit(solution)/shard_map/ppermute | solution.py:477
  20.4 6.1 %collective-permute-start.6 = (f32[128,256]{1,0:T(8,128)}, f32[128,256]{1,0:T(8,128)S(1)}, u32[]{:S(2)}, u32[]{:S(2)}) collective-permute-start(f32[128,256]{1,0:T(8,128)} %get-tuple-element.54), channel_id=1, source_target_pairs={{0,4},{4,0},{8,12},{12,8},{16,20},{20,16},{24,28},{28,24},{1,5},{5... | collective-permute-start | bytes 393224 | tf_op jit(solution)/shard_map/ppermute | solution.py:477
  26.5 11.4 %copy-start = (f32[256,1024]{1,0:T(8,128)S(1)}, f32[256,1024]{1,0:T(8,128)}, u32[]{:S(2)}) copy-start(f32[256,1024]{1,0:T(8,128)} %gate_hbm.3) | copy-start | bytes 3145732
  26.5 11.4 %copy-start.1 = (f32[128]{0:T(128)S(1)}, f32[128]{0:T(128)}, u32[]{:S(2)}) copy-start(f32[128]{0:T(128)} %param.14) | copy-start | bytes 1540
  27.6 5.8 %collective-permute-start.7 = (f32[128,128]{1,0:T(8,128)S(1)}, f32[128,128]{1,0:T(8,128)S(1)}, u32[]{:S(2)}, u32[]{:S(2)}) collective-permute-start(f32[128,128]{1,0:T(8,128)S(1)} %get-tuple-element.75), channel_id=1, source_target_pairs={{0,28},{4,24},{8,20},{12,16},{16,12},{20,8},{24,4},{28,0},{1,29},{... | collective-permute-start | bytes 196616 | tf_op jit(solution)/shard_map/ppermute | solution.py:477
  30.0 5.2 %collective-permute-start.8 = (f32[128,128]{1,0:T(8,128)S(1)}, f32[128,128]{1,0:T(8,128)S(1)}, u32[]{:S(2)}, u32[]{:S(2)}) collective-permute-start(f32[128,128]{1,0:T(8,128)S(1)} %get-tuple-element.76), channel_id=1, source_target_pairs={{0,24},{4,28},{8,16},{12,20},{16,8},{20,12},{24,0},{28,4},{1,25},{... | collective-permute-start | bytes 196616 | tf_op jit(solution)/shard_map/ppermute | solution.py:477
  30.3 5.5 %collective-permute-start.9 = (f32[128,128]{1,0:T(8,128)S(1)}, f32[128,128]{1,0:T(8,128)S(1)}, u32[]{:S(2)}, u32[]{:S(2)}) collective-permute-start(f32[128,128]{1,0:T(8,128)S(1)} %get-tuple-element.77), channel_id=1, source_target_pairs={{0,20},{4,16},{8,28},{12,24},{16,4},{20,0},{24,12},{28,8},{1,21},{... | collective-permute-start | bytes 196616 | tf_op jit(solution)/shard_map/ppermute | solution.py:477
  31.5 6.0 %collective-permute-start.10 = (f32[128,128]{1,0:T(8,128)S(1)}, f32[128,128]{1,0:T(8,128)S(1)}, u32[]{:S(2)}, u32[]{:S(2)}) collective-permute-start(f32[128,128]{1,0:T(8,128)S(1)} %get-tuple-element.78), channel_id=1, source_target_pairs={{0,16},{4,20},{8,24},{12,28},{16,0},{20,4},{24,8},{28,12},{1,17},{... | collective-permute-start | bytes 196616 | tf_op jit(solution)/shard_map/ppermute | solution.py:477
  32.1 5.4 %collective-permute-start.11 = (f32[128,128]{1,0:T(8,128)S(1)}, f32[128,128]{1,0:T(8,128)S(1)}, u32[]{:S(2)}, u32[]{:S(2)}) collective-permute-start(f32[128,128]{1,0:T(8,128)S(1)} %get-tuple-element.79), channel_id=1, source_target_pairs={{0,12},{4,8},{8,4},{12,0},{16,28},{20,24},{24,20},{28,16},{1,13},{... | collective-permute-start | bytes 196616 | tf_op jit(solution)/shard_map/ppermute | solution.py:477
  33.5 4.4 %collective-permute-start.12 = (f32[128,128]{1,0:T(8,128)S(1)}, f32[128,128]{1,0:T(8,128)S(1)}, u32[]{:S(2)}, u32[]{:S(2)}) collective-permute-start(f32[128,128]{1,0:T(8,128)S(1)} %get-tuple-element.80), channel_id=1, source_target_pairs={{0,8},{4,12},{8,0},{12,4},{16,24},{20,28},{24,16},{28,20},{1,9},{5... | collective-permute-start | bytes 196616 | tf_op jit(solution)/shard_map/ppermute | solution.py:477
  35.3 2.7 %collective-permute-start.13 = (f32[128,128]{1,0:T(8,128)S(1)}, f32[128,128]{1,0:T(8,128)S(1)}, u32[]{:S(2)}, u32[]{:S(2)}) collective-permute-start(f32[128,128]{1,0:T(8,128)S(1)} %get-tuple-element.81), channel_id=1, source_target_pairs={{0,4},{4,0},{8,12},{12,8},{16,20},{20,16},{24,28},{28,24},{1,5},{5... | collective-permute-start | bytes 196616 | tf_op jit(solution)/shard_map/ppermute | solution.py:477
  43.2 14.7 %collective-permute-start.15 = (f32[64,2048]{1,0:T(8,128)S(1)}, f32[64,2048]{1,0:T(8,128)S(1)}, u32[]{:S(2)}, u32[]{:S(2)}) collective-permute-start(f32[64,2048]{1,0:T(8,128)S(1)} %get-tuple-element.84), channel_id=1, source_target_pairs={{0,1},{3,2},{4,5},{7,6},{8,9},{11,10},{12,13},{15,14},{16,17},{19,... | collective-permute-start | bytes 1572872 | tf_op jit(solution)/shard_map/ppermute | solution.py:542
  46.7 14.9 %collective-permute-start.14 = (f32[64,2048]{1,0:T(8,128)S(1)}, f32[64,2048]{1,0:T(8,128)S(1)}, u32[]{:S(2)}, u32[]{:S(2)}) collective-permute-start(f32[64,2048]{1,0:T(8,128)S(1)} %get-tuple-element.84), channel_id=1, source_target_pairs={{1,2},{2,1},{5,6},{6,5},{9,10},{10,9},{13,14},{14,13},{17,18},{18,... | collective-permute-start | bytes 1572872 | tf_op jit(solution)/shard_map/ppermute | solution.py:543
  58.0 24.8 %collective-permute-start.16 = (f32[64,2048]{1,0:T(8,128)S(1)}, f32[64,2048]{1,0:T(8,128)S(1)}, u32[]{:S(2)}, u32[]{:S(2)}) collective-permute-start(f32[64,2048]{1,0:T(8,128)S(1)} %hand_on.1), channel_id=1, source_target_pairs={{0,1},{1,0},{2,3},{3,2},{4,5},{5,4},{6,7},{7,6},{8,9},{9,8},{10,11... | collective-permute-start | bytes 1572872 | tf_op jit(solution)/shard_map/ppermute | solution.py:561
  60.5 24.8 %collective-permute-start.17 = (f32[64,2048]{1,0:T(8,128)S(1)}, f32[64,2048]{1,0:T(8,128)S(1)}, u32[]{:S(2)}, u32[]{:S(2)}) collective-permute-start(f32[64,2048]{1,0:T(8,128)S(1)} %forward.1.__), channel_id=1, source_target_pairs={{0,2},{1,3},{2,0},{3,1},{4,6},{5,7},{6,4},{7,5},{8,10},{9,11},{10,... | collective-permute-start | bytes 1572872 | tf_op jit(solution)/shard_map/ppermute | solution.py:562

commit v12 on v11

--- a/solution.py
+++ b/solution.py
@@ -12,8 +12,8 @@
 DV = 128
 BLOCK = 128
 SMALL = 32
-BAND = 256
-SWAP_ORDER = (7, 6, 5, 4, 3, 2, 1)
+BAND = 512
+SWAP_ORDER = (1, 7, 6, 5, 4, 3, 2)
 WEIGHT_ROWS = 256
 MOST_VMEM = 56
 MAP_VMEM = 53.75

time: 86.5 us -> 87 us (level)
  waiting for transfers between devices: 34.2 us -> 35.2 us
where the time goes in v12:
time: 87 us; the launch traced here: 86.7 us
  waiting for transfers between devices  35.2 us (40%)
  Pallas kernels  27.4 us (31%)
  starting transfers between devices  23.2 us (27%)
  other arithmetic  0.92 us (1%)
    ppermute x1, waiting for transfers between devices, project_and_sum(): from_near = lax.ppermute(near, axis, [(i, i ^ 1) for i in range(4)])  21.4 us
    ppermute x14, starting transfers between devices, partners_swap(): lax.ppermute(array, axis, [(d, d ^ i) for d in range(count)])  15.3 us
    pallas_call x2, Pallas kernels, project(): pl.pallas_call(functools.partial(projection_kernel, pieces=[(index, start...  11.3 us
    pallas_call x1, Pallas kernels, per_device(): pl.pallas_call(functools.partial(summary_kernel, swap=swap.heads), in_spe...  9.52 us
    ppermute x14, waiting for transfers between devices, partners_swap(): lax.ppermute(array, axis, [(d, d ^ i) for d in range(count)])  6.79 us
    pallas_call x1, Pallas kernels, per_device(): pl.pallas_call(output_kernel, in_specs=[HBM] * 3, out_specs=[HBM, VMEM],...  5.31 us
    ppermute x1, waiting for transfers between devices, project_and_sum(): from_end = lax.ppermute(opposite, axis, [(0, 1), (3, 2)])  4.51 us
    ppermute x1, starting transfers between devices, project_and_sum(): from_end = lax.ppermute(opposite, axis, [(0, 1), (3, 2)])  3.51 us
  transfers between devices with their start and end apart: 18, of which 10 were waited for; matrix products, arithmetic and copies ran while one was open for 0% of the time, Pallas kernels for 13%

profile of v12, /device:TPU:0, one launch (start us, length us, event | category | flops | bytes accessed | tf_op | source)
XLA Modules:
  0.0 86.7 jit_solution(9341249188101184018)
XLA Ops:
  0.0 9.5 %state_summary.1 = (f32[9,256,256]{2,1,0:T(8,128)}, f32[128,256]{1,0:T(8,128)}, f32[128,256]{1,0:T(8,128)}, f32[128,256]{1,0:T(8,128)}, f32[128,256]{1,0:T(8,128...) custom-call(f32[8,256]{1,0:T(8,128)} %decay_hbm.1, f32[8,256]{1,0:T(8,128)} %strength_hbm.1, ...), custom_call_target="tpu_custom_call" | custom-call | tf_op jit(solution)/shard_map/state_summary/pallas_call | solution.py:586
  9.5 0.5 collective-permute-start
  10.0 3.6 %collective-permute-start.1 = (f32[128,256]{1,0:T(8,128)}, f32[128,256]{1,0:T(8,128)S(1)}, u32[]{:S(2)}, u32[]{:S(2)}) collective-permute-start(f32[128,256]{1,0:T(8,128)} %get-tuple-element.49), channel_id=1, source_target_pairs={{0,28},{4,24},{8,20},{12,16},{16,12},{20,8},{24,4},{28,0},{1,29},{... | collective-permute-start | bytes 393224 | tf_op jit(solution)/shard_map/ppermute | solution.py:477
  13.6 0.0 collective-permute-start.2
  13.7 1.3 %collective-permute-start.3 = (f32[128,256]{1,0:T(8,128)}, f32[128,256]{1,0:T(8,128)S(1)}, u32[]{:S(2)}, u32[]{:S(2)}) collective-permute-start(f32[128,256]{1,0:T(8,128)} %get-tuple-element.51), channel_id=1, source_target_pairs={{0,20},{4,16},{8,28},{12,24},{16,4},{20,0},{24,12},{28,8},{1,21},{... | collective-permute-start | bytes 393224 | tf_op jit(solution)/shard_map/ppermute | solution.py:477
  15.0 0.6 collective-permute-start.4
  15.7 0.0 collective-permute-done.rest_1_
  15.7 1.4 %collective-permute-start.5 = (f32[128,256]{1,0:T(8,128)}, f32[128,256]{1,0:T(8,128)S(1)}, u32[]{:S(2)}, u32[]{:S(2)}) collective-permute-start(f32[128,256]{1,0:T(8,128)} %get-tuple-element.53), channel_id=1, source_target_pairs={{0,12},{4,8},{8,4},{12,0},{16,28},{20,24},{24,20},{28,16},{1,13},{... | collective-permute-start | bytes 393224 | tf_op jit(solution)/shard_map/ppermute | solution.py:477
  17.1 0.7 collective-permute-done.1.rest_2_
  17.8 1.2 %collective-permute-start.6 = (f32[128,256]{1,0:T(8,128)}, f32[128,256]{1,0:T(8,128)S(1)}, u32[]{:S(2)}, u32[]{:S(2)}) collective-permute-start(f32[128,256]{1,0:T(8,128)} %get-tuple-element.54), channel_id=1, source_target_pairs={{0,8},{4,12},{8,0},{12,4},{16,24},{20,28},{24,16},{28,20},{1,9},{5... | collective-permute-start | bytes 393224 | tf_op jit(solution)/shard_map/ppermute | solution.py:477
  19.0 5.3 %output_maps.1 = (f32[64,256,256]{2,1,0:T(8,128)}, f32[128,256]{1,0:T(8,128)S(1)}) custom-call(f32[256,512]{1,0:T(8,128)} %q_hbm.1, f32[256,512]{1,0:T(8,128)} %k_hbm.3, f32[9,256,256]{2,1,0:T(8,128)} %get-tuple-element.46.factor_hbm), custom_call_target="tpu_custom_call" | custom-call | flops 1207959552 | bytes 5242880 | tf_op jit(solution)/shard_map/output_maps/pallas_call | solution.py:597
  24.3 0.0 collective-permute-done.2.rest_3_
  24.3 0.0 collective-permute-done.3.rest_4_
  24.3 2.0 %collective-permute-done.4.rest_5_ = f32[128,256]{1,0:T(8,128)S(1)} collective-permute-done((f32[128,256]{1,0:T(8,128)}, f32[128,256]{1,0:T(8,128)S(1)}, u32[]{:S(2)}, u32[]{:S(2)}) %collective-permute-start.4) | collective-permute-done | bytes 131104 | tf_op jit(solution)/shard_map/ppermute | solution.py:477
  26.3 0.0 collective-permute-done.5.rest_6_
  26.3 0.3 collective-permute-done.6.rest_7_
  26.6 0.0 copy-start
  26.6 0.0 copy-start.1
  26.6 1.1 %state_scan.1 = (f32[128,128]{1,0:T(8,128)S(1)}, f32[128,128]{1,0:T(8,128)S(1)}, f32[128,128]{1,0:T(8,128)S(1)}, f32[128,128]{1,0:T(8,128)S(1)}, f32[128,128]{1,...) custom-call(f32[64,256,256]{2,1,0:T(8,128)} %get-tuple-element.56._.map_hbm, ...), custom_call_target="tpu_custom_call" | custom-call | tf_op jit(solution)/shard_map/state_scan/pallas_call | solution.py:498
  27.7 0.1 collective-permute-start.7
  27.8 2.5 %collective-permute-start.8 = (f32[128,128]{1,0:T(8,128)S(1)}, f32[128,128]{1,0:T(8,128)S(1)}, u32[]{:S(2)}, u32[]{:S(2)}) collective-permute-start(f32[128,128]{1,0:T(8,128)S(1)} %get-tuple-element.76), channel_id=1, source_target_pairs={{0,28},{4,24},{8,20},{12,16},{16,12},{20,8},{24,4},{28,0},{1,29},{... | collective-permute-start | bytes 196616 | tf_op jit(solution)/shard_map/ppermute | solution.py:477
  30.2 0.6 collective-permute-start.9
  30.8 0.9 %collective-permute-start.10 = (f32[128,128]{1,0:T(8,128)S(1)}, f32[128,128]{1,0:T(8,128)S(1)}, u32[]{:S(2)}, u32[]{:S(2)}) collective-permute-start(f32[128,128]{1,0:T(8,128)S(1)} %get-tuple-element.78), channel_id=1, source_target_pairs={{0,20},{4,16},{8,28},{12,24},{16,4},{20,0},{24,12},{28,8},{1,21},{... | collective-permute-start | bytes 196616 | tf_op jit(solution)/shard_map/ppermute | solution.py:477
  31.7 0.6 collective-permute-start.11
  32.3 0.0 collective-permute-done.7.rest_1_
  32.3 1.5 %collective-permute-start.12 = (f32[128,128]{1,0:T(8,128)S(1)}, f32[128,128]{1,0:T(8,128)S(1)}, u32[]{:S(2)}, u32[]{:S(2)}) collective-permute-start(f32[128,128]{1,0:T(8,128)S(1)} %get-tuple-element.80), channel_id=1, source_target_pairs={{0,12},{4,8},{8,4},{12,0},{16,28},{20,24},{24,20},{28,16},{1,13},{... | collective-permute-start | bytes 196616 | tf_op jit(solution)/shard_map/ppermute | solution.py:477
  33.8 0.0 collective-permute-done.8.rest_2_
  33.8 0.5 collective-permute-start.13
  34.3 1.1 %collective-permute-done.9.rest_3_ = f32[128,128]{1,0:T(8,128)S(1)} collective-permute-done((f32[128,128]{1,0:T(8,128)S(1)}, f32[128,128]{1,0:T(8,128)S(1)}, u32[]{:S(2)}, u32[]{:S(2)}) %collective-permute-start.9) | collective-permute-done | bytes 65568 | tf_op jit(solution)/shard_map/ppermute | solution.py:477
  35.5 1.1 %collective-permute-done.10.rest_4_ = f32[128,128]{1,0:T(8,128)S(1)} collective-permute-done((f32[128,128]{1,0:T(8,128)S(1)}, f32[128,128]{1,0:T(8,128)S(1)}, u32[]{:S(2)}, u32[]{:S(2)}) %collective-permute-start.10) | collective-permute-done | bytes 65568 | tf_op jit(solution)/shard_map/ppermute | solution.py:477
  36.6 1.4 %collective-permute-done.11.rest_5_ = f32[128,128]{1,0:T(8,128)S(1)} collective-permute-done((f32[128,128]{1,0:T(8,128)S(1)}, f32[128,128]{1,0:T(8,128)S(1)}, u32[]{:S(2)}, u32[]{:S(2)}) %collective-permute-start.11) | collective-permute-done | bytes 65568 | tf_op jit(solution)/shard_map/ppermute | solution.py:477
  38.0 0.0 collective-permute-done.12.rest_6_
  38.0 0.1 collective-permute-done.13.rest_7_
  38.1 0.0 copy-done
  38.1 0.0 copy-done.1
  38.1 5.2 %projection.2 = (f32[64,2048]{1,0:T(8,128)S(1)}, bf16[2,1024,2048]{2,1,0:T(8,128)(2,1)S(1)}) custom-call(f32[64,256,256]{2,1,0:T(8,128)} %get-tuple-element.56._.map_hbm, f32[256,1024]{1,0:T(8,128)S(1)} %copy-done, f32[1,128]{1,0:T(1,128)S(1)} %bitcast.1, f32[1024,2048]{1,0:T(8,128)} %weight_ref, f32[128,128]{1,0:T(8,128)S(1)} %get-tuple-element.74.rest_0_, ...), custom_call_target="tpu_custom_call" | custom-call | flops 805306368 | bytes 8388608 | tf_op jit(solution)/shard_map/projection/pallas_call | solution.py:621
  43.3 3.5 %collective-permute-start.15 = (f32[64,2048]{1,0:T(8,128)S(1)}, f32[64,2048]{1,0:T(8,128)S(1)}, u32[]{:S(2)}, u32[]{:S(2)}) collective-permute-start(f32[64,2048]{1,0:T(8,128)S(1)} %get-tuple-element.84), channel_id=1, source_target_pairs={{0,1},{3,2},{4,5},{7,6},{8,9},{11,10},{12,13},{15,14},{16,17},{19,... | collective-permute-start | bytes 1572872 | tf_op jit(solution)/shard_map/ppermute | solution.py:542
  46.8 0.7 collective-permute-start.14
  47.5 6.2 %projection.3 = (f32[64,2048]{1,0:T(8,128)S(1)}, f32[64,2048]{1,0:T(8,128)S(1)}, f32[64,2048]{1,0:T(8,128)S(1)}) custom-call(f32[64,256,256]{2,1,0:T(8,128)} %get-tuple-element.56._.map_hbm, f32[256,1024]{1,0:T(8,128)S(1)} %copy-done, f32[1,128]{1,0:T(1,128)S(1)} %bitcast.2, bf16[2,1024,2048]{2,1,0:T(8,128)(2,1)S(1)} %get-tuple-element.82.weight_ref, ...), custom_call_target="tpu_custom_call" | custom-call | flops 2415919104 | bytes 8388608 | tf_op jit(solution)/shard_map/projection/pallas_call | solution.py:621
  53.7 4.5 %collective-permute-done.15.end_ref = f32[64,2048]{1,0:T(8,128)S(1)} collective-permute-done((f32[64,2048]{1,0:T(8,128)S(1)}, f32[64,2048]{1,0:T(8,128)S(1)}, u32[]{:S(2)}, u32[]{:S(2)}) %collective-permute-start.15) | collective-permute-done | bytes 524320 | tf_op jit(solution)/shard_map/ppermute | solution.py:542
  58.2 0.1 forward.1.__
  58.3 2.5 %collective-permute-start.16 = (f32[64,2048]{1,0:T(8,128)S(1)}, f32[64,2048]{1,0:T(8,128)S(1)}, u32[]{:S(2)}, u32[]{:S(2)}) collective-permute-start(f32[64,2048]{1,0:T(8,128)S(1)} %hand_on.1), channel_id=1, source_target_pairs={{0,1},{1,0},{2,3},{3,2},{4,5},{5,4},{6,7},{7,6},{8,9},{9,8},{10,11... | collective-permute-start | bytes 1572872 | tf_op jit(solution)/shard_map/ppermute | solution.py:561
  60.8 1.1 %collective-permute-start.17 = (f32[64,2048]{1,0:T(8,128)S(1)}, f32[64,2048]{1,0:T(8,128)S(1)}, u32[]{:S(2)}, u32[]{:S(2)}) collective-permute-start(f32[64,2048]{1,0:T(8,128)S(1)} %forward.1.__), channel_id=1, source_target_pairs={{0,2},{1,3},{2,0},{3,1},{4,6},{5,7},{6,4},{7,5},{8,10},{9,11},{10,... | collective-permute-start | bytes 1572872 | tf_op jit(solution)/shard_map/ppermute | solution.py:562
  61.9 0.0 collective-permute-done.14
  61.9 21.4 %collective-permute-done.16 = f32[64,2048]{1,0:T(8,128)S(1)} collective-permute-done((f32[64,2048]{1,0:T(8,128)S(1)}, f32[64,2048]{1,0:T(8,128)S(1)}, u32[]{:S(2)}, u32[]{:S(2)}) %collective-permute-start.16) | collective-permute-done | bytes 524320 | tf_op jit(solution)/shard_map/ppermute | solution.py:561
  83.4 2.4 %collective-permute-done.17 = f32[64,2048]{1,0:T(8,128)S(1)} collective-permute-done((f32[64,2048]{1,0:T(8,128)S(1)}, f32[64,2048]{1,0:T(8,128)S(1)}, u32[]{:S(2)}, u32[]{:S(2)}) %collective-permute-start.17) | collective-permute-done | bytes 524320 | tf_op jit(solution)/shard_map/ppermute | solution.py:562
  85.8 0.9 %add_add_fusion = f32[64,2048]{1,0:T(8,128)} fusion(f32[64,2048]{1,0:T(8,128)S(1)} %collective-permute-done.17, f32[64,2048]{1,0:T(8,128)S(1)} %collective-permute-done.16, f32[64,2048]{1,0:T(8,128)S(1)} %get-tuple-element.83, f32[64,2048]{1,0:T(8,128)S(1)} %collective-permute-done.14), kind=kLoop, calls=%fused_computation | loop fusion | flops 393216 | bytes 2621440 | tf_op jit(solution)/shard_map/add | solution.py:563
  (1 shorter events, 0.0 us)
Async XLA Ops:
  9.5 6.1 %collective-permute-start = (f32[128,256]{1,0:T(8,128)}, f32[128,256]{1,0:T(8,128)S(1)}, u32[]{:S(2)}, u32[]{:S(2)}) collective-permute-start(f32[128,256]{1,0:T(8,128)} %get-tuple-element.48), channel_id=1, source_target_pairs={{0,4},{4,0},{8,12},{12,8},{16,20},{20,16},{24,28},{28,24},{1,5},{5... | collective-permute-start | bytes 393224 | tf_op jit(solution)/shard_map/ppermute | solution.py:477
  10.0 7.7 %collective-permute-start.1 = (f32[128,256]{1,0:T(8,128)}, f32[128,256]{1,0:T(8,128)S(1)}, u32[]{:S(2)}, u32[]{:S(2)}) collective-permute-start(f32[128,256]{1,0:T(8,128)} %get-tuple-element.49), channel_id=1, source_target_pairs={{0,28},{4,24},{8,20},{12,16},{16,12},{20,8},{24,4},{28,0},{1,29},{... | collective-permute-start | bytes 393224 | tf_op jit(solution)/shard_map/ppermute | solution.py:477
  13.6 10.7 %collective-permute-start.2 = (f32[128,256]{1,0:T(8,128)}, f32[128,256]{1,0:T(8,128)S(1)}, u32[]{:S(2)}, u32[]{:S(2)}) collective-permute-start(f32[128,256]{1,0:T(8,128)} %get-tuple-element.50), channel_id=1, source_target_pairs={{0,24},{4,28},{8,16},{12,20},{16,8},{20,12},{24,0},{28,4},{1,25},{... | collective-permute-start | bytes 393224 | tf_op jit(solution)/shard_map/ppermute | solution.py:477
  13.7 10.6 %collective-permute-start.3 = (f32[128,256]{1,0:T(8,128)}, f32[128,256]{1,0:T(8,128)S(1)}, u32[]{:S(2)}, u32[]{:S(2)}) collective-permute-start(f32[128,256]{1,0:T(8,128)} %get-tuple-element.51), channel_id=1, source_target_pairs={{0,20},{4,16},{8,28},{12,24},{16,4},{20,0},{24,12},{28,8},{1,21},{... | collective-permute-start | bytes 393224 | tf_op jit(solution)/shard_map/ppermute | solution.py:477
  15.0 11.3 %collective-permute-start.4 = (f32[128,256]{1,0:T(8,128)}, f32[128,256]{1,0:T(8,128)S(1)}, u32[]{:S(2)}, u32[]{:S(2)}) collective-permute-start(f32[128,256]{1,0:T(8,128)} %get-tuple-element.52), channel_id=1, source_target_pairs={{0,16},{4,20},{8,24},{12,28},{16,0},{20,4},{24,8},{28,12},{1,17},{... | collective-permute-start | bytes 393224 | tf_op jit(solution)/shard_map/ppermute | solution.py:477
  15.7 10.6 %collective-permute-start.5 = (f32[128,256]{1,0:T(8,128)}, f32[128,256]{1,0:T(8,128)S(1)}, u32[]{:S(2)}, u32[]{:S(2)}) collective-permute-start(f32[128,256]{1,0:T(8,128)} %get-tuple-element.53), channel_id=1, source_target_pairs={{0,12},{4,8},{8,4},{12,0},{16,28},{20,24},{24,20},{28,16},{1,13},{... | collective-permute-start | bytes 393224 | tf_op jit(solution)/shard_map/ppermute | solution.py:477
  17.8 8.8 %collective-permute-start.6 = (f32[128,256]{1,0:T(8,128)}, f32[128,256]{1,0:T(8,128)S(1)}, u32[]{:S(2)}, u32[]{:S(2)}) collective-permute-start(f32[128,256]{1,0:T(8,128)} %get-tuple-element.54), channel_id=1, source_target_pairs={{0,8},{4,12},{8,0},{12,4},{16,24},{20,28},{24,16},{28,20},{1,9},{5... | collective-permute-start | bytes 393224 | tf_op jit(solution)/shard_map/ppermute | solution.py:477
  26.6 11.6 %copy-start = (f32[256,1024]{1,0:T(8,128)S(1)}, f32[256,1024]{1,0:T(8,128)}, u32[]{:S(2)}) copy-start(f32[256,1024]{1,0:T(8,128)} %gate_hbm.3) | copy-start | bytes 3145732
  26.6 11.6 %copy-start.1 = (f32[128]{0:T(128)S(1)}, f32[128]{0:T(128)}, u32[]{:S(2)}) copy-start(f32[128]{0:T(128)} %param.14) | copy-start | bytes 1540
  27.7 4.6 %collective-permute-start.7 = (f32[128,128]{1,0:T(8,128)S(1)}, f32[128,128]{1,0:T(8,128)S(1)}, u32[]{:S(2)}, u32[]{:S(2)}) collective-permute-start(f32[128,128]{1,0:T(8,128)S(1)} %get-tuple-element.75), channel_id=1, source_target_pairs={{0,4},{4,0},{8,12},{12,8},{16,20},{20,16},{24,28},{28,24},{1,5},{5... | collective-permute-start | bytes 196616 | tf_op jit(solution)/shard_map/ppermute | solution.py:477
  27.8 6.0 %collective-permute-start.8 = (f32[128,128]{1,0:T(8,128)S(1)}, f32[128,128]{1,0:T(8,128)S(1)}, u32[]{:S(2)}, u32[]{:S(2)}) collective-permute-start(f32[128,128]{1,0:T(8,128)S(1)} %get-tuple-element.76), channel_id=1, source_target_pairs={{0,28},{4,24},{8,20},{12,16},{16,12},{20,8},{24,4},{28,0},{1,29},{... | collective-permute-start | bytes 196616 | tf_op jit(solution)/shard_map/ppermute | solution.py:477
  30.2 5.2 %collective-permute-start.9 = (f32[128,128]{1,0:T(8,128)S(1)}, f32[128,128]{1,0:T(8,128)S(1)}, u32[]{:S(2)}, u32[]{:S(2)}) collective-permute-start(f32[128,128]{1,0:T(8,128)S(1)} %get-tuple-element.77), channel_id=1, source_target_pairs={{0,24},{4,28},{8,16},{12,20},{16,8},{20,12},{24,0},{28,4},{1,25},{... | collective-permute-start | bytes 196616 | tf_op jit(solution)/shard_map/ppermute | solution.py:477
  30.8 5.8 %collective-permute-start.10 = (f32[128,128]{1,0:T(8,128)S(1)}, f32[128,128]{1,0:T(8,128)S(1)}, u32[]{:S(2)}, u32[]{:S(2)}) collective-permute-start(f32[128,128]{1,0:T(8,128)S(1)} %get-tuple-element.78), channel_id=1, source_target_pairs={{0,20},{4,16},{8,28},{12,24},{16,4},{20,0},{24,12},{28,8},{1,21},{... | collective-permute-start | bytes 196616 | tf_op jit(solution)/shard_map/ppermute | solution.py:477
  31.7 6.3 %collective-permute-start.11 = (f32[128,128]{1,0:T(8,128)S(1)}, f32[128,128]{1,0:T(8,128)S(1)}, u32[]{:S(2)}, u32[]{:S(2)}) collective-permute-start(f32[128,128]{1,0:T(8,128)S(1)} %get-tuple-element.79), channel_id=1, source_target_pairs={{0,16},{4,20},{8,24},{12,28},{16,0},{20,4},{24,8},{28,12},{1,17},{... | collective-permute-start | bytes 196616 | tf_op jit(solution)/shard_map/ppermute | solution.py:477
  32.3 5.7 %collective-permute-start.12 = (f32[128,128]{1,0:T(8,128)S(1)}, f32[128,128]{1,0:T(8,128)S(1)}, u32[]{:S(2)}, u32[]{:S(2)}) collective-permute-start(f32[128,128]{1,0:T(8,128)S(1)} %get-tuple-element.80), channel_id=1, source_target_pairs={{0,12},{4,8},{8,4},{12,0},{16,28},{20,24},{24,20},{28,16},{1,13},{... | collective-permute-start | bytes 196616 | tf_op jit(solution)/shard_map/ppermute | solution.py:477
  33.8 4.3 %collective-permute-start.13 = (f32[128,128]{1,0:T(8,128)S(1)}, f32[128,128]{1,0:T(8,128)S(1)}, u32[]{:S(2)}, u32[]{:S(2)}) collective-permute-start(f32[128,128]{1,0:T(8,128)S(1)} %get-tuple-element.81), channel_id=1, source_target_pairs={{0,8},{4,12},{8,0},{12,4},{16,24},{20,28},{24,16},{28,20},{1,9},{5... | collective-permute-start | bytes 196616 | tf_op jit(solution)/shard_map/ppermute | solution.py:477
  43.3 14.9 %collective-permute-start.15 = (f32[64,2048]{1,0:T(8,128)S(1)}, f32[64,2048]{1,0:T(8,128)S(1)}, u32[]{:S(2)}, u32[]{:S(2)}) collective-permute-start(f32[64,2048]{1,0:T(8,128)S(1)} %get-tuple-element.84), channel_id=1, source_target_pairs={{0,1},{3,2},{4,5},{7,6},{8,9},{11,10},{12,13},{15,14},{16,17},{19,... | collective-permute-start | bytes 1572872 | tf_op jit(solution)/shard_map/ppermute | solution.py:542
  46.8 15.1 %collective-permute-start.14 = (f32[64,2048]{1,0:T(8,128)S(1)}, f32[64,2048]{1,0:T(8,128)S(1)}, u32[]{:S(2)}, u32[]{:S(2)}) collective-permute-start(f32[64,2048]{1,0:T(8,128)S(1)} %get-tuple-element.84), channel_id=1, source_target_pairs={{1,2},{2,1},{5,6},{6,5},{9,10},{10,9},{13,14},{14,13},{17,18},{18,... | collective-permute-start | bytes 1572872 | tf_op jit(solution)/shard_map/ppermute | solution.py:543
  58.3 25.1 %collective-permute-start.16 = (f32[64,2048]{1,0:T(8,128)S(1)}, f32[64,2048]{1,0:T(8,128)S(1)}, u32[]{:S(2)}, u32[]{:S(2)}) collective-permute-start(f32[64,2048]{1,0:T(8,128)S(1)} %hand_on.1), channel_id=1, source_target_pairs={{0,1},{1,0},{2,3},{3,2},{4,5},{5,4},{6,7},{7,6},{8,9},{9,8},{10,11... | collective-permute-start | bytes 1572872 | tf_op jit(solution)/shard_map/ppermute | solution.py:561
  60.8 25.0 %collective-permute-start.17 = (f32[64,2048]{1,0:T(8,128)S(1)}, f32[64,2048]{1,0:T(8,128)S(1)}, u32[]{:S(2)}, u32[]{:S(2)}) collective-permute-start(f32[64,2048]{1,0:T(8,128)S(1)} %forward.1.__), channel_id=1, source_target_pairs={{0,2},{1,3},{2,0},{3,1},{4,6},{5,7},{6,4},{7,5},{8,10},{9,11},{10,... | collective-permute-start | bytes 1572872 | tf_op jit(solution)/shard_map/ppermute | solution.py:562
